TPU v7x, 256 devices: a whole 4x4x8 slice. The times are simulated.
256 devices in a mesh: pair: 8 (over y, z_hi), pw: 32 (over x, z_lo, core).
Axes of the slice: x: 4, y: 4, z: 8 (z_hi: 2, z_lo: 4; z = z_hi * 4 + z_lo), core: 2. Of those that a mesh axis runs over, the one named last changes fastest.
Arguments:
- pair_elements: bfloat16 [32768, 32768], P('pair', 'pw'), may hold values from -6 to 6
- subspace: bfloat16 [32768, 512], P('pw'), may hold values from -0.03125 to 0.03125
- val_energy: float32 [16], replicated, may hold values from -10 to -1
- cond_energy: float32 [2048], replicated, may hold values from 0.5 to 12
- val_index: int32 [32768], P('pair'), may hold values from 0 to 15, as said below
- cond_index: int32 [32768], P('pair'), may hold values from 0 to 2047, as said below
- frequencies: float32 [32], P('pw'), may hold values from 0.1 to 30
Outputs:
- chi: float32 [32, 512, 512], P('pw', 'pair')
Inputs may be any that keep to these rules, and one draw needn't show every extreme that they name: `val_index`: every combination of a valence band and a conduction band is named by exactly one pair. `cond_index`: every combination of a valence band and a conduction band is named by exactly one pair.
All inputs are finite; a program needn't handle non-finite values.
Results may differ from a plain program's by a relative error of at most 0.00067.
Values may be sent and summed in bfloat16 or wider, within the bound.
No kernel may reach another device: no remote copies, remote signals or barrier semaphores. Data moves between devices by JAX's collectives and lax.ppermute only.
A program may use at most 64 MiB of HBM per device.

v0:
```python
import jax
import jax.numpy as jnp
from jax import lax
from jax.sharding import Mesh
from jax.sharding import PartitionSpec as P

PW = ("pw_0", "pw_1", "pw_2")


def split_up(value, dim, count):
    before, after = (value.shape[:dim], value.shape[dim + 1 :])
    return jnp.moveaxis(value.reshape(*before, count, -1, *after), dim, 0)


def scatter_pairs(value, chips, core, dim):
    sizes = (lax.axis_size(chips), lax.axis_size(core))
    pieces = split_up(value, dim, sizes[0] * sizes[1])
    inside = pieces.shape[1:]
    pieces = pieces.reshape(*sizes, *inside).swapaxes(0, 1).reshape(-1, *inside)
    pieces = lax.psum_scatter(pieces, core, scatter_dimension=0, tiled=True)
    return lax.psum_scatter(pieces, chips, scatter_dimension=0, tiled=True)[0]


def summed_on_arrival(value, axis, dim):
    count = lax.axis_size(axis)
    pieces = lax.all_to_all(split_up(value, dim, count), axis, 0, 0, tiled=True)
    return jnp.sum(pieces, axis=0)


def lookup(indices, table):
    levels = jnp.arange(table.shape[0], dtype=jnp.int32)
    return jnp.sum(jnp.where(indices[:, None] == levels[None, :], table[None, :], 0.0), axis=1)


def partial_gram(weights, rows):
    weighted = (weights.T[:, :, None] * rows.astype(jnp.float32)[None, :, :]).astype(jnp.bfloat16)
    return jnp.einsum("fps,pt->fst", weighted, rows, preferred_element_type=jnp.float32)


def on_device(pair_elements, subspace, val_energy, cond_energy, val_index, cond_index, frequencies):
    spacing = cond_energy[cond_index] - lookup(val_index, val_energy)
    weights = 2.0 * spacing[:, None] / (spacing[:, None] ** 2 + frequencies[None, :] ** 2)
    partial_value = jnp.dot(pair_elements, subspace, preferred_element_type=jnp.float32)
    local_pairs = pair_elements.shape[0]
    reduced = scatter_pairs(partial_value, ("pw_0", "pw_1"), "pw_2", 0).astype(jnp.bfloat16)
    gram_part = partial_gram(weights, lax.all_gather(reduced, PW, axis=0, tiled=True))
    summed_gram = summed_on_arrival(gram_part, "pair", 1)
    factor = -4.0 / (local_pairs * lax.axis_size("pair"))
    return summed_gram * factor


def solution(mesh):
    torus = Mesh(
        mesh.devices.reshape(mesh.shape["pair"], 4, 4, 2), ("pair", "pw_0", "pw_1", "pw_2")
    )
    return jax.shard_map(
        on_device,
        mesh=torus,
        in_specs=(P("pair", PW), P(PW, None), P(), P(), P("pair"), P("pair"), P(PW)),
        out_specs=P(PW, "pair", None),
        check_vma=False,
    )
```

profile of v0, /device:TPU:32, one launch (start us, length us, event | category | flops | bytes accessed | tf_op | source)
XLA Modules:
  0.0 275.7 jit_solution(7520206302714443325)
XLA Ops:
  6.5 0.0 copy-start
  6.5 0.0 reduce-scatter.3.cloned.1.call-start
  6.5 1.2 copy-done
  7.8 6.9 %fusion.7 = f32[4096,512]{1,0:T(8,128)S(1)} fusion(bf16[4096,1024]{1,0:T(8,128)(2,1)} %param.7, bf16[1024,512]{1,0:T(8,128)(2,1)S(1)} %copy-done), kind=kOutput, calls=%fused_computation.12 | convolution fusion | flops 4294967296 | bytes 17825792 | tf_op jit(solution)/shard_map/dot_general | solution.py:43
  14.7 4.2 %copy.15 = f32[2,16,128,512]{3,2,1,0:T(8,128)} copy(f32[2,16,128,512]{3,2,0,1:T(8,128)S(1)} %bitcast.25) | data formatting | bytes 16777216 | tf_op jit(solution)/shard_map/transpose | solution.py:19
  18.9 0.0 reduce-scatter.3.cloned.1.call-update
  19.0 0.0 copy-start.2
  19.0 0.0 copy-start.1
  19.0 0.0 reduce-scatter.5.cloned.1.call-start
  19.0 24.9 %reduce-scatter.3.cloned.1.call-done = f32[16,128,512]{2,1,0:T(8,128)} async-done(((f32[32,128,512]{2,1,0:T(8,128)}), f32[16,128,512]{2,1,0:T(8,128)}) %reduce-scatter.3.cloned.1.call-update) | async-done | bytes 4194320 | tf_op jit(solution)/shard_map/reduce_scatter | solution.py:20
  44.0 0.0 reduce-scatter.5.cloned.1.call-update
  44.0 0.0 all-gather.3.cloned.1.call-start
  44.0 105.0 %reduce-scatter.5.cloned.1.call-done = f32[1,128,512]{2,1,0:T(8,128)} async-done(((f32[16,128,512]{2,1,0:T(8,128)}), f32[1,128,512]{2,1,0:T(8,128)}) %reduce-scatter.5.cloned.1.call-update) | async-done | bytes 262160 | tf_op jit(solution)/shard_map/reduce_scatter | solution.py:21
  149.0 1.6 convert_element_type.13
  150.6 0.0 all-gather.3.cloned.1.call-update
  151.3 0.0 copy-done.2
  151.3 0.0 copy-done.1
  151.4 0.0 copy-start.3
  151.4 0.0 copy-start.4
  151.4 23.0 %gather_fusion = f32[4096]{0:T(1024)S(1)} fusion(f32[2048]{0:T(1024)S(1)} %copy-done.1, s32[4096]{0:T(1024)S(1)} %fusion.6), kind=kCustom, calls=%fused_computation | custom fusion | bytes 49152 | tf_op jit(solution)/shard_map/gather | solution.py:41
  174.4 0.0 copy-done.3
  174.4 0.0 copy-done.4
  174.4 0.1 select_reduce_fusion
  174.6 38.8 %all-gather.3.cloned.1.call-done = bf16[1,4096,512]{2,1,0:T(8,128)(2,1)} async-done(((bf16[1,128,512]{2,1,0:T(8,128)(2,1)}), bf16[1,4096,512]{2,1,0:T(8,128)(2,1)}) %all-gather.3.cloned.1.call-update) | async-done | bytes 4194320 | tf_op jit(solution)/shard_map/all_gather | solution.py:46
  213.4 4.0 %fusion = bf16[512,4096]{0,1:T(8,128)(2,1)} fusion(bf16[1,4096,512]{2,1,0:T(8,128)(2,1)} %all-gather.3.cloned.1.call-done, f32[4096]{0:T(1024)S(1)} %add_divide_fusion), kind=kLoop, calls=%fused_computation.2 | loop fusion | flops 6291456 | bytes 8404992 | tf_op jit(solution)/shard_map/fps,pt->fst/dot_general | solution.py:37
  217.4 6.5 %copy.16 = bf16[512,4096]{1,0:T(8,128)(2,1)} copy(bf16[512,4096]{0,1:T(8,128)(2,1)} %fusion) | data formatting | bytes 8388608 | tf_op jit(solution)/shard_map/fps,pt->fst/dot_general | solution.py:37
  223.9 5.8 %fusion.3 = f32[8,1,64,512]{3,2,1,0:T(8,128)S(1)} fusion(bf16[8,64,4096]{2,1,0:T(8,128)(2,1)} %bitcast.26, bf16[1,4096,512]{2,1,0:T(8,128)(2,1)} %all-gather.3.cloned.1.call-done), kind=kOutput, calls=%fused_computation.5 | convolution fusion | flops 2147483648 | bytes 9437184 | tf_op jit(solution)/shard_map/fps,pt->fst/dot_general | solution.py:37
  229.7 38.7 %all_to_all.5 = f32[8,1,64,512]{3,2,1,0:T(8,128)S(1)} all-to-all(f32[8,1,64,512]{3,2,1,0:T(8,128)S(1)} %fusion.3), channel_id=1, replica_groups=mesh['pair'=8,'pw_0'=4,'pw_1'=4,'pw_2'=2] {'pair'}, dimensions={0} | all-to-all | bytes 2097152 | tf_op jit(solution)/shard_map/all_to_all | solution.py:26
  268.4 0.1 reduce_sum.19
  268.5 0.7 multiply_bitcast_fusion
  (2 shorter events, 0.0 us)
Async XLA Ops:
  6.5 1.2 copy-start
  6.5 37.4 %reduce-scatter.3.cloned.1.call-start = ((), (), s32[]{:S(2)}) async-start(), calls=%async_computation.3 | async-start | bytes 12582912 | tf_op jit(solution)/shard_map/reduce_scatter | solution.py:20
  19.0 132.4 %copy-start.2 = (s32[4096]{0:T(1024)S(1)}, s32[4096]{0:T(1024)}, u32[]{:S(2)}) copy-start(s32[4096]{0:T(1024)} %param.12) | copy-start | bytes 49156
  19.0 132.4 %copy-start.1 = (f32[2048]{0:T(1024)S(1)}, f32[2048]{0:T(1024)}, u32[]{:S(2)}) copy-start(f32[2048]{0:T(1024)} %param.10) | copy-start | bytes 24580
  19.0 130.0 %reduce-scatter.5.cloned.1.call-start = ((), (), s32[]{:S(2)}) async-start(), calls=%async_computation.4 | async-start | bytes 4456448 | tf_op jit(solution)/shard_map/reduce_scatter | solution.py:21
  44.0 169.4 %all-gather.3.cloned.1.call-start = ((), (), s32[]{:S(2)}) async-start(), calls=%async_computation.5 | async-start | bytes 4325376 | tf_op jit(solution)/shard_map/all_gather | solution.py:46
  151.4 23.1 %copy-start.3 = (s32[4096]{0:T(1024)S(1)}, s32[4096]{0:T(1024)}, u32[]{:S(2)}) copy-start(s32[4096]{0:T(1024)} %param.11) | copy-start | bytes 49156
  151.4 23.1 %copy-start.4 = (f32[16]{0:T(128)S(1)}, f32[16]{0:T(128)}, u32[]{:S(2)}) copy-start(f32[16]{0:T(128)} %param.9) | copy-start | bytes 196
Sparse Core Ops, SparseCore 0:
  19.1 24.8 reduce-scatter.2
  46.7 102.2 reduce-scatter.4
  151.0 62.3 all-gather.2
where the time goes:
time: 276 us
  waiting for transfers between devices  169 us (61%)
  blocking collectives  38.7 us (14%)
  local copies, waits for them, and re-layouts  35 us (13%)
  between operations  13.9 us (5%)
  matrix products  12.7 us (5%)
  other arithmetic  6.51 us (2%)
    reduce_scatter x1, waiting for transfers between devices, scatter_pairs(): return lax.psum_scatter(pieces, chips, scatter_dimension=0, tiled=True)[0]  105 us
    all_gather x1, waiting for transfers between devices, on_device(): lax.all_gather(reduced, PW, axis=0, tiled=True)  38.8 us
    all_to_all x1, blocking collectives, summed_on_arrival(): pieces = lax.all_to_all(split_up(value, dim, count), axis, 0, 0, tiled=True)  38.7 us
    reduce_scatter x1, waiting for transfers between devices, scatter_pairs(): pieces = lax.psum_scatter(pieces, core, scatter_dimension=0, tiled=True)  24.9 us
    gather x1, local copies, waits for them, and re-layouts, on_device(): spacing = cond_energy[cond_index] - lookup(val_index, val_energy)  23 us
    dot_general x1, matrix products, on_device(): jnp.dot(pair_elements, subspace, preferred_element_type=jnp.float32)  6.94 us
    dot_general x1, local copies, waits for them, and re-layouts, partial_gram(): jnp.einsum('fps,pt->fst', weighted, rows, preferred_element_type=jnp.floa...  6.49 us
    dot_general x1, matrix products, partial_gram(): jnp.einsum('fps,pt->fst', weighted, rows, preferred_element_type=jnp.floa...  5.79 us
  transfers between devices with their start and end apart: 3, of which 3 were waited for; matrix products, arithmetic and copies ran while one was open for 8% of the time, Pallas kernels for 0%

commit v1 on v0

v1 whole, which is shorter than its diff:
```python
import jax
import jax.numpy as jnp
from jax import lax
from jax.experimental import pallas as pl
from jax.experimental.pallas import tpu as pltpu
from jax.sharding import Mesh
from jax.sharding import PartitionSpec as P

PW = ("pw_x", "pw_z", "pw_c")
F32, BF16, I16 = jnp.float32, jnp.bfloat16, jnp.int16
TAIL = 16
VMEM_LIMIT = 48 * 1024 * 1024


def xor_permute(value, axis, mask):
    count = lax.axis_size(axis)
    return lax.ppermute(value, axis, [(i, i ^ mask) for i in range(count)])


def call(body, outs, *args, cost=0, **kwargs):
    moved = sum(a.size * a.dtype.itemsize for a in args)
    return pl.pallas_call(
        body,
        out_shape=[jax.ShapeDtypeStruct(shape, dtype) for shape, dtype in outs],
        compiler_params=pltpu.CompilerParams(vmem_limit_bytes=VMEM_LIMIT),
        cost_estimate=pl.CostEstimate(flops=cost, bytes_accessed=moved, transcendentals=0),
        **kwargs,
    )(*args)


def project(ids, pair_elements, subspace):
    count, width = ids.shape[0], subspace.shape[1]
    depth = subspace.shape[0]

    def body(ids_ref, a_ref, b_ref, o_ref):
        o_ref[...] = jnp.dot(a_ref[...], b_ref[...], preferred_element_type=F32)

    return pl.pallas_call(
        body,
        out_shape=jax.ShapeDtypeStruct((count * 256, width), F32),
        grid_spec=pltpu.PrefetchScalarGridSpec(
            num_scalar_prefetch=1,
            grid=(count,),
            in_specs=[
                pl.BlockSpec((256, depth), lambda i, ids_ref: (ids_ref[i], 0)),
                pl.BlockSpec((depth, width), lambda i, ids_ref: (0, 0)),
            ],
            out_specs=pl.BlockSpec((256, width), lambda i, ids_ref: (i, 0)),
        ),
        compiler_params=pltpu.CompilerParams(vmem_limit_bytes=VMEM_LIMIT),
        cost_estimate=pl.CostEstimate(
            flops=2 * count * 256 * depth * width, bytes_accessed=count * 256 * (2 * depth + 4 * width), transcendentals=0
        ),
    )(ids, pair_elements, subspace)


def pack(ref, value):
    rows = value.shape[0]
    top = jnp.max(jnp.max(jnp.abs(value), axis=0, keepdims=True), axis=1, keepdims=True)
    exponent = jnp.clip(jnp.ceil(jnp.log2(jnp.maximum(top, 1e-30) * (1.0 / 32000.0))), -100.0, 100.0)
    scaled = value * jnp.exp2(-exponent)
    ref[:rows, :] = jnp.round(scaled).astype(jnp.int32).astype(I16)
    ref[rows:, :] = jnp.broadcast_to(exponent, (TAIL, value.shape[1])).astype(jnp.int32).astype(I16)


def unpack(ref):
    rows = ref.shape[0] - TAIL
    tail = ref[rows:, :].astype(jnp.int32).astype(F32)
    step = jnp.exp2(tail[0:1, 0:1])
    return ref[:rows, :].astype(jnp.int32).astype(F32) * step


def first_messages(own_ref, other_ref, a_ref, b_ref):
    half = own_ref.shape[0] // 2
    pack(a_ref, own_ref[:half, :] + other_ref[:half, :])
    pack(b_ref, own_ref[half:, :] + other_ref[half:, :])


def second_messages(own_ref, other_ref, a_in, b_in, kept_ref, a_ref, b_ref):
    rows = own_ref.shape[0] // 4
    for part, (came, out) in enumerate(((a_in, a_ref), (b_in, b_ref))):
        here = 2 * part * rows
        total = own_ref[here : here + 2 * rows, :] + other_ref[here : here + 2 * rows, :] + unpack(came)
        kept_ref[part * rows : (part + 1) * rows, :] = total[:rows, :]
        pack(out, total[rows:, :])


def third_messages(z_ref, kept_ref, a_in, b_in, own_ref, m1_ref, m2_ref, m3_ref, work_ref):
    half = kept_ref.shape[0] // 2
    quarter = half // 2
    work_ref[:half, :] = kept_ref[:half, :] + unpack(a_in)
    work_ref[half:, :] = kept_ref[half:, :] + unpack(b_in)
    z = z_ref[0]

    def rows_of(owner):
        return work_ref[pl.ds(pl.multiple_of(owner * quarter, quarter), quarter), :]

    own_ref[...] = rows_of(z)
    for mask, out in ((1, m1_ref), (2, m2_ref), (3, m3_ref)):
        pack(out, rows_of(lax.bitwise_xor(z, mask)))


def last_sum(own_ref, m1_in, m2_in, m3_in, out_ref):
    out_ref[...] = (own_ref[...] + unpack(m1_in) + unpack(m2_in) + unpack(m3_in)).astype(BF16)


def weights_of(cond_index, val_index, cond_energy, val_energy, frequencies):
    shape = cond_index.shape

    def body(val_table, freq_ref, ci_ref, vi_ref, ce_ref, out_ref):
        index = ci_ref[...]
        high, low = index // 128, index % 128
        cond = jnp.zeros(shape, F32)
        for row in range(ce_ref.shape[0]):
            table = jnp.broadcast_to(ce_ref[row : row + 1, :], shape)
            cond = jnp.where(high == row, jnp.take_along_axis(table, low, axis=1), cond)
        level = vi_ref[...]
        val = jnp.zeros(shape, F32)
        for row in range(val_table.shape[0]):
            val = jnp.where(level == row, val_table[row], val)
        spacing = cond - val
        freq = freq_ref[0]
        out_ref[...] = 2.0 * spacing / (spacing * spacing + freq * freq)

    smem, vmem = pl.BlockSpec(memory_space=pltpu.SMEM), pl.BlockSpec(memory_space=pltpu.VMEM)
    return call(
        body,
        [(shape, F32)],
        val_energy,
        frequencies,
        cond_index,
        val_index,
        cond_energy,
        in_specs=[smem, smem, vmem, vmem, vmem],
        out_specs=[vmem],
    )[0]


def gram_step(blocks, weights, pieces, gram):
    width = pieces[0].shape[1]
    count = len(pieces)

    def body(blocks_ref, w_ref, *refs):
        came, out_ref = refs[:count], refs[-1]
        total = refs[count][...] if gram is not None else None
        for i, ref in enumerate(came):
            per = ref.shape[0] // 128
            parts = []
            for j in range(per):
                rows = ref[128 * j : 128 * (j + 1), :].astype(F32).T
                w = w_ref[pl.ds(blocks_ref[i * per + j], 1), :]
                parts.append((rows * w).astype(BF16))
            term = jnp.dot(jnp.concatenate(parts, axis=1), ref[...], preferred_element_type=F32)
            total = term if total is None else total + term
        out_ref[...] = total

    extra = [] if gram is None else [gram]
    smem, vmem = pl.BlockSpec(memory_space=pltpu.SMEM), pl.BlockSpec(memory_space=pltpu.VMEM)
    return call(
        body,
        [((width, width), F32)],
        blocks,
        weights,
        *pieces,
        *extra,
        cost=2 * width * width * sum(p.shape[0] for p in pieces),
        in_specs=[smem] + [vmem] * (1 + count + len(extra)),
        out_specs=[vmem],
    )[0]


def on_device(pair_elements, subspace, val_energy, cond_energy, val_index, cond_index, frequencies):
    x, z, core = (lax.axis_index(name).astype(jnp.int32) for name in PW)
    rows, width = pair_elements.shape[0], subspace.shape[1]
    eighth = rows // 8

    def block(owner, part):
        return 2 * (x ^ owner) + part

    sent = jnp.stack([block(1, 0), block(2, 0), block(3, 1), block(2, 1)])
    kept = jnp.stack([block(0, 0), block(3, 0), block(0, 1), block(1, 1)])
    mine, theirs = 8 * core, 8 * (1 - core)
    sent_other = project(sent + theirs, pair_elements, subspace)
    sent_in = xor_permute(sent_other, "pw_c", 1)
    sent_own = project(sent + mine, pair_elements, subspace)
    kept_other = project(kept + theirs, pair_elements, subspace)
    kept_in = xor_permute(kept_other, "pw_c", 1)
    message = lambda count: ((count + TAIL, width), I16)
    a, b = call(first_messages, [message(eighth)] * 2, sent_own, sent_in)
    a, b = xor_permute(a, "pw_x", 1), xor_permute(b, "pw_x", 3)
    kept_own = project(kept + mine, pair_elements, subspace)
    weights = weights_of(
        cond_index.reshape(-1, 128), val_index.reshape(-1, 128), cond_energy.reshape(-1, 128), val_energy, frequencies
    )
    held, a, b = call(
        second_messages, [((eighth, width), F32)] + [message(eighth // 2)] * 2, kept_own, kept_in, a, b
    )
    a, b = xor_permute(a, "pw_x", 3), xor_permute(b, "pw_x", 1)
    smem, vmem = pl.BlockSpec(memory_space=pltpu.SMEM), pl.BlockSpec(memory_space=pltpu.VMEM)
    piece = eighth // 4
    own, *out = call(
        third_messages,
        [((piece, width), F32)] + [message(piece)] * 3,
        z[None],
        held,
        a,
        b,
        in_specs=[smem] + [vmem] * 3,
        out_specs=[vmem] * 4,
        scratch_shapes=[pltpu.VMEM((eighth, width), F32)],
    )
    came = [xor_permute(value, "pw_z", mask + 1) for mask, value in enumerate(out)]
    coeffs = call(last_sum, [((piece, width), BF16)], own, *came)[0]

    quarter = jnp.concatenate([coeffs] + [xor_permute(coeffs, "pw_z", mask) for mask in (1, 2, 3)], axis=0)
    by_owner = [quarter] + [xor_permute(quarter, "pw_x", mask) for mask in (1, 3, 2)]
    by_core = [xor_permute(value, "pw_c", 1) for value in by_owner]
    place = jnp.stack([z ^ mask for mask in range(4)])

    def places(masks):
        return jnp.concatenate([16 * k + 4 * (x ^ mask) + place for mask in masks for k in (core, 1 - core)])

    gram = gram_step(places((0,)), weights, [by_owner[0], by_core[0]], None)
    gram = gram_step(places((1, 3)), weights, [by_owner[1], by_core[1], by_owner[2], by_core[2]], gram)
    gram = gram_step(places((2,)), weights, [by_owner[3], by_core[3]], gram)
    groups = lax.axis_size("pair")
    pieces = lax.all_to_all(gram.reshape(groups, -1, width), "pair", 0, 0, tiled=True)
    factor = -4.0 / (rows * groups)
    return (jnp.sum(pieces, axis=0) * factor)[None]


def solution(mesh):
    torus = Mesh(mesh.devices.reshape(mesh.shape["pair"], 4, 4, 2), ("pair",) + PW)
    return jax.shard_map(
        on_device,
        mesh=torus,
        in_specs=(P("pair", PW), P(PW, None), P(), P(), P("pair"), P("pair"), P(PW)),
        out_specs=P(PW, "pair", None),
        check_vma=False,
    )
```

time: 276 us -> 144 us (0.52)
  waiting for transfers between devices: 169 us -> 54.5 us
  local copies, waits for them, and re-layouts: 35 us -> 1.26 us
  Pallas kernels: 0 us -> 27.2 us
  starting transfers between devices: 0.08 us -> 19 us
  between operations: 13.9 us -> 0.86 us
  matrix products: 12.7 us -> 0 us
  other arithmetic: 6.51 us -> 1.17 us
    reduce_scatter x2 -> x0, waiting for transfers between devices: 130 us -> none  [the longest x1 105 us: scatter_pairs(): return lax.psum_scatter(pieces, chips, scatter_dimension=0, tiled=True)[0]]
    ppermute x0 -> x19, waiting for transfers between devices: none -> 54.5 us  [xor_permute(): return lax.ppermute(value, axis, [(i, i ^ mask) for i in range(count)])]
    all_gather x1 -> x0, waiting for transfers between devices: 38.8 us -> none  [on_device(): lax.all_gather(reduced, PW, axis=0, tiled=True)]
    pallas_call x0 -> x12, Pallas kernels: none -> 27.2 us  [the longest x4 18.3 us: project(): pl.pallas_call(body, out_shape=jax.ShapeDtypeStruct((count * 256, width),...]
    gather x1 -> x0, local copies, waits for them, and re-layouts: 23 us -> none  [on_device(): spacing = cond_energy[cond_index] - lookup(val_index, val_energy)]
    ppermute x0 -> x19, starting transfers between devices: none -> 19 us  [xor_permute(): return lax.ppermute(value, axis, [(i, i ^ mask) for i in range(count)])]
    dot_general x2 -> x0, matrix products: 12.7 us -> none  [the longest x1 6.94 us: on_device(): jnp.dot(pair_elements, subspace, preferred_element_type=jnp.float32)]
    dot_general x1 -> x0, local copies, waits for them, and re-layouts: 6.49 us -> none  [partial_gram(): jnp.einsum('fps,pt->fst', weighted, rows, preferred_element_type=jnp.floa...]
  transfers between devices with their start and end apart: 3 -> 19, of which waited for: 3 -> 12; matrix products, arithmetic and copies ran while one was open for 8% -> 0% of each run, Pallas kernels for 0% -> 12%
where the time goes in v1:
time: 144 us; the launch traced here: 143 us
  waiting for transfers between devices  54.5 us (38%)
  blocking collectives  39.5 us (27%)
  Pallas kernels  27.2 us (19%)
  starting transfers between devices  19 us (13%)
    ppermute x19, waiting for transfers between devices, xor_permute(): return lax.ppermute(value, axis, [(i, i ^ mask) for i in range(count)])  54.5 us
    all_to_all x1, blocking collectives, on_device(): lax.all_to_all(gram.reshape(groups, -1, width), 'pair', 0, 0, tiled=True)  39.5 us
    ppermute x19, starting transfers between devices, xor_permute(): return lax.ppermute(value, axis, [(i, i ^ mask) for i in range(count)])  19 us
    pallas_call x4, Pallas kernels, project(): pl.pallas_call(body, out_shape=jax.ShapeDtypeStruct((count * 256, width),...  18.3 us
    pallas_call x8, Pallas kernels, call(): pl.pallas_call(body, out_shape=[jax.ShapeDtypeStruct(shape, dtype) for sh...  8.82 us
  transfers between devices with their start and end apart: 19, of which 12 were waited for; matrix products, arithmetic and copies ran while one was open for 0% of the time, Pallas kernels for 12%

profile of v1, /device:TPU:32, one launch (start us, length us, event | category | flops | bytes accessed | tf_op | source)
XLA Modules:
  0.0 143.4 jit_solution(12165650971714768466)
XLA Ops:
  0.0 0.1 broadcast_add_fusion.6
  0.1 1.2 copy-done
  1.3 5.2 %shard_map.77 = f32[1024,512]{1,0:T(8,128)} custom-call(s32[4]{0:T(128)S(1)} %get-tuple-element.25.ids_ref, bf16[4096,1024]{1,0:T(8,128)(2,1)} %a_ref.7, bf16[1024,512]{1,0:T(8,128)(2,1)S(1)} %copy-done), custom_call_target="tpu_custom_call" | custom-call | flops 1073741824 | bytes 4194304 | tf_op jit(solution)/shard_map/pallas_call | solution.py:38
  6.5 5.1 %shard_map.75 = f32[1024,512]{1,0:T(8,128)} custom-call(s32[4]{0:T(128)S(1)} %get-tuple-element.36.ids_ref, bf16[4096,1024]{1,0:T(8,128)(2,1)} %a_ref.7, bf16[1024,512]{1,0:T(8,128)(2,1)S(1)} %copy-done), custom_call_target="tpu_custom_call" | custom-call | flops 1073741824 | bytes 4194304 | tf_op jit(solution)/shard_map/pallas_call | solution.py:38
  11.6 0.5 collective-permute-start
  12.1 4.0 %shard_map.76.own_ref = f32[1024,512]{1,0:T(8,128)S(1)} custom-call(s32[4]{0:T(128)S(1)} %broadcast_add_fusion.8.ids_ref, bf16[4096,1024]{1,0:T(8,128)(2,1)} %a_ref.7, bf16[1024,512]{1,0:T(8,128)(2,1)S(1)} %copy-done.1), custom_call_target="tpu_custom_call" | custom-call | flops 1073741824 | bytes 4194304 | tf_op jit(solution)/shard_map/pallas_call | solution.py:38
  16.2 0.5 shard_map.78
  16.7 1.6 %collective-permute-start.2 = (s16[528,512]{1,0:T(8,128)(2,1)S(1)}, s16[528,512]{1,0:T(8,128)(2,1)S(1)}, u32[]{:S(2)}, u32[]{:S(2)}) collective-permute-start(s16[528,512]{1,0:T(8,128)(2,1)S(1)} %get-tuple-element.14), channel_id=1, source_target_pairs={{0,8},{8,0},{16,24},{24,16},{1,9},{9,1},{17,25},{25,17},{2,10},{10... | collective-permute-start | bytes 1622024 | tf_op jit(solution)/shard_map/ppermute | solution.py:17
  18.2 2.1 %collective-permute-start.3 = (s16[528,512]{1,0:T(8,128)(2,1)S(1)}, s16[528,512]{1,0:T(8,128)(2,1)S(1)}, u32[]{:S(2)}, u32[]{:S(2)}) collective-permute-start(s16[528,512]{1,0:T(8,128)(2,1)S(1)} %get-tuple-element.15), channel_id=1, source_target_pairs={{0,24},{8,16},{16,8},{24,0},{1,25},{9,17},{17,9},{25,1},{2,26},{10... | collective-permute-start | bytes 1622024 | tf_op jit(solution)/shard_map/ppermute | solution.py:17
  20.3 4.0 %shard_map.74.own_ref = f32[1024,512]{1,0:T(8,128)S(1)} custom-call(s32[4]{0:T(128)S(1)} %broadcast_add_fusion.9.ids_ref, bf16[4096,1024]{1,0:T(8,128)(2,1)} %a_ref.7, bf16[1024,512]{1,0:T(8,128)(2,1)S(1)} %copy-done.1), custom_call_target="tpu_custom_call" | custom-call | flops 1073741824 | bytes 4194304 | tf_op jit(solution)/shard_map/pallas_call | solution.py:38
  24.4 6.6 %collective-permute-done.2.a_in = s16[528,512]{1,0:T(8,128)(2,1)S(1)} collective-permute-done((s16[528,512]{1,0:T(8,128)(2,1)S(1)}, s16[528,512]{1,0:T(8,128)(2,1)S(1)}, u32[]{:S(2)}, u32[]{:S(2)}) %collective-permute-start.2) | collective-permute-done | bytes 540704 | tf_op jit(solution)/shard_map/ppermute | solution.py:17
  30.9 2.4 %collective-permute-done.3.b_in = s16[528,512]{1,0:T(8,128)(2,1)S(1)} collective-permute-done((s16[528,512]{1,0:T(8,128)(2,1)S(1)}, s16[528,512]{1,0:T(8,128)(2,1)S(1)}, u32[]{:S(2)}, u32[]{:S(2)}) %collective-permute-start.3) | collective-permute-done | bytes 540704 | tf_op jit(solution)/shard_map/ppermute | solution.py:17
  33.4 2.4 %shard_map.79 = (f32[512,512]{1,0:T(8,128)S(1)}, s16[272,512]{1,0:T(8,128)(2,1)S(1)}, s16[272,512]{1,0:T(8,128)(2,1)S(1)}) custom-call(f32[1024,512]{1,0:T(8,128)S(1)} %shard_map.74.own_ref, f32[1024,512]{1,0:T(8,128)} %collective-permute-done.other_ref, s16[528,512]{1,0:T(8,128)(2,1)S(1)} %collective-permute-done.2.a_in, ...), custom_call_target="tpu_custom_call" | custom-call | bytes 5275648 | tf_op jit(solution)/shard_map/pallas_call | solution.py:22
  35.8 0.0 copy-start.4
  35.8 2.2 %collective-permute-start.4 = (s16[272,512]{1,0:T(8,128)(2,1)S(1)}, s16[272,512]{1,0:T(8,128)(2,1)S(1)}, u32[]{:S(2)}, u32[]{:S(2)}) collective-permute-start(s16[272,512]{1,0:T(8,128)(2,1)S(1)} %get-tuple-element.17), channel_id=1, source_target_pairs={{0,24},{8,16},{16,8},{24,0},{1,25},{9,17},{17,9},{25,1},{2,26},{10... | collective-permute-start | bytes 835592 | tf_op jit(solution)/shard_map/ppermute | solution.py:17
  38.0 6.5 %collective-permute-done.4.a_in = s16[272,512]{1,0:T(8,128)(2,1)S(1)} collective-permute-done((s16[272,512]{1,0:T(8,128)(2,1)S(1)}, s16[272,512]{1,0:T(8,128)(2,1)S(1)}, u32[]{:S(2)}, u32[]{:S(2)}) %collective-permute-start.4) | collective-permute-done | bytes 278560 | tf_op jit(solution)/shard_map/ppermute | solution.py:17
  44.5 0.6 collective-permute-done.5.b_in
  45.1 0.5 shard_map.80
  45.6 0.5 collective-permute-start.6
  46.2 2.9 %collective-permute-start.7 = (s16[144,512]{1,0:T(8,128)(2,1)S(1)}, s16[144,512]{1,0:T(8,128)(2,1)S(1)}, u32[]{:S(2)}, u32[]{:S(2)}) collective-permute-start(s16[144,512]{1,0:T(8,128)(2,1)S(1)} %get-tuple-element.21), channel_id=1, source_target_pairs={{0,4},{2,6},{4,0},{6,2},{1,5},{3,7},{5,1},{7,3},{8,12},{10,14},{12... | collective-permute-start | bytes 442376 | tf_op jit(solution)/shard_map/ppermute | solution.py:17
  49.1 0.5 collective-permute-start.8
  49.6 2.9 %collective-permute-done.6.m1_in = s16[144,512]{1,0:T(8,128)(2,1)S(1)} collective-permute-done((s16[144,512]{1,0:T(8,128)(2,1)S(1)}, s16[144,512]{1,0:T(8,128)(2,1)S(1)}, u32[]{:S(2)}, u32[]{:S(2)}) %collective-permute-start.6) | collective-permute-done | bytes 147488 | tf_op jit(solution)/shard_map/ppermute | solution.py:17
  52.4 5.5 %collective-permute-done.7.m2_in = s16[144,512]{1,0:T(8,128)(2,1)S(1)} collective-permute-done((s16[144,512]{1,0:T(8,128)(2,1)S(1)}, s16[144,512]{1,0:T(8,128)(2,1)S(1)}, u32[]{:S(2)}, u32[]{:S(2)}) %collective-permute-start.7) | collective-permute-done | bytes 147488 | tf_op jit(solution)/shard_map/ppermute | solution.py:17
  58.0 2.5 %collective-permute-done.8.m3_in = s16[144,512]{1,0:T(8,128)(2,1)S(1)} collective-permute-done((s16[144,512]{1,0:T(8,128)(2,1)S(1)}, s16[144,512]{1,0:T(8,128)(2,1)S(1)}, u32[]{:S(2)}, u32[]{:S(2)}) %collective-permute-start.8) | collective-permute-done | bytes 147488 | tf_op jit(solution)/shard_map/ppermute | solution.py:17
  60.4 0.2 shard_map.81
  60.6 1.0 collective-permute-start.10
  61.6 1.1 collective-permute-start.11
  62.7 2.3 %collective-permute-start.9 = (bf16[128,512]{1,0:T(8,128)(2,1)S(1)}, bf16[128,512]{1,0:T(8,128)(2,1)S(1)}, u32[]{:S(2)}, u32[]{:S(2)}) collective-permute-start(bf16[128,512]{1,0:T(8,128)(2,1)S(1)} %shard_map.81), channel_id=1, source_target_pairs={{0,2},{2,0},{4,6},{6,4},{1,3},{3,1},{5,7},{7,5},{8,10},{10,8},{12,... | collective-permute-start | bytes 393224 | tf_op jit(solution)/shard_map/ppermute | solution.py:17
  65.1 4.3 %collective-permute-done.10 = bf16[128,512]{1,0:T(8,128)(2,1)S(1)} collective-permute-done((bf16[128,512]{1,0:T(8,128)(2,1)S(1)}, bf16[128,512]{1,0:T(8,128)(2,1)S(1)}, u32[]{:S(2)}, u32[]{:S(2)}) %collective-permute-start.10) | collective-permute-done | bytes 131104 | tf_op jit(solution)/shard_map/ppermute | solution.py:17
  69.4 2.7 %collective-permute-done.11 = bf16[128,512]{1,0:T(8,128)(2,1)S(1)} collective-permute-done((bf16[128,512]{1,0:T(8,128)(2,1)S(1)}, bf16[128,512]{1,0:T(8,128)(2,1)S(1)}, u32[]{:S(2)}, u32[]{:S(2)}) %collective-permute-start.11) | collective-permute-done | bytes 131104 | tf_op jit(solution)/shard_map/ppermute | solution.py:17
  72.2 0.6 collective-permute-start.14
  72.8 1.4 collective-permute-start.16
  74.2 2.2 %collective-permute-start.12 = (bf16[512,512]{1,0:T(8,128)(2,1)S(1)}, bf16[512,512]{1,0:T(8,128)(2,1)S(1)}, u32[]{:S(2)}, u32[]{:S(2)}) collective-permute-start(bf16[512,512]{1,0:T(8,128)(2,1)S(1)} %pad_maximum_fusion.refs_0_), channel_id=1, source_target_pairs={{0,16},{8,24},{16,0},{24,8},{1,17},{9,25},{17,1},{25,9},{2,18},{10... | collective-permute-start | bytes 1572872 | tf_op jit(solution)/shard_map/ppermute | solution.py:17
  76.3 0.1 broadcast_add_fusion.1
  76.4 0.0 collective-permute-start.18
  76.5 10.7 %collective-permute-done.14.refs_0_ = bf16[512,512]{1,0:T(8,128)(2,1)S(1)} collective-permute-done((bf16[512,512]{1,0:T(8,128)(2,1)S(1)}, bf16[512,512]{1,0:T(8,128)(2,1)S(1)}, u32[]{:S(2)}, u32[]{:S(2)}) %collective-permute-start.14) | collective-permute-done | bytes 524320 | tf_op jit(solution)/shard_map/ppermute | solution.py:17
  87.1 8.0 %collective-permute-done.16.refs_2_ = bf16[512,512]{1,0:T(8,128)(2,1)S(1)} collective-permute-done((bf16[512,512]{1,0:T(8,128)(2,1)S(1)}, bf16[512,512]{1,0:T(8,128)(2,1)S(1)}, u32[]{:S(2)}, u32[]{:S(2)}) %collective-permute-start.16) | collective-permute-done | bytes 524320 | tf_op jit(solution)/shard_map/ppermute | solution.py:17
  95.1 1.8 %collective-permute-done.12.refs_0_ = bf16[512,512]{1,0:T(8,128)(2,1)S(1)} collective-permute-done((bf16[512,512]{1,0:T(8,128)(2,1)S(1)}, bf16[512,512]{1,0:T(8,128)(2,1)S(1)}, u32[]{:S(2)}, u32[]{:S(2)}) %collective-permute-start.12) | collective-permute-done | bytes 524320 | tf_op jit(solution)/shard_map/ppermute | solution.py:17
  97.6 0.8 shard_map.73.w_ref
  98.4 0.1 pad_add_fusion.5.blocks_ref
  98.5 0.1 pad_add_fusion.1.blocks_ref
  98.6 0.1 pad_add_fusion.4.blocks_ref
  98.6 1.3 shard_map.82.refs_4_
  100.0 1.9 %shard_map.83.refs_2_ = f32[512,512]{1,0:T(8,128)S(1)} custom-call(s32[16]{0:T(128)S(1)} %pad_add_fusion.4.blocks_ref, f32[32,128]{1,0:T(8,128)S(1)} %shard_map.73.w_ref, bf16[512,512]{1,0:T(8,128)(2,1)S(1)} %collective-permute-done.14.refs_0_, bf16[512,512]{1,0:T(8,128)(2,1)S(1)} %collective-permute-done.15.refs_1_, ...), custom_call_target="tpu_custom_call" | custom-call | flops 1073741824 | bytes 3162176 | tf_op jit(solution)/shard_map/pallas_call | solution.py:22
  101.8 1.3 shard_map.84
  103.2 39.5 %all_to_all.5 = f32[8,64,512]{2,1,0:T(8,128)S(1)} all-to-all(f32[8,64,512]{2,1,0:T(8,128)S(1)} %bitcast.18), channel_id=1, replica_groups=mesh['pair'=8,'pw_x'=4,'pw_z'=4,'pw_c'=2] {'pair'}, dimensions={0} | all-to-all | bytes 2097152 | tf_op jit(solution)/shard_map/all_to_all | solution.py:227
  142.7 0.1 reduce_sum.9
  142.8 0.7 multiply_bitcast_fusion
  (26 shorter events, 0.1 us)
Async XLA Ops:
  0.1 1.2 copy-start
  6.5 9.7 %collective-permute-start.1 = (f32[1024,512]{1,0:T(8,128)}, f32[1024,512]{1,0:T(8,128)S(1)}, u32[]{:S(2)}, u32[]{:S(2)}) collective-permute-start(f32[1024,512]{1,0:T(8,128)} %shard_map.77), channel_id=1, source_target_pairs={{0,1},{1,0},{2,3},{3,2},{4,5},{5,4},{6,7},{7,6},{8,9},{9,8},{10,11... | collective-permute-start | bytes 6291464 | tf_op jit(solution)/shard_map/ppermute | solution.py:17
  6.5 5.7 %copy-start.1 = (bf16[1024,512]{1,0:T(8,128)(2,1)S(1)}, bf16[1024,512]{1,0:T(8,128)(2,1)}, u32[]{:S(2)}) copy-start(bf16[1024,512]{1,0:T(8,128)(2,1)} %b_ref.7) | copy-start | bytes 3145732
  11.6 12.7 %collective-permute-start = (f32[1024,512]{1,0:T(8,128)}, f32[1024,512]{1,0:T(8,128)}, u32[]{:S(2)}, u32[]{:S(2)}) collective-permute-start(f32[1024,512]{1,0:T(8,128)} %shard_map.75), channel_id=1, source_target_pairs={{0,1},{1,0},{2,3},{3,2},{4,5},{5,4},{6,7},{7,6},{8,9},{9,8},{10,11... | collective-permute-start | bytes 6291464 | tf_op jit(solution)/shard_map/ppermute | solution.py:17
  16.7 14.3 %collective-permute-start.2 = (s16[528,512]{1,0:T(8,128)(2,1)S(1)}, s16[528,512]{1,0:T(8,128)(2,1)S(1)}, u32[]{:S(2)}, u32[]{:S(2)}) collective-permute-start(s16[528,512]{1,0:T(8,128)(2,1)S(1)} %get-tuple-element.14), channel_id=1, source_target_pairs={{0,8},{8,0},{16,24},{24,16},{1,9},{9,1},{17,25},{25,17},{2,10},{10... | collective-permute-start | bytes 1622024 | tf_op jit(solution)/shard_map/ppermute | solution.py:17
  18.2 15.1 %collective-permute-start.3 = (s16[528,512]{1,0:T(8,128)(2,1)S(1)}, s16[528,512]{1,0:T(8,128)(2,1)S(1)}, u32[]{:S(2)}, u32[]{:S(2)}) collective-permute-start(s16[528,512]{1,0:T(8,128)(2,1)S(1)} %get-tuple-element.15), channel_id=1, source_target_pairs={{0,24},{8,16},{16,8},{24,0},{1,25},{9,17},{17,9},{25,1},{2,26},{10... | collective-permute-start | bytes 1622024 | tf_op jit(solution)/shard_map/ppermute | solution.py:17
  35.8 61.8 %copy-start.2 = (s32[4096]{0:T(1024)S(1)}, s32[4096]{0:T(1024)}, u32[]{:S(2)}) copy-start(s32[4096]{0:T(1024)} %param.12) | copy-start | bytes 49156
  35.8 61.8 %copy-start.3 = (s32[4096]{0:T(1024)S(1)}, s32[4096]{0:T(1024)}, u32[]{:S(2)}) copy-start(s32[4096]{0:T(1024)} %param.11) | copy-start | bytes 49156
  35.8 61.8 %copy-start.4 = (f32[2048]{0:T(1024)S(1)}, f32[2048]{0:T(1024)}, u32[]{:S(2)}) copy-start(f32[2048]{0:T(1024)} %param.10) | copy-start | bytes 24580
  35.8 61.8 %copy-start.5 = (f32[16]{0:T(128)S(1)}, f32[16]{0:T(128)}, u32[]{:S(2)}) copy-start(f32[16]{0:T(128)} %val_table.1) | copy-start | bytes 196
  35.8 8.7 %collective-permute-start.4 = (s16[272,512]{1,0:T(8,128)(2,1)S(1)}, s16[272,512]{1,0:T(8,128)(2,1)S(1)}, u32[]{:S(2)}, u32[]{:S(2)}) collective-permute-start(s16[272,512]{1,0:T(8,128)(2,1)S(1)} %get-tuple-element.17), channel_id=1, source_target_pairs={{0,24},{8,16},{16,8},{24,0},{1,25},{9,17},{17,9},{25,1},{2,26},{10... | collective-permute-start | bytes 835592 | tf_op jit(solution)/shard_map/ppermute | solution.py:17
  38.0 7.1 %collective-permute-start.5 = (s16[272,512]{1,0:T(8,128)(2,1)S(1)}, s16[272,512]{1,0:T(8,128)(2,1)S(1)}, u32[]{:S(2)}, u32[]{:S(2)}) collective-permute-start(s16[272,512]{1,0:T(8,128)(2,1)S(1)} %get-tuple-element.18), channel_id=1, source_target_pairs={{0,8},{8,0},{16,24},{24,16},{1,9},{9,1},{17,25},{25,17},{2,10},{10... | collective-permute-start | bytes 835592 | tf_op jit(solution)/shard_map/ppermute | solution.py:17
  45.6 6.8 %collective-permute-start.6 = (s16[144,512]{1,0:T(8,128)(2,1)S(1)}, s16[144,512]{1,0:T(8,128)(2,1)S(1)}, u32[]{:S(2)}, u32[]{:S(2)}) collective-permute-start(s16[144,512]{1,0:T(8,128)(2,1)S(1)} %get-tuple-element.20), channel_id=1, source_target_pairs={{0,2},{2,0},{4,6},{6,4},{1,3},{3,1},{5,7},{7,5},{8,10},{10,8},{12,... | collective-permute-start | bytes 442376 | tf_op jit(solution)/shard_map/ppermute | solution.py:17
  46.2 11.8 %collective-permute-start.7 = (s16[144,512]{1,0:T(8,128)(2,1)S(1)}, s16[144,512]{1,0:T(8,128)(2,1)S(1)}, u32[]{:S(2)}, u32[]{:S(2)}) collective-permute-start(s16[144,512]{1,0:T(8,128)(2,1)S(1)} %get-tuple-element.21), channel_id=1, source_target_pairs={{0,4},{2,6},{4,0},{6,2},{1,5},{3,7},{5,1},{7,3},{8,12},{10,14},{12... | collective-permute-start | bytes 442376 | tf_op jit(solution)/shard_map/ppermute | solution.py:17
  49.1 11.3 %collective-permute-start.8 = (s16[144,512]{1,0:T(8,128)(2,1)S(1)}, s16[144,512]{1,0:T(8,128)(2,1)S(1)}, u32[]{:S(2)}, u32[]{:S(2)}) collective-permute-start(s16[144,512]{1,0:T(8,128)(2,1)S(1)} %get-tuple-element.22), channel_id=1, source_target_pairs={{0,6},{2,4},{4,2},{6,0},{1,7},{3,5},{5,3},{7,1},{8,14},{10,12},{12... | collective-permute-start | bytes 442376 | tf_op jit(solution)/shard_map/ppermute | solution.py:17
  60.6 8.8 %collective-permute-start.10 = (bf16[128,512]{1,0:T(8,128)(2,1)S(1)}, bf16[128,512]{1,0:T(8,128)(2,1)S(1)}, u32[]{:S(2)}, u32[]{:S(2)}) collective-permute-start(bf16[128,512]{1,0:T(8,128)(2,1)S(1)} %shard_map.81), channel_id=1, source_target_pairs={{0,4},{2,6},{4,0},{6,2},{1,5},{3,7},{5,1},{7,3},{8,12},{10,14},{12... | collective-permute-start | bytes 393224 | tf_op jit(solution)/shard_map/ppermute | solution.py:17
  61.6 10.5 %collective-permute-start.11 = (bf16[128,512]{1,0:T(8,128)(2,1)S(1)}, bf16[128,512]{1,0:T(8,128)(2,1)S(1)}, u32[]{:S(2)}, u32[]{:S(2)}) collective-permute-start(bf16[128,512]{1,0:T(8,128)(2,1)S(1)} %shard_map.81), channel_id=1, source_target_pairs={{0,6},{2,4},{4,2},{6,0},{1,7},{3,5},{5,3},{7,1},{8,14},{10,12},{12... | collective-permute-start | bytes 393224 | tf_op jit(solution)/shard_map/ppermute | solution.py:17
  62.7 9.4 %collective-permute-start.9 = (bf16[128,512]{1,0:T(8,128)(2,1)S(1)}, bf16[128,512]{1,0:T(8,128)(2,1)S(1)}, u32[]{:S(2)}, u32[]{:S(2)}) collective-permute-start(bf16[128,512]{1,0:T(8,128)(2,1)S(1)} %shard_map.81), channel_id=1, source_target_pairs={{0,2},{2,0},{4,6},{6,4},{1,3},{3,1},{5,7},{7,5},{8,10},{10,8},{12,... | collective-permute-start | bytes 393224 | tf_op jit(solution)/shard_map/ppermute | solution.py:17
  72.2 14.9 %collective-permute-start.14 = (bf16[512,512]{1,0:T(8,128)(2,1)S(1)}, bf16[512,512]{1,0:T(8,128)(2,1)S(1)}, u32[]{:S(2)}, u32[]{:S(2)}) collective-permute-start(bf16[512,512]{1,0:T(8,128)(2,1)S(1)} %pad_maximum_fusion.refs_0_), channel_id=1, source_target_pairs={{0,8},{8,0},{16,24},{24,16},{1,9},{9,1},{17,25},{25,17},{2,10},{10... | collective-permute-start | bytes 1572872 | tf_op jit(solution)/shard_map/ppermute | solution.py:17
  72.8 22.3 %collective-permute-start.16 = (bf16[512,512]{1,0:T(8,128)(2,1)S(1)}, bf16[512,512]{1,0:T(8,128)(2,1)S(1)}, u32[]{:S(2)}, u32[]{:S(2)}) collective-permute-start(bf16[512,512]{1,0:T(8,128)(2,1)S(1)} %pad_maximum_fusion.refs_0_), channel_id=1, source_target_pairs={{0,24},{8,16},{16,8},{24,0},{1,25},{9,17},{17,9},{25,1},{2,26},{10... | collective-permute-start | bytes 1572872 | tf_op jit(solution)/shard_map/ppermute | solution.py:17
  74.2 22.7 %collective-permute-start.12 = (bf16[512,512]{1,0:T(8,128)(2,1)S(1)}, bf16[512,512]{1,0:T(8,128)(2,1)S(1)}, u32[]{:S(2)}, u32[]{:S(2)}) collective-permute-start(bf16[512,512]{1,0:T(8,128)(2,1)S(1)} %pad_maximum_fusion.refs_0_), channel_id=1, source_target_pairs={{0,16},{8,24},{16,0},{24,8},{1,17},{9,25},{17,1},{25,9},{2,18},{10... | collective-permute-start | bytes 1572872 | tf_op jit(solution)/shard_map/ppermute | solution.py:17
  76.4 22.2 %collective-permute-start.18 = (bf16[512,512]{1,0:T(8,128)(2,1)S(1)}, bf16[512,512]{1,0:T(8,128)(2,1)S(1)}, u32[]{:S(2)}, u32[]{:S(2)}) collective-permute-start(bf16[512,512]{1,0:T(8,128)(2,1)S(1)} %pad_maximum_fusion.refs_0_), channel_id=1, source_target_pairs={{0,1},{1,0},{2,3},{3,2},{4,5},{5,4},{6,7},{7,6},{8,9},{9,8},{10,11... | collective-permute-start | bytes 1572872 | tf_op jit(solution)/shard_map/ppermute | solution.py:17
  87.1 12.8 %collective-permute-start.15 = (bf16[512,512]{1,0:T(8,128)(2,1)S(1)}, bf16[512,512]{1,0:T(8,128)(2,1)S(1)}, u32[]{:S(2)}, u32[]{:S(2)}) collective-permute-start(bf16[512,512]{1,0:T(8,128)(2,1)S(1)} %collective-permute-done.14.refs_0_), channel_id=1, source_target_pairs={{0,1},{1,0},{2,3},{3,2},{4,5},{5,4},{6,7},{7,6},{8,9},{9,8},{10,11... | collective-permute-start | bytes 1572872 | tf_op jit(solution)/shard_map/ppermute | solution.py:17
  95.1 4.8 %collective-permute-start.17 = (bf16[512,512]{1,0:T(8,128)(2,1)S(1)}, bf16[512,512]{1,0:T(8,128)(2,1)S(1)}, u32[]{:S(2)}, u32[]{:S(2)}) collective-permute-start(bf16[512,512]{1,0:T(8,128)(2,1)S(1)} %collective-permute-done.16.refs_2_), channel_id=1, source_target_pairs={{0,1},{1,0},{2,3},{3,2},{4,5},{5,4},{6,7},{7,6},{8,9},{9,8},{10,11... | collective-permute-start | bytes 1572872 | tf_op jit(solution)/shard_map/ppermute | solution.py:17
  96.9 4.9 %collective-permute-start.13 = (bf16[512,512]{1,0:T(8,128)(2,1)S(1)}, bf16[512,512]{1,0:T(8,128)(2,1)S(1)}, u32[]{:S(2)}, u32[]{:S(2)}) collective-permute-start(bf16[512,512]{1,0:T(8,128)(2,1)S(1)} %collective-permute-done.12.refs_0_), channel_id=1, source_target_pairs={{0,1},{1,0},{2,3},{3,2},{4,5},{5,4},{6,7},{7,6},{8,9},{9,8},{10,11... | collective-permute-start | bytes 1572872 | tf_op jit(solution)/shard_map/ppermute | solution.py:17

commit v2 on v1

v2 whole, which is shorter than its diff:
```python
import jax
import jax.numpy as jnp
from jax import lax
from jax.experimental import pallas as pl
from jax.experimental.pallas import tpu as pltpu
from jax.sharding import Mesh
from jax.sharding import PartitionSpec as P

PW = ("pw_x", "pw_z", "pw_c")
F32, BF16, I16 = jnp.float32, jnp.bfloat16, jnp.int16
TAIL = 16
VMEM_LIMIT, VMEM_FULL = 48 * 1024 * 1024, 63 * 1024 * 1024
SMEM, VMEM = pl.BlockSpec(memory_space=pltpu.SMEM), pl.BlockSpec(memory_space=pltpu.VMEM)


def xor_permute(value, axis, mask):
    count = lax.axis_size(axis)
    return lax.ppermute(value, axis, [(i, i ^ mask) for i in range(count)])


def call(body, outs, *args, cost=0, **kwargs):
    moved = sum(a.size * a.dtype.itemsize for a in args)
    return pl.pallas_call(
        body,
        out_shape=[jax.ShapeDtypeStruct(shape, dtype) for shape, dtype in outs],
        compiler_params=pltpu.CompilerParams(vmem_limit_bytes=VMEM_LIMIT),
        cost_estimate=pl.CostEstimate(flops=cost, bytes_accessed=moved, transcendentals=0),
        **kwargs,
    )(*args)


def project(ids, pair_elements, subspace, fetch, outs):
    count, (depth, width) = ids.shape[0], subspace.shape
    per = count // outs

    def body(ids_ref, a_ref, b_ref, *refs):
        out_refs, (held, sems), (b_held,) = refs[:outs], refs[outs : outs + 2], refs[outs + 2 :] or (b_ref,)
        copies = []
        if fetch:
            copies.append(pltpu.make_async_copy(b_ref, b_held, sems.at[count]))
        for i in range(count):
            block = a_ref.at[pl.ds(pl.multiple_of(ids_ref[i] * 256, 256), 256), :]
            copies.append(pltpu.make_async_copy(block, held.at[pl.ds(256 * i, 256), :], sems.at[i]))
        for copy in copies:
            copy.start()
        if fetch:
            copies.pop(0).wait()
        for o, out_ref in enumerate(out_refs):
            for copy in copies[o * per : (o + 1) * per]:
                copy.wait()
            rows = held[o * per * 256 : (o + 1) * per * 256, :]
            out_ref[...] = jnp.dot(rows, b_held[...], preferred_element_type=F32)

    return pl.pallas_call(
        body,
        out_shape=[jax.ShapeDtypeStruct((per * 256, width), F32)] * outs,
        in_specs=[SMEM, pl.BlockSpec(memory_space=pl.ANY), pl.BlockSpec(memory_space=pl.ANY) if fetch else VMEM],
        out_specs=[VMEM] * outs,
        scratch_shapes=[pltpu.VMEM((count * 256, depth), BF16), pltpu.SemaphoreType.DMA((count + 1,))]
        + ([pltpu.VMEM((depth, width), BF16)] if fetch else []),
        compiler_params=pltpu.CompilerParams(vmem_limit_bytes=VMEM_FULL if fetch else VMEM_LIMIT),
        cost_estimate=pl.CostEstimate(
            flops=2 * count * 256 * depth * width, bytes_accessed=count * 256 * (2 * depth + 4 * width), transcendentals=0
        ),
    )(ids, pair_elements, subspace)


def pack(ref, value):
    rows = value.shape[0]
    top = jnp.maximum(jnp.max(jnp.abs(value), axis=0, keepdims=True), 1e-30)
    level = jnp.clip(jnp.ceil(jnp.log2(top * (1.0 / 32000.0)) * 256.0), -32000.0, 32000.0)
    scaled = value * jnp.exp2(level * (-1.0 / 256.0))
    ref[:rows, :] = jnp.round(scaled).astype(jnp.int32).astype(I16)
    ref[rows:, :] = jnp.broadcast_to(level, (TAIL, value.shape[1])).astype(jnp.int32).astype(I16)


def unpack(ref):
    rows = ref.shape[0] - TAIL
    level = ref[rows:, :].astype(jnp.int32).astype(F32)[0:1, :]
    return ref[:rows, :].astype(jnp.int32).astype(F32) * jnp.exp2(level * (1.0 / 256.0))


def first_messages(own_ref, other_ref, a_ref, b_ref):
    half = own_ref.shape[0] // 2
    pack(a_ref, own_ref[:half, :] + other_ref[:half, :])
    pack(b_ref, own_ref[half:, :] + other_ref[half:, :])


def add(a_ref, b_ref, out_ref):
    out_ref[...] = a_ref[...] + b_ref[...]


def second_messages(sum_ref, a_in, b_in, kept_ref, a_ref, b_ref):
    rows = sum_ref.shape[0] // 4
    for part, (came, out) in enumerate(((a_in, a_ref), (b_in, b_ref))):
        here = 2 * part * rows
        total = sum_ref[here : here + 2 * rows, :] + unpack(came)
        kept_ref[part * rows : (part + 1) * rows, :] = total[:rows, :]
        pack(out, total[rows:, :])


def third_messages(z_ref, kept_ref, a_in, b_in, own_ref, m1_ref, m2_ref, m3_ref, work_ref):
    half = kept_ref.shape[0] // 2
    work_ref[:half, :] = kept_ref[:half, :] + unpack(a_in)
    work_ref[half:, :] = kept_ref[half:, :] + unpack(b_in)
    split_four(z_ref[0], work_ref, own_ref, (m1_ref, m2_ref, m3_ref))


def split_four(here, work_ref, own_ref, message_refs):
    quarter = work_ref.shape[0] // 4

    def rows_of(owner):
        return work_ref[pl.ds(pl.multiple_of(owner * quarter, quarter), quarter), :]

    own_ref[...] = rows_of(here)
    for mask, out in enumerate(message_refs):
        pack(out, rows_of(lax.bitwise_xor(here, mask + 1)))


def last_sum(own_ref, m1_in, m2_in, m3_in, out_ref):
    out_ref[...] = (own_ref[...] + unpack(m1_in) + unpack(m2_in) + unpack(m3_in)).astype(BF16)


def gram_messages(y_ref, mine_ref, came_ref, own_ref, m1_ref, m2_ref, m3_ref, work_ref):
    work_ref[...] = mine_ref[...] + came_ref[...]
    split_four(y_ref[0], work_ref, own_ref, (m1_ref, m2_ref, m3_ref))


def gram_halves(half_ref, own_ref, m1_in, m2_in, m3_in, kept_ref, out_ref, work_ref):
    rows = kept_ref.shape[0]
    work_ref[...] = own_ref[...] + unpack(m1_in) + unpack(m2_in) + unpack(m3_in)
    here = half_ref[0]
    kept_ref[...] = work_ref[pl.ds(pl.multiple_of(here * rows, rows), rows), :]
    pack(out_ref, work_ref[pl.ds(pl.multiple_of((1 - here) * rows, rows), rows), :])


def weights_of(cond_index, val_index, cond_energy, val_energy, *frequencies):
    shape, count = cond_index.shape, len(frequencies)

    def body(val_table, *refs):
        freq_refs, (ci_ref, vi_ref, ce_ref), out_refs = refs[:count], refs[count : count + 3], refs[count + 3 :]
        index = ci_ref[...]
        high, low = index // 128, index % 128
        cond = jnp.zeros(shape, F32)
        for row in range(ce_ref.shape[0]):
            table = jnp.broadcast_to(ce_ref[row : row + 1, :], shape)
            cond = jnp.where(high == row, jnp.take_along_axis(table, low, axis=1), cond)
        level = vi_ref[...]
        val = jnp.zeros(shape, F32)
        for row in range(val_table.shape[0]):
            val = jnp.where(level == row, val_table[row], val)
        spacing = cond - val
        for freq_ref, out_ref in zip(freq_refs, out_refs):
            freq = freq_ref[0]
            out_ref[...] = 2.0 * spacing / (spacing * spacing + freq * freq)

    return call(
        body,
        [(shape, F32)] * count,
        val_energy,
        *frequencies,
        cond_index,
        val_index,
        cond_energy,
        in_specs=[SMEM] * (1 + count) + [VMEM] * 3,
        out_specs=[VMEM] * count,
    )


def gram_step(blocks, weights, pieces, grams):
    width = pieces[0].shape[1]
    count, kinds = len(pieces), len(weights)

    def body(blocks_ref, *refs):
        w_refs, came, before, out_refs = refs[:kinds], refs[kinds : kinds + count], refs[kinds + count : -kinds], refs[-kinds:]
        totals = [ref[...] for ref in before] or [None] * kinds
        place = 0
        for ref in came:
            parts = [[] for _ in range(kinds)]
            for j in range(ref.shape[0] // 128):
                rows = ref[128 * j : 128 * (j + 1), :].astype(F32).T
                for part, w_ref in zip(parts, w_refs):
                    part.append((rows * w_ref[pl.ds(blocks_ref[place], 1), :]).astype(BF16))
                place += 1
            for kind, part in enumerate(parts):
                term = jnp.dot(jnp.concatenate(part, axis=1), ref[...], preferred_element_type=F32)
                totals[kind] = term if totals[kind] is None else totals[kind] + term
        for out_ref, total in zip(out_refs, totals):
            out_ref[...] = total

    return call(
        body,
        [((width, width), F32)] * kinds,
        blocks,
        *weights,
        *pieces,
        *grams,
        cost=2 * kinds * width * width * sum(p.shape[0] for p in pieces),
        in_specs=[SMEM] + [VMEM] * (kinds + count + len(grams)),
        out_specs=[VMEM] * kinds,
    )


def on_device(pair_elements, subspace, val_energy, cond_energy, val_index, cond_index, frequencies):
    x, z, core = (lax.axis_index(name).astype(jnp.int32) for name in PW)
    pair = lax.axis_index("pair").astype(jnp.int32)
    rows, width = pair_elements.shape[0], subspace.shape[1]
    eighth = rows // 8
    message = lambda count: ((count + TAIL, width), I16)
    sums = lambda count: ((count, width), F32)

    def block(owner, part):
        return 2 * (x ^ owner) + part

    sent = jnp.stack([block(1, 0), block(2, 0), block(3, 1), block(2, 1)])
    kept = jnp.stack([block(0, 0), block(3, 0), block(0, 1), block(1, 1)])
    mine, theirs = 8 * core, 8 * (1 - core)
    (sent_other,) = project(sent + theirs, pair_elements, subspace, True, 1)
    sent_in = xor_permute(sent_other, "pw_c", 1)
    sent_own, kept_other = project(jnp.concatenate([sent + mine, kept + theirs]), pair_elements, subspace, True, 2)
    kept_in = xor_permute(kept_other, "pw_c", 1)
    a, b = call(first_messages, [message(eighth)] * 2, sent_own, sent_in)
    kept_ids, a, b = lax.optimization_barrier((kept + mine, a, b))
    a, b = xor_permute(a, "pw_x", 1), xor_permute(b, "pw_x", 3)
    (kept_own,) = project(kept_ids, pair_elements, subspace, False, 1)
    kept_sum = call(add, [sums(2 * eighth)], kept_own, kept_in)[0]
    weights = weights_of(
        cond_index.reshape(-1, 128),
        val_index.reshape(-1, 128),
        cond_energy.reshape(-1, 128),
        val_energy,
        frequencies,
        xor_permute(frequencies, "pw_c", 1),
    )
    kept_sum, weights = lax.optimization_barrier((kept_sum, weights))
    held, a, b = call(second_messages, [sums(eighth)] + [message(eighth // 2)] * 2, kept_sum, a, b)
    a, b = xor_permute(a, "pw_x", 3), xor_permute(b, "pw_x", 1)
    piece = eighth // 4
    own, *out = call(
        third_messages,
        [sums(piece)] + [message(piece)] * 3,
        z[None],
        held,
        a,
        b,
        in_specs=[SMEM] + [VMEM] * 3,
        out_specs=[VMEM] * 4,
        scratch_shapes=[pltpu.VMEM((eighth, width), F32)],
    )
    came = [xor_permute(value, "pw_z", mask + 1) for mask, value in enumerate(out)]
    coeffs = call(last_sum, [((piece, width), BF16)], own, *came)[0]

    near, far, across = (xor_permute(coeffs, "pw_z", mask) for mask in (1, 2, 3))
    top, bottom = jnp.concatenate([coeffs, near], axis=0), jnp.concatenate([far, across], axis=0)
    place = jnp.stack([z ^ mask for mask in range(4)]) + 16 * core
    top1, top3 = xor_permute(top, "pw_x", 1), xor_permute(top, "pw_x", 3)
    bottom1, bottom3 = xor_permute(bottom, "pw_x", 1), xor_permute(bottom, "pw_x", 3)

    def places(*masks):
        return jnp.concatenate([4 * (x ^ mask) + place for mask in masks])

    grams = gram_step(places(0), weights, [top, bottom], [])
    bottom1, top3, grams = lax.optimization_barrier((bottom1, top3, grams))
    top2, bottom2 = xor_permute(top3, "pw_x", 1), xor_permute(bottom1, "pw_x", 3)
    grams = gram_step(places(1, 3), weights, [top1, bottom1, top3, bottom3], grams)
    mine, theirs = gram_step(places(2), weights, [top2, bottom2], grams)

    across = width // 4
    own, *out = call(
        gram_messages,
        [sums(across)] + [message(across)] * 3,
        (pair // 2)[None],
        mine,
        xor_permute(theirs, "pw_c", 1),
        in_specs=[SMEM] + [VMEM] * 2,
        out_specs=[VMEM] * 4,
        scratch_shapes=[pltpu.VMEM((width, width), F32)],
    )
    came = [xor_permute(value, "pair", 2 * (mask + 1)) for mask, value in enumerate(out)]
    own, out = call(
        gram_halves,
        [sums(across // 2), message(across // 2)],
        (pair % 2)[None],
        own,
        *came,
        in_specs=[SMEM] + [VMEM] * 4,
        out_specs=[VMEM] * 2,
        scratch_shapes=[pltpu.VMEM((across, width), F32)],
    )
    factor = -4.0 / (rows * lax.axis_size("pair"))

    def finish(own_ref, came_ref, out_ref):
        out_ref[...] = (own_ref[...] + unpack(came_ref)) * factor

    return call(finish, [sums(across // 2)], own, xor_permute(out, "pair", 1))[0][None]


def solution(mesh):
    torus = Mesh(mesh.devices.reshape(mesh.shape["pair"], 4, 4, 2), ("pair",) + PW)
    return jax.shard_map(
        on_device,
        mesh=torus,
        in_specs=(P("pair", PW), P(PW, None), P(), P(), P("pair"), P("pair"), P(PW)),
        out_specs=P(PW, "pair", None),
        check_vma=False,
    )
```

time: 144 us -> 121 us (0.84)
  blocking collectives: 39.5 us -> 0 us
  starting transfers between devices: 19 us -> 33.7 us
  local copies, waits for them, and re-layouts: 1.26 us -> 2.99 us
    all_to_all x1 -> x0, blocking collectives: 39.5 us -> none  [on_device(): lax.all_to_all(gram.reshape(groups, -1, width), 'pair', 0, 0, tiled=True)]
    ppermute x19 -> x24, starting transfers between devices: 19 us -> 33.7 us  [xor_permute(): return lax.ppermute(value, axis, [(i, i ^ mask) for i in range(count)])]
    pallas_call x4 -> x3, Pallas kernels: 18.3 us -> 14.9 us  [project(): pl.pallas_call(body, out_shape=[jax.ShapeDtypeStruct((per * 256, width),...]
    pallas_call x8 -> x12, Pallas kernels: 8.82 us -> 12.1 us  [call(): pl.pallas_call(body, out_shape=[jax.ShapeDtypeStruct(shape, dtype) for sh...]
    unnamed x12 -> x15, local copies, waits for them, and re-layouts: 1.26 us -> 2.98 us
    ppermute x19 -> x24, waiting for transfers between devices: 54.5 us -> 55.4 us  [xor_permute(): return lax.ppermute(value, axis, [(i, i ^ mask) for i in range(count)])]
  transfers between devices with their start and end apart: 19 -> 24, of which waited for: 12 -> 19; matrix products, arithmetic and copies ran while one was open for 0% -> 1% of each run, Pallas kernels for 12% -> 15%
where the time goes in v2:
time: 121 us
  waiting for transfers between devices  55.4 us (46%)
  starting transfers between devices  33.7 us (28%)
  Pallas kernels  27 us (22%)
  local copies, waits for them, and re-layouts  2.99 us (2%)
  other arithmetic  1.39 us (1%)
    ppermute x24, waiting for transfers between devices, xor_permute(): return lax.ppermute(value, axis, [(i, i ^ mask) for i in range(count)])  55.4 us
    ppermute x24, starting transfers between devices, xor_permute(): return lax.ppermute(value, axis, [(i, i ^ mask) for i in range(count)])  33.7 us
    pallas_call x3, Pallas kernels, project(): pl.pallas_call(body, out_shape=[jax.ShapeDtypeStruct((per * 256, width),...  14.9 us
    pallas_call x12, Pallas kernels, call(): pl.pallas_call(body, out_shape=[jax.ShapeDtypeStruct(shape, dtype) for sh...  12.1 us
    unnamed x15, local copies, waits for them, and re-layouts  2.98 us
  transfers between devices with their start and end apart: 24, of which 19 were waited for; matrix products, arithmetic and copies ran while one was open for 1% of the time, Pallas kernels for 15%

profile of v2, /device:TPU:32, one launch (start us, length us, event | category | flops | bytes accessed | tf_op | source)
XLA Modules:
  0.0 121.2 jit_solution(6725103918942068939)
XLA Ops:
  0.0 0.6 broadcast_add_fusion.3
  0.6 5.1 %shard_map.74 = f32[1024,512]{1,0:T(8,128)} custom-call(s32[4]{0:T(128)} %get-tuple-element.77.ids_ref, bf16[4096,1024]{1,0:T(8,128)(2,1)} %a_ref.5, bf16[1024,512]{1,0:T(8,128)(2,1)} %b_ref.5), custom_call_target="tpu_custom_call" | custom-call | flops 1073741824 | bytes 4194304 | tf_op jit(solution)/shard_map/pallas_call | solution.py:54
  5.9 0.6 pad_add_fusion.2.ids_ref
  6.4 6.4 %shard_map.73 = (f32[1024,512]{1,0:T(8,128)}, f32[1024,512]{1,0:T(8,128)}) custom-call(s32[8]{0:T(128)} %pad_add_fusion.2.ids_ref, bf16[4096,1024]{1,0:T(8,128)(2,1)} %a_ref.5, bf16[1024,512]{1,0:T(8,128)(2,1)} %b_ref.5), custom_call_target="tpu_custom_call" | custom-call | flops 2147483648 | bytes 8388608 | tf_op jit(solution)/shard_map/pallas_call | solution.py:54
  12.9 0.6 collective-permute-start.1
  13.5 1.6 %copy-done.1 = f32[1024,512]{1,0:T(8,128)S(1)} copy-done((f32[1024,512]{1,0:T(8,128)S(1)}, f32[1024,512]{1,0:T(8,128)}, u32[]{:S(2)}) %copy-start.1) | copy-done | bytes 2097176
  15.1 2.1 %shard_map.75 = (s16[528,512]{1,0:T(8,128)(2,1)S(1)}, s16[528,512]{1,0:T(8,128)(2,1)S(1)}) custom-call(f32[1024,512]{1,0:T(8,128)S(1)} %copy-done.1, f32[1024,512]{1,0:T(8,128)} %collective-permute-done.other_ref), custom_call_target="tpu_custom_call" | custom-call | bytes 4194304 | tf_op jit(solution)/shard_map/pallas_call | solution.py:23
  17.2 1.6 %collective-permute-start.3 = (s16[528,512]{1,0:T(8,128)(2,1)S(1)}, s16[528,512]{1,0:T(8,128)(2,1)S(1)}, u32[]{:S(2)}, u32[]{:S(2)}) collective-permute-start(s16[528,512]{1,0:T(8,128)(2,1)S(1)} %get-tuple-element.50), channel_id=1, source_target_pairs={{0,8},{8,0},{16,24},{24,16},{1,9},{9,1},{17,25},{25,17},{2,10},{10... | collective-permute-start | bytes 1622024 | tf_op jit(solution)/shard_map/ppermute | solution.py:18
  18.8 2.1 %collective-permute-start.4 = (s16[528,512]{1,0:T(8,128)(2,1)S(1)}, s16[528,512]{1,0:T(8,128)(2,1)S(1)}, u32[]{:S(2)}, u32[]{:S(2)}) collective-permute-start(s16[528,512]{1,0:T(8,128)(2,1)S(1)} %get-tuple-element.51), channel_id=1, source_target_pairs={{0,24},{8,16},{16,8},{24,0},{1,25},{9,17},{17,9},{25,1},{2,26},{10... | collective-permute-start | bytes 1622024 | tf_op jit(solution)/shard_map/ppermute | solution.py:18
  21.5 0.6 collective-permute-done.2.refs_1_
  22.1 1.4 %shard_map.78 = (f32[32,128]{1,0:T(8,128)S(1)}, f32[32,128]{1,0:T(8,128)S(1)}) custom-call(f32[16]{0:T(128)S(1)} %copy-done.5, f32[1]{0:T(128)S(6)} %copy.9.refs_0_, f32[1]{0:T(128)} %collective-permute-done.2.refs_1_, s32[32,128]{1,0:T(8,128)S(1)} %bitcast.18, s32[32,128]{1,0:T(8,128)S(1)} %bitcast.19, f32[16,128]{1,0:T(8,128)S(1)} %bitcast.20), custom_call_target="tpu_custom_call" | custom-call | bytes 41032 | tf_op jit(solution)/shard_map/pallas_call | solution.py:23
  23.6 3.4 %shard_map.76.a_ref = f32[1024,512]{1,0:T(8,128)S(1)} custom-call(s32[4]{0:T(128)S(1)} %broadcast_add_fusion.6.ids_ref, bf16[4096,1024]{1,0:T(8,128)(2,1)} %a_ref.5, bf16[1024,512]{1,0:T(8,128)(2,1)S(1)} %copy-done), custom_call_target="tpu_custom_call" | custom-call | flops 1073741824 | bytes 4194304 | tf_op jit(solution)/shard_map/pallas_call | solution.py:54
  27.0 1.4 %copy-done.6 = f32[1024,512]{1,0:T(8,128)} copy-done((f32[1024,512]{1,0:T(8,128)}, f32[1024,512]{1,0:T(8,128)S(1)}, u32[]{:S(2)}) %copy-start.6) | copy-done | bytes 2097176
  28.3 1.8 %shard_map.77.sum_ref = f32[1024,512]{1,0:T(8,128)S(1)} custom-call(f32[1024,512]{1,0:T(8,128)S(1)} %shard_map.76.a_ref, f32[1024,512]{1,0:T(8,128)} %copy-done.6), custom_call_target="tpu_custom_call" | custom-call | bytes 4194304 | tf_op jit(solution)/shard_map/pallas_call | solution.py:23
  30.1 1.4 %collective-permute-done.3.a_in = s16[528,512]{1,0:T(8,128)(2,1)S(1)} collective-permute-done((s16[528,512]{1,0:T(8,128)(2,1)S(1)}, s16[528,512]{1,0:T(8,128)(2,1)S(1)}, u32[]{:S(2)}, u32[]{:S(2)}) %collective-permute-start.3) | collective-permute-done | bytes 540704 | tf_op jit(solution)/shard_map/ppermute | solution.py:18
  31.5 2.4 %collective-permute-done.4.b_in = s16[528,512]{1,0:T(8,128)(2,1)S(1)} collective-permute-done((s16[528,512]{1,0:T(8,128)(2,1)S(1)}, s16[528,512]{1,0:T(8,128)(2,1)S(1)}, u32[]{:S(2)}, u32[]{:S(2)}) %collective-permute-start.4) | collective-permute-done | bytes 540704 | tf_op jit(solution)/shard_map/ppermute | solution.py:18
  34.5 2.2 %collective-permute-start.5 = (s16[272,512]{1,0:T(8,128)(2,1)S(1)}, s16[272,512]{1,0:T(8,128)(2,1)S(1)}, u32[]{:S(2)}, u32[]{:S(2)}) collective-permute-start(s16[272,512]{1,0:T(8,128)(2,1)S(1)} %get-tuple-element.53), channel_id=1, source_target_pairs={{0,24},{8,16},{16,8},{24,0},{1,25},{9,17},{17,9},{25,1},{2,26},{10... | collective-permute-start | bytes 835592 | tf_op jit(solution)/shard_map/ppermute | solution.py:18
  36.7 6.6 %collective-permute-done.5.a_in = s16[272,512]{1,0:T(8,128)(2,1)S(1)} collective-permute-done((s16[272,512]{1,0:T(8,128)(2,1)S(1)}, s16[272,512]{1,0:T(8,128)(2,1)S(1)}, u32[]{:S(2)}, u32[]{:S(2)}) %collective-permute-start.5) | collective-permute-done | bytes 278560 | tf_op jit(solution)/shard_map/ppermute | solution.py:18
  43.3 0.6 collective-permute-done.6.b_in
  44.8 2.9 %collective-permute-start.8 = (s16[144,512]{1,0:T(8,128)(2,1)S(1)}, s16[144,512]{1,0:T(8,128)(2,1)S(1)}, u32[]{:S(2)}, u32[]{:S(2)}) collective-permute-start(s16[144,512]{1,0:T(8,128)(2,1)S(1)} %get-tuple-element.57), channel_id=1, source_target_pairs={{0,4},{2,6},{4,0},{6,2},{1,5},{3,7},{5,1},{7,3},{8,12},{10,14},{12... | collective-permute-start | bytes 442376 | tf_op jit(solution)/shard_map/ppermute | solution.py:18
  48.2 2.9 %collective-permute-done.7.m1_in = s16[144,512]{1,0:T(8,128)(2,1)S(1)} collective-permute-done((s16[144,512]{1,0:T(8,128)(2,1)S(1)}, s16[144,512]{1,0:T(8,128)(2,1)S(1)}, u32[]{:S(2)}, u32[]{:S(2)}) %collective-permute-start.7) | collective-permute-done | bytes 147488 | tf_op jit(solution)/shard_map/ppermute | solution.py:18
  51.1 5.5 %collective-permute-done.8.m2_in = s16[144,512]{1,0:T(8,128)(2,1)S(1)} collective-permute-done((s16[144,512]{1,0:T(8,128)(2,1)S(1)}, s16[144,512]{1,0:T(8,128)(2,1)S(1)}, u32[]{:S(2)}, u32[]{:S(2)}) %collective-permute-start.8) | collective-permute-done | bytes 147488 | tf_op jit(solution)/shard_map/ppermute | solution.py:18
  56.6 2.5 %collective-permute-done.9.m3_in = s16[144,512]{1,0:T(8,128)(2,1)S(1)} collective-permute-done((s16[144,512]{1,0:T(8,128)(2,1)S(1)}, s16[144,512]{1,0:T(8,128)(2,1)S(1)}, u32[]{:S(2)}, u32[]{:S(2)}) %collective-permute-start.9) | collective-permute-done | bytes 147488 | tf_op jit(solution)/shard_map/ppermute | solution.py:18
  59.2 1.0 collective-permute-start.10
  60.2 1.2 collective-permute-start.11
  61.5 2.3 %collective-permute-start.13 = (bf16[128,512]{1,0:T(8,128)(2,1)S(1)}, bf16[128,512]{1,0:T(8,128)(2,1)S(1)}, u32[]{:S(2)}, u32[]{:S(2)}) collective-permute-start(bf16[128,512]{1,0:T(8,128)(2,1)S(1)} %shard_map.81), channel_id=1, source_target_pairs={{0,2},{2,0},{4,6},{6,4},{1,3},{3,1},{5,7},{7,5},{8,10},{10,8},{12,... | collective-permute-start | bytes 393224 | tf_op jit(solution)/shard_map/ppermute | solution.py:18
  63.8 4.3 %collective-permute-done.10 = bf16[128,512]{1,0:T(8,128)(2,1)S(1)} collective-permute-done((bf16[128,512]{1,0:T(8,128)(2,1)S(1)}, bf16[128,512]{1,0:T(8,128)(2,1)S(1)}, u32[]{:S(2)}, u32[]{:S(2)}) %collective-permute-start.10) | collective-permute-done | bytes 131104 | tf_op jit(solution)/shard_map/ppermute | solution.py:18
  68.1 2.6 %collective-permute-done.11 = bf16[128,512]{1,0:T(8,128)(2,1)S(1)} collective-permute-done((bf16[128,512]{1,0:T(8,128)(2,1)S(1)}, bf16[128,512]{1,0:T(8,128)(2,1)S(1)}, u32[]{:S(2)}, u32[]{:S(2)}) %collective-permute-start.11) | collective-permute-done | bytes 131104 | tf_op jit(solution)/shard_map/ppermute | solution.py:18
  70.7 2.1 %collective-permute-start.18 = (bf16[256,512]{1,0:T(8,128)(2,1)S(1)}, bf16[256,512]{1,0:T(8,128)(2,1)S(1)}, u32[]{:S(2)}, u32[]{:S(2)}) collective-permute-start(bf16[256,512]{1,0:T(8,128)(2,1)S(1)} %constant_dynamic-update-slice_fusion.refs_3_), channel_id=1, source_target_pairs={{0,24},{8,16},{16,8},{24,0},{1,25},{9,17},{17,9},{25,1},{2,26},{10... | collective-permute-start | bytes 786440 | tf_op jit(solution)/shard_map/ppermute | solution.py:18
  72.8 2.1 %collective-permute-start.17 = (bf16[256,512]{1,0:T(8,128)(2,1)S(1)}, bf16[256,512]{1,0:T(8,128)(2,1)S(1)}, u32[]{:S(2)}, u32[]{:S(2)}) collective-permute-start(bf16[256,512]{1,0:T(8,128)(2,1)S(1)} %pad_maximum_fusion.refs_2_), channel_id=1, source_target_pairs={{0,8},{8,0},{16,24},{24,16},{1,9},{9,1},{17,25},{25,17},{2,10},{10... | collective-permute-start | bytes 786440 | tf_op jit(solution)/shard_map/ppermute | solution.py:18
  75.0 1.4 %collective-permute-start.14 = (bf16[256,512]{1,0:T(8,128)(2,1)S(1)}, bf16[256,512]{1,0:T(8,128)(2,1)S(1)}, u32[]{:S(2)}, u32[]{:S(2)}) collective-permute-start(bf16[256,512]{1,0:T(8,128)(2,1)S(1)} %pad_maximum_fusion.refs_2_), channel_id=1, source_target_pairs={{0,24},{8,16},{16,8},{24,0},{1,25},{9,17},{17,9},{25,1},{2,26},{10... | collective-permute-start | bytes 786440 | tf_op jit(solution)/shard_map/ppermute | solution.py:18
  76.4 1.3 %shard_map.82 = (f32[512,512]{1,0:T(8,128)S(1)}, f32[512,512]{1,0:T(8,128)S(1)}) custom-call(s32[4]{0:T(128)S(1)} %get-tuple-element.82.blocks_ref, f32[32,128]{1,0:T(8,128)S(1)} %get-tuple-element.47.refs_0_, f32[32,128]{1,0:T(8,128)S(1)} %get-tuple-element.48.refs_1_, bf16[256,512]{1,0:T(8,128)(2,1)S(1)} %pad_maximum_fusion.refs_2_, ...), custom_call_target="tpu_custom_call" | custom-call | flops 536870912 | bytes 557072 | tf_op jit(solution)/shard_map/pallas_call | solution.py:23
  77.7 4.1 %collective-permute-done.12.refs_3_ = bf16[256,512]{1,0:T(8,128)(2,1)S(1)} collective-permute-done((bf16[256,512]{1,0:T(8,128)(2,1)S(1)}, bf16[256,512]{1,0:T(8,128)(2,1)S(1)}, u32[]{:S(2)}, u32[]{:S(2)}) %collective-permute-start.12) | collective-permute-done | bytes 262176 | tf_op jit(solution)/shard_map/ppermute | solution.py:18
  81.8 2.4 %collective-permute-done.14.refs_4_ = bf16[256,512]{1,0:T(8,128)(2,1)S(1)} collective-permute-done((bf16[256,512]{1,0:T(8,128)(2,1)S(1)}, bf16[256,512]{1,0:T(8,128)(2,1)S(1)}, u32[]{:S(2)}, u32[]{:S(2)}) %collective-permute-start.14) | collective-permute-done | bytes 262176 | tf_op jit(solution)/shard_map/ppermute | solution.py:18
  84.2 1.9 %collective-permute-start.16 = (bf16[256,512]{1,0:T(8,128)(2,1)S(1)}, bf16[256,512]{1,0:T(8,128)(2,1)S(1)}, u32[]{:S(2)}, u32[]{:S(2)}) collective-permute-start(bf16[256,512]{1,0:T(8,128)(2,1)S(1)} %collective-permute-done.12.refs_3_), channel_id=1, source_target_pairs={{0,24},{8,16},{16,8},{24,0},{1,25},{9,17},{17,9},{25,1},{2,26},{10... | collective-permute-start | bytes 786440 | tf_op jit(solution)/shard_map/ppermute | solution.py:18
  86.2 1.8 %shard_map.83 = (f32[512,512]{1,0:T(8,128)S(1)}, f32[512,512]{1,0:T(8,128)S(1)}) custom-call(s32[8]{0:T(128)S(1)} %pad_add_fusion.3.blocks_ref, f32[32,128]{1,0:T(8,128)S(1)} %get-tuple-element.47.refs_0_, f32[32,128]{1,0:T(8,128)S(1)} %get-tuple-element.48.refs_1_, bf16[256,512]{1,0:T(8,128)(2,1)S(1)} %collective-permute-done.17.refs_2_, ...), custom_call_target="tpu_custom_call" | custom-call | flops 1073741824 | bytes 3178528 | tf_op jit(solution)/shard_map/pallas_call | solution.py:23
  88.1 2.5 %collective-permute-done.15.refs_2_ = bf16[256,512]{1,0:T(8,128)(2,1)S(1)} collective-permute-done((bf16[256,512]{1,0:T(8,128)(2,1)S(1)}, bf16[256,512]{1,0:T(8,128)(2,1)S(1)}, u32[]{:S(2)}, u32[]{:S(2)}) %collective-permute-start.15) | collective-permute-done | bytes 262176 | tf_op jit(solution)/shard_map/ppermute | solution.py:18
  90.6 1.2 %collective-permute-done.16.refs_3_ = bf16[256,512]{1,0:T(8,128)(2,1)S(1)} collective-permute-done((bf16[256,512]{1,0:T(8,128)(2,1)S(1)}, bf16[256,512]{1,0:T(8,128)(2,1)S(1)}, u32[]{:S(2)}, u32[]{:S(2)}) %collective-permute-start.16) | collective-permute-done | bytes 262176 | tf_op jit(solution)/shard_map/ppermute | solution.py:18
  91.8 1.3 %shard_map.84 = (f32[512,512]{1,0:T(8,128)S(1)}, f32[512,512]{1,0:T(8,128)S(1)}) custom-call(s32[4]{0:T(128)S(1)} %get-tuple-element.83.blocks_ref, f32[32,128]{1,0:T(8,128)S(1)} %get-tuple-element.47.refs_0_, f32[32,128]{1,0:T(8,128)S(1)} %get-tuple-element.48.refs_1_, bf16[256,512]{1,0:T(8,128)(2,1)S(1)} %collective-permute-done.15.refs_2_, ...), custom_call_target="tpu_custom_call" | custom-call | flops 536870912 | bytes 2654224 | tf_op jit(solution)/shard_map/pallas_call | solution.py:23
  93.2 2.6 %collective-permute-done.19.came_ref = f32[512,512]{1,0:T(8,128)S(1)} collective-permute-done((f32[512,512]{1,0:T(8,128)S(1)}, f32[512,512]{1,0:T(8,128)S(1)}, u32[]{:S(2)}, u32[]{:S(2)}) %collective-permute-start.19) | collective-permute-done | bytes 1048608 | tf_op jit(solution)/shard_map/ppermute | solution.py:18
  96.1 1.7 %collective-permute-start.20 = (s16[144,512]{1,0:T(8,128)(2,1)S(1)}, s16[144,512]{1,0:T(8,128)(2,1)S(1)}, u32[]{:S(2)}, u32[]{:S(2)}) collective-permute-start(s16[144,512]{1,0:T(8,128)(2,1)S(1)} %get-tuple-element.70), channel_id=1, source_target_pairs={{0,64},{32,96},{64,0},{96,32},{128,192},{160,224},{192,128},{224,1... | collective-permute-start | bytes 442376 | tf_op jit(solution)/shard_map/ppermute | solution.py:18
  97.8 2.9 %collective-permute-start.21 = (s16[144,512]{1,0:T(8,128)(2,1)S(1)}, s16[144,512]{1,0:T(8,128)(2,1)S(1)}, u32[]{:S(2)}, u32[]{:S(2)}) collective-permute-start(s16[144,512]{1,0:T(8,128)(2,1)S(1)} %get-tuple-element.71), channel_id=1, source_target_pairs={{0,128},{32,160},{64,192},{96,224},{128,0},{160,32},{192,64},{224,... | collective-permute-start | bytes 442376 | tf_op jit(solution)/shard_map/ppermute | solution.py:18
  100.9 2.0 %collective-permute-done.20.m1_in = s16[144,512]{1,0:T(8,128)(2,1)S(1)} collective-permute-done((s16[144,512]{1,0:T(8,128)(2,1)S(1)}, s16[144,512]{1,0:T(8,128)(2,1)S(1)}, u32[]{:S(2)}, u32[]{:S(2)}) %collective-permute-start.20) | collective-permute-done | bytes 147488 | tf_op jit(solution)/shard_map/ppermute | solution.py:18
  102.9 4.9 %collective-permute-done.21.m2_in = s16[144,512]{1,0:T(8,128)(2,1)S(1)} collective-permute-done((s16[144,512]{1,0:T(8,128)(2,1)S(1)}, s16[144,512]{1,0:T(8,128)(2,1)S(1)}, u32[]{:S(2)}, u32[]{:S(2)}) %collective-permute-start.21) | collective-permute-done | bytes 147488 | tf_op jit(solution)/shard_map/ppermute | solution.py:18
  107.8 2.4 %collective-permute-done.22.m3_in = s16[144,512]{1,0:T(8,128)(2,1)S(1)} collective-permute-done((s16[144,512]{1,0:T(8,128)(2,1)S(1)}, s16[144,512]{1,0:T(8,128)(2,1)S(1)}, u32[]{:S(2)}, u32[]{:S(2)}) %collective-permute-start.22) | collective-permute-done | bytes 147488 | tf_op jit(solution)/shard_map/ppermute | solution.py:18
  110.5 6.3 %collective-permute-start.23 = (s16[80,512]{1,0:T(8,128)(2,1)S(1)}, s16[80,512]{1,0:T(8,128)(2,1)S(1)}, u32[]{:S(2)}, u32[]{:S(2)}) collective-permute-start(s16[80,512]{1,0:T(8,128)(2,1)S(1)} %get-tuple-element.74), channel_id=1, source_target_pairs={{0,32},{32,0},{64,96},{96,64},{128,160},{160,128},{192,224},{224,1... | collective-permute-start | bytes 245768 | tf_op jit(solution)/shard_map/ppermute | solution.py:18
  116.8 3.8 %collective-permute-done.23.came_ref = s16[80,512]{1,0:T(8,128)(2,1)S(1)} collective-permute-done((s16[80,512]{1,0:T(8,128)(2,1)S(1)}, s16[80,512]{1,0:T(8,128)(2,1)S(1)}, u32[]{:S(2)}, u32[]{:S(2)}) %collective-permute-start.23) | collective-permute-done | bytes 81952 | tf_op jit(solution)/shard_map/ppermute | solution.py:18
  120.6 0.7 shard_map.87
  (39 shorter events, 3.2 us)
Async XLA Ops:
  5.7 7.7 %collective-permute-start = (f32[1024,512]{1,0:T(8,128)}, f32[1024,512]{1,0:T(8,128)}, u32[]{:S(2)}, u32[]{:S(2)}) collective-permute-start(f32[1024,512]{1,0:T(8,128)} %shard_map.74), channel_id=1, source_target_pairs={{0,1},{1,0},{2,3},{3,2},{4,5},{5,4},{6,7},{7,6},{8,9},{9,8},{10,11... | collective-permute-start | bytes 6291464 | tf_op jit(solution)/shard_map/ppermute | solution.py:18
  12.9 14.1 %collective-permute-start.1 = (f32[1024,512]{1,0:T(8,128)}, f32[1024,512]{1,0:T(8,128)S(1)}, u32[]{:S(2)}, u32[]{:S(2)}) collective-permute-start(f32[1024,512]{1,0:T(8,128)} %get-tuple-element.44), channel_id=1, source_target_pairs={{0,1},{1,0},{2,3},{3,2},{4,5},{5,4},{6,7},{7,6},{8,9},{9,8},{10,11... | collective-permute-start | bytes 6291464 | tf_op jit(solution)/shard_map/ppermute | solution.py:18
  13.5 1.6 %copy-start.1 = (f32[1024,512]{1,0:T(8,128)S(1)}, f32[1024,512]{1,0:T(8,128)}, u32[]{:S(2)}) copy-start(f32[1024,512]{1,0:T(8,128)} %get-tuple-element.40.own_ref) | copy-start | bytes 6291460
  15.0 7.1 %copy-start.2 = (s32[4096]{0:T(1024)S(1)}, s32[4096]{0:T(1024)}, u32[]{:S(2)}) copy-start(s32[4096]{0:T(1024)} %param.12) | copy-start | bytes 49156
  15.1 7.1 %copy-start.3 = (s32[4096]{0:T(1024)S(1)}, s32[4096]{0:T(1024)}, u32[]{:S(2)}) copy-start(s32[4096]{0:T(1024)} %param.11) | copy-start | bytes 49156
  15.1 7.1 %copy-start.4 = (f32[2048]{0:T(1024)S(1)}, f32[2048]{0:T(1024)}, u32[]{:S(2)}) copy-start(f32[2048]{0:T(1024)} %param.10) | copy-start | bytes 24580
  15.1 7.1 %copy-start.5 = (f32[16]{0:T(128)S(1)}, f32[16]{0:T(128)}, u32[]{:S(2)}) copy-start(f32[16]{0:T(128)} %val_table.1) | copy-start | bytes 196
  15.1 8.5 %copy-start = (bf16[1024,512]{1,0:T(8,128)(2,1)S(1)}, bf16[1024,512]{1,0:T(8,128)(2,1)}, u32[]{:S(2)}) copy-start(bf16[1024,512]{1,0:T(8,128)(2,1)} %b_ref.5) | copy-start | bytes 3145732
  17.2 14.3 %collective-permute-start.3 = (s16[528,512]{1,0:T(8,128)(2,1)S(1)}, s16[528,512]{1,0:T(8,128)(2,1)S(1)}, u32[]{:S(2)}, u32[]{:S(2)}) collective-permute-start(s16[528,512]{1,0:T(8,128)(2,1)S(1)} %get-tuple-element.50), channel_id=1, source_target_pairs={{0,8},{8,0},{16,24},{24,16},{1,9},{9,1},{17,25},{25,17},{2,10},{10... | collective-permute-start | bytes 1622024 | tf_op jit(solution)/shard_map/ppermute | solution.py:18
  18.8 15.1 %collective-permute-start.4 = (s16[528,512]{1,0:T(8,128)(2,1)S(1)}, s16[528,512]{1,0:T(8,128)(2,1)S(1)}, u32[]{:S(2)}, u32[]{:S(2)}) collective-permute-start(s16[528,512]{1,0:T(8,128)(2,1)S(1)} %get-tuple-element.51), channel_id=1, source_target_pairs={{0,24},{8,16},{16,8},{24,0},{1,25},{9,17},{17,9},{25,1},{2,26},{10... | collective-permute-start | bytes 1622024 | tf_op jit(solution)/shard_map/ppermute | solution.py:18
  20.9 1.2 %collective-permute-start.2 = (f32[1]{0:T(128)}, f32[1]{0:T(128)}, u32[]{:S(2)}, u32[]{:S(2)}) collective-permute-start(f32[1]{0:T(128)} %param.13), channel_id=1, source_target_pairs={{0,1},{1,0},{2,3},{3,2},{4,5},{5,4},{6,7},{7,6},{8,9},{9,8},{10,11... | collective-permute-start | bytes 20 | tf_op jit(solution)/shard_map/ppermute | solution.py:18
  27.0 1.4 %copy-start.6 = (f32[1024,512]{1,0:T(8,128)}, f32[1024,512]{1,0:T(8,128)S(1)}, u32[]{:S(2)}) copy-start(f32[1024,512]{1,0:T(8,128)S(1)} %collective-permute-done.1.b_ref) | copy-start | bytes 6291460
  34.5 8.7 %collective-permute-start.5 = (s16[272,512]{1,0:T(8,128)(2,1)S(1)}, s16[272,512]{1,0:T(8,128)(2,1)S(1)}, u32[]{:S(2)}, u32[]{:S(2)}) collective-permute-start(s16[272,512]{1,0:T(8,128)(2,1)S(1)} %get-tuple-element.53), channel_id=1, source_target_pairs={{0,24},{8,16},{16,8},{24,0},{1,25},{9,17},{17,9},{25,1},{2,26},{10... | collective-permute-start | bytes 835592 | tf_op jit(solution)/shard_map/ppermute | solution.py:18
  36.7 7.1 %collective-permute-start.6 = (s16[272,512]{1,0:T(8,128)(2,1)S(1)}, s16[272,512]{1,0:T(8,128)(2,1)S(1)}, u32[]{:S(2)}, u32[]{:S(2)}) collective-permute-start(s16[272,512]{1,0:T(8,128)(2,1)S(1)} %get-tuple-element.54), channel_id=1, source_target_pairs={{0,8},{8,0},{16,24},{24,16},{1,9},{9,1},{17,25},{25,17},{2,10},{10... | collective-permute-start | bytes 835592 | tf_op jit(solution)/shard_map/ppermute | solution.py:18
  44.3 6.8 %collective-permute-start.7 = (s16[144,512]{1,0:T(8,128)(2,1)S(1)}, s16[144,512]{1,0:T(8,128)(2,1)S(1)}, u32[]{:S(2)}, u32[]{:S(2)}) collective-permute-start(s16[144,512]{1,0:T(8,128)(2,1)S(1)} %get-tuple-element.56), channel_id=1, source_target_pairs={{0,2},{2,0},{4,6},{6,4},{1,3},{3,1},{5,7},{7,5},{8,10},{10,8},{12,... | collective-permute-start | bytes 442376 | tf_op jit(solution)/shard_map/ppermute | solution.py:18
  44.8 11.8 %collective-permute-start.8 = (s16[144,512]{1,0:T(8,128)(2,1)S(1)}, s16[144,512]{1,0:T(8,128)(2,1)S(1)}, u32[]{:S(2)}, u32[]{:S(2)}) collective-permute-start(s16[144,512]{1,0:T(8,128)(2,1)S(1)} %get-tuple-element.57), channel_id=1, source_target_pairs={{0,4},{2,6},{4,0},{6,2},{1,5},{3,7},{5,1},{7,3},{8,12},{10,14},{12... | collective-permute-start | bytes 442376 | tf_op jit(solution)/shard_map/ppermute | solution.py:18
  47.7 11.3 %collective-permute-start.9 = (s16[144,512]{1,0:T(8,128)(2,1)S(1)}, s16[144,512]{1,0:T(8,128)(2,1)S(1)}, u32[]{:S(2)}, u32[]{:S(2)}) collective-permute-start(s16[144,512]{1,0:T(8,128)(2,1)S(1)} %get-tuple-element.58), channel_id=1, source_target_pairs={{0,6},{2,4},{4,2},{6,0},{1,7},{3,5},{5,3},{7,1},{8,14},{10,12},{12... | collective-permute-start | bytes 442376 | tf_op jit(solution)/shard_map/ppermute | solution.py:18
  59.2 8.9 %collective-permute-start.10 = (bf16[128,512]{1,0:T(8,128)(2,1)S(1)}, bf16[128,512]{1,0:T(8,128)(2,1)S(1)}, u32[]{:S(2)}, u32[]{:S(2)}) collective-permute-start(bf16[128,512]{1,0:T(8,128)(2,1)S(1)} %shard_map.81), channel_id=1, source_target_pairs={{0,4},{2,6},{4,0},{6,2},{1,5},{3,7},{5,1},{7,3},{8,12},{10,14},{12... | collective-permute-start | bytes 393224 | tf_op jit(solution)/shard_map/ppermute | solution.py:18
  60.2 10.5 %collective-permute-start.11 = (bf16[128,512]{1,0:T(8,128)(2,1)S(1)}, bf16[128,512]{1,0:T(8,128)(2,1)S(1)}, u32[]{:S(2)}, u32[]{:S(2)}) collective-permute-start(bf16[128,512]{1,0:T(8,128)(2,1)S(1)} %shard_map.81), channel_id=1, source_target_pairs={{0,6},{2,4},{4,2},{6,0},{1,7},{3,5},{5,3},{7,1},{8,14},{10,12},{12... | collective-permute-start | bytes 393224 | tf_op jit(solution)/shard_map/ppermute | solution.py:18
  61.5 11.3 %collective-permute-start.13 = (bf16[128,512]{1,0:T(8,128)(2,1)S(1)}, bf16[128,512]{1,0:T(8,128)(2,1)S(1)}, u32[]{:S(2)}, u32[]{:S(2)}) collective-permute-start(bf16[128,512]{1,0:T(8,128)(2,1)S(1)} %shard_map.81), channel_id=1, source_target_pairs={{0,2},{2,0},{4,6},{6,4},{1,3},{3,1},{5,7},{7,5},{8,10},{10,8},{12,... | collective-permute-start | bytes 393224 | tf_op jit(solution)/shard_map/ppermute | solution.py:18
  70.7 15.5 %collective-permute-start.18 = (bf16[256,512]{1,0:T(8,128)(2,1)S(1)}, bf16[256,512]{1,0:T(8,128)(2,1)S(1)}, u32[]{:S(2)}, u32[]{:S(2)}) collective-permute-start(bf16[256,512]{1,0:T(8,128)(2,1)S(1)} %constant_dynamic-update-slice_fusion.refs_3_), channel_id=1, source_target_pairs={{0,24},{8,16},{16,8},{24,0},{1,25},{9,17},{17,9},{25,1},{2,26},{10... | collective-permute-start | bytes 786440 | tf_op jit(solution)/shard_map/ppermute | solution.py:18
  72.8 9.0 %collective-permute-start.12 = (bf16[256,512]{1,0:T(8,128)(2,1)S(1)}, bf16[256,512]{1,0:T(8,128)(2,1)S(1)}, u32[]{:S(2)}, u32[]{:S(2)}) collective-permute-start(bf16[256,512]{1,0:T(8,128)(2,1)S(1)} %constant_dynamic-update-slice_fusion.refs_3_), channel_id=1, source_target_pairs={{0,8},{8,0},{16,24},{24,16},{1,9},{9,1},{17,25},{25,17},{2,10},{10... | collective-permute-start | bytes 786440 | tf_op jit(solution)/shard_map/ppermute | solution.py:18
  72.8 13.4 %collective-permute-start.17 = (bf16[256,512]{1,0:T(8,128)(2,1)S(1)}, bf16[256,512]{1,0:T(8,128)(2,1)S(1)}, u32[]{:S(2)}, u32[]{:S(2)}) collective-permute-start(bf16[256,512]{1,0:T(8,128)(2,1)S(1)} %pad_maximum_fusion.refs_2_), channel_id=1, source_target_pairs={{0,8},{8,0},{16,24},{24,16},{1,9},{9,1},{17,25},{25,17},{2,10},{10... | collective-permute-start | bytes 786440 | tf_op jit(solution)/shard_map/ppermute | solution.py:18
  75.0 9.3 %collective-permute-start.14 = (bf16[256,512]{1,0:T(8,128)(2,1)S(1)}, bf16[256,512]{1,0:T(8,128)(2,1)S(1)}, u32[]{:S(2)}, u32[]{:S(2)}) collective-permute-start(bf16[256,512]{1,0:T(8,128)(2,1)S(1)} %pad_maximum_fusion.refs_2_), channel_id=1, source_target_pairs={{0,24},{8,16},{16,8},{24,0},{1,25},{9,17},{17,9},{25,1},{2,26},{10... | collective-permute-start | bytes 786440 | tf_op jit(solution)/shard_map/ppermute | solution.py:18
  84.2 6.4 %collective-permute-start.15 = (bf16[256,512]{1,0:T(8,128)(2,1)S(1)}, bf16[256,512]{1,0:T(8,128)(2,1)S(1)}, u32[]{:S(2)}, u32[]{:S(2)}) collective-permute-start(bf16[256,512]{1,0:T(8,128)(2,1)S(1)} %collective-permute-done.14.refs_4_), channel_id=1, source_target_pairs={{0,8},{8,0},{16,24},{24,16},{1,9},{9,1},{17,25},{25,17},{2,10},{10... | collective-permute-start | bytes 786440 | tf_op jit(solution)/shard_map/ppermute | solution.py:18
  84.2 7.6 %collective-permute-start.16 = (bf16[256,512]{1,0:T(8,128)(2,1)S(1)}, bf16[256,512]{1,0:T(8,128)(2,1)S(1)}, u32[]{:S(2)}, u32[]{:S(2)}) collective-permute-start(bf16[256,512]{1,0:T(8,128)(2,1)S(1)} %collective-permute-done.12.refs_3_), channel_id=1, source_target_pairs={{0,24},{8,16},{16,8},{24,0},{1,25},{9,17},{17,9},{25,1},{2,26},{10... | collective-permute-start | bytes 786440 | tf_op jit(solution)/shard_map/ppermute | solution.py:18
  93.1 2.7 %collective-permute-start.19 = (f32[512,512]{1,0:T(8,128)S(1)}, f32[512,512]{1,0:T(8,128)S(1)}, u32[]{:S(2)}, u32[]{:S(2)}) collective-permute-start(f32[512,512]{1,0:T(8,128)S(1)} %get-tuple-element.68), channel_id=1, source_target_pairs={{0,1},{1,0},{2,3},{3,2},{4,5},{5,4},{6,7},{7,6},{8,9},{9,8},{10,11... | collective-permute-start | bytes 3145736 | tf_op jit(solution)/shard_map/ppermute | solution.py:18
  96.1 6.8 %collective-permute-start.20 = (s16[144,512]{1,0:T(8,128)(2,1)S(1)}, s16[144,512]{1,0:T(8,128)(2,1)S(1)}, u32[]{:S(2)}, u32[]{:S(2)}) collective-permute-start(s16[144,512]{1,0:T(8,128)(2,1)S(1)} %get-tuple-element.70), channel_id=1, source_target_pairs={{0,64},{32,96},{64,0},{96,32},{128,192},{160,224},{192,128},{224,1... | collective-permute-start | bytes 442376 | tf_op jit(solution)/shard_map/ppermute | solution.py:18
  97.8 10.0 %collective-permute-start.21 = (s16[144,512]{1,0:T(8,128)(2,1)S(1)}, s16[144,512]{1,0:T(8,128)(2,1)S(1)}, u32[]{:S(2)}, u32[]{:S(2)}) collective-permute-start(s16[144,512]{1,0:T(8,128)(2,1)S(1)} %get-tuple-element.71), channel_id=1, source_target_pairs={{0,128},{32,160},{64,192},{96,224},{128,0},{160,32},{192,64},{224,... | collective-permute-start | bytes 442376 | tf_op jit(solution)/shard_map/ppermute | solution.py:18
  100.7 9.5 %collective-permute-start.22 = (s16[144,512]{1,0:T(8,128)(2,1)S(1)}, s16[144,512]{1,0:T(8,128)(2,1)S(1)}, u32[]{:S(2)}, u32[]{:S(2)}) collective-permute-start(s16[144,512]{1,0:T(8,128)(2,1)S(1)} %get-tuple-element.72), channel_id=1, source_target_pairs={{0,192},{32,224},{64,128},{96,160},{128,64},{160,96},{192,0},{224,... | collective-permute-start | bytes 442376 | tf_op jit(solution)/shard_map/ppermute | solution.py:18
  110.5 10.1 %collective-permute-start.23 = (s16[80,512]{1,0:T(8,128)(2,1)S(1)}, s16[80,512]{1,0:T(8,128)(2,1)S(1)}, u32[]{:S(2)}, u32[]{:S(2)}) collective-permute-start(s16[80,512]{1,0:T(8,128)(2,1)S(1)} %get-tuple-element.74), channel_id=1, source_target_pairs={{0,32},{32,0},{64,96},{96,64},{128,160},{160,128},{192,224},{224,1... | collective-permute-start | bytes 245768 | tf_op jit(solution)/shard_map/ppermute | solution.py:18

commit v3 on v2

v3 whole, which is shorter than its diff:
```python
import jax
import jax.numpy as jnp
from jax import lax
from jax.experimental import pallas as pl
from jax.experimental.pallas import tpu as pltpu
from jax.sharding import Mesh
from jax.sharding import PartitionSpec as P

PW = ("pw_x", "pw_z", "pw_c")
F32, BF16, I16 = jnp.float32, jnp.bfloat16, jnp.int16
TAIL = 16
STREAMS = 2
VMEM_LIMIT = 48 * 1024 * 1024
SMEM, VMEM = pl.BlockSpec(memory_space=pltpu.SMEM), pl.BlockSpec(memory_space=pltpu.VMEM)
ANY = pl.BlockSpec(memory_space=pl.ANY)


def xor_permute(value, axis, mask):
    count = lax.axis_size(axis)
    return lax.ppermute(value, axis, [(i, i ^ mask) for i in range(count)])


def call(body, outs, *args, specs=None, after=(), cost=0, scratch=()):
    specs = specs or [VMEM] * len(args)

    def kernel(*refs):
        body(*refs[: len(args)], *refs[len(args) + len(after) :])

    moved = sum(a.size * a.dtype.itemsize for a in args)
    return pl.pallas_call(
        kernel,
        out_shape=[jax.ShapeDtypeStruct(shape, dtype) for shape, dtype in outs],
        in_specs=specs + [VMEM] * len(after),
        out_specs=[VMEM] * len(outs),
        scratch_shapes=list(scratch),
        compiler_params=pltpu.CompilerParams(vmem_limit_bytes=VMEM_LIMIT),
        cost_estimate=pl.CostEstimate(flops=cost, bytes_accessed=moved, transcendentals=0),
    )(*args, *after)


def project(here, pair_elements, subspace, parts, after=()):
    depth, width = subspace.shape
    rows = pair_elements.shape[0] // (32 * STREAMS) * 2
    order = ((1, 0), (2, 0), (3, 1), (2, 1), (0, 0), (3, 0), (0, 1), (1, 1))
    per = len(order)

    def body(here_ref, a_ref, b_ref, *refs):
        out_refs, (held, sems) = refs[: len(parts)], refs[len(parts) :]
        x, core = here_ref[0], here_ref[2]
        copies = []
        for stream, own in parts:
            base = (core if own else 1 - core) * (16 // 2 * STREAMS) + stream * 2
            for owner, part in order:
                start = (base + lax.bitwise_xor(x, owner) * (2 * STREAMS) + part) * rows
                to = held.at[pl.ds(rows * len(copies), rows), :]
                copies.append(
                    pltpu.make_async_copy(a_ref.at[pl.ds(pl.multiple_of(start, rows), rows), :], to, sems.at[len(copies)])
                )
        for copy in copies:
            copy.start()
        for o, out_ref in enumerate(out_refs):
            for copy in copies[o * per : (o + 1) * per]:
                copy.wait()
            out_ref[...] = jnp.dot(held[o * per * rows : (o + 1) * per * rows, :], b_ref[...], preferred_element_type=F32)

    count = per * len(parts)
    return call(
        body,
        [((per * rows, width), F32)] * len(parts),
        here,
        pair_elements,
        subspace,
        specs=[SMEM, ANY, VMEM],
        after=after,
        cost=2 * count * rows * depth * width,
        scratch=[pltpu.VMEM((count * rows, depth), BF16), pltpu.SemaphoreType.DMA((count,))],
    )


def pack(ref, value):
    rows = value.shape[0]
    top = jnp.maximum(jnp.max(jnp.abs(value), axis=0, keepdims=True), 1e-30)
    level = jnp.clip(jnp.ceil(jnp.log2(top * (1.0 / 32000.0)) * 256.0), -32000.0, 32000.0)
    scaled = value * jnp.exp2(level * (-1.0 / 256.0))
    ref[:rows, :] = jnp.round(scaled).astype(jnp.int32).astype(I16)
    ref[rows:, :] = jnp.broadcast_to(level, (TAIL, value.shape[1])).astype(jnp.int32).astype(I16)


def unpack(ref):
    rows = ref.shape[0] - TAIL
    level = ref[rows:, :].astype(jnp.int32).astype(F32)[0:1, :]
    return ref[:rows, :].astype(jnp.int32).astype(F32) * jnp.exp2(level * (1.0 / 256.0))


def first_messages(own_ref, other_ref, kept_ref, a_ref, b_ref):
    rows = own_ref.shape[0] // 4
    pack(a_ref, own_ref[:rows, :] + other_ref[:rows, :])
    pack(b_ref, own_ref[rows : 2 * rows, :] + other_ref[rows : 2 * rows, :])
    kept_ref[...] = own_ref[2 * rows :, :] + other_ref[2 * rows :, :]


def second_messages(sum_ref, a_in, b_in, kept_ref, a_ref, b_ref):
    rows = sum_ref.shape[0] // 4
    for part, (came, out) in enumerate(((a_in, a_ref), (b_in, b_ref))):
        at = 2 * part * rows
        total = sum_ref[at : at + 2 * rows, :] + unpack(came)
        kept_ref[part * rows : (part + 1) * rows, :] = total[:rows, :]
        pack(out, total[rows:, :])


def split_four(mine, work_ref, own_ref, message_refs):
    quarter = work_ref.shape[0] // 4

    def rows_of(owner):
        return work_ref[pl.ds(pl.multiple_of(owner * quarter, quarter), quarter), :]

    own_ref[...] = rows_of(mine)
    for mask, out in enumerate(message_refs):
        pack(out, rows_of(lax.bitwise_xor(mine, mask + 1)))


def third_messages(here_ref, kept_ref, a_in, b_in, own_ref, m1_ref, m2_ref, m3_ref, work_ref):
    half = kept_ref.shape[0] // 2
    work_ref[:half, :] = kept_ref[:half, :] + unpack(a_in)
    work_ref[half:, :] = kept_ref[half:, :] + unpack(b_in)
    split_four(here_ref[1], work_ref, own_ref, (m1_ref, m2_ref, m3_ref))


def last_sum(own_ref, m1_in, m2_in, m3_in, out_ref):
    out_ref[...] = (own_ref[...] + unpack(m1_in) + unpack(m2_in) + unpack(m3_in)).astype(BF16)


def join(here_ref, p0_ref, p1_ref, p2_ref, p3_ref, out_ref):
    rows = p0_ref.shape[0]
    for mask, ref in enumerate((p0_ref, p1_ref, p2_ref, p3_ref)):
        owner = lax.bitwise_xor(here_ref[1], mask)
        out_ref[pl.ds(pl.multiple_of(owner * rows, rows), rows), :] = ref[...]


def gram_messages(here_ref, mine_ref, came_ref, own_ref, m1_ref, m2_ref, m3_ref, work_ref):
    work_ref[...] = mine_ref[...] + came_ref[...]
    split_four(here_ref[3] // 2, work_ref, own_ref, (m1_ref, m2_ref, m3_ref))


def gram_halves(here_ref, own_ref, m1_in, m2_in, m3_in, kept_ref, out_ref, work_ref):
    rows = kept_ref.shape[0]
    work_ref[...] = own_ref[...] + unpack(m1_in) + unpack(m2_in) + unpack(m3_in)
    half = here_ref[3] % 2
    kept_ref[...] = work_ref[pl.ds(pl.multiple_of(half * rows, rows), rows), :]
    pack(out_ref, work_ref[pl.ds(pl.multiple_of((1 - half) * rows, rows), rows), :])


def weights_of(cond_index, val_index, cond_energy, val_energy, frequencies, after):
    shape, count = cond_index.shape, len(frequencies)

    def body(val_table, *refs):
        freq_refs, (ci_ref, vi_ref, ce_ref), out_refs = refs[:count], refs[count : count + 3], refs[count + 3 :]
        index = ci_ref[...]
        high, low = index // 128, index % 128
        cond = jnp.zeros(shape, F32)
        for row in range(ce_ref.shape[0]):
            table = jnp.broadcast_to(ce_ref[row : row + 1, :], shape)
            cond = jnp.where(high == row, jnp.take_along_axis(table, low, axis=1), cond)
        level = vi_ref[...]
        val = jnp.zeros(shape, F32)
        for row in range(val_table.shape[0]):
            val = jnp.where(level == row, val_table[row], val)
        spacing = cond - val
        for freq_ref, out_ref in zip(freq_refs, out_refs):
            freq = freq_ref[0]
            out_ref[...] = 2.0 * spacing / (spacing * spacing + freq * freq)

    return call(
        body,
        [(shape, F32)] * count,
        val_energy,
        *frequencies,
        cond_index,
        val_index,
        cond_energy,
        specs=[SMEM] * (1 + count) + [VMEM] * 3,
        after=after,
    )


def gram_step(here, weights, pieces, places, grams, after=()):
    width = pieces[0].shape[1]
    count, kinds = len(pieces), len(weights)
    blocks = pieces[0].shape[0] // 128

    def body(here_ref, *refs):
        w_refs, came, before, out_refs = refs[:kinds], refs[kinds : kinds + count], refs[kinds + count : -kinds], refs[-kinds:]
        totals = [ref[...] for ref in before] or [None] * kinds
        for ref, (stream, owner) in zip(came, places):
            first = ((here_ref[2] * 4 + lax.bitwise_xor(here_ref[0], owner)) * STREAMS + stream) * blocks
            parts = [[] for _ in range(kinds)]
            for j in range(blocks):
                rows = ref[128 * j : 128 * (j + 1), :].astype(F32).T
                for part, w_ref in zip(parts, w_refs):
                    part.append((rows * w_ref[pl.ds(first + j, 1), :]).astype(BF16))
            for kind, part in enumerate(parts):
                term = jnp.dot(jnp.concatenate(part, axis=1), ref[...], preferred_element_type=F32)
                totals[kind] = term if totals[kind] is None else totals[kind] + term
        for out_ref, total in zip(out_refs, totals):
            out_ref[...] = total

    return call(
        body,
        [((width, width), F32)] * kinds,
        here,
        *weights,
        *pieces,
        *grams,
        cost=2 * kinds * width * width * sum(p.shape[0] for p in pieces),
        specs=[SMEM] + [VMEM] * (kinds + count + len(grams)),
        after=after,
    )


def on_device(pair_elements, subspace, val_energy, cond_energy, val_index, cond_index, frequencies):
    here = jnp.stack([lax.axis_index(name).astype(jnp.int32) for name in PW + ("pair",)])
    rows, width = pair_elements.shape[0], subspace.shape[1]
    unit = rows // (32 * STREAMS)
    message = lambda count: ((count + TAIL, width), I16)
    sums = lambda count: ((count, width), F32)
    both = range(STREAMS)

    (other,) = project(here, pair_elements, subspace, [(0, False)])
    came = [xor_permute(other, "pw_c", 1)]
    own, other = project(here, pair_elements, subspace, [(0, True), (1, False)], [other])
    came.append(xor_permute(other, "pw_c", 1))
    first = [message(4 * unit)] * 2
    kept, a, b = [None] * 2, [None] * 2, [None] * 2
    kept[0], a[0], b[0] = call(first_messages, [sums(8 * unit)] + first, own, came[0], after=[other])
    (own,) = project(here, pair_elements, subspace, [(1, True)], [kept[0]])
    kept[1], a[1], b[1] = call(first_messages, [sums(8 * unit)] + first, own, came[1])
    weights = weights_of(
        cond_index.reshape(-1, 128),
        val_index.reshape(-1, 128),
        cond_energy.reshape(-1, 128),
        val_energy,
        (frequencies, xor_permute(frequencies, "pw_c", 1)),
        [kept[1]],
    )

    last = weights[0]
    for s in both:
        a[s], b[s] = xor_permute(a[s], "pw_x", 1), xor_permute(b[s], "pw_x", 3)
    for s in both:
        last, a[s], b[s] = call(
            second_messages, [sums(4 * unit)] + [message(2 * unit)] * 2, kept[s], a[s], b[s], after=[last]
        )
        kept[s] = last
        a[s], b[s] = xor_permute(a[s], "pw_x", 3), xor_permute(b[s], "pw_x", 1)
    came = [None] * 2
    for s in both:
        last, *out = call(
            third_messages,
            [sums(unit)] + [message(unit)] * 3,
            here,
            kept[s],
            a[s],
            b[s],
            specs=[SMEM] + [VMEM] * 3,
            after=[last],
            scratch=[pltpu.VMEM((4 * unit, width), F32)],
        )
        came[s] = [last] + [xor_permute(value, "pw_z", mask + 1) for mask, value in enumerate(out)]

    pieces = [None] * 2
    for s in both:
        last = call(last_sum, [((unit, width), BF16)], *came[s], after=[last])[0]
        pieces[s] = [last] + [xor_permute(last, "pw_z", mask) for mask in (1, 2, 3)]
    quarters, near, far = [None] * 2, [None] * 2, [None] * 2
    for s in both:
        last = call(join, [((4 * unit, width), BF16)], here, *pieces[s], specs=[SMEM] + [VMEM] * 4, after=[last])[0]
        quarters[s] = last
        near[s], far[s] = xor_permute(last, "pw_x", 1), xor_permute(last, "pw_x", 3)
        near[s], far[s] = lax.optimization_barrier((near[s], far[s]))
    across = [xor_permute(far[0], "pw_x", 1), xor_permute(near[1], "pw_x", 3)]
    grams = gram_step(here, weights, quarters, [(0, 0), (1, 0)], [], [last])
    grams = gram_step(here, weights, [near[0], far[0]], [(0, 1), (0, 3)], grams)
    grams = gram_step(here, weights, [near[1], far[1], across[0]], [(1, 1), (1, 3), (0, 2)], grams)
    mine, theirs = gram_step(here, weights, [across[1]], [(1, 2)], grams)

    part = width // 4
    own, *out = call(
        gram_messages,
        [sums(part)] + [message(part)] * 3,
        here,
        mine,
        xor_permute(theirs, "pw_c", 1),
        specs=[SMEM] + [VMEM] * 2,
        scratch=[pltpu.VMEM((width, width), F32)],
    )
    came = [xor_permute(value, "pair", 2 * (mask + 1)) for mask, value in enumerate(out)]
    own, out = call(
        gram_halves,
        [sums(part // 2), message(part // 2)],
        here,
        own,
        *came,
        specs=[SMEM] + [VMEM] * 4,
        scratch=[pltpu.VMEM((part, width), F32)],
    )
    factor = -4.0 / (rows * lax.axis_size("pair"))

    def finish(own_ref, came_ref, out_ref):
        out_ref[...] = (own_ref[...] + unpack(came_ref)) * factor

    return call(finish, [sums(part // 2)], own, xor_permute(out, "pair", 1))[0][None]


def solution(mesh):
    torus = Mesh(mesh.devices.reshape(mesh.shape["pair"], 4, 4, 2), ("pair",) + PW)
    return jax.shard_map(
        on_device,
        mesh=torus,
        in_specs=(P("pair", PW), P(PW, None), P(), P(), P("pair"), P("pair"), P(PW)),
        out_specs=P(PW, "pair", None),
        check_vma=False,
    )
```

time: 121 us -> 119 us (0.983)
  waiting for transfers between devices: 55.4 us -> 41.1 us
  starting transfers between devices: 33.7 us -> 45.6 us
  other arithmetic: 1.39 us -> 0.08 us
    ppermute x24 -> x34, waiting for transfers between devices: 55.4 us -> 41.1 us  [xor_permute(): return lax.ppermute(value, axis, [(i, i ^ mask) for i in range(count)])]
    ppermute x24 -> x34, starting transfers between devices: 33.7 us -> 45.6 us  [xor_permute(): return lax.ppermute(value, axis, [(i, i ^ mask) for i in range(count)])]
    unnamed x15 -> x16, local copies, waits for them, and re-layouts: 2.98 us -> 3.71 us
    pallas_call x15 -> x21, Pallas kernels: 27 us -> 26.9 us  [call(): pl.pallas_call(kernel, out_shape=[jax.ShapeDtypeStruct(shape, dtype) for...]
  transfers between devices with their start and end apart: 24 -> 34, of which waited for: 19 -> 18; matrix products, arithmetic and copies ran while one was open for 1% -> 0% of each run, Pallas kernels for 15% -> 17%
where the time goes in v3:
time: 119 us; the launch traced here: 118 us
  starting transfers between devices  45.6 us (38%)
  waiting for transfers between devices  41.1 us (35%)
  Pallas kernels  26.9 us (23%)
  local copies, waits for them, and re-layouts  3.71 us (3%)
    ppermute x34, starting transfers between devices, xor_permute(): return lax.ppermute(value, axis, [(i, i ^ mask) for i in range(count)])  45.6 us
    ppermute x34, waiting for transfers between devices, xor_permute(): return lax.ppermute(value, axis, [(i, i ^ mask) for i in range(count)])  41.1 us
    pallas_call x21, Pallas kernels, call(): pl.pallas_call(kernel, out_shape=[jax.ShapeDtypeStruct(shape, dtype) for...  26.9 us
    unnamed x16, local copies, waits for them, and re-layouts  3.71 us
  transfers between devices with their start and end apart: 34, of which 18 were waited for; matrix products, arithmetic and copies ran while one was open for 0% of the time, Pallas kernels for 17%

profile of v3, /device:TPU:32, one launch (start us, length us, event | category | flops | bytes accessed | tf_op | source)
XLA Modules:
  0.0 118.4 jit_solution(17137904276785317025)
XLA Ops:
  0.1 1.2 %copy-done = bf16[1024,512]{1,0:T(8,128)(2,1)S(1)} copy-done((bf16[1024,512]{1,0:T(8,128)(2,1)S(1)}, bf16[1024,512]{1,0:T(8,128)(2,1)}, u32[]{:S(2)}) %copy-start) | copy-done | bytes 1048600
  1.3 3.4 %shard_map.73.refs_3_ = f32[1024,512]{1,0:T(8,128)S(1)} custom-call(s32[4]{0:T(128)S(1)} %pad_add_fusion.refs_0_, bf16[4096,1024]{1,0:T(8,128)(2,1)} %refs_1_.6, bf16[1024,512]{1,0:T(8,128)(2,1)S(1)} %copy-done), custom_call_target="tpu_custom_call" | custom-call | flops 1073741824 | bytes 9437200 | tf_op jit(solution)/shard_map/pallas_call | solution.py:30
  4.8 1.2 %copy-done.2 = f32[1024,512]{1,0:T(8,128)} copy-done((f32[1024,512]{1,0:T(8,128)}, f32[1024,512]{1,0:T(8,128)S(1)}, u32[]{:S(2)}) %copy-start.2) | copy-done | bytes 2097176
  6.0 5.8 %shard_map.74 = (f32[1024,512]{1,0:T(8,128)S(1)}, f32[1024,512]{1,0:T(8,128)S(1)}) custom-call(s32[4]{0:T(128)S(1)} %pad_add_fusion.refs_0_, bf16[4096,1024]{1,0:T(8,128)(2,1)} %refs_1_.6, bf16[1024,512]{1,0:T(8,128)(2,1)S(1)} %copy-done, f32[1024,512]{1,0:T(8,128)} %copy-done.2), custom_call_target="tpu_custom_call" | custom-call | flops 2147483648 | bytes 9437200 | tf_op jit(solution)/shard_map/pallas_call | solution.py:30
  11.9 1.2 %copy-done.3 = f32[1024,512]{1,0:T(8,128)} copy-done((f32[1024,512]{1,0:T(8,128)}, f32[1024,512]{1,0:T(8,128)S(1)}, u32[]{:S(2)}) %copy-start.3) | copy-done | bytes 2097176
  13.1 2.0 %shard_map.75 = (f32[512,512]{1,0:T(8,128)S(1)}, s16[272,512]{1,0:T(8,128)(2,1)S(1)}, s16[272,512]{1,0:T(8,128)(2,1)S(1)}) custom-call(f32[1024,512]{1,0:T(8,128)S(1)} %get-tuple-element.47.refs_0_, f32[1024,512]{1,0:T(8,128)S(1)} %collective-permute-done.1.refs_1_, f32[1024,512]{1,0:T(8,128)} %copy-done.3), custom_call_target="tpu_custom_call" | custom-call | bytes 4194304 | tf_op jit(solution)/shard_map/pallas_call | solution.py:30
  15.2 1.6 %collective-permute-start.5 = (s16[272,512]{1,0:T(8,128)(2,1)S(1)}, s16[272,512]{1,0:T(8,128)(2,1)S(1)}, u32[]{:S(2)}, u32[]{:S(2)}) collective-permute-start(s16[272,512]{1,0:T(8,128)(2,1)S(1)} %get-tuple-element.55), channel_id=1, source_target_pairs={{0,8},{8,0},{16,24},{24,16},{1,9},{9,1},{17,25},{25,17},{2,10},{10... | collective-permute-start | bytes 835592 | tf_op jit(solution)/shard_map/ppermute | solution.py:20
  16.7 2.1 %collective-permute-start.6 = (s16[272,512]{1,0:T(8,128)(2,1)S(1)}, s16[272,512]{1,0:T(8,128)(2,1)S(1)}, u32[]{:S(2)}, u32[]{:S(2)}) collective-permute-start(s16[272,512]{1,0:T(8,128)(2,1)S(1)} %get-tuple-element.56), channel_id=1, source_target_pairs={{0,24},{8,16},{16,8},{24,0},{1,25},{9,17},{17,9},{25,1},{2,26},{10... | collective-permute-start | bytes 835592 | tf_op jit(solution)/shard_map/ppermute | solution.py:20
  18.8 3.4 %shard_map.76.refs_0_ = f32[1024,512]{1,0:T(8,128)S(1)} custom-call(s32[4]{0:T(128)S(1)} %pad_add_fusion.refs_0_, bf16[4096,1024]{1,0:T(8,128)(2,1)} %refs_1_.6, bf16[1024,512]{1,0:T(8,128)(2,1)S(1)} %copy-done.1, f32[512,512]{1,0:T(8,128)S(1)} %get-tuple-element.49.refs_3_.refs_0_), custom_call_target="tpu_custom_call" | custom-call | flops 1073741824 | bytes 9437200 | tf_op jit(solution)/shard_map/pallas_call | solution.py:30
  25.2 1.4 %shard_map.78 = (f32[32,128]{1,0:T(8,128)S(1)}, f32[32,128]{1,0:T(8,128)S(1)}) custom-call(f32[16]{0:T(128)S(1)} %copy-done.7, f32[1]{0:T(128)S(6)} %copy.8.refs_1_, f32[1]{0:T(128)} %collective-permute-done.refs_2_, s32[32,128]{1,0:T(8,128)S(1)} %bitcast.8, s32[32,128]{1,0:T(8,128)S(1)} %bitcast.9, f32[16,128]{1,0:T(8,128)S(1)} %bitcast.10, ...), custom_call_target="tpu_custom_call" | custom-call | bytes 41032 | tf_op jit(solution)/shard_map/pallas_call | solution.py:30
  26.9 2.7 %collective-permute-start.9 = (s16[144,512]{1,0:T(8,128)(2,1)S(1)}, s16[144,512]{1,0:T(8,128)(2,1)S(1)}, u32[]{:S(2)}, u32[]{:S(2)}) collective-permute-start(s16[144,512]{1,0:T(8,128)(2,1)S(1)} %get-tuple-element.61), channel_id=1, source_target_pairs={{0,24},{8,16},{16,8},{24,0},{1,25},{9,17},{17,9},{25,1},{2,26},{10... | collective-permute-start | bytes 442376 | tf_op jit(solution)/shard_map/ppermute | solution.py:20
  30.5 2.5 %collective-permute-done.4.refs_2_ = s16[272,512]{1,0:T(8,128)(2,1)S(1)} collective-permute-done((s16[272,512]{1,0:T(8,128)(2,1)S(1)}, s16[272,512]{1,0:T(8,128)(2,1)S(1)}, u32[]{:S(2)}, u32[]{:S(2)}) %collective-permute-start.4) | collective-permute-done | bytes 278560 | tf_op jit(solution)/shard_map/ppermute | solution.py:20
  33.3 1.7 %collective-permute-start.7 = (s16[144,512]{1,0:T(8,128)(2,1)S(1)}, s16[144,512]{1,0:T(8,128)(2,1)S(1)}, u32[]{:S(2)}, u32[]{:S(2)}) collective-permute-start(s16[144,512]{1,0:T(8,128)(2,1)S(1)} %get-tuple-element.59), channel_id=1, source_target_pairs={{0,24},{8,16},{16,8},{24,0},{1,25},{9,17},{17,9},{25,1},{2,26},{10... | collective-permute-start | bytes 442376 | tf_op jit(solution)/shard_map/ppermute | solution.py:20
  35.0 1.0 collective-permute-done.9.refs_2_
  37.4 2.8 %collective-permute-start.15 = (s16[80,512]{1,0:T(8,128)(2,1)S(1)}, s16[80,512]{1,0:T(8,128)(2,1)S(1)}, u32[]{:S(2)}, u32[]{:S(2)}) collective-permute-start(s16[80,512]{1,0:T(8,128)(2,1)S(1)} %get-tuple-element.69), channel_id=1, source_target_pairs={{0,4},{2,6},{4,0},{6,2},{1,5},{3,7},{5,1},{7,3},{8,12},{10,14},{12... | collective-permute-start | bytes 245768 | tf_op jit(solution)/shard_map/ppermute | solution.py:20
  41.4 1.6 %collective-permute-start.11 = (s16[80,512]{1,0:T(8,128)(2,1)S(1)}, s16[80,512]{1,0:T(8,128)(2,1)S(1)}, u32[]{:S(2)}, u32[]{:S(2)}) collective-permute-start(s16[80,512]{1,0:T(8,128)(2,1)S(1)} %get-tuple-element.65), channel_id=1, source_target_pairs={{0,2},{2,0},{4,6},{6,4},{1,3},{3,1},{5,7},{7,5},{8,10},{10,8},{12,... | collective-permute-start | bytes 245768 | tf_op jit(solution)/shard_map/ppermute | solution.py:20
  43.0 2.5 %collective-permute-start.12 = (s16[80,512]{1,0:T(8,128)(2,1)S(1)}, s16[80,512]{1,0:T(8,128)(2,1)S(1)}, u32[]{:S(2)}, u32[]{:S(2)}) collective-permute-start(s16[80,512]{1,0:T(8,128)(2,1)S(1)} %get-tuple-element.66), channel_id=1, source_target_pairs={{0,4},{2,6},{4,0},{6,2},{1,5},{3,7},{5,1},{7,3},{8,12},{10,14},{12... | collective-permute-start | bytes 245768 | tf_op jit(solution)/shard_map/ppermute | solution.py:20
  45.9 6.4 %collective-permute-done.16.refs_3_ = s16[80,512]{1,0:T(8,128)(2,1)S(1)} collective-permute-done((s16[80,512]{1,0:T(8,128)(2,1)S(1)}, s16[80,512]{1,0:T(8,128)(2,1)S(1)}, u32[]{:S(2)}, u32[]{:S(2)}) %collective-permute-start.16) | collective-permute-done | bytes 81952 | tf_op jit(solution)/shard_map/ppermute | solution.py:20
  52.4 1.8 %collective-permute-start.22 = (bf16[64,512]{1,0:T(8,128)(2,1)S(1)}, bf16[64,512]{1,0:T(8,128)(2,1)S(1)}, u32[]{:S(2)}, u32[]{:S(2)}) collective-permute-start(bf16[64,512]{1,0:T(8,128)(2,1)S(1)} %shard_map.83.refs_4_.refs_1_), channel_id=1, source_target_pairs={{0,6},{2,4},{4,2},{6,0},{1,7},{3,5},{5,3},{7,1},{8,14},{10,12},{12... | collective-permute-start | bytes 196616 | tf_op jit(solution)/shard_map/ppermute | solution.py:20
  54.2 1.8 %collective-permute-start.20 = (bf16[64,512]{1,0:T(8,128)(2,1)S(1)}, bf16[64,512]{1,0:T(8,128)(2,1)S(1)}, u32[]{:S(2)}, u32[]{:S(2)}) collective-permute-start(bf16[64,512]{1,0:T(8,128)(2,1)S(1)} %shard_map.83.refs_4_.refs_1_), channel_id=1, source_target_pairs={{0,2},{2,0},{4,6},{6,4},{1,3},{3,1},{5,7},{7,5},{8,10},{10,8},{12,... | collective-permute-start | bytes 196616 | tf_op jit(solution)/shard_map/ppermute | solution.py:20
  56.0 0.9 collective-permute-done.13.refs_3_
  57.0 0.8 collective-permute-done.22.refs_4_
  57.8 1.5 %collective-permute-done.21.refs_3_ = bf16[64,512]{1,0:T(8,128)(2,1)S(1)} collective-permute-done((bf16[64,512]{1,0:T(8,128)(2,1)S(1)}, bf16[64,512]{1,0:T(8,128)(2,1)S(1)}, u32[]{:S(2)}, u32[]{:S(2)}) %collective-permute-start.21) | collective-permute-done | bytes 65568 | tf_op jit(solution)/shard_map/ppermute | solution.py:20
  59.9 2.9 %collective-permute-start.27 = (bf16[256,512]{1,0:T(8,128)(2,1)S(1)}, bf16[256,512]{1,0:T(8,128)(2,1)S(1)}, u32[]{:S(2)}, u32[]{:S(2)}) collective-permute-start(bf16[256,512]{1,0:T(8,128)(2,1)S(1)} %shard_map.85.refs_5_.refs_3_), channel_id=1, source_target_pairs={{0,24},{8,16},{16,8},{24,0},{1,25},{9,17},{17,9},{25,1},{2,26},{10... | collective-permute-start | bytes 786440 | tf_op jit(solution)/shard_map/ppermute | solution.py:20
  62.9 1.3 %collective-permute-start.19 = (bf16[64,512]{1,0:T(8,128)(2,1)S(1)}, bf16[64,512]{1,0:T(8,128)(2,1)S(1)}, u32[]{:S(2)}, u32[]{:S(2)}) collective-permute-start(bf16[64,512]{1,0:T(8,128)(2,1)S(1)} %shard_map.84.refs_5_.refs_1_), channel_id=1, source_target_pairs={{0,6},{2,4},{4,2},{6,0},{1,7},{3,5},{5,3},{7,1},{8,14},{10,12},{12... | collective-permute-start | bytes 196616 | tf_op jit(solution)/shard_map/ppermute | solution.py:20
  64.1 2.2 %collective-permute-start.18 = (bf16[64,512]{1,0:T(8,128)(2,1)S(1)}, bf16[64,512]{1,0:T(8,128)(2,1)S(1)}, u32[]{:S(2)}, u32[]{:S(2)}) collective-permute-start(bf16[64,512]{1,0:T(8,128)(2,1)S(1)} %shard_map.84.refs_5_.refs_1_), channel_id=1, source_target_pairs={{0,4},{2,6},{4,0},{6,2},{1,5},{3,7},{5,1},{7,3},{8,12},{10,14},{12... | collective-permute-start | bytes 196616 | tf_op jit(solution)/shard_map/ppermute | solution.py:20
  67.7 1.9 %collective-permute-done.18.refs_3_ = bf16[64,512]{1,0:T(8,128)(2,1)S(1)} collective-permute-done((bf16[64,512]{1,0:T(8,128)(2,1)S(1)}, bf16[64,512]{1,0:T(8,128)(2,1)S(1)}, u32[]{:S(2)}, u32[]{:S(2)}) %collective-permute-start.18) | collective-permute-done | bytes 65568 | tf_op jit(solution)/shard_map/ppermute | solution.py:20
  69.5 1.2 %collective-permute-done.17.refs_2_ = bf16[64,512]{1,0:T(8,128)(2,1)S(1)} collective-permute-done((bf16[64,512]{1,0:T(8,128)(2,1)S(1)}, bf16[64,512]{1,0:T(8,128)(2,1)S(1)}, u32[]{:S(2)}, u32[]{:S(2)}) %collective-permute-start.17) | collective-permute-done | bytes 65568 | tf_op jit(solution)/shard_map/ppermute | solution.py:20
  71.3 0.9 collective-permute-start.24
  72.3 1.3 %collective-permute-start.23 = (bf16[256,512]{1,0:T(8,128)(2,1)S(1)}, bf16[256,512]{1,0:T(8,128)(2,1)S(1)}, u32[]{:S(2)}, u32[]{:S(2)}) collective-permute-start(bf16[256,512]{1,0:T(8,128)(2,1)S(1)} %shard_map.86.refs_4_.refs_5_), channel_id=1, source_target_pairs={{0,8},{8,0},{16,24},{24,16},{1,9},{9,1},{17,25},{25,17},{2,10},{10... | collective-permute-start | bytes 786440 | tf_op jit(solution)/shard_map/ppermute | solution.py:20
  73.5 0.8 collective-permute-start.28
  74.3 5.6 %collective-permute-done.24.refs_4_ = bf16[256,512]{1,0:T(8,128)(2,1)S(1)} collective-permute-done((bf16[256,512]{1,0:T(8,128)(2,1)S(1)}, bf16[256,512]{1,0:T(8,128)(2,1)S(1)}, u32[]{:S(2)}, u32[]{:S(2)}) %collective-permute-start.24) | collective-permute-done | bytes 262176 | tf_op jit(solution)/shard_map/ppermute | solution.py:20
  79.9 1.9 %collective-permute-start.25 = (bf16[256,512]{1,0:T(8,128)(2,1)S(1)}, bf16[256,512]{1,0:T(8,128)(2,1)S(1)}, u32[]{:S(2)}, u32[]{:S(2)}) collective-permute-start(bf16[256,512]{1,0:T(8,128)(2,1)S(1)} %collective-permute-done.23.refs_3_), channel_id=1, source_target_pairs={{0,24},{8,16},{16,8},{24,0},{1,25},{9,17},{17,9},{25,1},{2,26},{10... | collective-permute-start | bytes 786440 | tf_op jit(solution)/shard_map/ppermute | solution.py:20
  81.8 1.3 %shard_map.87 = (f32[512,512]{1,0:T(8,128)S(1)}, f32[512,512]{1,0:T(8,128)S(1)}) custom-call(s32[4]{0:T(128)S(1)} %pad_add_fusion.refs_0_, f32[32,128]{1,0:T(8,128)S(1)} %get-tuple-element.51.refs_3_.refs_1_, f32[32,128]{1,0:T(8,128)S(1)} %get-tuple-element.52.refs_2_, bf16[256,512]{1,0:T(8,128)(2,1)S(1)} %shard_map.85.refs_5_.refs_3_, ...), custom_call_target="tpu_custom_call" | custom-call | flops 536870912 | bytes 557072 | tf_op jit(solution)/shard_map/pallas_call | solution.py:30
  83.1 1.3 %shard_map.88 = (f32[512,512]{1,0:T(8,128)S(1)}, f32[512,512]{1,0:T(8,128)S(1)}) custom-call(s32[4]{0:T(128)S(1)} %pad_add_fusion.refs_0_, f32[32,128]{1,0:T(8,128)S(1)} %get-tuple-element.51.refs_3_.refs_1_, f32[32,128]{1,0:T(8,128)S(1)} %get-tuple-element.52.refs_2_, bf16[256,512]{1,0:T(8,128)(2,1)S(1)} %collective-permute-done.26.refs_3_, ...), custom_call_target="tpu_custom_call" | custom-call | flops 536870912 | bytes 2654224 | tf_op jit(solution)/shard_map/pallas_call | solution.py:30
  84.4 1.6 %shard_map.89 = (f32[512,512]{1,0:T(8,128)S(1)}, f32[512,512]{1,0:T(8,128)S(1)}) custom-call(s32[4]{0:T(128)S(1)} %pad_add_fusion.refs_0_, f32[32,128]{1,0:T(8,128)S(1)} %get-tuple-element.51.refs_3_.refs_1_, f32[32,128]{1,0:T(8,128)S(1)} %get-tuple-element.52.refs_2_, bf16[256,512]{1,0:T(8,128)(2,1)S(1)} %collective-permute-done.23.refs_3_, ...), custom_call_target="tpu_custom_call" | custom-call | flops 805306368 | bytes 2916368 | tf_op jit(solution)/shard_map/pallas_call | solution.py:30
  86.0 1.5 %collective-permute-done.25.refs_3_ = bf16[256,512]{1,0:T(8,128)(2,1)S(1)} collective-permute-done((bf16[256,512]{1,0:T(8,128)(2,1)S(1)}, bf16[256,512]{1,0:T(8,128)(2,1)S(1)}, u32[]{:S(2)}, u32[]{:S(2)}) %collective-permute-start.25) | collective-permute-done | bytes 262176 | tf_op jit(solution)/shard_map/ppermute | solution.py:20
  87.4 1.0 shard_map.90
  88.8 2.6 %collective-permute-done.29.refs_2_ = f32[512,512]{1,0:T(8,128)S(1)} collective-permute-done((f32[512,512]{1,0:T(8,128)S(1)}, f32[512,512]{1,0:T(8,128)S(1)}, u32[]{:S(2)}, u32[]{:S(2)}) %collective-permute-start.29) | collective-permute-done | bytes 1048608 | tf_op jit(solution)/shard_map/ppermute | solution.py:20
  91.5 0.8 shard_map.91
  92.2 1.7 %collective-permute-start.30 = (s16[144,512]{1,0:T(8,128)(2,1)S(1)}, s16[144,512]{1,0:T(8,128)(2,1)S(1)}, u32[]{:S(2)}, u32[]{:S(2)}) collective-permute-start(s16[144,512]{1,0:T(8,128)(2,1)S(1)} %get-tuple-element.84), channel_id=1, source_target_pairs={{0,64},{32,96},{64,0},{96,32},{128,192},{160,224},{192,128},{224,1... | collective-permute-start | bytes 442376 | tf_op jit(solution)/shard_map/ppermute | solution.py:20
  93.9 2.9 %collective-permute-start.31 = (s16[144,512]{1,0:T(8,128)(2,1)S(1)}, s16[144,512]{1,0:T(8,128)(2,1)S(1)}, u32[]{:S(2)}, u32[]{:S(2)}) collective-permute-start(s16[144,512]{1,0:T(8,128)(2,1)S(1)} %get-tuple-element.85), channel_id=1, source_target_pairs={{0,128},{32,160},{64,192},{96,224},{128,0},{160,32},{192,64},{224,... | collective-permute-start | bytes 442376 | tf_op jit(solution)/shard_map/ppermute | solution.py:20
  97.0 2.0 %collective-permute-done.30.refs_2_ = s16[144,512]{1,0:T(8,128)(2,1)S(1)} collective-permute-done((s16[144,512]{1,0:T(8,128)(2,1)S(1)}, s16[144,512]{1,0:T(8,128)(2,1)S(1)}, u32[]{:S(2)}, u32[]{:S(2)}) %collective-permute-start.30) | collective-permute-done | bytes 147488 | tf_op jit(solution)/shard_map/ppermute | solution.py:20
  99.0 4.9 %collective-permute-done.31.refs_3_ = s16[144,512]{1,0:T(8,128)(2,1)S(1)} collective-permute-done((s16[144,512]{1,0:T(8,128)(2,1)S(1)}, s16[144,512]{1,0:T(8,128)(2,1)S(1)}, u32[]{:S(2)}, u32[]{:S(2)}) %collective-permute-start.31) | collective-permute-done | bytes 147488 | tf_op jit(solution)/shard_map/ppermute | solution.py:20
  103.9 2.4 %collective-permute-done.32.refs_4_ = s16[144,512]{1,0:T(8,128)(2,1)S(1)} collective-permute-done((s16[144,512]{1,0:T(8,128)(2,1)S(1)}, s16[144,512]{1,0:T(8,128)(2,1)S(1)}, u32[]{:S(2)}, u32[]{:S(2)}) %collective-permute-start.32) | collective-permute-done | bytes 147488 | tf_op jit(solution)/shard_map/ppermute | solution.py:20
  106.3 0.8 shard_map.92
  107.1 6.8 %collective-permute-start.33 = (s16[80,512]{1,0:T(8,128)(2,1)S(1)}, s16[80,512]{1,0:T(8,128)(2,1)S(1)}, u32[]{:S(2)}, u32[]{:S(2)}) collective-permute-start(s16[80,512]{1,0:T(8,128)(2,1)S(1)} %get-tuple-element.88), channel_id=1, source_target_pairs={{0,32},{32,0},{64,96},{96,64},{128,160},{160,128},{192,224},{224,1... | collective-permute-start | bytes 245768 | tf_op jit(solution)/shard_map/ppermute | solution.py:20
  113.9 3.8 %collective-permute-done.33.refs_1_ = s16[80,512]{1,0:T(8,128)(2,1)S(1)} collective-permute-done((s16[80,512]{1,0:T(8,128)(2,1)S(1)}, s16[80,512]{1,0:T(8,128)(2,1)S(1)}, u32[]{:S(2)}, u32[]{:S(2)}) %collective-permute-start.33) | collective-permute-done | bytes 81952 | tf_op jit(solution)/shard_map/ppermute | solution.py:20
  (58 shorter events, 10.9 us)
Async XLA Ops:
  0.1 1.2 %copy-start = (bf16[1024,512]{1,0:T(8,128)(2,1)S(1)}, bf16[1024,512]{1,0:T(8,128)(2,1)}, u32[]{:S(2)}) copy-start(bf16[1024,512]{1,0:T(8,128)(2,1)} %refs_2_.5) | copy-start | bytes 3145732
  4.7 1.3 %copy-start.2 = (f32[1024,512]{1,0:T(8,128)}, f32[1024,512]{1,0:T(8,128)S(1)}, u32[]{:S(2)}) copy-start(f32[1024,512]{1,0:T(8,128)S(1)} %shard_map.73.refs_3_) | copy-start | bytes 6291460
  4.7 7.2 %collective-permute-start.1 = (f32[1024,512]{1,0:T(8,128)S(1)}, f32[1024,512]{1,0:T(8,128)S(1)}, u32[]{:S(2)}, u32[]{:S(2)}) collective-permute-start(f32[1024,512]{1,0:T(8,128)S(1)} %shard_map.73.refs_3_), channel_id=1, source_target_pairs={{0,1},{1,0},{2,3},{3,2},{4,5},{5,4},{6,7},{7,6},{8,9},{9,8},{10,11... | collective-permute-start | bytes 6291464 | tf_op jit(solution)/shard_map/ppermute | solution.py:20
  11.8 1.3 %copy-start.3 = (f32[1024,512]{1,0:T(8,128)}, f32[1024,512]{1,0:T(8,128)S(1)}, u32[]{:S(2)}) copy-start(f32[1024,512]{1,0:T(8,128)S(1)} %get-tuple-element.48.refs_2_) | copy-start | bytes 6291460
  11.8 10.5 %collective-permute-start.2 = (f32[1024,512]{1,0:T(8,128)S(1)}, f32[1024,512]{1,0:T(8,128)S(1)}, u32[]{:S(2)}, u32[]{:S(2)}) collective-permute-start(f32[1024,512]{1,0:T(8,128)S(1)} %get-tuple-element.48.refs_2_), channel_id=1, source_target_pairs={{0,1},{1,0},{2,3},{3,2},{4,5},{5,4},{6,7},{7,6},{8,9},{9,8},{10,11... | collective-permute-start | bytes 6291464 | tf_op jit(solution)/shard_map/ppermute | solution.py:20
  13.1 5.7 %copy-start.1 = (bf16[1024,512]{1,0:T(8,128)(2,1)S(1)}, bf16[1024,512]{1,0:T(8,128)(2,1)}, u32[]{:S(2)}) copy-start(bf16[1024,512]{1,0:T(8,128)(2,1)} %refs_2_.5) | copy-start | bytes 3145732
  15.2 11.4 %collective-permute-start.5 = (s16[272,512]{1,0:T(8,128)(2,1)S(1)}, s16[272,512]{1,0:T(8,128)(2,1)S(1)}, u32[]{:S(2)}, u32[]{:S(2)}) collective-permute-start(s16[272,512]{1,0:T(8,128)(2,1)S(1)} %get-tuple-element.55), channel_id=1, source_target_pairs={{0,8},{8,0},{16,24},{24,16},{1,9},{9,1},{17,25},{25,17},{2,10},{10... | collective-permute-start | bytes 835592 | tf_op jit(solution)/shard_map/ppermute | solution.py:20
  16.7 9.9 %collective-permute-start.6 = (s16[272,512]{1,0:T(8,128)(2,1)S(1)}, s16[272,512]{1,0:T(8,128)(2,1)S(1)}, u32[]{:S(2)}, u32[]{:S(2)}) collective-permute-start(s16[272,512]{1,0:T(8,128)(2,1)S(1)} %get-tuple-element.56), channel_id=1, source_target_pairs={{0,24},{8,16},{16,8},{24,0},{1,25},{9,17},{17,9},{25,1},{2,26},{10... | collective-permute-start | bytes 835592 | tf_op jit(solution)/shard_map/ppermute | solution.py:20
  22.2 2.9 %copy-start.4 = (s32[4096]{0:T(1024)S(1)}, s32[4096]{0:T(1024)}, u32[]{:S(2)}) copy-start(s32[4096]{0:T(1024)} %param.12) | copy-start | bytes 49156
  22.2 2.9 %copy-start.5 = (s32[4096]{0:T(1024)S(1)}, s32[4096]{0:T(1024)}, u32[]{:S(2)}) copy-start(s32[4096]{0:T(1024)} %param.11) | copy-start | bytes 49156
  22.2 2.9 %copy-start.6 = (f32[2048]{0:T(1024)S(1)}, f32[2048]{0:T(1024)}, u32[]{:S(2)}) copy-start(f32[2048]{0:T(1024)} %param.10) | copy-start | bytes 24580
  22.2 2.9 %copy-start.7 = (f32[16]{0:T(128)S(1)}, f32[16]{0:T(128)}, u32[]{:S(2)}) copy-start(f32[16]{0:T(128)} %refs_0_.1) | copy-start | bytes 196
  22.6 7.9 %collective-permute-start.3 = (s16[272,512]{1,0:T(8,128)(2,1)S(1)}, s16[272,512]{1,0:T(8,128)(2,1)S(1)}, u32[]{:S(2)}, u32[]{:S(2)}) collective-permute-start(s16[272,512]{1,0:T(8,128)(2,1)S(1)} %get-tuple-element.53), channel_id=1, source_target_pairs={{0,8},{8,0},{16,24},{24,16},{1,9},{9,1},{17,25},{25,17},{2,10},{10... | collective-permute-start | bytes 835592 | tf_op jit(solution)/shard_map/ppermute | solution.py:20
  23.3 9.8 %collective-permute-start.4 = (s16[272,512]{1,0:T(8,128)(2,1)S(1)}, s16[272,512]{1,0:T(8,128)(2,1)S(1)}, u32[]{:S(2)}, u32[]{:S(2)}) collective-permute-start(s16[272,512]{1,0:T(8,128)(2,1)S(1)} %get-tuple-element.54), channel_id=1, source_target_pairs={{0,24},{8,16},{16,8},{24,0},{1,25},{9,17},{17,9},{25,1},{2,26},{10... | collective-permute-start | bytes 835592 | tf_op jit(solution)/shard_map/ppermute | solution.py:20
  23.9 1.2 %collective-permute-start = (f32[1]{0:T(128)}, f32[1]{0:T(128)}, u32[]{:S(2)}, u32[]{:S(2)}) collective-permute-start(f32[1]{0:T(128)} %param.13), channel_id=1, source_target_pairs={{0,1},{1,0},{2,3},{3,2},{4,5},{5,4},{6,7},{7,6},{8,9},{9,8},{10,11... | collective-permute-start | bytes 20 | tf_op jit(solution)/shard_map/ppermute | solution.py:20
  26.9 9.1 %collective-permute-start.9 = (s16[144,512]{1,0:T(8,128)(2,1)S(1)}, s16[144,512]{1,0:T(8,128)(2,1)S(1)}, u32[]{:S(2)}, u32[]{:S(2)}) collective-permute-start(s16[144,512]{1,0:T(8,128)(2,1)S(1)} %get-tuple-element.61), channel_id=1, source_target_pairs={{0,24},{8,16},{16,8},{24,0},{1,25},{9,17},{17,9},{25,1},{2,26},{10... | collective-permute-start | bytes 442376 | tf_op jit(solution)/shard_map/ppermute | solution.py:20
  29.6 6.4 %collective-permute-start.10 = (s16[144,512]{1,0:T(8,128)(2,1)S(1)}, s16[144,512]{1,0:T(8,128)(2,1)S(1)}, u32[]{:S(2)}, u32[]{:S(2)}) collective-permute-start(s16[144,512]{1,0:T(8,128)(2,1)S(1)} %get-tuple-element.62), channel_id=1, source_target_pairs={{0,8},{8,0},{16,24},{24,16},{1,9},{9,1},{17,25},{25,17},{2,10},{10... | collective-permute-start | bytes 442376 | tf_op jit(solution)/shard_map/ppermute | solution.py:20
  33.3 7.4 %collective-permute-start.7 = (s16[144,512]{1,0:T(8,128)(2,1)S(1)}, s16[144,512]{1,0:T(8,128)(2,1)S(1)}, u32[]{:S(2)}, u32[]{:S(2)}) collective-permute-start(s16[144,512]{1,0:T(8,128)(2,1)S(1)} %get-tuple-element.59), channel_id=1, source_target_pairs={{0,24},{8,16},{16,8},{24,0},{1,25},{9,17},{17,9},{25,1},{2,26},{10... | collective-permute-start | bytes 442376 | tf_op jit(solution)/shard_map/ppermute | solution.py:20
  35.0 5.7 %collective-permute-start.8 = (s16[144,512]{1,0:T(8,128)(2,1)S(1)}, s16[144,512]{1,0:T(8,128)(2,1)S(1)}, u32[]{:S(2)}, u32[]{:S(2)}) collective-permute-start(s16[144,512]{1,0:T(8,128)(2,1)S(1)} %get-tuple-element.60), channel_id=1, source_target_pairs={{0,8},{8,0},{16,24},{24,16},{1,9},{9,1},{17,25},{25,17},{2,10},{10... | collective-permute-start | bytes 442376 | tf_op jit(solution)/shard_map/ppermute | solution.py:20
  36.7 8.7 %collective-permute-start.14 = (s16[80,512]{1,0:T(8,128)(2,1)S(1)}, s16[80,512]{1,0:T(8,128)(2,1)S(1)}, u32[]{:S(2)}, u32[]{:S(2)}) collective-permute-start(s16[80,512]{1,0:T(8,128)(2,1)S(1)} %get-tuple-element.68), channel_id=1, source_target_pairs={{0,2},{2,0},{4,6},{6,4},{1,3},{3,1},{5,7},{7,5},{8,10},{10,8},{12,... | collective-permute-start | bytes 245768 | tf_op jit(solution)/shard_map/ppermute | solution.py:20
  37.4 8.5 %collective-permute-start.15 = (s16[80,512]{1,0:T(8,128)(2,1)S(1)}, s16[80,512]{1,0:T(8,128)(2,1)S(1)}, u32[]{:S(2)}, u32[]{:S(2)}) collective-permute-start(s16[80,512]{1,0:T(8,128)(2,1)S(1)} %get-tuple-element.69), channel_id=1, source_target_pairs={{0,4},{2,6},{4,0},{6,2},{1,5},{3,7},{5,1},{7,3},{8,12},{10,14},{12... | collective-permute-start | bytes 245768 | tf_op jit(solution)/shard_map/ppermute | solution.py:20
  40.2 12.1 %collective-permute-start.16 = (s16[80,512]{1,0:T(8,128)(2,1)S(1)}, s16[80,512]{1,0:T(8,128)(2,1)S(1)}, u32[]{:S(2)}, u32[]{:S(2)}) collective-permute-start(s16[80,512]{1,0:T(8,128)(2,1)S(1)} %get-tuple-element.70), channel_id=1, source_target_pairs={{0,6},{2,4},{4,2},{6,0},{1,7},{3,5},{5,3},{7,1},{8,14},{10,12},{12... | collective-permute-start | bytes 245768 | tf_op jit(solution)/shard_map/ppermute | solution.py:20
  41.4 12.8 %collective-permute-start.11 = (s16[80,512]{1,0:T(8,128)(2,1)S(1)}, s16[80,512]{1,0:T(8,128)(2,1)S(1)}, u32[]{:S(2)}, u32[]{:S(2)}) collective-permute-start(s16[80,512]{1,0:T(8,128)(2,1)S(1)} %get-tuple-element.65), channel_id=1, source_target_pairs={{0,2},{2,0},{4,6},{6,4},{1,3},{3,1},{5,7},{7,5},{8,10},{10,8},{12,... | collective-permute-start | bytes 245768 | tf_op jit(solution)/shard_map/ppermute | solution.py:20
  43.0 13.0 %collective-permute-start.12 = (s16[80,512]{1,0:T(8,128)(2,1)S(1)}, s16[80,512]{1,0:T(8,128)(2,1)S(1)}, u32[]{:S(2)}, u32[]{:S(2)}) collective-permute-start(s16[80,512]{1,0:T(8,128)(2,1)S(1)} %get-tuple-element.66), channel_id=1, source_target_pairs={{0,4},{2,6},{4,0},{6,2},{1,5},{3,7},{5,1},{7,3},{8,12},{10,14},{12... | collective-permute-start | bytes 245768 | tf_op jit(solution)/shard_map/ppermute | solution.py:20
  45.4 11.5 %collective-permute-start.13 = (s16[80,512]{1,0:T(8,128)(2,1)S(1)}, s16[80,512]{1,0:T(8,128)(2,1)S(1)}, u32[]{:S(2)}, u32[]{:S(2)}) collective-permute-start(s16[80,512]{1,0:T(8,128)(2,1)S(1)} %get-tuple-element.67), channel_id=1, source_target_pairs={{0,6},{2,4},{4,2},{6,0},{1,7},{3,5},{5,3},{7,1},{8,14},{10,12},{12... | collective-permute-start | bytes 245768 | tf_op jit(solution)/shard_map/ppermute | solution.py:20
  52.4 5.4 %collective-permute-start.22 = (bf16[64,512]{1,0:T(8,128)(2,1)S(1)}, bf16[64,512]{1,0:T(8,128)(2,1)S(1)}, u32[]{:S(2)}, u32[]{:S(2)}) collective-permute-start(bf16[64,512]{1,0:T(8,128)(2,1)S(1)} %shard_map.83.refs_4_.refs_1_), channel_id=1, source_target_pairs={{0,6},{2,4},{4,2},{6,0},{1,7},{3,5},{5,3},{7,1},{8,14},{10,12},{12... | collective-permute-start | bytes 196616 | tf_op jit(solution)/shard_map/ppermute | solution.py:20
  54.2 5.2 %collective-permute-start.21 = (bf16[64,512]{1,0:T(8,128)(2,1)S(1)}, bf16[64,512]{1,0:T(8,128)(2,1)S(1)}, u32[]{:S(2)}, u32[]{:S(2)}) collective-permute-start(bf16[64,512]{1,0:T(8,128)(2,1)S(1)} %shard_map.83.refs_4_.refs_1_), channel_id=1, source_target_pairs={{0,4},{2,6},{4,0},{6,2},{1,5},{3,7},{5,1},{7,3},{8,12},{10,14},{12... | collective-permute-start | bytes 196616 | tf_op jit(solution)/shard_map/ppermute | solution.py:20
  54.2 5.2 %collective-permute-start.20 = (bf16[64,512]{1,0:T(8,128)(2,1)S(1)}, bf16[64,512]{1,0:T(8,128)(2,1)S(1)}, u32[]{:S(2)}, u32[]{:S(2)}) collective-permute-start(bf16[64,512]{1,0:T(8,128)(2,1)S(1)} %shard_map.83.refs_4_.refs_1_), channel_id=1, source_target_pairs={{0,2},{2,0},{4,6},{6,4},{1,3},{3,1},{5,7},{7,5},{8,10},{10,8},{12,... | collective-permute-start | bytes 196616 | tf_op jit(solution)/shard_map/ppermute | solution.py:20
  59.9 13.6 %collective-permute-start.27 = (bf16[256,512]{1,0:T(8,128)(2,1)S(1)}, bf16[256,512]{1,0:T(8,128)(2,1)S(1)}, u32[]{:S(2)}, u32[]{:S(2)}) collective-permute-start(bf16[256,512]{1,0:T(8,128)(2,1)S(1)} %shard_map.85.refs_5_.refs_3_), channel_id=1, source_target_pairs={{0,24},{8,16},{16,8},{24,0},{1,25},{9,17},{17,9},{25,1},{2,26},{10... | collective-permute-start | bytes 786440 | tf_op jit(solution)/shard_map/ppermute | solution.py:20
  62.9 10.7 %collective-permute-start.26 = (bf16[256,512]{1,0:T(8,128)(2,1)S(1)}, bf16[256,512]{1,0:T(8,128)(2,1)S(1)}, u32[]{:S(2)}, u32[]{:S(2)}) collective-permute-start(bf16[256,512]{1,0:T(8,128)(2,1)S(1)} %shard_map.85.refs_5_.refs_3_), channel_id=1, source_target_pairs={{0,8},{8,0},{16,24},{24,16},{1,9},{9,1},{17,25},{25,17},{2,10},{10... | collective-permute-start | bytes 786440 | tf_op jit(solution)/shard_map/ppermute | solution.py:20
  62.9 4.8 %collective-permute-start.19 = (bf16[64,512]{1,0:T(8,128)(2,1)S(1)}, bf16[64,512]{1,0:T(8,128)(2,1)S(1)}, u32[]{:S(2)}, u32[]{:S(2)}) collective-permute-start(bf16[64,512]{1,0:T(8,128)(2,1)S(1)} %shard_map.84.refs_5_.refs_1_), channel_id=1, source_target_pairs={{0,6},{2,4},{4,2},{6,0},{1,7},{3,5},{5,3},{7,1},{8,14},{10,12},{12... | collective-permute-start | bytes 196616 | tf_op jit(solution)/shard_map/ppermute | solution.py:20
  64.1 5.4 %collective-permute-start.18 = (bf16[64,512]{1,0:T(8,128)(2,1)S(1)}, bf16[64,512]{1,0:T(8,128)(2,1)S(1)}, u32[]{:S(2)}, u32[]{:S(2)}) collective-permute-start(bf16[64,512]{1,0:T(8,128)(2,1)S(1)} %shard_map.84.refs_5_.refs_1_), channel_id=1, source_target_pairs={{0,4},{2,6},{4,0},{6,2},{1,5},{3,7},{5,1},{7,3},{8,12},{10,14},{12... | collective-permute-start | bytes 196616 | tf_op jit(solution)/shard_map/ppermute | solution.py:20
  66.3 4.4 %collective-permute-start.17 = (bf16[64,512]{1,0:T(8,128)(2,1)S(1)}, bf16[64,512]{1,0:T(8,128)(2,1)S(1)}, u32[]{:S(2)}, u32[]{:S(2)}) collective-permute-start(bf16[64,512]{1,0:T(8,128)(2,1)S(1)} %shard_map.84.refs_5_.refs_1_), channel_id=1, source_target_pairs={{0,2},{2,0},{4,6},{6,4},{1,3},{3,1},{5,7},{7,5},{8,10},{10,8},{12,... | collective-permute-start | bytes 196616 | tf_op jit(solution)/shard_map/ppermute | solution.py:20
  71.3 8.6 %collective-permute-start.24 = (bf16[256,512]{1,0:T(8,128)(2,1)S(1)}, bf16[256,512]{1,0:T(8,128)(2,1)S(1)}, u32[]{:S(2)}, u32[]{:S(2)}) collective-permute-start(bf16[256,512]{1,0:T(8,128)(2,1)S(1)} %shard_map.86.refs_4_.refs_5_), channel_id=1, source_target_pairs={{0,24},{8,16},{16,8},{24,0},{1,25},{9,17},{17,9},{25,1},{2,26},{10... | collective-permute-start | bytes 786440 | tf_op jit(solution)/shard_map/ppermute | solution.py:20
  72.3 7.6 %collective-permute-start.23 = (bf16[256,512]{1,0:T(8,128)(2,1)S(1)}, bf16[256,512]{1,0:T(8,128)(2,1)S(1)}, u32[]{:S(2)}, u32[]{:S(2)}) collective-permute-start(bf16[256,512]{1,0:T(8,128)(2,1)S(1)} %shard_map.86.refs_4_.refs_5_), channel_id=1, source_target_pairs={{0,8},{8,0},{16,24},{24,16},{1,9},{9,1},{17,25},{25,17},{2,10},{10... | collective-permute-start | bytes 786440 | tf_op jit(solution)/shard_map/ppermute | solution.py:20
  73.5 10.9 %collective-permute-start.28 = (bf16[256,512]{1,0:T(8,128)(2,1)S(1)}, bf16[256,512]{1,0:T(8,128)(2,1)S(1)}, u32[]{:S(2)}, u32[]{:S(2)}) collective-permute-start(bf16[256,512]{1,0:T(8,128)(2,1)S(1)} %collective-permute-done.27.refs_4_), channel_id=1, source_target_pairs={{0,8},{8,0},{16,24},{24,16},{1,9},{9,1},{17,25},{25,17},{2,10},{10... | collective-permute-start | bytes 786440 | tf_op jit(solution)/shard_map/ppermute | solution.py:20
  79.9 7.6 %collective-permute-start.25 = (bf16[256,512]{1,0:T(8,128)(2,1)S(1)}, bf16[256,512]{1,0:T(8,128)(2,1)S(1)}, u32[]{:S(2)}, u32[]{:S(2)}) collective-permute-start(bf16[256,512]{1,0:T(8,128)(2,1)S(1)} %collective-permute-done.23.refs_3_), channel_id=1, source_target_pairs={{0,24},{8,16},{16,8},{24,0},{1,25},{9,17},{17,9},{25,1},{2,26},{10... | collective-permute-start | bytes 786440 | tf_op jit(solution)/shard_map/ppermute | solution.py:20
  88.5 3.0 %collective-permute-start.29 = (f32[512,512]{1,0:T(8,128)S(1)}, f32[512,512]{1,0:T(8,128)S(1)}, u32[]{:S(2)}, u32[]{:S(2)}) collective-permute-start(f32[512,512]{1,0:T(8,128)S(1)} %get-tuple-element.82), channel_id=1, source_target_pairs={{0,1},{1,0},{2,3},{3,2},{4,5},{5,4},{6,7},{7,6},{8,9},{9,8},{10,11... | collective-permute-start | bytes 3145736 | tf_op jit(solution)/shard_map/ppermute | solution.py:20
  92.2 6.8 %collective-permute-start.30 = (s16[144,512]{1,0:T(8,128)(2,1)S(1)}, s16[144,512]{1,0:T(8,128)(2,1)S(1)}, u32[]{:S(2)}, u32[]{:S(2)}) collective-permute-start(s16[144,512]{1,0:T(8,128)(2,1)S(1)} %get-tuple-element.84), channel_id=1, source_target_pairs={{0,64},{32,96},{64,0},{96,32},{128,192},{160,224},{192,128},{224,1... | collective-permute-start | bytes 442376 | tf_op jit(solution)/shard_map/ppermute | solution.py:20
  93.9 10.0 %collective-permute-start.31 = (s16[144,512]{1,0:T(8,128)(2,1)S(1)}, s16[144,512]{1,0:T(8,128)(2,1)S(1)}, u32[]{:S(2)}, u32[]{:S(2)}) collective-permute-start(s16[144,512]{1,0:T(8,128)(2,1)S(1)} %get-tuple-element.85), channel_id=1, source_target_pairs={{0,128},{32,160},{64,192},{96,224},{128,0},{160,32},{192,64},{224,... | collective-permute-start | bytes 442376 | tf_op jit(solution)/shard_map/ppermute | solution.py:20
  96.8 9.5 %collective-permute-start.32 = (s16[144,512]{1,0:T(8,128)(2,1)S(1)}, s16[144,512]{1,0:T(8,128)(2,1)S(1)}, u32[]{:S(2)}, u32[]{:S(2)}) collective-permute-start(s16[144,512]{1,0:T(8,128)(2,1)S(1)} %get-tuple-element.86), channel_id=1, source_target_pairs={{0,192},{32,224},{64,128},{96,160},{128,64},{160,96},{192,0},{224,... | collective-permute-start | bytes 442376 | tf_op jit(solution)/shard_map/ppermute | solution.py:20
  107.1 10.6 %collective-permute-start.33 = (s16[80,512]{1,0:T(8,128)(2,1)S(1)}, s16[80,512]{1,0:T(8,128)(2,1)S(1)}, u32[]{:S(2)}, u32[]{:S(2)}) collective-permute-start(s16[80,512]{1,0:T(8,128)(2,1)S(1)} %get-tuple-element.88), channel_id=1, source_target_pairs={{0,32},{32,0},{64,96},{96,64},{128,160},{160,128},{192,224},{224,1... | collective-permute-start | bytes 245768 | tf_op jit(solution)/shard_map/ppermute | solution.py:20

commit v4 on v3

v4 whole, which is shorter than its diff:
```python
import jax
import jax.numpy as jnp
from jax import lax
from jax.experimental import pallas as pl
from jax.experimental.pallas import tpu as pltpu
from jax.sharding import Mesh
from jax.sharding import PartitionSpec as P

PW = ("pw_x", "pw_z", "pw_c")
F32, BF16, I16 = jnp.float32, jnp.bfloat16, jnp.int16
TAIL = 16
VMEM_LIMIT = 48 * 1024 * 1024
SMEM, VMEM = pl.BlockSpec(memory_space=pltpu.SMEM), pl.BlockSpec(memory_space=pltpu.VMEM)
ANY = pl.BlockSpec(memory_space=pl.ANY)


def xor_permute(value, axis, mask):
    count = lax.axis_size(axis)
    return lax.ppermute(value, axis, [(i, i ^ mask) for i in range(count)])


def call(body, outs, *args, specs=None, after=(), flag=False, cost=0, scratch=()):
    specs = specs or [VMEM] * len(args)
    outs = list(outs) + [((8, 128), F32)] * flag

    def kernel(*refs):
        refs = list(refs[: len(args)] + refs[len(args) + len(after) :])
        if flag:
            ref = refs.pop(len(args) + len(outs) - 1)
            ref[...] = jnp.zeros(ref.shape, F32)
        body(*refs)

    moved = sum(a.size * a.dtype.itemsize for a in args)
    return pl.pallas_call(
        kernel,
        out_shape=[jax.ShapeDtypeStruct(shape, dtype) for shape, dtype in outs],
        in_specs=specs + [VMEM] * len(after),
        out_specs=[VMEM] * len(outs),
        scratch_shapes=list(scratch),
        compiler_params=pltpu.CompilerParams(vmem_limit_bytes=VMEM_LIMIT),
        cost_estimate=pl.CostEstimate(flops=cost, bytes_accessed=moved, transcendentals=0),
    )(*args, *after)


SENT = ((1, 0), (2, 0), (3, 1), (2, 1))
KEPT = ((0, 0), (3, 0), (0, 1), (1, 1))


def products(here_ref, a_ref, b_ref, out_refs, held, sems, parts):
    rows = held.shape[0] // (len(parts) * len(SENT))
    copies = []
    for own, order in parts:
        base = (here_ref[2] if own else 1 - here_ref[2]) * 8
        for owner, part in order:
            start = (base + lax.bitwise_xor(here_ref[0], owner) * 2 + part) * rows
            to = held.at[pl.ds(rows * len(copies), rows), :]
            copies.append(
                pltpu.make_async_copy(a_ref.at[pl.ds(pl.multiple_of(start, rows), rows), :], to, sems.at[len(copies)])
            )
    for copy in copies:
        copy.start()
    per = len(SENT)
    for o, out_ref in enumerate(out_refs):
        for copy in copies[o * per : (o + 1) * per]:
            copy.wait()
        here = held[o * per * rows : (o + 1) * per * rows, :]
        out_ref[: per * rows, :] = jnp.dot(here, b_ref[...], preferred_element_type=F32)


def product_scratch(pair_elements, parts):
    rows, depth = pair_elements.shape
    return [pltpu.VMEM((rows // 4 * parts, depth), BF16), pltpu.SemaphoreType.DMA((4 * parts,))]


def pack(ref, value):
    rows = value.shape[0]
    top = jnp.maximum(jnp.max(jnp.abs(value), axis=0, keepdims=True), 1e-30)
    level = jnp.clip(jnp.ceil(jnp.log2(top * (1.0 / 32000.0)) * 256.0), -32000.0, 32000.0)
    scaled = value * jnp.exp2(level * (-1.0 / 256.0))
    ref[:rows, :] = jnp.round(scaled).astype(jnp.int32).astype(I16)
    ref[rows:, :] = jnp.broadcast_to(level, (TAIL, value.shape[1])).astype(jnp.int32).astype(I16)


def unpack(ref):
    rows = ref.shape[0] - TAIL
    level = ref[rows:, :].astype(jnp.int32).astype(F32)[0:1, :]
    return ref[:rows, :].astype(jnp.int32).astype(F32) * jnp.exp2(level * (1.0 / 256.0))


def first_messages(own_ref, other_ref, a_ref, b_ref):
    rows = own_ref.shape[0] // 2
    pack(a_ref, own_ref[:rows, :] + other_ref[:rows, :])
    pack(b_ref, own_ref[rows:, :] + other_ref[rows : 2 * rows, :])


def second_messages(own_ref, other_ref, a_in, b_in, kept_ref, a_ref, b_ref):
    rows = own_ref.shape[0] // 4
    for part, (came, out) in enumerate(((a_in, a_ref), (b_in, b_ref))):
        at = 2 * part * rows
        total = own_ref[at : at + 2 * rows, :] + other_ref[at : at + 2 * rows, :] + unpack(came)
        kept_ref[part * rows : (part + 1) * rows, :] = total[:rows, :]
        pack(out, total[rows:, :])


def split_four(mine, work_ref, own_ref, message_refs):
    quarter = work_ref.shape[0] // 4

    def rows_of(owner):
        return work_ref[pl.ds(pl.multiple_of(owner * quarter, quarter), quarter), :]

    own_ref[...] = rows_of(mine)
    for mask, out in enumerate(message_refs):
        pack(out, rows_of(lax.bitwise_xor(mine, mask + 1)))


def third_messages(here_ref, kept_ref, a_in, b_in, own_ref, m1_ref, m2_ref, m3_ref, work_ref):
    half = kept_ref.shape[0] // 2
    work_ref[:half, :] = kept_ref[:half, :] + unpack(a_in)
    work_ref[half:, :] = kept_ref[half:, :] + unpack(b_in)
    split_four(here_ref[1], work_ref, own_ref, (m1_ref, m2_ref, m3_ref))


def last_sum(own_ref, m1_in, m2_in, m3_in, out_ref):
    out_ref[...] = (own_ref[...] + unpack(m1_in) + unpack(m2_in) + unpack(m3_in)).astype(BF16)


def gram_messages(here_ref, mine_ref, came_ref, own_ref, m1_ref, m2_ref, m3_ref, work_ref):
    work_ref[...] = mine_ref[...] + came_ref[...]
    split_four(here_ref[3] // 2, work_ref, own_ref, (m1_ref, m2_ref, m3_ref))


def gram_halves(here_ref, own_ref, m1_in, m2_in, m3_in, kept_ref, out_ref, work_ref):
    rows = kept_ref.shape[0]
    work_ref[...] = own_ref[...] + unpack(m1_in) + unpack(m2_in) + unpack(m3_in)
    half = here_ref[3] % 2
    kept_ref[...] = work_ref[pl.ds(pl.multiple_of(half * rows, rows), rows), :]
    pack(out_ref, work_ref[pl.ds(pl.multiple_of((1 - half) * rows, rows), rows), :])


def fill_weights(val_table, freq_ref, other_freq, ci_ref, vi_ref, ce_ref, out_refs):
    shape = ci_ref.shape
    index = ci_ref[...]
    high, low = index // 128, index % 128
    cond = jnp.zeros(shape, F32)
    for row in range(ce_ref.shape[0]):
        table = jnp.broadcast_to(ce_ref[row : row + 1, :], shape)
        cond = jnp.where(high == row, jnp.take_along_axis(table, low, axis=1), cond)
    level = vi_ref[...]
    val = jnp.zeros(shape, F32)
    for row in range(val_table.shape[0]):
        val = jnp.where(level == row, val_table[row], val)
    spacing = cond - val
    for freq, out_ref in zip((freq_ref[0], other_freq), out_refs):
        out_ref[...] = 2.0 * spacing / (spacing * spacing + freq * freq)


def gram_step(here, weights, pieces, owners, grams, after=()):
    width = pieces[0].shape[1]
    count, kinds = len(pieces), len(weights)

    def body(here_ref, *refs):
        w_refs, came, before, out_refs = refs[:kinds], refs[kinds : kinds + count], refs[kinds + count : -kinds], refs[-kinds:]
        totals = [ref[...] for ref in before] or [None] * kinds
        for ref, (owner, masks) in zip(came, owners):
            first = (here_ref[2] * 4 + lax.bitwise_xor(here_ref[0], owner)) * 4
            parts = [[] for _ in range(kinds)]
            for j, mask in enumerate(masks):
                rows = ref[128 * j : 128 * (j + 1), :].astype(F32).T
                for part, w_ref in zip(parts, w_refs):
                    w = w_ref[pl.ds(first + lax.bitwise_xor(here_ref[1], mask), 1), :]
                    part.append((rows * w).astype(BF16))
            for kind, part in enumerate(parts):
                term = jnp.dot(jnp.concatenate(part, axis=1), ref[...], preferred_element_type=F32)
                totals[kind] = term if totals[kind] is None else totals[kind] + term
        for out_ref, total in zip(out_refs, totals):
            out_ref[...] = total

    return call(
        body,
        [((width, width), F32)] * kinds,
        here,
        *weights,
        *pieces,
        *grams,
        cost=2 * kinds * width * width * sum(p.shape[0] for p in pieces),
        specs=[SMEM] + [VMEM] * (kinds + count + len(grams)),
        after=after,
    )


def on_device(pair_elements, subspace, val_energy, cond_energy, val_index, cond_index, frequencies):
    here = jnp.stack([lax.axis_index(name).astype(jnp.int32) for name in PW + ("pair",)])
    rows, width = pair_elements.shape[0], subspace.shape[1]
    quarter, eighth, piece = rows // 4, rows // 8, rows // 32
    message = lambda count: ((count + TAIL, width), I16)
    sums = lambda count: ((count, width), F32)
    flops = 2 * quarter * pair_elements.shape[1] * width

    def first_products(here_ref, freq_ref, a_ref, b_ref, out_ref, held, sems):
        out_ref[quarter:, :] = jnp.full((8, width), freq_ref[0], F32)
        products(here_ref, a_ref, b_ref, (out_ref,), held, sems, [(False, SENT)])

    def second_products(here_ref, a_ref, b_ref, own_ref, other_ref, held, sems):
        products(here_ref, a_ref, b_ref, (own_ref, other_ref), held, sems, [(True, SENT), (False, KEPT)])

    sent_other, done = call(
        first_products,
        [sums(quarter + 8)],
        here,
        frequencies,
        pair_elements,
        subspace,
        specs=[SMEM, SMEM, ANY, VMEM],
        flag=True,
        cost=flops,
        scratch=product_scratch(pair_elements, 1),
    )
    sent_in = xor_permute(sent_other, "pw_c", 1)
    sent_own, kept_other = call(
        second_products,
        [sums(quarter)] * 2,
        here,
        pair_elements,
        subspace,
        specs=[SMEM, ANY, VMEM],
        after=[done],
        cost=2 * flops,
        scratch=product_scratch(pair_elements, 2),
    )
    kept_in = xor_permute(kept_other, "pw_c", 1)

    late = [sums(quarter), ((rows // 128, 128), F32), ((rows // 128, 128), F32)]

    def late_work(core, before, done):
        def body(here_ref, val_table, freq_ref, a_ref, b_ref, other_ref, ci_ref, vi_ref, ce_ref, *refs):
            old, (kept_ref, *w_refs), (held, sems) = refs[: len(before)], refs[len(before) : len(before) + 3], refs[-2:]

            @pl.when(here_ref[2] == core)
            def _():
                products(here_ref, a_ref, b_ref, (kept_ref,), held, sems, [(True, KEPT)])
                fill_weights(val_table, freq_ref, other_ref[0:1, 0:1], ci_ref, vi_ref, ce_ref, w_refs)

            if before:

                @pl.when(here_ref[2] != core)
                def _():
                    for old_ref, ref in zip(old, (kept_ref, *w_refs)):
                        ref[...] = old_ref[...]

        return call(
            body,
            late,
            here,
            val_energy,
            frequencies,
            pair_elements,
            subspace,
            other_frequency,
            cond_index.reshape(-1, 128),
            val_index.reshape(-1, 128),
            cond_energy.reshape(-1, 128),
            *before,
            specs=[SMEM] * 3 + [ANY] + [VMEM] * (5 + len(before)),
            after=done,
            flag=True,
            cost=flops,
            scratch=product_scratch(pair_elements, 1),
        )

    other_frequency = sent_in[quarter:, :128]
    *early, done = late_work(1, [], [])
    a, b, done = call(first_messages, [message(eighth)] * 2, sent_own, sent_in, after=[done], flag=True)
    kept_own, *weights, done = late_work(0, early, [done])

    a, b = xor_permute(a, "pw_x", 1), xor_permute(b, "pw_x", 3)
    kept, a, b = call(
        second_messages, [sums(eighth)] + [message(eighth // 2)] * 2, kept_own, kept_in, a, b
    )
    a, b = xor_permute(a, "pw_x", 3), xor_permute(b, "pw_x", 1)
    own, *out = call(
        third_messages,
        [sums(piece)] + [message(piece)] * 3,
        here,
        kept,
        a,
        b,
        specs=[SMEM] + [VMEM] * 3,
        scratch=[pltpu.VMEM((eighth, width), F32)],
    )
    came = [xor_permute(value, "pw_z", mask + 1) for mask, value in enumerate(out)]
    coeffs = call(last_sum, [((piece, width), BF16)], own, *came)[0]

    whole = jnp.concatenate([coeffs] + [xor_permute(coeffs, "pw_z", mask) for mask in (1, 2, 3)], axis=0)
    near, far = xor_permute(whole, "pw_x", 1), xor_permute(whole, "pw_x", 3)
    grams = gram_step(here, weights, [whole], [(0, (0, 1, 2, 3))], [])
    near, far, grams = lax.optimization_barrier((near, far, grams))
    top = xor_permute(far[: eighth // 2], "pw_x", 1)
    bottom = xor_permute(near[eighth // 2 :], "pw_x", 3)
    grams = gram_step(here, weights, [near, far], [(1, (0, 1, 2, 3)), (3, (0, 1, 2, 3))], grams)
    mine, theirs = gram_step(here, weights, [top, bottom], [(2, (0, 1)), (2, (2, 3))], grams)

    part = width // 4
    own, *out = call(
        gram_messages,
        [sums(part)] + [message(part)] * 3,
        here,
        mine,
        xor_permute(theirs, "pw_c", 1),
        specs=[SMEM] + [VMEM] * 2,
        scratch=[pltpu.VMEM((width, width), F32)],
    )
    came = [xor_permute(value, "pair", 2 * (mask + 1)) for mask, value in enumerate(out)]
    own, out = call(
        gram_halves,
        [sums(part // 2), message(part // 2)],
        here,
        own,
        *came,
        specs=[SMEM] + [VMEM] * 4,
        scratch=[pltpu.VMEM((part, width), F32)],
    )
    factor = -4.0 / (rows * lax.axis_size("pair"))

    def finish(own_ref, came_ref, out_ref):
        out_ref[...] = (own_ref[...] + unpack(came_ref)) * factor

    return call(finish, [sums(part // 2)], own, xor_permute(out, "pair", 1))[0][None]


def solution(mesh):
    torus = Mesh(mesh.devices.reshape(mesh.shape["pair"], 4, 4, 2), ("pair",) + PW)
    return jax.shard_map(
        on_device,
        mesh=torus,
        in_specs=(P("pair", PW), P(PW, None), P(), P(), P("pair"), P("pair"), P(PW)),
        out_specs=P(PW, "pair", None),
        check_vma=False,
    )
```

time: 119 us -> 124 us (1.042)
  waiting for transfers between devices: 41.1 us -> 70.7 us
  starting transfers between devices: 45.6 us -> 26.4 us
  Pallas kernels: 26.9 us -> 23.1 us
  local copies, waits for them, and re-layouts: 3.71 us -> 1.3 us
    ppermute x34 -> x21, waiting for transfers between devices: 41.1 us -> 70.7 us  [xor_permute(): return lax.ppermute(value, axis, [(i, i ^ mask) for i in range(count)])]
    ppermute x34 -> x21, starting transfers between devices: 45.6 us -> 26.4 us  [xor_permute(): return lax.ppermute(value, axis, [(i, i ^ mask) for i in range(count)])]
    pallas_call x21 -> x14, Pallas kernels: 26.9 us -> 23.1 us  [call(): pl.pallas_call(kernel, out_shape=[jax.ShapeDtypeStruct(shape, dtype) for...]
    unnamed x16 -> x12, local copies, waits for them, and re-layouts: 3.71 us -> 1.26 us
  transfers between devices with their start and end apart: 34 -> 21, of which waited for: 18 -> 17; matrix products, arithmetic and copies ran while one was open for 0% -> 0% of each run, Pallas kernels for 17% -> 10%
where the time goes in v4:
time: 124 us; the launch traced here: 123 us
  waiting for transfers between devices  70.7 us (57%)
  starting transfers between devices  26.4 us (21%)
  Pallas kernels  23.1 us (19%)
  local copies, waits for them, and re-layouts  1.3 us (1%)
    ppermute x21, waiting for transfers between devices, xor_permute(): return lax.ppermute(value, axis, [(i, i ^ mask) for i in range(count)])  70.7 us
    ppermute x21, starting transfers between devices, xor_permute(): return lax.ppermute(value, axis, [(i, i ^ mask) for i in range(count)])  26.4 us
    pallas_call x14, Pallas kernels, call(): pl.pallas_call(kernel, out_shape=[jax.ShapeDtypeStruct(shape, dtype) for...  23.1 us
  transfers between devices with their start and end apart: 21, of which 17 were waited for; matrix products, arithmetic and copies ran while one was open for 0% of the time, Pallas kernels for 10%

profile of v4, /device:TPU:32, one launch (start us, length us, event | category | flops | bytes accessed | tf_op | source)
XLA Modules:
  0.0 122.5 jit_solution(4907561501255756439)
XLA Ops:
  0.7 1.2 copy-done
  2.0 3.3 %shard_map.73 = (f32[1032,512]{1,0:T(8,128)S(1)}, f32[8,128]{1,0:T(8,128)S(1)}) custom-call(s32[4]{0:T(128)S(1)} %pad_add_fusion.refs_0_, f32[1]{0:T(128)S(6)} %copy.8.refs_1_.refs_2_, bf16[4096,1024]{1,0:T(8,128)(2,1)} %refs_3_.5, bf16[1024,512]{1,0:T(8,128)(2,1)S(1)} %copy-done), custom_call_target="tpu_custom_call" | custom-call | flops 1073741824 | bytes 9437204 | tf_op jit(solution)/shard_map/pallas_call | solution.py:34
  5.3 0.1 collective-permute-start
  5.5 4.6 %shard_map.75 = (f32[1024,512]{1,0:T(8,128)S(1)}, f32[1024,512]{1,0:T(8,128)S(1)}) custom-call(s32[4]{0:T(128)S(1)} %pad_add_fusion.refs_0_, bf16[4096,1024]{1,0:T(8,128)(2,1)} %refs_3_.5, bf16[1024,512]{1,0:T(8,128)(2,1)S(1)} %copy-done, f32[8,128]{1,0:T(8,128)S(1)} %get-tuple-element.46.refs_3_), custom_call_target="tpu_custom_call" | custom-call | flops 2147483648 | bytes 9437200 | tf_op jit(solution)/shard_map/pallas_call | solution.py:34
  10.1 0.5 collective-permute-start.1
  10.7 0.6 shard_map.74
  11.3 0.5 shard_map.76
  11.8 1.6 %collective-permute-start.2 = (s16[528,512]{1,0:T(8,128)(2,1)S(1)}, s16[528,512]{1,0:T(8,128)(2,1)S(1)}, u32[]{:S(2)}, u32[]{:S(2)}) collective-permute-start(s16[528,512]{1,0:T(8,128)(2,1)S(1)} %get-tuple-element.54), channel_id=1, source_target_pairs={{0,8},{8,0},{16,24},{24,16},{1,9},{9,1},{17,25},{25,17},{2,10},{10... | collective-permute-start | bytes 1622024 | tf_op jit(solution)/shard_map/ppermute | solution.py:19
  13.4 2.1 %collective-permute-start.3 = (s16[528,512]{1,0:T(8,128)(2,1)S(1)}, s16[528,512]{1,0:T(8,128)(2,1)S(1)}, u32[]{:S(2)}, u32[]{:S(2)}) collective-permute-start(s16[528,512]{1,0:T(8,128)(2,1)S(1)} %get-tuple-element.55), channel_id=1, source_target_pairs={{0,24},{8,16},{16,8},{24,0},{1,25},{9,17},{17,9},{25,1},{2,26},{10... | collective-permute-start | bytes 1622024 | tf_op jit(solution)/shard_map/ppermute | solution.py:19
  15.5 3.9 %shard_map.77 = (f32[1024,512]{1,0:T(8,128)S(1)}, f32[32,128]{1,0:T(8,128)S(1)}, f32[32,128]{1,0:T(8,128)S(1)}, f32[8,128]{1,0:T(8,128)}) custom-call(s32[4]{0:T(128)S(1)} %pad_add_fusion.refs_0_, f32[16]{0:T(128)S(1)} %copy-done.5, f32[1]{0:T(128)S(6)} %copy.8.refs_1_.refs_2_, bf16[4096,1024]{1,0:T(8,128)(2,1)} %refs_3_.5, bf16[1024,512]{1,0:T(8,128)(2,1)S(1)} %copy-done.1, ...), custom_call_target="tpu_custom_call" | custom-call | flops 1073741824 | bytes 11612244 | tf_op jit(solution)/shard_map/pallas_call | solution.py:34
  19.4 5.7 %collective-permute-done.2.refs_2_ = s16[528,512]{1,0:T(8,128)(2,1)S(1)} collective-permute-done((s16[528,512]{1,0:T(8,128)(2,1)S(1)}, s16[528,512]{1,0:T(8,128)(2,1)S(1)}, u32[]{:S(2)}, u32[]{:S(2)}) %collective-permute-start.2) | collective-permute-done | bytes 540704 | tf_op jit(solution)/shard_map/ppermute | solution.py:19
  25.1 3.0 %collective-permute-done.3.refs_3_ = s16[528,512]{1,0:T(8,128)(2,1)S(1)} collective-permute-done((s16[528,512]{1,0:T(8,128)(2,1)S(1)}, s16[528,512]{1,0:T(8,128)(2,1)S(1)}, u32[]{:S(2)}, u32[]{:S(2)}) %collective-permute-start.3) | collective-permute-done | bytes 540704 | tf_op jit(solution)/shard_map/ppermute | solution.py:19
  28.1 2.3 %shard_map.78 = (f32[512,512]{1,0:T(8,128)S(1)}, s16[272,512]{1,0:T(8,128)(2,1)S(1)}, s16[272,512]{1,0:T(8,128)(2,1)S(1)}) custom-call(f32[1024,512]{1,0:T(8,128)S(1)} %get-tuple-element.52.refs_0_, f32[1024,512]{1,0:T(8,128)} %collective-permute-done.1.refs_1_, s16[528,512]{1,0:T(8,128)(2,1)S(1)} %collective-permute-done.2.refs_2_, ...), custom_call_target="tpu_custom_call" | custom-call | bytes 5275648 | tf_op jit(solution)/shard_map/pallas_call | solution.py:34
  30.4 2.2 %collective-permute-start.4 = (s16[272,512]{1,0:T(8,128)(2,1)S(1)}, s16[272,512]{1,0:T(8,128)(2,1)S(1)}, u32[]{:S(2)}, u32[]{:S(2)}) collective-permute-start(s16[272,512]{1,0:T(8,128)(2,1)S(1)} %get-tuple-element.57), channel_id=1, source_target_pairs={{0,24},{8,16},{16,8},{24,0},{1,25},{9,17},{17,9},{25,1},{2,26},{10... | collective-permute-start | bytes 835592 | tf_op jit(solution)/shard_map/ppermute | solution.py:19
  32.6 8.2 %collective-permute-done.4.refs_2_ = s16[272,512]{1,0:T(8,128)(2,1)S(1)} collective-permute-done((s16[272,512]{1,0:T(8,128)(2,1)S(1)}, s16[272,512]{1,0:T(8,128)(2,1)S(1)}, u32[]{:S(2)}, u32[]{:S(2)}) %collective-permute-start.4) | collective-permute-done | bytes 278560 | tf_op jit(solution)/shard_map/ppermute | solution.py:19
  40.9 1.1 collective-permute-done.5.refs_3_
  41.9 1.0 shard_map.79
  42.9 0.2 collective-permute-start.6
  43.1 3.3 %collective-permute-start.7 = (s16[144,512]{1,0:T(8,128)(2,1)S(1)}, s16[144,512]{1,0:T(8,128)(2,1)S(1)}, u32[]{:S(2)}, u32[]{:S(2)}) collective-permute-start(s16[144,512]{1,0:T(8,128)(2,1)S(1)} %get-tuple-element.61), channel_id=1, source_target_pairs={{0,4},{2,6},{4,0},{6,2},{1,5},{3,7},{5,1},{7,3},{8,12},{10,14},{12... | collective-permute-start | bytes 442376 | tf_op jit(solution)/shard_map/ppermute | solution.py:19
  46.4 0.5 collective-permute-start.8
  46.8 2.1 %collective-permute-done.6.refs_1_ = s16[144,512]{1,0:T(8,128)(2,1)S(1)} collective-permute-done((s16[144,512]{1,0:T(8,128)(2,1)S(1)}, s16[144,512]{1,0:T(8,128)(2,1)S(1)}, u32[]{:S(2)}, u32[]{:S(2)}) %collective-permute-start.6) | collective-permute-done | bytes 147488 | tf_op jit(solution)/shard_map/ppermute | solution.py:19
  49.0 8.0 %collective-permute-done.7.refs_2_ = s16[144,512]{1,0:T(8,128)(2,1)S(1)} collective-permute-done((s16[144,512]{1,0:T(8,128)(2,1)S(1)}, s16[144,512]{1,0:T(8,128)(2,1)S(1)}, u32[]{:S(2)}, u32[]{:S(2)}) %collective-permute-start.7) | collective-permute-done | bytes 147488 | tf_op jit(solution)/shard_map/ppermute | solution.py:19
  57.0 3.2 %collective-permute-done.8.refs_3_ = s16[144,512]{1,0:T(8,128)(2,1)S(1)} collective-permute-done((s16[144,512]{1,0:T(8,128)(2,1)S(1)}, s16[144,512]{1,0:T(8,128)(2,1)S(1)}, u32[]{:S(2)}, u32[]{:S(2)}) %collective-permute-start.8) | collective-permute-done | bytes 147488 | tf_op jit(solution)/shard_map/ppermute | solution.py:19
  60.2 0.1 shard_map.80
  60.3 1.6 %collective-permute-start.11 = (bf16[128,512]{1,0:T(8,128)(2,1)S(1)}, bf16[128,512]{1,0:T(8,128)(2,1)S(1)}, u32[]{:S(2)}, u32[]{:S(2)}) collective-permute-start(bf16[128,512]{1,0:T(8,128)(2,1)S(1)} %shard_map.80), channel_id=1, source_target_pairs={{0,6},{2,4},{4,2},{6,0},{1,7},{3,5},{5,3},{7,1},{8,14},{10,12},{12... | collective-permute-start | bytes 393224 | tf_op jit(solution)/shard_map/ppermute | solution.py:19
  62.0 1.9 %collective-permute-start.9 = (bf16[128,512]{1,0:T(8,128)(2,1)S(1)}, bf16[128,512]{1,0:T(8,128)(2,1)S(1)}, u32[]{:S(2)}, u32[]{:S(2)}) collective-permute-start(bf16[128,512]{1,0:T(8,128)(2,1)S(1)} %shard_map.80), channel_id=1, source_target_pairs={{0,2},{2,0},{4,6},{6,4},{1,3},{3,1},{5,7},{7,5},{8,10},{10,8},{12,... | collective-permute-start | bytes 393224 | tf_op jit(solution)/shard_map/ppermute | solution.py:19
  63.9 6.7 %collective-permute-done.11 = bf16[128,512]{1,0:T(8,128)(2,1)S(1)} collective-permute-done((bf16[128,512]{1,0:T(8,128)(2,1)S(1)}, bf16[128,512]{1,0:T(8,128)(2,1)S(1)}, u32[]{:S(2)}, u32[]{:S(2)}) %collective-permute-start.11) | collective-permute-done | bytes 131104 | tf_op jit(solution)/shard_map/ppermute | solution.py:19
  70.6 0.6 collective-permute-done.10
  71.3 1.2 %collective-permute-start.13 = (bf16[512,512]{1,0:T(8,128)(2,1)S(1)}, bf16[512,512]{1,0:T(8,128)(2,1)S(1)}, u32[]{:S(2)}, u32[]{:S(2)}) collective-permute-start(bf16[512,512]{1,0:T(8,128)(2,1)S(1)} %pad_maximum_fusion.refs_3_), channel_id=1, source_target_pairs={{0,24},{8,16},{16,8},{24,0},{1,25},{9,17},{17,9},{25,1},{2,26},{10... | collective-permute-start | bytes 1572872 | tf_op jit(solution)/shard_map/ppermute | solution.py:19
  72.5 1.3 %shard_map.81 = (f32[512,512]{1,0:T(8,128)S(1)}, f32[512,512]{1,0:T(8,128)S(1)}) custom-call(s32[4]{0:T(128)S(1)} %pad_add_fusion.refs_0_, f32[32,128]{1,0:T(8,128)S(1)} %get-tuple-element.50.refs_1_, f32[32,128]{1,0:T(8,128)S(1)} %get-tuple-element.51.refs_2_, bf16[512,512]{1,0:T(8,128)(2,1)S(1)} %pad_maximum_fusion.refs_3_), custom_call_target="tpu_custom_call" | custom-call | flops 536870912 | bytes 557072 | tf_op jit(solution)/shard_map/pallas_call | solution.py:34
  73.8 11.5 %collective-permute-done.13.refs_4_ = bf16[512,512]{1,0:T(8,128)(2,1)S(1)} collective-permute-done((bf16[512,512]{1,0:T(8,128)(2,1)S(1)}, bf16[512,512]{1,0:T(8,128)(2,1)S(1)}, u32[]{:S(2)}, u32[]{:S(2)}) %collective-permute-start.13) | collective-permute-done | bytes 524320 | tf_op jit(solution)/shard_map/ppermute | solution.py:19
  85.4 1.8 %collective-permute-start.15 = (bf16[256,512]{1,0:T(8,128)(2,1)S(1)}, bf16[256,512]{1,0:T(8,128)(2,1)S(1)}, u32[]{:S(2)}, u32[]{:S(2)}) collective-permute-start(bf16[256,512]{1,0:T(8,128)(2,1)S(1)} %slice.11), channel_id=1, source_target_pairs={{0,24},{8,16},{16,8},{24,0},{1,25},{9,17},{17,9},{25,1},{2,26},{10... | collective-permute-start | bytes 786440 | tf_op jit(solution)/shard_map/ppermute | solution.py:19
  87.2 1.9 %shard_map.82 = (f32[512,512]{1,0:T(8,128)S(1)}, f32[512,512]{1,0:T(8,128)S(1)}) custom-call(s32[4]{0:T(128)S(1)} %pad_add_fusion.refs_0_, f32[32,128]{1,0:T(8,128)S(1)} %get-tuple-element.50.refs_1_, f32[32,128]{1,0:T(8,128)S(1)} %get-tuple-element.51.refs_2_, bf16[512,512]{1,0:T(8,128)(2,1)S(1)} %collective-permute-done.12.refs_3_, ...), custom_call_target="tpu_custom_call" | custom-call | flops 1073741824 | bytes 3178512 | tf_op jit(solution)/shard_map/pallas_call | solution.py:34
  89.1 4.0 %collective-permute-done.15.refs_4_ = bf16[256,512]{1,0:T(8,128)(2,1)S(1)} collective-permute-done((bf16[256,512]{1,0:T(8,128)(2,1)S(1)}, bf16[256,512]{1,0:T(8,128)(2,1)S(1)}, u32[]{:S(2)}, u32[]{:S(2)}) %collective-permute-start.15) | collective-permute-done | bytes 262176 | tf_op jit(solution)/shard_map/ppermute | solution.py:19
  93.0 0.5 collective-permute-done.14.refs_3_
  93.6 1.3 %shard_map.83 = (f32[512,512]{1,0:T(8,128)S(1)}, f32[512,512]{1,0:T(8,128)S(1)}) custom-call(s32[4]{0:T(128)S(1)} %pad_add_fusion.refs_0_, f32[32,128]{1,0:T(8,128)S(1)} %get-tuple-element.50.refs_1_, f32[32,128]{1,0:T(8,128)S(1)} %get-tuple-element.51.refs_2_, bf16[256,512]{1,0:T(8,128)(2,1)S(1)} %collective-permute-done.14.refs_3_, ...), custom_call_target="tpu_custom_call" | custom-call | flops 536870912 | bytes 2654224 | tf_op jit(solution)/shard_map/pallas_call | solution.py:34
  95.0 2.6 %collective-permute-done.16.refs_2_ = f32[512,512]{1,0:T(8,128)S(1)} collective-permute-done((f32[512,512]{1,0:T(8,128)S(1)}, f32[512,512]{1,0:T(8,128)S(1)}, u32[]{:S(2)}, u32[]{:S(2)}) %collective-permute-start.16) | collective-permute-done | bytes 1048608 | tf_op jit(solution)/shard_map/ppermute | solution.py:19
  97.6 0.8 shard_map.84
  98.4 1.7 %collective-permute-start.17 = (s16[144,512]{1,0:T(8,128)(2,1)S(1)}, s16[144,512]{1,0:T(8,128)(2,1)S(1)}, u32[]{:S(2)}, u32[]{:S(2)}) collective-permute-start(s16[144,512]{1,0:T(8,128)(2,1)S(1)} %get-tuple-element.74), channel_id=1, source_target_pairs={{0,64},{32,96},{64,0},{96,32},{128,192},{160,224},{192,128},{224,1... | collective-permute-start | bytes 442376 | tf_op jit(solution)/shard_map/ppermute | solution.py:19
  100.1 2.9 %collective-permute-start.18 = (s16[144,512]{1,0:T(8,128)(2,1)S(1)}, s16[144,512]{1,0:T(8,128)(2,1)S(1)}, u32[]{:S(2)}, u32[]{:S(2)}) collective-permute-start(s16[144,512]{1,0:T(8,128)(2,1)S(1)} %get-tuple-element.75), channel_id=1, source_target_pairs={{0,128},{32,160},{64,192},{96,224},{128,0},{160,32},{192,64},{224,... | collective-permute-start | bytes 442376 | tf_op jit(solution)/shard_map/ppermute | solution.py:19
  103.0 0.2 collective-permute-start.19
  103.2 2.0 %collective-permute-done.17.refs_2_ = s16[144,512]{1,0:T(8,128)(2,1)S(1)} collective-permute-done((s16[144,512]{1,0:T(8,128)(2,1)S(1)}, s16[144,512]{1,0:T(8,128)(2,1)S(1)}, u32[]{:S(2)}, u32[]{:S(2)}) %collective-permute-start.17) | collective-permute-done | bytes 147488 | tf_op jit(solution)/shard_map/ppermute | solution.py:19
  105.2 4.9 %collective-permute-done.18.refs_3_ = s16[144,512]{1,0:T(8,128)(2,1)S(1)} collective-permute-done((s16[144,512]{1,0:T(8,128)(2,1)S(1)}, s16[144,512]{1,0:T(8,128)(2,1)S(1)}, u32[]{:S(2)}, u32[]{:S(2)}) %collective-permute-start.18) | collective-permute-done | bytes 147488 | tf_op jit(solution)/shard_map/ppermute | solution.py:19
  110.1 2.4 %collective-permute-done.19.refs_4_ = s16[144,512]{1,0:T(8,128)(2,1)S(1)} collective-permute-done((s16[144,512]{1,0:T(8,128)(2,1)S(1)}, s16[144,512]{1,0:T(8,128)(2,1)S(1)}, u32[]{:S(2)}, u32[]{:S(2)}) %collective-permute-start.19) | collective-permute-done | bytes 147488 | tf_op jit(solution)/shard_map/ppermute | solution.py:19
  112.5 0.8 shard_map.85
  113.3 4.5 %collective-permute-start.20 = (s16[80,512]{1,0:T(8,128)(2,1)S(1)}, s16[80,512]{1,0:T(8,128)(2,1)S(1)}, u32[]{:S(2)}, u32[]{:S(2)}) collective-permute-start(s16[80,512]{1,0:T(8,128)(2,1)S(1)} %get-tuple-element.78), channel_id=1, source_target_pairs={{0,32},{32,0},{64,96},{96,64},{128,160},{160,128},{192,224},{224,1... | collective-permute-start | bytes 245768 | tf_op jit(solution)/shard_map/ppermute | solution.py:19
  117.8 4.0 %collective-permute-done.20.refs_1_ = s16[80,512]{1,0:T(8,128)(2,1)S(1)} collective-permute-done((s16[80,512]{1,0:T(8,128)(2,1)S(1)}, s16[80,512]{1,0:T(8,128)(2,1)S(1)}, u32[]{:S(2)}, u32[]{:S(2)}) %collective-permute-start.20) | collective-permute-done | bytes 81952 | tf_op jit(solution)/shard_map/ppermute | solution.py:19
  121.8 0.7 shard_map.86
  (25 shorter events, 0.3 us)
Async XLA Ops:
  0.7 1.2 %copy-start = (bf16[1024,512]{1,0:T(8,128)(2,1)S(1)}, bf16[1024,512]{1,0:T(8,128)(2,1)}, u32[]{:S(2)}) copy-start(bf16[1024,512]{1,0:T(8,128)(2,1)} %refs_4_.3) | copy-start | bytes 3145732
  5.3 5.4 %collective-permute-start = (f32[1032,512]{1,0:T(8,128)S(1)}, f32[1032,512]{1,0:T(8,128)S(1)}, u32[]{:S(2)}, u32[]{:S(2)}) collective-permute-start(f32[1032,512]{1,0:T(8,128)S(1)} %get-tuple-element.42), channel_id=1, source_target_pairs={{0,1},{1,0},{2,3},{3,2},{4,5},{5,4},{6,7},{7,6},{8,9},{9,8},{10,11... | collective-permute-start | bytes 6340616 | tf_op jit(solution)/shard_map/ppermute | solution.py:19
  5.4 5.3 %copy-start.2 = (s32[4096]{0:T(1024)S(1)}, s32[4096]{0:T(1024)}, u32[]{:S(2)}) copy-start(s32[4096]{0:T(1024)} %param.12) | copy-start | bytes 49156
  5.4 5.2 %copy-start.3 = (s32[4096]{0:T(1024)S(1)}, s32[4096]{0:T(1024)}, u32[]{:S(2)}) copy-start(s32[4096]{0:T(1024)} %param.11) | copy-start | bytes 49156
  5.4 5.2 %copy-start.4 = (f32[2048]{0:T(1024)S(1)}, f32[2048]{0:T(1024)}, u32[]{:S(2)}) copy-start(f32[2048]{0:T(1024)} %param.10) | copy-start | bytes 24580
  5.4 5.2 %copy-start.5 = (f32[16]{0:T(128)S(1)}, f32[16]{0:T(128)}, u32[]{:S(2)}) copy-start(f32[16]{0:T(128)} %refs_1_.6) | copy-start | bytes 196
  10.1 9.3 %collective-permute-start.1 = (f32[1024,512]{1,0:T(8,128)S(1)}, f32[1024,512]{1,0:T(8,128)}, u32[]{:S(2)}, u32[]{:S(2)}) collective-permute-start(f32[1024,512]{1,0:T(8,128)S(1)} %get-tuple-element.53), channel_id=1, source_target_pairs={{0,1},{1,0},{2,3},{3,2},{4,5},{5,4},{6,7},{7,6},{8,9},{9,8},{10,11... | collective-permute-start | bytes 6291464 | tf_op jit(solution)/shard_map/ppermute | solution.py:19
  11.3 4.2 %copy-start.1 = (bf16[1024,512]{1,0:T(8,128)(2,1)S(1)}, bf16[1024,512]{1,0:T(8,128)(2,1)}, u32[]{:S(2)}) copy-start(bf16[1024,512]{1,0:T(8,128)(2,1)} %refs_4_.3) | copy-start | bytes 3145732
  11.8 13.3 %collective-permute-start.2 = (s16[528,512]{1,0:T(8,128)(2,1)S(1)}, s16[528,512]{1,0:T(8,128)(2,1)S(1)}, u32[]{:S(2)}, u32[]{:S(2)}) collective-permute-start(s16[528,512]{1,0:T(8,128)(2,1)S(1)} %get-tuple-element.54), channel_id=1, source_target_pairs={{0,8},{8,0},{16,24},{24,16},{1,9},{9,1},{17,25},{25,17},{2,10},{10... | collective-permute-start | bytes 1622024 | tf_op jit(solution)/shard_map/ppermute | solution.py:19
  13.4 14.7 %collective-permute-start.3 = (s16[528,512]{1,0:T(8,128)(2,1)S(1)}, s16[528,512]{1,0:T(8,128)(2,1)S(1)}, u32[]{:S(2)}, u32[]{:S(2)}) collective-permute-start(s16[528,512]{1,0:T(8,128)(2,1)S(1)} %get-tuple-element.55), channel_id=1, source_target_pairs={{0,24},{8,16},{16,8},{24,0},{1,25},{9,17},{17,9},{25,1},{2,26},{10... | collective-permute-start | bytes 1622024 | tf_op jit(solution)/shard_map/ppermute | solution.py:19
  30.4 10.4 %collective-permute-start.4 = (s16[272,512]{1,0:T(8,128)(2,1)S(1)}, s16[272,512]{1,0:T(8,128)(2,1)S(1)}, u32[]{:S(2)}, u32[]{:S(2)}) collective-permute-start(s16[272,512]{1,0:T(8,128)(2,1)S(1)} %get-tuple-element.57), channel_id=1, source_target_pairs={{0,24},{8,16},{16,8},{24,0},{1,25},{9,17},{17,9},{25,1},{2,26},{10... | collective-permute-start | bytes 835592 | tf_op jit(solution)/shard_map/ppermute | solution.py:19
  32.6 9.3 %collective-permute-start.5 = (s16[272,512]{1,0:T(8,128)(2,1)S(1)}, s16[272,512]{1,0:T(8,128)(2,1)S(1)}, u32[]{:S(2)}, u32[]{:S(2)}) collective-permute-start(s16[272,512]{1,0:T(8,128)(2,1)S(1)} %get-tuple-element.58), channel_id=1, source_target_pairs={{0,8},{8,0},{16,24},{24,16},{1,9},{9,1},{17,25},{25,17},{2,10},{10... | collective-permute-start | bytes 835592 | tf_op jit(solution)/shard_map/ppermute | solution.py:19
  42.9 6.0 %collective-permute-start.6 = (s16[144,512]{1,0:T(8,128)(2,1)S(1)}, s16[144,512]{1,0:T(8,128)(2,1)S(1)}, u32[]{:S(2)}, u32[]{:S(2)}) collective-permute-start(s16[144,512]{1,0:T(8,128)(2,1)S(1)} %get-tuple-element.60), channel_id=1, source_target_pairs={{0,2},{2,0},{4,6},{6,4},{1,3},{3,1},{5,7},{7,5},{8,10},{10,8},{12,... | collective-permute-start | bytes 442376 | tf_op jit(solution)/shard_map/ppermute | solution.py:19
  43.1 13.9 %collective-permute-start.7 = (s16[144,512]{1,0:T(8,128)(2,1)S(1)}, s16[144,512]{1,0:T(8,128)(2,1)S(1)}, u32[]{:S(2)}, u32[]{:S(2)}) collective-permute-start(s16[144,512]{1,0:T(8,128)(2,1)S(1)} %get-tuple-element.61), channel_id=1, source_target_pairs={{0,4},{2,6},{4,0},{6,2},{1,5},{3,7},{5,1},{7,3},{8,12},{10,14},{12... | collective-permute-start | bytes 442376 | tf_op jit(solution)/shard_map/ppermute | solution.py:19
  46.4 13.8 %collective-permute-start.8 = (s16[144,512]{1,0:T(8,128)(2,1)S(1)}, s16[144,512]{1,0:T(8,128)(2,1)S(1)}, u32[]{:S(2)}, u32[]{:S(2)}) collective-permute-start(s16[144,512]{1,0:T(8,128)(2,1)S(1)} %get-tuple-element.62), channel_id=1, source_target_pairs={{0,6},{2,4},{4,2},{6,0},{1,7},{3,5},{5,3},{7,1},{8,14},{10,12},{12... | collective-permute-start | bytes 442376 | tf_op jit(solution)/shard_map/ppermute | solution.py:19
  60.3 10.3 %collective-permute-start.11 = (bf16[128,512]{1,0:T(8,128)(2,1)S(1)}, bf16[128,512]{1,0:T(8,128)(2,1)S(1)}, u32[]{:S(2)}, u32[]{:S(2)}) collective-permute-start(bf16[128,512]{1,0:T(8,128)(2,1)S(1)} %shard_map.80), channel_id=1, source_target_pairs={{0,6},{2,4},{4,2},{6,0},{1,7},{3,5},{5,3},{7,1},{8,14},{10,12},{12... | collective-permute-start | bytes 393224 | tf_op jit(solution)/shard_map/ppermute | solution.py:19
  62.0 9.3 %collective-permute-start.10 = (bf16[128,512]{1,0:T(8,128)(2,1)S(1)}, bf16[128,512]{1,0:T(8,128)(2,1)S(1)}, u32[]{:S(2)}, u32[]{:S(2)}) collective-permute-start(bf16[128,512]{1,0:T(8,128)(2,1)S(1)} %shard_map.80), channel_id=1, source_target_pairs={{0,4},{2,6},{4,0},{6,2},{1,5},{3,7},{5,1},{7,3},{8,12},{10,14},{12... | collective-permute-start | bytes 393224 | tf_op jit(solution)/shard_map/ppermute | solution.py:19
  62.0 9.3 %collective-permute-start.9 = (bf16[128,512]{1,0:T(8,128)(2,1)S(1)}, bf16[128,512]{1,0:T(8,128)(2,1)S(1)}, u32[]{:S(2)}, u32[]{:S(2)}) collective-permute-start(bf16[128,512]{1,0:T(8,128)(2,1)S(1)} %shard_map.80), channel_id=1, source_target_pairs={{0,2},{2,0},{4,6},{6,4},{1,3},{3,1},{5,7},{7,5},{8,10},{10,8},{12,... | collective-permute-start | bytes 393224 | tf_op jit(solution)/shard_map/ppermute | solution.py:19
  71.3 14.0 %collective-permute-start.13 = (bf16[512,512]{1,0:T(8,128)(2,1)S(1)}, bf16[512,512]{1,0:T(8,128)(2,1)S(1)}, u32[]{:S(2)}, u32[]{:S(2)}) collective-permute-start(bf16[512,512]{1,0:T(8,128)(2,1)S(1)} %pad_maximum_fusion.refs_3_), channel_id=1, source_target_pairs={{0,24},{8,16},{16,8},{24,0},{1,25},{9,17},{17,9},{25,1},{2,26},{10... | collective-permute-start | bytes 1572872 | tf_op jit(solution)/shard_map/ppermute | solution.py:19
  72.5 12.8 %collective-permute-start.12 = (bf16[512,512]{1,0:T(8,128)(2,1)S(1)}, bf16[512,512]{1,0:T(8,128)(2,1)S(1)}, u32[]{:S(2)}, u32[]{:S(2)}) collective-permute-start(bf16[512,512]{1,0:T(8,128)(2,1)S(1)} %pad_maximum_fusion.refs_3_), channel_id=1, source_target_pairs={{0,8},{8,0},{16,24},{24,16},{1,9},{9,1},{17,25},{25,17},{2,10},{10... | collective-permute-start | bytes 1572872 | tf_op jit(solution)/shard_map/ppermute | solution.py:19
  85.4 7.7 %collective-permute-start.15 = (bf16[256,512]{1,0:T(8,128)(2,1)S(1)}, bf16[256,512]{1,0:T(8,128)(2,1)S(1)}, u32[]{:S(2)}, u32[]{:S(2)}) collective-permute-start(bf16[256,512]{1,0:T(8,128)(2,1)S(1)} %slice.11), channel_id=1, source_target_pairs={{0,24},{8,16},{16,8},{24,0},{1,25},{9,17},{17,9},{25,1},{2,26},{10... | collective-permute-start | bytes 786440 | tf_op jit(solution)/shard_map/ppermute | solution.py:19
  87.2 6.4 %collective-permute-start.14 = (bf16[256,512]{1,0:T(8,128)(2,1)S(1)}, bf16[256,512]{1,0:T(8,128)(2,1)S(1)}, u32[]{:S(2)}, u32[]{:S(2)}) collective-permute-start(bf16[256,512]{1,0:T(8,128)(2,1)S(1)} %slice.10), channel_id=1, source_target_pairs={{0,8},{8,0},{16,24},{24,16},{1,9},{9,1},{17,25},{25,17},{2,10},{10... | collective-permute-start | bytes 786440 | tf_op jit(solution)/shard_map/ppermute | solution.py:19
  94.9 2.7 %collective-permute-start.16 = (f32[512,512]{1,0:T(8,128)S(1)}, f32[512,512]{1,0:T(8,128)S(1)}, u32[]{:S(2)}, u32[]{:S(2)}) collective-permute-start(f32[512,512]{1,0:T(8,128)S(1)} %get-tuple-element.72), channel_id=1, source_target_pairs={{0,1},{1,0},{2,3},{3,2},{4,5},{5,4},{6,7},{7,6},{8,9},{9,8},{10,11... | collective-permute-start | bytes 3145736 | tf_op jit(solution)/shard_map/ppermute | solution.py:19
  98.4 6.8 %collective-permute-start.17 = (s16[144,512]{1,0:T(8,128)(2,1)S(1)}, s16[144,512]{1,0:T(8,128)(2,1)S(1)}, u32[]{:S(2)}, u32[]{:S(2)}) collective-permute-start(s16[144,512]{1,0:T(8,128)(2,1)S(1)} %get-tuple-element.74), channel_id=1, source_target_pairs={{0,64},{32,96},{64,0},{96,32},{128,192},{160,224},{192,128},{224,1... | collective-permute-start | bytes 442376 | tf_op jit(solution)/shard_map/ppermute | solution.py:19
  100.1 10.0 %collective-permute-start.18 = (s16[144,512]{1,0:T(8,128)(2,1)S(1)}, s16[144,512]{1,0:T(8,128)(2,1)S(1)}, u32[]{:S(2)}, u32[]{:S(2)}) collective-permute-start(s16[144,512]{1,0:T(8,128)(2,1)S(1)} %get-tuple-element.75), channel_id=1, source_target_pairs={{0,128},{32,160},{64,192},{96,224},{128,0},{160,32},{192,64},{224,... | collective-permute-start | bytes 442376 | tf_op jit(solution)/shard_map/ppermute | solution.py:19
  103.0 9.5 %collective-permute-start.19 = (s16[144,512]{1,0:T(8,128)(2,1)S(1)}, s16[144,512]{1,0:T(8,128)(2,1)S(1)}, u32[]{:S(2)}, u32[]{:S(2)}) collective-permute-start(s16[144,512]{1,0:T(8,128)(2,1)S(1)} %get-tuple-element.76), channel_id=1, source_target_pairs={{0,192},{32,224},{64,128},{96,160},{128,64},{160,96},{192,0},{224,... | collective-permute-start | bytes 442376 | tf_op jit(solution)/shard_map/ppermute | solution.py:19
  113.3 8.5 %collective-permute-start.20 = (s16[80,512]{1,0:T(8,128)(2,1)S(1)}, s16[80,512]{1,0:T(8,128)(2,1)S(1)}, u32[]{:S(2)}, u32[]{:S(2)}) collective-permute-start(s16[80,512]{1,0:T(8,128)(2,1)S(1)} %get-tuple-element.78), channel_id=1, source_target_pairs={{0,32},{32,0},{64,96},{96,64},{128,160},{160,128},{192,224},{224,1... | collective-permute-start | bytes 245768 | tf_op jit(solution)/shard_map/ppermute | solution.py:19

commit v5 on v4

v5 whole, which is shorter than its diff:
```python
import jax
import jax.numpy as jnp
from jax import lax
from jax.experimental import pallas as pl
from jax.experimental.pallas import tpu as pltpu
from jax.sharding import Mesh
from jax.sharding import PartitionSpec as P

PW = ("pw_x", "pw_z", "pw_c")
F32, BF16, I16 = jnp.float32, jnp.bfloat16, jnp.int16
TAIL = 16
Z_ORDER, Y_ORDER = (3, 2, 1), (2, 3, 1)
VMEM_LIMIT, VMEM_LARGE = 24 * 1024 * 1024, 46 * 1024 * 1024
SMEM, VMEM = pl.BlockSpec(memory_space=pltpu.SMEM), pl.BlockSpec(memory_space=pltpu.VMEM)
ANY = pl.BlockSpec(memory_space=pl.ANY)


def xor_permute(value, axis, mask):
    count = lax.axis_size(axis)
    return lax.ppermute(value, axis, [(i, i ^ mask) for i in range(count)])


def call(body, outs, *args, specs=None, after=(), flag=False, scratch=(), limit=VMEM_LIMIT):
    specs = specs or [VMEM] * len(args)
    outs = list(outs) + [((8, 128), F32)] * flag

    def kernel(*refs):
        refs = list(refs[: len(args)] + refs[len(args) + len(after) :])
        if flag:
            ref = refs.pop(len(args) + len(outs) - 1)
            ref[...] = jnp.zeros(ref.shape, F32)
        body(*refs)

    return pl.pallas_call(
        kernel,
        out_shape=[jax.ShapeDtypeStruct(shape, dtype) for shape, dtype in outs],
        in_specs=specs + [VMEM] * len(after),
        out_specs=[VMEM] * len(outs),
        scratch_shapes=list(scratch),
        compiler_params=pltpu.CompilerParams(vmem_limit_bytes=limit),
        cost_estimate=pl.CostEstimate(flops=0, bytes_accessed=0, transcendentals=0),
    )(*args, *after)


def products(here_ref, a_ref, b_ref, held, sems, parts):
    rows = held.shape[0] // len(parts)
    copies = []
    for i, (own, owner, _, _) in enumerate(parts):
        core = here_ref[2] if own else 1 - here_ref[2]
        start = (core * 4 + lax.bitwise_xor(here_ref[0], owner)) * rows
        block = a_ref.at[pl.ds(pl.multiple_of(start, rows), rows), :]
        copies.append(pltpu.make_async_copy(block, held.at[pl.ds(rows * i, rows), :], sems.at[i]))
    for copy in copies:
        copy.start()
    for i, (_, _, out_ref, to) in enumerate(parts):
        copies[i].wait()
        here = held[rows * i : rows * (i + 1), :]
        out_ref[to : to + rows, :] = jnp.dot(here, b_ref[...], preferred_element_type=F32)


def product_scratch(pair_elements, parts):
    rows, depth = pair_elements.shape
    return [pltpu.VMEM((rows // 8 * parts, depth), BF16), pltpu.SemaphoreType.DMA((parts,))]


def pack(ref, value):
    rows = value.shape[0]
    top = jnp.maximum(jnp.max(jnp.abs(value), axis=0, keepdims=True), 1e-30)
    level = jnp.clip(jnp.ceil(jnp.log2(top * (1.0 / 32000.0)) * 256.0), -32000.0, 32000.0)
    scaled = value * jnp.exp2(level * (-1.0 / 256.0))
    ref[:rows, :] = jnp.round(scaled).astype(jnp.int32).astype(I16)
    ref[rows:, :] = jnp.broadcast_to(level, (TAIL, value.shape[1])).astype(jnp.int32).astype(I16)


def unpack(ref):
    rows = ref.shape[0] - TAIL
    level = ref[rows:, :].astype(jnp.int32).astype(F32)[0:1, :]
    return ref[:rows, :].astype(jnp.int32).astype(F32) * jnp.exp2(level * (1.0 / 256.0))


def x_messages(own_ref, other_ref, *out_refs):
    rows = own_ref.shape[0] // len(out_refs)
    for i, out in enumerate(out_refs):
        pack(out, own_ref[rows * i : rows * (i + 1), :] + other_ref[rows * i : rows * (i + 1), :])


def split_four(mine, work_ref, own_ref, message_refs, masks):
    quarter = work_ref.shape[0] // 4

    def rows_of(owner):
        return work_ref[pl.ds(pl.multiple_of(owner * quarter, quarter), quarter), :]

    for mask, out in zip(masks, message_refs):
        pack(out, rows_of(lax.bitwise_xor(mine, mask)))
    own_ref[...] = rows_of(mine)


def z_messages(here_ref, own_ref, other_ref, m1_in, m2_in, m3_in, out_ref, m1_ref, m2_ref, m3_ref, work_ref):
    work_ref[...] = own_ref[...] + other_ref[...] + unpack(m1_in) + unpack(m2_in) + unpack(m3_in)
    split_four(here_ref[1], work_ref, out_ref, (m1_ref, m2_ref, m3_ref), Z_ORDER)


def last_sum(own_ref, m1_in, m2_in, m3_in, out_ref):
    out_ref[...] = (own_ref[...] + unpack(m1_in) + unpack(m2_in) + unpack(m3_in)).astype(BF16)


def gram_messages(here_ref, mine_ref, came_ref, own_ref, m1_ref, m2_ref, m3_ref, work_ref):
    work_ref[...] = mine_ref[...] + came_ref[...]
    split_four(here_ref[3] // 2, work_ref, own_ref, (m1_ref, m2_ref, m3_ref), Y_ORDER)


def gram_halves(here_ref, own_ref, m1_in, m2_in, m3_in, kept_ref, out_ref, work_ref):
    rows = kept_ref.shape[0]
    work_ref[...] = own_ref[...] + unpack(m1_in) + unpack(m2_in) + unpack(m3_in)
    half = here_ref[3] % 2
    kept_ref[...] = work_ref[pl.ds(pl.multiple_of(half * rows, rows), rows), :]
    pack(out_ref, work_ref[pl.ds(pl.multiple_of((1 - half) * rows, rows), rows), :])


def fill_weights(val_table, freq_ref, other_freq, ci_ref, vi_ref, ce_ref, out_refs):
    shape = ci_ref.shape
    index = ci_ref[...]
    high, low = index // 128, index % 128
    cond = jnp.zeros(shape, F32)
    for row in range(ce_ref.shape[0]):
        table = jnp.broadcast_to(ce_ref[row : row + 1, :], shape)
        cond = jnp.where(high == row, jnp.take_along_axis(table, low, axis=1), cond)
    level = vi_ref[...]
    val = jnp.zeros(shape, F32)
    for row in range(val_table.shape[0]):
        val = jnp.where(level == row, val_table[row], val)
    spacing = cond - val
    for freq, out_ref in zip((freq_ref[0], other_freq), out_refs):
        out_ref[...] = 2.0 * spacing / (spacing * spacing + freq * freq)


def gram_step(here, weights, pieces, owners, grams, after=()):
    width = pieces[0].shape[1]
    count, kinds = len(pieces), len(weights)

    def body(here_ref, *refs):
        w_refs, came, before, out_refs = refs[:kinds], refs[kinds : kinds + count], refs[kinds + count : -kinds], refs[-kinds:]
        totals = [ref[...] for ref in before] or [None] * kinds
        for ref, (owner, masks) in zip(came, owners):
            first = (here_ref[2] * 4 + lax.bitwise_xor(here_ref[0], owner)) * 4
            parts = [[] for _ in range(kinds)]
            for j, mask in enumerate(masks):
                rows = ref[128 * j : 128 * (j + 1), :].astype(F32).T
                for part, w_ref in zip(parts, w_refs):
                    w = w_ref[pl.ds(first + lax.bitwise_xor(here_ref[1], mask), 1), :]
                    part.append((rows * w).astype(BF16))
            for kind, part in enumerate(parts):
                term = jnp.dot(jnp.concatenate(part, axis=1), ref[...], preferred_element_type=F32)
                totals[kind] = term if totals[kind] is None else totals[kind] + term
        for out_ref, total in zip(out_refs, totals):
            out_ref[...] = total

    return call(
        body,
        [((width, width), F32)] * kinds,
        here,
        *weights,
        *pieces,
        *grams,
        specs=[SMEM] + [VMEM] * (kinds + count + len(grams)),
        after=after,
    )


def on_device(pair_elements, subspace, val_energy, cond_energy, val_index, cond_index, frequencies):
    here = jnp.stack([lax.axis_index(name).astype(jnp.int32) for name in PW + ("pair",)])
    rows, width = pair_elements.shape[0], subspace.shape[1]
    eighth, piece = rows // 8, rows // 32
    message = lambda count: ((count + TAIL, width), I16)
    sums = lambda count: ((count, width), F32)

    def product_call(body, outs, *args, after=(), flag=False, parts=1):
        specs = [SMEM] * (len(args) + 1) + [ANY, VMEM]
        scratch = product_scratch(pair_elements, parts)
        arrays = (here, *args, pair_elements, subspace)
        return call(body, outs, *arrays, specs=specs, after=after, flag=flag, scratch=scratch, limit=VMEM_LARGE)

    def far_other(here_ref, freq_ref, a_ref, b_ref, out_ref, held, sems):
        out_ref[eighth:, :] = jnp.full((8, width), freq_ref[0], F32)
        products(here_ref, a_ref, b_ref, held, sems, [(False, 2, out_ref, 0)])

    def far_own(here_ref, a_ref, b_ref, far_ref, near_ref, kept_ref, held, sems):
        parts = [(True, 2, far_ref, 0), (False, 1, near_ref, 0), (False, 3, near_ref, eighth), (False, 0, kept_ref, 0)]
        products(here_ref, a_ref, b_ref, held, sems, parts)

    def near_messages(here_ref, a_ref, b_ref, other_ref, one_ref, three_ref, held, sems, own_ref):
        products(here_ref, a_ref, b_ref, held, sems, [(True, 1, own_ref, 0), (True, 3, own_ref, eighth)])
        x_messages(own_ref, other_ref, one_ref, three_ref)

    def rest(here_ref, val_table, freq_ref, a_ref, b_ref, other_ref, ci_ref, vi_ref, ce_ref, *refs):
        (kept_ref, *w_refs), (held, sems) = refs[:3], refs[3:]
        products(here_ref, a_ref, b_ref, held, sems, [(True, 0, kept_ref, 0)])
        fill_weights(val_table, freq_ref, other_ref[0:1, 0:1], ci_ref, vi_ref, ce_ref, w_refs)

    other, done = product_call(far_other, [sums(eighth + 8)], frequencies, flag=True)
    far_in = xor_permute(other, "pw_c", 1)
    own, near_other, kept_other = product_call(
        far_own, [sums(eighth), sums(2 * eighth), sums(eighth)], after=[done], parts=4
    )
    near_other, far_in = lax.optimization_barrier((near_other, far_in))
    near_in, kept_in = xor_permute(near_other, "pw_c", 1), xor_permute(kept_other, "pw_c", 1)
    far, done = call(x_messages, [message(eighth)], own, far_in, flag=True)
    far = xor_permute(far, "pw_x", 2)
    near1, near3, done = call(
        near_messages,
        [message(eighth)] * 2,
        here,
        pair_elements,
        subspace,
        near_in,
        specs=[SMEM, ANY, VMEM, VMEM],
        after=[done],
        flag=True,
        scratch=product_scratch(pair_elements, 2) + [pltpu.VMEM((2 * eighth, width), F32)],
        limit=VMEM_LARGE,
    )
    near1, near3 = xor_permute(near1, "pw_x", 1), xor_permute(near3, "pw_x", 3)
    kept, *weights = call(
        rest,
        [sums(eighth), ((rows // 128, 128), F32), ((rows // 128, 128), F32)],
        here,
        val_energy,
        frequencies,
        pair_elements,
        subspace,
        far_in[eighth:, :128],
        cond_index.reshape(-1, 128),
        val_index.reshape(-1, 128),
        cond_energy.reshape(-1, 128),
        specs=[SMEM] * 3 + [ANY] + [VMEM] * 5,
        after=[done],
        scratch=product_scratch(pair_elements, 1),
        limit=VMEM_LARGE,
    )

    own, *out = call(
        z_messages,
        [sums(piece)] + [message(piece)] * 3,
        here,
        kept,
        kept_in,
        far,
        near1,
        near3,
        specs=[SMEM] + [VMEM] * 5,
        scratch=[pltpu.VMEM((eighth, width), F32)],
    )
    came = [xor_permute(value, "pw_z", mask) for mask, value in zip(Z_ORDER, out)]
    coeffs = call(last_sum, [((piece, width), BF16)], own, *came)[0]

    whole = jnp.concatenate([coeffs] + [xor_permute(coeffs, "pw_z", mask) for mask in (1, 2, 3)], axis=0)
    near, far = xor_permute(whole, "pw_x", 1), xor_permute(whole, "pw_x", 3)
    grams = gram_step(here, weights, [whole], [(0, (0, 1, 2, 3))], [])
    near, far, grams = lax.optimization_barrier((near, far, grams))
    top = xor_permute(far[: eighth // 2], "pw_x", 1)
    bottom = xor_permute(near[eighth // 2 :], "pw_x", 3)
    grams = gram_step(here, weights, [near, far], [(1, (0, 1, 2, 3)), (3, (0, 1, 2, 3))], grams)
    mine, theirs = gram_step(here, weights, [top, bottom], [(2, (0, 1)), (2, (2, 3))], grams)

    part = width // 4
    own, *out = call(
        gram_messages,
        [sums(part)] + [message(part)] * 3,
        here,
        mine,
        xor_permute(theirs, "pw_c", 1),
        specs=[SMEM] + [VMEM] * 2,
        scratch=[pltpu.VMEM((width, width), F32)],
    )
    came = [xor_permute(value, "pair", 2 * mask) for mask, value in zip(Y_ORDER, out)]
    own, out = call(
        gram_halves,
        [sums(part // 2), message(part // 2)],
        here,
        own,
        *came,
        specs=[SMEM] + [VMEM] * 4,
        scratch=[pltpu.VMEM((part, width), F32)],
    )
    factor = -4.0 / (rows * lax.axis_size("pair"))

    def finish(own_ref, came_ref, out_ref):
        out_ref[...] = (own_ref[...] + unpack(came_ref)) * factor

    return call(finish, [sums(part // 2)], own, xor_permute(out, "pair", 1))[0][None]


def solution(mesh):
    torus = Mesh(mesh.devices.reshape(mesh.shape["pair"], 4, 4, 2), ("pair",) + PW)
    return jax.shard_map(
        on_device,
        mesh=torus,
        in_specs=(P("pair", PW), P(PW, None), P(), P(), P("pair"), P("pair"), P(PW)),
        out_specs=P(PW, "pair", None),
        check_vma=False,
    )
```

time: 124 us -> 122 us (0.984)
  the two profiles are of different devices: /device:TPU:32 before, /device:TPU:24 now
where the time goes in v5:
time: 122 us
  waiting for transfers between devices  65.2 us (53%)
  starting transfers between devices  32.1 us (26%)
  Pallas kernels  22.1 us (18%)
  local copies, waits for them, and re-layouts  1.28 us (1%)
    ppermute x21, waiting for transfers between devices, xor_permute(): return lax.ppermute(value, axis, [(i, i ^ mask) for i in range(count)])  65.2 us
    ppermute x21, starting transfers between devices, xor_permute(): return lax.ppermute(value, axis, [(i, i ^ mask) for i in range(count)])  32.1 us
    pallas_call x13, Pallas kernels, call(): pl.pallas_call(kernel, out_shape=[jax.ShapeDtypeStruct(shape, dtype) for...  22.1 us
  transfers between devices with their start and end apart: 21, of which 15 were waited for; matrix products, arithmetic and copies ran while one was open for 0% of the time, Pallas kernels for 12%

profile of v5, /device:TPU:24, one launch (start us, length us, event | category | flops | bytes accessed | tf_op | source)
XLA Modules:
  0.0 121.7 jit_solution(68476242868354592)
XLA Ops:
  0.7 0.1 pad_add_fusion.refs_0_
  0.7 1.2 %copy-done = bf16[1024,512]{1,0:T(8,128)(2,1)S(1)} copy-done((bf16[1024,512]{1,0:T(8,128)(2,1)S(1)}, bf16[1024,512]{1,0:T(8,128)(2,1)}, u32[]{:S(2)}) %copy-start) | copy-done | bytes 1048600
  2.0 2.5 %shard_map.73 = (f32[520,512]{1,0:T(8,128)S(1)}, f32[8,128]{1,0:T(8,128)S(1)}) custom-call(s32[4]{0:T(128)S(1)} %pad_add_fusion.refs_0_, f32[1]{0:T(128)S(6)} %copy.8.refs_1_.refs_2_, bf16[4096,1024]{1,0:T(8,128)(2,1)} %refs_3_.3, bf16[1024,512]{1,0:T(8,128)(2,1)S(1)} %copy-done), custom_call_target="tpu_custom_call" | custom-call | tf_op jit(solution)/shard_map/pallas_call | solution.py:34
  4.5 0.1 collective-permute-start
  4.6 4.7 %shard_map.74 = (f32[512,512]{1,0:T(8,128)S(1)}, f32[1024,512]{1,0:T(8,128)S(1)}, f32[512,512]{1,0:T(8,128)S(1)}) custom-call(s32[4]{0:T(128)S(1)} %pad_add_fusion.refs_0_, bf16[4096,1024]{1,0:T(8,128)(2,1)} %refs_3_.3, bf16[1024,512]{1,0:T(8,128)(2,1)S(1)} %copy-done, f32[8,128]{1,0:T(8,128)S(1)} %get-tuple-element.40.refs_3_), custom_call_target="tpu_custom_call" | custom-call | tf_op jit(solution)/shard_map/pallas_call | solution.py:34
  9.3 0.6 collective-permute-start.1
  9.8 0.1 collective-permute-start.2
  9.9 0.3 shard_map.75
  10.3 3.1 %collective-permute-start.3 = (s16[528,512]{1,0:T(8,128)(2,1)S(1)}, s16[528,512]{1,0:T(8,128)(2,1)S(1)}, u32[]{:S(2)}, u32[]{:S(2)}) collective-permute-start(s16[528,512]{1,0:T(8,128)(2,1)S(1)} %get-tuple-element.52), channel_id=1, source_target_pairs={{0,16},{8,24},{16,0},{24,8},{1,17},{9,25},{17,1},{25,9},{2,18},{10... | collective-permute-start | bytes 1622024 | tf_op jit(solution)/shard_map/ppermute | solution.py:20
  13.4 0.3 collective-permute-done.1.refs_3_
  13.6 3.6 %shard_map.76 = (s16[528,512]{1,0:T(8,128)(2,1)S(1)}, s16[528,512]{1,0:T(8,128)(2,1)S(1)}, f32[8,128]{1,0:T(8,128)S(1)}) custom-call(s32[4]{0:T(128)S(1)} %pad_add_fusion.refs_0_, bf16[4096,1024]{1,0:T(8,128)(2,1)} %refs_3_.3, bf16[1024,512]{1,0:T(8,128)(2,1)S(1)} %copy-done, f32[1024,512]{1,0:T(8,128)S(1)} %collective-permute-done.1.refs_3_, ...), custom_call_target="tpu_custom_call" | custom-call | tf_op jit(solution)/shard_map/pallas_call | solution.py:34
  17.3 1.6 %collective-permute-start.4 = (s16[528,512]{1,0:T(8,128)(2,1)S(1)}, s16[528,512]{1,0:T(8,128)(2,1)S(1)}, u32[]{:S(2)}, u32[]{:S(2)}) collective-permute-start(s16[528,512]{1,0:T(8,128)(2,1)S(1)} %get-tuple-element.53), channel_id=1, source_target_pairs={{0,8},{8,0},{16,24},{24,16},{1,9},{9,1},{17,25},{25,17},{2,10},{10... | collective-permute-start | bytes 1622024 | tf_op jit(solution)/shard_map/ppermute | solution.py:20
  18.9 2.1 %collective-permute-start.5 = (s16[528,512]{1,0:T(8,128)(2,1)S(1)}, s16[528,512]{1,0:T(8,128)(2,1)S(1)}, u32[]{:S(2)}, u32[]{:S(2)}) collective-permute-start(s16[528,512]{1,0:T(8,128)(2,1)S(1)} %get-tuple-element.54), channel_id=1, source_target_pairs={{0,24},{8,16},{16,8},{24,0},{1,25},{9,17},{17,9},{25,1},{2,26},{10... | collective-permute-start | bytes 1622024 | tf_op jit(solution)/shard_map/ppermute | solution.py:20
  21.0 2.5 %shard_map.77 = (f32[512,512]{1,0:T(8,128)S(1)}, f32[32,128]{1,0:T(8,128)S(1)}, f32[32,128]{1,0:T(8,128)S(1)}) custom-call(s32[4]{0:T(128)S(1)} %pad_add_fusion.refs_0_, f32[16]{0:T(128)S(1)} %copy-done.4, f32[1]{0:T(128)S(6)} %copy.8.refs_1_.refs_2_, bf16[4096,1024]{1,0:T(8,128)(2,1)} %refs_3_.3, bf16[1024,512]{1,0:T(8,128)(2,1)S(1)} %copy-done, ...), custom_call_target="tpu_custom_call" | custom-call | tf_op jit(solution)/shard_map/pallas_call | solution.py:34
  23.5 3.4 %collective-permute-done.3.refs_3_ = s16[528,512]{1,0:T(8,128)(2,1)S(1)} collective-permute-done((s16[528,512]{1,0:T(8,128)(2,1)S(1)}, s16[528,512]{1,0:T(8,128)(2,1)S(1)}, u32[]{:S(2)}, u32[]{:S(2)}) %collective-permute-start.3) | collective-permute-done | bytes 540704 | tf_op jit(solution)/shard_map/ppermute | solution.py:20
  27.0 11.2 %collective-permute-done.4.refs_4_ = s16[528,512]{1,0:T(8,128)(2,1)S(1)} collective-permute-done((s16[528,512]{1,0:T(8,128)(2,1)S(1)}, s16[528,512]{1,0:T(8,128)(2,1)S(1)}, u32[]{:S(2)}, u32[]{:S(2)}) %collective-permute-start.4) | collective-permute-done | bytes 540704 | tf_op jit(solution)/shard_map/ppermute | solution.py:20
  38.2 1.7 %shard_map.78 = (f32[128,512]{1,0:T(8,128)S(1)}, s16[144,512]{1,0:T(8,128)(2,1)S(1)}, s16[144,512]{1,0:T(8,128)(2,1)S(1)}, s16[144,512]{1,0:T(8,128)(2,1)S(1)}) custom-call(s32[4]{0:T(128)S(1)} %pad_add_fusion.refs_0_, f32[512,512]{1,0:T(8,128)S(1)} %get-tuple-element.50.refs_1_, f32[512,512]{1,0:T(8,128)S(1)} %collective-permute-done.2.refs_2_, ...), custom_call_target="tpu_custom_call" | custom-call | tf_op jit(solution)/shard_map/pallas_call | solution.py:34
  39.8 4.7 %collective-permute-start.6 = (s16[144,512]{1,0:T(8,128)(2,1)S(1)}, s16[144,512]{1,0:T(8,128)(2,1)S(1)}, u32[]{:S(2)}, u32[]{:S(2)}) collective-permute-start(s16[144,512]{1,0:T(8,128)(2,1)S(1)} %get-tuple-element.56), channel_id=1, source_target_pairs={{0,6},{2,4},{4,2},{6,0},{1,7},{3,5},{5,3},{7,1},{8,14},{10,12},{12... | collective-permute-start | bytes 442376 | tf_op jit(solution)/shard_map/ppermute | solution.py:20
  44.6 0.7 collective-permute-start.8
  45.2 4.1 %collective-permute-done.6.refs_1_ = s16[144,512]{1,0:T(8,128)(2,1)S(1)} collective-permute-done((s16[144,512]{1,0:T(8,128)(2,1)S(1)}, s16[144,512]{1,0:T(8,128)(2,1)S(1)}, u32[]{:S(2)}, u32[]{:S(2)}) %collective-permute-start.6) | collective-permute-done | bytes 147488 | tf_op jit(solution)/shard_map/ppermute | solution.py:20
  49.3 7.3 %collective-permute-done.7.refs_2_ = s16[144,512]{1,0:T(8,128)(2,1)S(1)} collective-permute-done((s16[144,512]{1,0:T(8,128)(2,1)S(1)}, s16[144,512]{1,0:T(8,128)(2,1)S(1)}, u32[]{:S(2)}, u32[]{:S(2)}) %collective-permute-start.7) | collective-permute-done | bytes 147488 | tf_op jit(solution)/shard_map/ppermute | solution.py:20
  56.6 0.1 shard_map.79
  56.7 2.8 %collective-permute-start.11 = (bf16[128,512]{1,0:T(8,128)(2,1)S(1)}, bf16[128,512]{1,0:T(8,128)(2,1)S(1)}, u32[]{:S(2)}, u32[]{:S(2)}) collective-permute-start(bf16[128,512]{1,0:T(8,128)(2,1)S(1)} %shard_map.79), channel_id=1, source_target_pairs={{0,6},{2,4},{4,2},{6,0},{1,7},{3,5},{5,3},{7,1},{8,14},{10,12},{12... | collective-permute-start | bytes 393224 | tf_op jit(solution)/shard_map/ppermute | solution.py:20
  59.5 1.6 %collective-permute-start.9 = (bf16[128,512]{1,0:T(8,128)(2,1)S(1)}, bf16[128,512]{1,0:T(8,128)(2,1)S(1)}, u32[]{:S(2)}, u32[]{:S(2)}) collective-permute-start(bf16[128,512]{1,0:T(8,128)(2,1)S(1)} %shard_map.79), channel_id=1, source_target_pairs={{0,2},{2,0},{4,6},{6,4},{1,3},{3,1},{5,7},{7,5},{8,10},{10,8},{12,... | collective-permute-start | bytes 393224 | tf_op jit(solution)/shard_map/ppermute | solution.py:20
  61.2 3.8 %collective-permute-done.11 = bf16[128,512]{1,0:T(8,128)(2,1)S(1)} collective-permute-done((bf16[128,512]{1,0:T(8,128)(2,1)S(1)}, bf16[128,512]{1,0:T(8,128)(2,1)S(1)}, u32[]{:S(2)}, u32[]{:S(2)}) %collective-permute-start.11) | collective-permute-done | bytes 131104 | tf_op jit(solution)/shard_map/ppermute | solution.py:20
  65.0 4.6 %collective-permute-done.10 = bf16[128,512]{1,0:T(8,128)(2,1)S(1)} collective-permute-done((bf16[128,512]{1,0:T(8,128)(2,1)S(1)}, bf16[128,512]{1,0:T(8,128)(2,1)S(1)}, u32[]{:S(2)}, u32[]{:S(2)}) %collective-permute-start.10) | collective-permute-done | bytes 131104 | tf_op jit(solution)/shard_map/ppermute | solution.py:20
  69.7 3.0 %collective-permute-start.13 = (bf16[512,512]{1,0:T(8,128)(2,1)S(1)}, bf16[512,512]{1,0:T(8,128)(2,1)S(1)}, u32[]{:S(2)}, u32[]{:S(2)}) collective-permute-start(bf16[512,512]{1,0:T(8,128)(2,1)S(1)} %pad_maximum_fusion.refs_3_), channel_id=1, source_target_pairs={{0,24},{8,16},{16,8},{24,0},{1,25},{9,17},{17,9},{25,1},{2,26},{10... | collective-permute-start | bytes 1572872 | tf_op jit(solution)/shard_map/ppermute | solution.py:20
  72.7 0.2 collective-permute-start.12
  72.9 1.3 %shard_map.80 = (f32[512,512]{1,0:T(8,128)S(1)}, f32[512,512]{1,0:T(8,128)S(1)}) custom-call(s32[4]{0:T(128)S(1)} %pad_add_fusion.refs_0_, f32[32,128]{1,0:T(8,128)S(1)} %get-tuple-element.48.refs_1_, f32[32,128]{1,0:T(8,128)S(1)} %get-tuple-element.49.refs_2_, bf16[512,512]{1,0:T(8,128)(2,1)S(1)} %pad_maximum_fusion.refs_3_), custom_call_target="tpu_custom_call" | custom-call | tf_op jit(solution)/shard_map/pallas_call | solution.py:34
  74.2 10.2 %collective-permute-done.13.refs_4_ = bf16[512,512]{1,0:T(8,128)(2,1)S(1)} collective-permute-done((bf16[512,512]{1,0:T(8,128)(2,1)S(1)}, bf16[512,512]{1,0:T(8,128)(2,1)S(1)}, u32[]{:S(2)}, u32[]{:S(2)}) %collective-permute-start.13) | collective-permute-done | bytes 524320 | tf_op jit(solution)/shard_map/ppermute | solution.py:20
  84.5 1.4 %collective-permute-done.12.refs_3_ = bf16[512,512]{1,0:T(8,128)(2,1)S(1)} collective-permute-done((bf16[512,512]{1,0:T(8,128)(2,1)S(1)}, bf16[512,512]{1,0:T(8,128)(2,1)S(1)}, u32[]{:S(2)}, u32[]{:S(2)}) %collective-permute-start.12) | collective-permute-done | bytes 524320 | tf_op jit(solution)/shard_map/ppermute | solution.py:20
  85.9 1.6 %collective-permute-start.15 = (bf16[256,512]{1,0:T(8,128)(2,1)S(1)}, bf16[256,512]{1,0:T(8,128)(2,1)S(1)}, u32[]{:S(2)}, u32[]{:S(2)}) collective-permute-start(bf16[256,512]{1,0:T(8,128)(2,1)S(1)} %slice.11), channel_id=1, source_target_pairs={{0,24},{8,16},{16,8},{24,0},{1,25},{9,17},{17,9},{25,1},{2,26},{10... | collective-permute-start | bytes 786440 | tf_op jit(solution)/shard_map/ppermute | solution.py:20
  87.5 1.9 %shard_map.81 = (f32[512,512]{1,0:T(8,128)S(1)}, f32[512,512]{1,0:T(8,128)S(1)}) custom-call(s32[4]{0:T(128)S(1)} %pad_add_fusion.refs_0_, f32[32,128]{1,0:T(8,128)S(1)} %get-tuple-element.48.refs_1_, f32[32,128]{1,0:T(8,128)S(1)} %get-tuple-element.49.refs_2_, bf16[512,512]{1,0:T(8,128)(2,1)S(1)} %collective-permute-done.12.refs_3_, ...), custom_call_target="tpu_custom_call" | custom-call | tf_op jit(solution)/shard_map/pallas_call | solution.py:34
  89.4 4.5 %collective-permute-done.15.refs_4_ = bf16[256,512]{1,0:T(8,128)(2,1)S(1)} collective-permute-done((bf16[256,512]{1,0:T(8,128)(2,1)S(1)}, bf16[256,512]{1,0:T(8,128)(2,1)S(1)}, u32[]{:S(2)}, u32[]{:S(2)}) %collective-permute-start.15) | collective-permute-done | bytes 262176 | tf_op jit(solution)/shard_map/ppermute | solution.py:20
  93.8 0.3 collective-permute-done.14.refs_3_
  94.1 1.3 %shard_map.82 = (f32[512,512]{1,0:T(8,128)S(1)}, f32[512,512]{1,0:T(8,128)S(1)}) custom-call(s32[4]{0:T(128)S(1)} %pad_add_fusion.refs_0_, f32[32,128]{1,0:T(8,128)S(1)} %get-tuple-element.48.refs_1_, f32[32,128]{1,0:T(8,128)S(1)} %get-tuple-element.49.refs_2_, bf16[256,512]{1,0:T(8,128)(2,1)S(1)} %collective-permute-done.14.refs_3_, ...), custom_call_target="tpu_custom_call" | custom-call | tf_op jit(solution)/shard_map/pallas_call | solution.py:34
  95.5 0.1 collective-permute-start.16
  95.6 2.6 %collective-permute-done.16.refs_2_ = f32[512,512]{1,0:T(8,128)S(1)} collective-permute-done((f32[512,512]{1,0:T(8,128)S(1)}, f32[512,512]{1,0:T(8,128)S(1)}, u32[]{:S(2)}, u32[]{:S(2)}) %collective-permute-start.16) | collective-permute-done | bytes 1048608 | tf_op jit(solution)/shard_map/ppermute | solution.py:20
  98.2 0.8 shard_map.83
  99.0 1.3 %collective-permute-start.17 = (s16[144,512]{1,0:T(8,128)(2,1)S(1)}, s16[144,512]{1,0:T(8,128)(2,1)S(1)}, u32[]{:S(2)}, u32[]{:S(2)}) collective-permute-start(s16[144,512]{1,0:T(8,128)(2,1)S(1)} %get-tuple-element.70), channel_id=1, source_target_pairs={{0,128},{32,160},{64,192},{96,224},{128,0},{160,32},{192,64},{224,... | collective-permute-start | bytes 442376 | tf_op jit(solution)/shard_map/ppermute | solution.py:20
  100.3 2.2 %collective-permute-start.18 = (s16[144,512]{1,0:T(8,128)(2,1)S(1)}, s16[144,512]{1,0:T(8,128)(2,1)S(1)}, u32[]{:S(2)}, u32[]{:S(2)}) collective-permute-start(s16[144,512]{1,0:T(8,128)(2,1)S(1)} %get-tuple-element.71), channel_id=1, source_target_pairs={{0,192},{32,224},{64,128},{96,160},{128,64},{160,96},{192,0},{224,... | collective-permute-start | bytes 442376 | tf_op jit(solution)/shard_map/ppermute | solution.py:20
  102.5 0.1 collective-permute-start.19
  102.6 4.7 %collective-permute-done.17.refs_2_ = s16[144,512]{1,0:T(8,128)(2,1)S(1)} collective-permute-done((s16[144,512]{1,0:T(8,128)(2,1)S(1)}, s16[144,512]{1,0:T(8,128)(2,1)S(1)}, u32[]{:S(2)}, u32[]{:S(2)}) %collective-permute-start.17) | collective-permute-done | bytes 147488 | tf_op jit(solution)/shard_map/ppermute | solution.py:20
  107.3 2.3 %collective-permute-done.18.refs_3_ = s16[144,512]{1,0:T(8,128)(2,1)S(1)} collective-permute-done((s16[144,512]{1,0:T(8,128)(2,1)S(1)}, s16[144,512]{1,0:T(8,128)(2,1)S(1)}, u32[]{:S(2)}, u32[]{:S(2)}) %collective-permute-start.18) | collective-permute-done | bytes 147488 | tf_op jit(solution)/shard_map/ppermute | solution.py:20
  109.6 0.8 shard_map.84
  110.4 6.2 %collective-permute-start.20 = (s16[80,512]{1,0:T(8,128)(2,1)S(1)}, s16[80,512]{1,0:T(8,128)(2,1)S(1)}, u32[]{:S(2)}, u32[]{:S(2)}) collective-permute-start(s16[80,512]{1,0:T(8,128)(2,1)S(1)} %get-tuple-element.74), channel_id=1, source_target_pairs={{0,32},{32,0},{64,96},{96,64},{128,160},{160,128},{192,224},{224,1... | collective-permute-start | bytes 245768 | tf_op jit(solution)/shard_map/ppermute | solution.py:20
  116.6 4.4 %collective-permute-done.20.refs_1_ = s16[80,512]{1,0:T(8,128)(2,1)S(1)} collective-permute-done((s16[80,512]{1,0:T(8,128)(2,1)S(1)}, s16[80,512]{1,0:T(8,128)(2,1)S(1)}, u32[]{:S(2)}, u32[]{:S(2)}) %collective-permute-start.20) | collective-permute-done | bytes 81952 | tf_op jit(solution)/shard_map/ppermute | solution.py:20
  121.0 0.7 shard_map.85
  (22 shorter events, 0.1 us)
Async XLA Ops:
  0.7 1.2 %copy-start = (bf16[1024,512]{1,0:T(8,128)(2,1)S(1)}, bf16[1024,512]{1,0:T(8,128)(2,1)}, u32[]{:S(2)}) copy-start(bf16[1024,512]{1,0:T(8,128)(2,1)} %refs_4_.1) | copy-start | bytes 3145732
  4.5 4.8 %collective-permute-start = (f32[520,512]{1,0:T(8,128)S(1)}, f32[520,512]{1,0:T(8,128)S(1)}, u32[]{:S(2)}, u32[]{:S(2)}) collective-permute-start(f32[520,512]{1,0:T(8,128)S(1)} %get-tuple-element.42), channel_id=1, source_target_pairs={{0,1},{1,0},{2,3},{3,2},{4,5},{5,4},{6,7},{7,6},{8,9},{9,8},{10,11... | collective-permute-start | bytes 3194888 | tf_op jit(solution)/shard_map/ppermute | solution.py:20
  9.3 4.4 %collective-permute-start.1 = (f32[1024,512]{1,0:T(8,128)S(1)}, f32[1024,512]{1,0:T(8,128)S(1)}, u32[]{:S(2)}, u32[]{:S(2)}) collective-permute-start(f32[1024,512]{1,0:T(8,128)S(1)} %get-tuple-element.44), channel_id=1, source_target_pairs={{0,1},{1,0},{2,3},{3,2},{4,5},{5,4},{6,7},{7,6},{8,9},{9,8},{10,11... | collective-permute-start | bytes 6291464 | tf_op jit(solution)/shard_map/ppermute | solution.py:20
  9.8 13.7 %collective-permute-start.2 = (f32[512,512]{1,0:T(8,128)S(1)}, f32[512,512]{1,0:T(8,128)S(1)}, u32[]{:S(2)}, u32[]{:S(2)}) collective-permute-start(f32[512,512]{1,0:T(8,128)S(1)} %get-tuple-element.51), channel_id=1, source_target_pairs={{0,1},{1,0},{2,3},{3,2},{4,5},{5,4},{6,7},{7,6},{8,9},{9,8},{10,11... | collective-permute-start | bytes 3145736 | tf_op jit(solution)/shard_map/ppermute | solution.py:20
  10.3 16.7 %collective-permute-start.3 = (s16[528,512]{1,0:T(8,128)(2,1)S(1)}, s16[528,512]{1,0:T(8,128)(2,1)S(1)}, u32[]{:S(2)}, u32[]{:S(2)}) collective-permute-start(s16[528,512]{1,0:T(8,128)(2,1)S(1)} %get-tuple-element.52), channel_id=1, source_target_pairs={{0,16},{8,24},{16,0},{24,8},{1,17},{9,25},{17,1},{25,9},{2,18},{10... | collective-permute-start | bytes 1622024 | tf_op jit(solution)/shard_map/ppermute | solution.py:20
  13.6 7.3 %copy-start.1 = (s32[4096]{0:T(1024)S(1)}, s32[4096]{0:T(1024)}, u32[]{:S(2)}) copy-start(s32[4096]{0:T(1024)} %param.12) | copy-start | bytes 49156
  13.6 7.3 %copy-start.2 = (s32[4096]{0:T(1024)S(1)}, s32[4096]{0:T(1024)}, u32[]{:S(2)}) copy-start(s32[4096]{0:T(1024)} %param.11) | copy-start | bytes 49156
  13.6 7.3 %copy-start.3 = (f32[2048]{0:T(1024)S(1)}, f32[2048]{0:T(1024)}, u32[]{:S(2)}) copy-start(f32[2048]{0:T(1024)} %param.10) | copy-start | bytes 24580
  13.6 7.3 %copy-start.4 = (f32[16]{0:T(128)S(1)}, f32[16]{0:T(128)}, u32[]{:S(2)}) copy-start(f32[16]{0:T(128)} %refs_1_.6) | copy-start | bytes 196
  17.3 20.9 %collective-permute-start.4 = (s16[528,512]{1,0:T(8,128)(2,1)S(1)}, s16[528,512]{1,0:T(8,128)(2,1)S(1)}, u32[]{:S(2)}, u32[]{:S(2)}) collective-permute-start(s16[528,512]{1,0:T(8,128)(2,1)S(1)} %get-tuple-element.53), channel_id=1, source_target_pairs={{0,8},{8,0},{16,24},{24,16},{1,9},{9,1},{17,25},{25,17},{2,10},{10... | collective-permute-start | bytes 1622024 | tf_op jit(solution)/shard_map/ppermute | solution.py:20
  18.9 19.3 %collective-permute-start.5 = (s16[528,512]{1,0:T(8,128)(2,1)S(1)}, s16[528,512]{1,0:T(8,128)(2,1)S(1)}, u32[]{:S(2)}, u32[]{:S(2)}) collective-permute-start(s16[528,512]{1,0:T(8,128)(2,1)S(1)} %get-tuple-element.54), channel_id=1, source_target_pairs={{0,24},{8,16},{16,8},{24,0},{1,25},{9,17},{17,9},{25,1},{2,26},{10... | collective-permute-start | bytes 1622024 | tf_op jit(solution)/shard_map/ppermute | solution.py:20
  39.8 9.5 %collective-permute-start.6 = (s16[144,512]{1,0:T(8,128)(2,1)S(1)}, s16[144,512]{1,0:T(8,128)(2,1)S(1)}, u32[]{:S(2)}, u32[]{:S(2)}) collective-permute-start(s16[144,512]{1,0:T(8,128)(2,1)S(1)} %get-tuple-element.56), channel_id=1, source_target_pairs={{0,6},{2,4},{4,2},{6,0},{1,7},{3,5},{5,3},{7,1},{8,14},{10,12},{12... | collective-permute-start | bytes 442376 | tf_op jit(solution)/shard_map/ppermute | solution.py:20
  44.6 12.0 %collective-permute-start.7 = (s16[144,512]{1,0:T(8,128)(2,1)S(1)}, s16[144,512]{1,0:T(8,128)(2,1)S(1)}, u32[]{:S(2)}, u32[]{:S(2)}) collective-permute-start(s16[144,512]{1,0:T(8,128)(2,1)S(1)} %get-tuple-element.57), channel_id=1, source_target_pairs={{0,4},{2,6},{4,0},{6,2},{1,5},{3,7},{5,1},{7,3},{8,12},{10,14},{12... | collective-permute-start | bytes 442376 | tf_op jit(solution)/shard_map/ppermute | solution.py:20
  44.6 12.0 %collective-permute-start.8 = (s16[144,512]{1,0:T(8,128)(2,1)S(1)}, s16[144,512]{1,0:T(8,128)(2,1)S(1)}, u32[]{:S(2)}, u32[]{:S(2)}) collective-permute-start(s16[144,512]{1,0:T(8,128)(2,1)S(1)} %get-tuple-element.58), channel_id=1, source_target_pairs={{0,2},{2,0},{4,6},{6,4},{1,3},{3,1},{5,7},{7,5},{8,10},{10,8},{12,... | collective-permute-start | bytes 442376 | tf_op jit(solution)/shard_map/ppermute | solution.py:20
  56.7 8.3 %collective-permute-start.11 = (bf16[128,512]{1,0:T(8,128)(2,1)S(1)}, bf16[128,512]{1,0:T(8,128)(2,1)S(1)}, u32[]{:S(2)}, u32[]{:S(2)}) collective-permute-start(bf16[128,512]{1,0:T(8,128)(2,1)S(1)} %shard_map.79), channel_id=1, source_target_pairs={{0,6},{2,4},{4,2},{6,0},{1,7},{3,5},{5,3},{7,1},{8,14},{10,12},{12... | collective-permute-start | bytes 393224 | tf_op jit(solution)/shard_map/ppermute | solution.py:20
  59.5 10.1 %collective-permute-start.10 = (bf16[128,512]{1,0:T(8,128)(2,1)S(1)}, bf16[128,512]{1,0:T(8,128)(2,1)S(1)}, u32[]{:S(2)}, u32[]{:S(2)}) collective-permute-start(bf16[128,512]{1,0:T(8,128)(2,1)S(1)} %shard_map.79), channel_id=1, source_target_pairs={{0,4},{2,6},{4,0},{6,2},{1,5},{3,7},{5,1},{7,3},{8,12},{10,14},{12... | collective-permute-start | bytes 393224 | tf_op jit(solution)/shard_map/ppermute | solution.py:20
  59.5 10.1 %collective-permute-start.9 = (bf16[128,512]{1,0:T(8,128)(2,1)S(1)}, bf16[128,512]{1,0:T(8,128)(2,1)S(1)}, u32[]{:S(2)}, u32[]{:S(2)}) collective-permute-start(bf16[128,512]{1,0:T(8,128)(2,1)S(1)} %shard_map.79), channel_id=1, source_target_pairs={{0,2},{2,0},{4,6},{6,4},{1,3},{3,1},{5,7},{7,5},{8,10},{10,8},{12,... | collective-permute-start | bytes 393224 | tf_op jit(solution)/shard_map/ppermute | solution.py:20
  69.7 14.8 %collective-permute-start.13 = (bf16[512,512]{1,0:T(8,128)(2,1)S(1)}, bf16[512,512]{1,0:T(8,128)(2,1)S(1)}, u32[]{:S(2)}, u32[]{:S(2)}) collective-permute-start(bf16[512,512]{1,0:T(8,128)(2,1)S(1)} %pad_maximum_fusion.refs_3_), channel_id=1, source_target_pairs={{0,24},{8,16},{16,8},{24,0},{1,25},{9,17},{17,9},{25,1},{2,26},{10... | collective-permute-start | bytes 1572872 | tf_op jit(solution)/shard_map/ppermute | solution.py:20
  72.7 13.2 %collective-permute-start.12 = (bf16[512,512]{1,0:T(8,128)(2,1)S(1)}, bf16[512,512]{1,0:T(8,128)(2,1)S(1)}, u32[]{:S(2)}, u32[]{:S(2)}) collective-permute-start(bf16[512,512]{1,0:T(8,128)(2,1)S(1)} %pad_maximum_fusion.refs_3_), channel_id=1, source_target_pairs={{0,8},{8,0},{16,24},{24,16},{1,9},{9,1},{17,25},{25,17},{2,10},{10... | collective-permute-start | bytes 1572872 | tf_op jit(solution)/shard_map/ppermute | solution.py:20
  85.9 7.9 %collective-permute-start.15 = (bf16[256,512]{1,0:T(8,128)(2,1)S(1)}, bf16[256,512]{1,0:T(8,128)(2,1)S(1)}, u32[]{:S(2)}, u32[]{:S(2)}) collective-permute-start(bf16[256,512]{1,0:T(8,128)(2,1)S(1)} %slice.11), channel_id=1, source_target_pairs={{0,24},{8,16},{16,8},{24,0},{1,25},{9,17},{17,9},{25,1},{2,26},{10... | collective-permute-start | bytes 786440 | tf_op jit(solution)/shard_map/ppermute | solution.py:20
  87.5 6.6 %collective-permute-start.14 = (bf16[256,512]{1,0:T(8,128)(2,1)S(1)}, bf16[256,512]{1,0:T(8,128)(2,1)S(1)}, u32[]{:S(2)}, u32[]{:S(2)}) collective-permute-start(bf16[256,512]{1,0:T(8,128)(2,1)S(1)} %slice.10), channel_id=1, source_target_pairs={{0,8},{8,0},{16,24},{24,16},{1,9},{9,1},{17,25},{25,17},{2,10},{10... | collective-permute-start | bytes 786440 | tf_op jit(solution)/shard_map/ppermute | solution.py:20
  95.5 2.7 %collective-permute-start.16 = (f32[512,512]{1,0:T(8,128)S(1)}, f32[512,512]{1,0:T(8,128)S(1)}, u32[]{:S(2)}, u32[]{:S(2)}) collective-permute-start(f32[512,512]{1,0:T(8,128)S(1)} %get-tuple-element.68), channel_id=1, source_target_pairs={{0,1},{1,0},{2,3},{3,2},{4,5},{5,4},{6,7},{7,6},{8,9},{9,8},{10,11... | collective-permute-start | bytes 3145736 | tf_op jit(solution)/shard_map/ppermute | solution.py:20
  99.0 8.3 %collective-permute-start.17 = (s16[144,512]{1,0:T(8,128)(2,1)S(1)}, s16[144,512]{1,0:T(8,128)(2,1)S(1)}, u32[]{:S(2)}, u32[]{:S(2)}) collective-permute-start(s16[144,512]{1,0:T(8,128)(2,1)S(1)} %get-tuple-element.70), channel_id=1, source_target_pairs={{0,128},{32,160},{64,192},{96,224},{128,0},{160,32},{192,64},{224,... | collective-permute-start | bytes 442376 | tf_op jit(solution)/shard_map/ppermute | solution.py:20
  100.3 9.3 %collective-permute-start.18 = (s16[144,512]{1,0:T(8,128)(2,1)S(1)}, s16[144,512]{1,0:T(8,128)(2,1)S(1)}, u32[]{:S(2)}, u32[]{:S(2)}) collective-permute-start(s16[144,512]{1,0:T(8,128)(2,1)S(1)} %get-tuple-element.71), channel_id=1, source_target_pairs={{0,192},{32,224},{64,128},{96,160},{128,64},{160,96},{192,0},{224,... | collective-permute-start | bytes 442376 | tf_op jit(solution)/shard_map/ppermute | solution.py:20
  102.5 7.1 %collective-permute-start.19 = (s16[144,512]{1,0:T(8,128)(2,1)S(1)}, s16[144,512]{1,0:T(8,128)(2,1)S(1)}, u32[]{:S(2)}, u32[]{:S(2)}) collective-permute-start(s16[144,512]{1,0:T(8,128)(2,1)S(1)} %get-tuple-element.72), channel_id=1, source_target_pairs={{0,64},{32,96},{64,0},{96,32},{128,192},{160,224},{192,128},{224,1... | collective-permute-start | bytes 442376 | tf_op jit(solution)/shard_map/ppermute | solution.py:20
  110.4 10.6 %collective-permute-start.20 = (s16[80,512]{1,0:T(8,128)(2,1)S(1)}, s16[80,512]{1,0:T(8,128)(2,1)S(1)}, u32[]{:S(2)}, u32[]{:S(2)}) collective-permute-start(s16[80,512]{1,0:T(8,128)(2,1)S(1)} %get-tuple-element.74), channel_id=1, source_target_pairs={{0,32},{32,0},{64,96},{96,64},{128,160},{160,128},{192,224},{224,1... | collective-permute-start | bytes 245768 | tf_op jit(solution)/shard_map/ppermute | solution.py:20

commit v6 on v5

v6 whole, which is shorter than its diff:
```python
import jax
import jax.numpy as jnp
from jax import lax
from jax.experimental import pallas as pl
from jax.experimental.pallas import tpu as pltpu
from jax.sharding import Mesh
from jax.sharding import PartitionSpec as P

PW = ("pw_x", "pw_z", "pw_c")
F32, BF16, I16 = jnp.float32, jnp.bfloat16, jnp.int16
TAIL = 16
Z_ORDER, Y_ORDER = (3, 2, 1), (2, 3, 1)
VMEM_LIMIT, VMEM_LARGE = 24 * 1024 * 1024, 46 * 1024 * 1024
SMEM, VMEM = pl.BlockSpec(memory_space=pltpu.SMEM), pl.BlockSpec(memory_space=pltpu.VMEM)
ANY = pl.BlockSpec(memory_space=pl.ANY)


def xor_permute(value, axis, mask):
    count = lax.axis_size(axis)
    return lax.ppermute(value, axis, [(i, i ^ mask) for i in range(count)])


def call(body, outs, *args, specs=None, after=(), flag=False, cost=0, scratch=(), limit=VMEM_LIMIT):
    specs = specs or [VMEM] * len(args)
    moved = sum(a.size * a.dtype.itemsize for a in args)
    outs = list(outs) + [((8, 128), F32)] * flag

    def kernel(*refs):
        refs = list(refs[: len(args)] + refs[len(args) + len(after) :])
        if flag:
            ref = refs.pop(len(args) + len(outs) - 1)
            ref[...] = jnp.zeros(ref.shape, F32)
        body(*refs)

    return pl.pallas_call(
        kernel,
        out_shape=[jax.ShapeDtypeStruct(shape, dtype) for shape, dtype in outs],
        in_specs=specs + [VMEM] * len(after),
        out_specs=[VMEM] * len(outs),
        scratch_shapes=list(scratch),
        compiler_params=pltpu.CompilerParams(vmem_limit_bytes=limit),
        cost_estimate=pl.CostEstimate(flops=cost, bytes_accessed=moved, transcendentals=0),
    )(*args, *after)


SENT = ((1, 0), (2, 0), (3, 1), (2, 1))
KEPT = ((0, 0), (3, 0), (0, 1), (1, 1))


def products(here_ref, a_ref, b_ref, out_refs, held, sems, parts):
    order = SENT + KEPT
    per = len(order)
    rows = held.shape[0] // (len(parts) * per)
    copies = []
    for own, stream in parts:
        base = (here_ref[2] if own else 1 - here_ref[2]) * 16 + stream * 2
        for owner, part in order:
            start = (base + lax.bitwise_xor(here_ref[0], owner) * 4 + part) * rows
            to = held.at[pl.ds(rows * len(copies), rows), :]
            copies.append(
                pltpu.make_async_copy(a_ref.at[pl.ds(pl.multiple_of(start, rows), rows), :], to, sems.at[len(copies)])
            )
    for copy in copies:
        copy.start()
    for o, out_ref in enumerate(out_refs):
        for copy in copies[o * per : (o + 1) * per]:
            copy.wait()
        here = held[o * per * rows : (o + 1) * per * rows, :]
        out_ref[: per * rows, :] = jnp.dot(here, b_ref[...], preferred_element_type=F32)


def product_scratch(pair_elements, parts):
    rows, depth = pair_elements.shape
    return [pltpu.VMEM((rows // 4 * parts, depth), BF16), pltpu.SemaphoreType.DMA((8 * parts,))]


def pack(ref, value):
    rows = value.shape[0]
    top = jnp.maximum(jnp.max(jnp.abs(value), axis=0, keepdims=True), 1e-30)
    level = jnp.clip(jnp.ceil(jnp.log2(top * (1.0 / 32000.0)) * 256.0), -32000.0, 32000.0)
    scaled = value * jnp.exp2(level * (-1.0 / 256.0))
    ref[:rows, :] = jnp.round(scaled).astype(jnp.int32).astype(I16)
    ref[rows:, :] = jnp.broadcast_to(level, (TAIL, value.shape[1])).astype(jnp.int32).astype(I16)


def unpack(ref):
    rows = ref.shape[0] - TAIL
    level = ref[rows:, :].astype(jnp.int32).astype(F32)[0:1, :]
    return ref[:rows, :].astype(jnp.int32).astype(F32) * jnp.exp2(level * (1.0 / 256.0))


def first_messages(own_ref, other_ref, kept_ref, a_ref, b_ref):
    rows = own_ref.shape[0] // 4
    pack(a_ref, own_ref[:rows, :] + other_ref[:rows, :])
    pack(b_ref, own_ref[rows : 2 * rows, :] + other_ref[rows : 2 * rows, :])
    kept_ref[...] = own_ref[2 * rows :, :] + other_ref[2 * rows : 4 * rows, :]


def second_messages(sum_ref, a_in, b_in, kept_ref, a_ref, b_ref):
    rows = sum_ref.shape[0] // 4
    for part, (came, out) in enumerate(((a_in, a_ref), (b_in, b_ref))):
        at = 2 * part * rows
        total = sum_ref[at : at + 2 * rows, :] + unpack(came)
        kept_ref[part * rows : (part + 1) * rows, :] = total[:rows, :]
        pack(out, total[rows:, :])


def split_four(mine, work_ref, own_ref, message_refs, masks):
    quarter = work_ref.shape[0] // 4

    def rows_of(owner):
        return work_ref[pl.ds(pl.multiple_of(owner * quarter, quarter), quarter), :]

    for mask, out in zip(masks, message_refs):
        pack(out, rows_of(lax.bitwise_xor(mine, mask)))
    own_ref[...] = rows_of(mine)


def third_messages(here_ref, kept_ref, a_in, b_in, own_ref, m1_ref, m2_ref, m3_ref, work_ref):
    half = kept_ref.shape[0] // 2
    work_ref[:half, :] = kept_ref[:half, :] + unpack(a_in)
    work_ref[half:, :] = kept_ref[half:, :] + unpack(b_in)
    split_four(here_ref[1], work_ref, own_ref, (m1_ref, m2_ref, m3_ref), Z_ORDER)


def last_sum(own_ref, m1_in, m2_in, m3_in, out_ref):
    out_ref[...] = (own_ref[...] + unpack(m1_in) + unpack(m2_in) + unpack(m3_in)).astype(BF16)


def join(p0_ref, p1_ref, p2_ref, p3_ref, out_ref):
    rows = p0_ref.shape[0]
    for i, ref in enumerate((p0_ref, p1_ref, p2_ref, p3_ref)):
        out_ref[rows * i : rows * (i + 1), :] = ref[...]


def gram_messages(here_ref, mine_ref, came_ref, own_ref, m1_ref, m2_ref, m3_ref, work_ref):
    work_ref[...] = mine_ref[...] + came_ref[...]
    split_four(here_ref[3] // 2, work_ref, own_ref, (m1_ref, m2_ref, m3_ref), Y_ORDER)


def gram_halves(here_ref, own_ref, m1_in, m2_in, m3_in, kept_ref, out_ref, work_ref):
    rows = kept_ref.shape[0]
    work_ref[...] = own_ref[...] + unpack(m1_in) + unpack(m2_in) + unpack(m3_in)
    half = here_ref[3] % 2
    kept_ref[...] = work_ref[pl.ds(pl.multiple_of(half * rows, rows), rows), :]
    pack(out_ref, work_ref[pl.ds(pl.multiple_of((1 - half) * rows, rows), rows), :])


def weights_kernel(here_ref, val_table, freq_ref, other_ref, ci_ref, vi_ref, ce_ref, *out_refs):
    shape = ci_ref.shape
    half = shape[1] // 2
    index = ci_ref[...]
    high, low = index // 128, index % 128
    cond = jnp.zeros(shape, F32)
    for row in range(ce_ref.shape[0]):
        table = jnp.broadcast_to(ce_ref[row : row + 1, :], shape)
        cond = jnp.where(high == row, jnp.take_along_axis(table, low, axis=1), cond)
    level = vi_ref[...]
    val = jnp.zeros(shape, F32)
    for row in range(val_table.shape[0]):
        val = jnp.where(level == row, val_table[row], val)
    spacing = cond - val
    swapped = jnp.concatenate([spacing[:, half:], spacing[:, :half]], axis=1)
    spacing = jnp.where(here_ref[1] % 2 == 1, swapped, spacing)
    for freq, out_ref in zip((freq_ref[0], other_ref[0:1, 0:1]), out_refs):
        out_ref[...] = 2.0 * spacing / (spacing * spacing + freq * freq)


def gram_step(here, weights, pieces, places, grams, after=()):
    width = pieces[0].shape[1]
    count, kinds = len(pieces), len(weights)

    def body(here_ref, *refs):
        w_refs, came, before, out_refs = refs[:kinds], refs[kinds : kinds + count], refs[kinds + count : -kinds], refs[-kinds:]
        totals = [ref[...] for ref in before] or [None] * kinds
        for ref, (stream, owner) in zip(came, places):
            first = (here_ref[2] * 4 + lax.bitwise_xor(here_ref[0], owner)) * 4 + stream * 2
            parts = [[] for _ in range(kinds)]
            for j in range(2):
                rows = ref[128 * j : 128 * (j + 1), :].astype(F32).T
                for part, w_ref in zip(parts, w_refs):
                    w = w_ref[pl.ds(first + lax.bitwise_xor(here_ref[1] // 2, j), 1), :]
                    part.append((rows * w).astype(BF16))
            for kind, part in enumerate(parts):
                term = jnp.dot(jnp.concatenate(part, axis=1), ref[...], preferred_element_type=F32)
                totals[kind] = term if totals[kind] is None else totals[kind] + term
        for out_ref, total in zip(out_refs, totals):
            out_ref[...] = total

    return call(
        body,
        [((width, width), F32)] * kinds,
        here,
        *weights,
        *pieces,
        *grams,
        cost=2 * kinds * width * width * sum(p.shape[0] for p in pieces),
        specs=[SMEM] + [VMEM] * (kinds + count + len(grams)),
        after=after,
    )


def on_device(pair_elements, subspace, val_energy, cond_energy, val_index, cond_index, frequencies):
    here = jnp.stack([lax.axis_index(name).astype(jnp.int32) for name in PW + ("pair",)])
    rows, width = pair_elements.shape[0], subspace.shape[1]
    unit = rows // 64
    message = lambda count: ((count + TAIL, width), I16)
    sums = lambda count: ((count, width), F32)
    both = range(2)

    def product_call(body, outs, *args, after=(), flag=False, parts=1):
        specs = [SMEM] * (len(args) + 1) + [ANY, VMEM]
        scratch, cost = product_scratch(pair_elements, parts), 2 * parts * 16 * unit * pair_elements.shape[1] * width
        arrays = (here, *args, pair_elements, subspace)
        return call(body, outs, *arrays, specs=specs, after=after, flag=flag, cost=cost, scratch=scratch, limit=VMEM_LARGE)

    def first_other(here_ref, freq_ref, a_ref, b_ref, out_ref, held, sems):
        out_ref[16 * unit :, :] = jnp.full((8, width), freq_ref[0], F32)
        products(here_ref, a_ref, b_ref, (out_ref,), held, sems, [(False, 0)])

    def first_own(here_ref, a_ref, b_ref, own_ref, other_ref, held, sems):
        products(here_ref, a_ref, b_ref, (own_ref, other_ref), held, sems, [(True, 0), (False, 1)])

    def second_own(here_ref, a_ref, b_ref, own_ref, held, sems):
        products(here_ref, a_ref, b_ref, (own_ref,), held, sems, [(True, 1)])

    kept, a, b = [None] * 2, [None] * 2, [None] * 2
    first = [sums(8 * unit)] + [message(4 * unit)] * 2
    other, done = product_call(first_other, [sums(16 * unit + 8)], frequencies, flag=True)
    other_in = xor_permute(other, "pw_c", 1)
    own, other = product_call(first_own, [sums(16 * unit)] * 2, after=[done], parts=2)
    other, other_in = lax.optimization_barrier((other, other_in))
    kept[0], a[0], b[0], done = call(first_messages, first, own, other_in, flag=True)
    own = product_call(second_own, [sums(16 * unit)], after=[done])[0]
    kept[1], a[1], b[1] = call(first_messages, first, own, xor_permute(other, "pw_c", 1))

    last = None
    for s in both:
        a[s], b[s] = xor_permute(a[s], "pw_x", 1), xor_permute(b[s], "pw_x", 3)
    for s in both:
        after = [] if last is None else [last]
        kept[s], a[s], b[s], last = call(
            second_messages, [sums(4 * unit)] + [message(2 * unit)] * 2, kept[s], a[s], b[s], after=after, flag=True
        )
        a[s], b[s] = xor_permute(a[s], "pw_x", 3), xor_permute(b[s], "pw_x", 1)
    came = [None] * 2
    for s in both:
        own, *out, last = call(
            third_messages,
            [sums(unit)] + [message(unit)] * 3,
            here,
            kept[s],
            a[s],
            b[s],
            specs=[SMEM] + [VMEM] * 3,
            after=[last],
            flag=True,
            scratch=[pltpu.VMEM((4 * unit, width), F32)],
        )
        came[s] = [own] + [xor_permute(value, "pw_z", mask) for mask, value in zip(Z_ORDER, out)]
    weights = call(
        weights_kernel,
        [((rows // 128, 128), F32)] * 2,
        here,
        val_energy,
        frequencies,
        other_in[16 * unit :, :128],
        cond_index.reshape(-1, 128),
        val_index.reshape(-1, 128),
        cond_energy.reshape(-1, 128),
        specs=[SMEM] * 3 + [VMEM] * 4,
        after=[last],
    )

    last = weights[0]
    pieces = [None] * 2
    for s in both:
        own, last = call(last_sum, [((unit, width), BF16)], *came[s], after=[last], flag=True)
        pieces[s] = [own] + [xor_permute(own, "pw_z", mask) for mask in (1, 2, 3)]
    quarters, near, far = [None] * 2, [None] * 2, [None] * 2
    for s in both:
        quarters[s], last = call(join, [((4 * unit, width), BF16)], *pieces[s], after=[last], flag=True)
        near[s], far[s] = xor_permute(quarters[s], "pw_x", 1), xor_permute(quarters[s], "pw_x", 3)
        near[s], far[s] = lax.optimization_barrier((near[s], far[s]))
    across = [xor_permute(far[0], "pw_x", 1), xor_permute(near[1], "pw_x", 3)]
    grams = gram_step(here, weights, quarters, [(0, 0), (1, 0)], [])
    grams = gram_step(here, weights, [near[0], far[0]], [(0, 1), (0, 3)], grams)
    grams = gram_step(here, weights, [near[1], far[1], across[0]], [(1, 1), (1, 3), (0, 2)], grams)
    mine, theirs = gram_step(here, weights, [across[1]], [(1, 2)], grams)

    part = width // 4
    own, *out = call(
        gram_messages,
        [sums(part)] + [message(part)] * 3,
        here,
        mine,
        xor_permute(theirs, "pw_c", 1),
        specs=[SMEM] + [VMEM] * 2,
        scratch=[pltpu.VMEM((width, width), F32)],
    )
    came = [xor_permute(value, "pair", 2 * mask) for mask, value in zip(Y_ORDER, out)]
    own, out = call(
        gram_halves,
        [sums(part // 2), message(part // 2)],
        here,
        own,
        *came,
        specs=[SMEM] + [VMEM] * 4,
        scratch=[pltpu.VMEM((part, width), F32)],
    )
    factor = -4.0 / (rows * lax.axis_size("pair"))

    def finish(own_ref, came_ref, out_ref):
        out_ref[...] = (own_ref[...] + unpack(came_ref)) * factor

    return call(finish, [sums(part // 2)], own, xor_permute(out, "pair", 1))[0][None]


def solution(mesh):
    torus = Mesh(mesh.devices.reshape(mesh.shape["pair"], 4, 4, 2), ("pair",) + PW)
    return jax.shard_map(
        on_device,
        mesh=torus,
        in_specs=(P("pair", PW), P(PW, None), P(), P(), P("pair"), P("pair"), P(PW)),
        out_specs=P(PW, "pair", None),
        check_vma=False,
    )
```

time: 122 us -> 111 us (0.910)
  the two profiles are of different devices: /device:TPU:24 before, /device:TPU:32 now
where the time goes in v6:
time: 111 us
  starting transfers between devices  50.7 us (46%)
  waiting for transfers between devices  34.6 us (31%)
  Pallas kernels  23.2 us (21%)
  local copies, waits for them, and re-layouts  1.24 us (1%)
    ppermute x33, starting transfers between devices, xor_permute(): return lax.ppermute(value, axis, [(i, i ^ mask) for i in range(count)])  50.7 us
    ppermute x33, waiting for transfers between devices, xor_permute(): return lax.ppermute(value, axis, [(i, i ^ mask) for i in range(count)])  34.6 us
    pallas_call x21, Pallas kernels, call(): pl.pallas_call(kernel, out_shape=[jax.ShapeDtypeStruct(shape, dtype) for...  23.2 us
  transfers between devices with their start and end apart: 33, of which 17 were waited for; matrix products, arithmetic and copies ran while one was open for 0% of the time, Pallas kernels for 15%

profile of v6, /device:TPU:32, one launch (start us, length us, event | category | flops | bytes accessed | tf_op | source)
XLA Modules:
  0.0 110.8 jit_solution(14050013922434573636)
XLA Ops:
  0.7 1.2 %copy-done = bf16[1024,512]{1,0:T(8,128)(2,1)S(1)} copy-done((bf16[1024,512]{1,0:T(8,128)(2,1)S(1)}, bf16[1024,512]{1,0:T(8,128)(2,1)}, u32[]{:S(2)}) %copy-start) | copy-done | bytes 1048600
  2.0 3.4 %shard_map.73 = (f32[1032,512]{1,0:T(8,128)S(1)}, f32[8,128]{1,0:T(8,128)S(1)}) custom-call(s32[4]{0:T(128)S(1)} %pad_add_fusion.refs_0_, f32[1]{0:T(128)S(6)} %copy.8.refs_1_.refs_2_, bf16[4096,1024]{1,0:T(8,128)(2,1)} %refs_1_.5, bf16[1024,512]{1,0:T(8,128)(2,1)S(1)} %copy-done), custom_call_target="tpu_custom_call" | custom-call | flops 1073741824 | bytes 9437204 | tf_op jit(solution)/shard_map/pallas_call | solution.py:35
  5.4 4.7 %shard_map.74 = (f32[1024,512]{1,0:T(8,128)S(1)}, f32[1024,512]{1,0:T(8,128)S(1)}) custom-call(s32[4]{0:T(128)S(1)} %pad_add_fusion.refs_0_, bf16[4096,1024]{1,0:T(8,128)(2,1)} %refs_1_.5, bf16[1024,512]{1,0:T(8,128)(2,1)S(1)} %copy-done, f32[8,128]{1,0:T(8,128)S(1)} %get-tuple-element.63.refs_3_), custom_call_target="tpu_custom_call" | custom-call | flops 2147483648 | bytes 9437200 | tf_op jit(solution)/shard_map/pallas_call | solution.py:35
  11.1 1.6 %collective-permute-start.4 = (s16[272,512]{1,0:T(8,128)(2,1)S(1)}, s16[272,512]{1,0:T(8,128)(2,1)S(1)}, u32[]{:S(2)}, u32[]{:S(2)}) collective-permute-start(s16[272,512]{1,0:T(8,128)(2,1)S(1)} %get-tuple-element.74), channel_id=1, source_target_pairs={{0,8},{8,0},{16,24},{24,16},{1,9},{9,1},{17,25},{25,17},{2,10},{10... | collective-permute-start | bytes 835592 | tf_op jit(solution)/shard_map/ppermute | solution.py:20
  12.7 2.1 %collective-permute-start.5 = (s16[272,512]{1,0:T(8,128)(2,1)S(1)}, s16[272,512]{1,0:T(8,128)(2,1)S(1)}, u32[]{:S(2)}, u32[]{:S(2)}) collective-permute-start(s16[272,512]{1,0:T(8,128)(2,1)S(1)} %get-tuple-element.75), channel_id=1, source_target_pairs={{0,24},{8,16},{16,8},{24,0},{1,25},{9,17},{17,9},{25,1},{2,26},{10... | collective-permute-start | bytes 835592 | tf_op jit(solution)/shard_map/ppermute | solution.py:20
  14.8 3.4 %shard_map.76.refs_0_ = f32[1024,512]{1,0:T(8,128)S(1)} custom-call(s32[4]{0:T(128)S(1)} %pad_add_fusion.refs_0_, bf16[4096,1024]{1,0:T(8,128)(2,1)} %refs_1_.5, bf16[1024,512]{1,0:T(8,128)(2,1)S(1)} %copy-done, f32[8,128]{1,0:T(8,128)S(1)} %get-tuple-element.68.refs_3_), custom_call_target="tpu_custom_call" | custom-call | flops 1073741824 | bytes 9437200 | tf_op jit(solution)/shard_map/pallas_call | solution.py:35
  19.8 2.4 %collective-permute-done.5.refs_2_ = s16[272,512]{1,0:T(8,128)(2,1)S(1)} collective-permute-done((s16[272,512]{1,0:T(8,128)(2,1)S(1)}, s16[272,512]{1,0:T(8,128)(2,1)S(1)}, u32[]{:S(2)}, u32[]{:S(2)}) %collective-permute-start.5) | collective-permute-done | bytes 278560 | tf_op jit(solution)/shard_map/ppermute | solution.py:20
  22.4 3.3 %collective-permute-start.8 = (s16[144,512]{1,0:T(8,128)(2,1)S(1)}, s16[144,512]{1,0:T(8,128)(2,1)S(1)}, u32[]{:S(2)}, u32[]{:S(2)}) collective-permute-start(s16[144,512]{1,0:T(8,128)(2,1)S(1)} %get-tuple-element.81), channel_id=1, source_target_pairs={{0,24},{8,16},{16,8},{24,0},{1,25},{9,17},{17,9},{25,1},{2,26},{10... | collective-permute-start | bytes 442376 | tf_op jit(solution)/shard_map/ppermute | solution.py:20
  25.8 1.6 %collective-permute-done.2.refs_1_ = s16[272,512]{1,0:T(8,128)(2,1)S(1)} collective-permute-done((s16[272,512]{1,0:T(8,128)(2,1)S(1)}, s16[272,512]{1,0:T(8,128)(2,1)S(1)}, u32[]{:S(2)}, u32[]{:S(2)}) %collective-permute-start.2) | collective-permute-done | bytes 278560 | tf_op jit(solution)/shard_map/ppermute | solution.py:20
  27.3 2.4 %collective-permute-done.3.refs_2_ = s16[272,512]{1,0:T(8,128)(2,1)S(1)} collective-permute-done((s16[272,512]{1,0:T(8,128)(2,1)S(1)}, s16[272,512]{1,0:T(8,128)(2,1)S(1)}, u32[]{:S(2)}, u32[]{:S(2)}) %collective-permute-start.3) | collective-permute-done | bytes 278560 | tf_op jit(solution)/shard_map/ppermute | solution.py:20
  30.0 1.7 %collective-permute-start.6 = (s16[144,512]{1,0:T(8,128)(2,1)S(1)}, s16[144,512]{1,0:T(8,128)(2,1)S(1)}, u32[]{:S(2)}, u32[]{:S(2)}) collective-permute-start(s16[144,512]{1,0:T(8,128)(2,1)S(1)} %get-tuple-element.78), channel_id=1, source_target_pairs={{0,24},{8,16},{16,8},{24,0},{1,25},{9,17},{17,9},{25,1},{2,26},{10... | collective-permute-start | bytes 442376 | tf_op jit(solution)/shard_map/ppermute | solution.py:20
  32.7 2.0 %collective-permute-start.13 = (s16[80,512]{1,0:T(8,128)(2,1)S(1)}, s16[80,512]{1,0:T(8,128)(2,1)S(1)}, u32[]{:S(2)}, u32[]{:S(2)}) collective-permute-start(s16[80,512]{1,0:T(8,128)(2,1)S(1)} %get-tuple-element.93), channel_id=1, source_target_pairs={{0,6},{2,4},{4,2},{6,0},{1,7},{3,5},{5,3},{7,1},{8,14},{10,12},{12... | collective-permute-start | bytes 245768 | tf_op jit(solution)/shard_map/ppermute | solution.py:20
  34.7 1.5 %collective-permute-start.14 = (s16[80,512]{1,0:T(8,128)(2,1)S(1)}, s16[80,512]{1,0:T(8,128)(2,1)S(1)}, u32[]{:S(2)}, u32[]{:S(2)}) collective-permute-start(s16[80,512]{1,0:T(8,128)(2,1)S(1)} %get-tuple-element.94), channel_id=1, source_target_pairs={{0,4},{2,6},{4,0},{6,2},{1,5},{3,7},{5,1},{7,3},{8,12},{10,14},{12... | collective-permute-start | bytes 245768 | tf_op jit(solution)/shard_map/ppermute | solution.py:20
  36.2 1.4 %collective-permute-start.15 = (s16[80,512]{1,0:T(8,128)(2,1)S(1)}, s16[80,512]{1,0:T(8,128)(2,1)S(1)}, u32[]{:S(2)}, u32[]{:S(2)}) collective-permute-start(s16[80,512]{1,0:T(8,128)(2,1)S(1)} %get-tuple-element.95), channel_id=1, source_target_pairs={{0,2},{2,0},{4,6},{6,4},{1,3},{3,1},{5,7},{7,5},{8,10},{10,8},{12,... | collective-permute-start | bytes 245768 | tf_op jit(solution)/shard_map/ppermute | solution.py:20
  38.3 1.7 %collective-permute-start.10 = (s16[80,512]{1,0:T(8,128)(2,1)S(1)}, s16[80,512]{1,0:T(8,128)(2,1)S(1)}, u32[]{:S(2)}, u32[]{:S(2)}) collective-permute-start(s16[80,512]{1,0:T(8,128)(2,1)S(1)} %get-tuple-element.89), channel_id=1, source_target_pairs={{0,6},{2,4},{4,2},{6,0},{1,7},{3,5},{5,3},{7,1},{8,14},{10,12},{12... | collective-permute-start | bytes 245768 | tf_op jit(solution)/shard_map/ppermute | solution.py:20
  40.0 1.6 %collective-permute-start.11 = (s16[80,512]{1,0:T(8,128)(2,1)S(1)}, s16[80,512]{1,0:T(8,128)(2,1)S(1)}, u32[]{:S(2)}, u32[]{:S(2)}) collective-permute-start(s16[80,512]{1,0:T(8,128)(2,1)S(1)} %get-tuple-element.90), channel_id=1, source_target_pairs={{0,4},{2,6},{4,0},{6,2},{1,5},{3,7},{5,1},{7,3},{8,12},{10,14},{12... | collective-permute-start | bytes 245768 | tf_op jit(solution)/shard_map/ppermute | solution.py:20
  41.6 1.4 %collective-permute-start.12 = (s16[80,512]{1,0:T(8,128)(2,1)S(1)}, s16[80,512]{1,0:T(8,128)(2,1)S(1)}, u32[]{:S(2)}, u32[]{:S(2)}) collective-permute-start(s16[80,512]{1,0:T(8,128)(2,1)S(1)} %get-tuple-element.91), channel_id=1, source_target_pairs={{0,2},{2,0},{4,6},{6,4},{1,3},{3,1},{5,7},{7,5},{8,10},{10,8},{12,... | collective-permute-start | bytes 245768 | tf_op jit(solution)/shard_map/ppermute | solution.py:20
  43.0 0.9 shard_map.82
  43.9 1.6 %collective-permute-start.21 = (bf16[64,512]{1,0:T(8,128)(2,1)S(1)}, bf16[64,512]{1,0:T(8,128)(2,1)S(1)}, u32[]{:S(2)}, u32[]{:S(2)}) collective-permute-start(bf16[64,512]{1,0:T(8,128)(2,1)S(1)} %get-tuple-element.98.refs_0_), channel_id=1, source_target_pairs={{0,6},{2,4},{4,2},{6,0},{1,7},{3,5},{5,3},{7,1},{8,14},{10,12},{12... | collective-permute-start | bytes 196616 | tf_op jit(solution)/shard_map/ppermute | solution.py:20
  45.5 5.5 %collective-permute-start.20 = (bf16[64,512]{1,0:T(8,128)(2,1)S(1)}, bf16[64,512]{1,0:T(8,128)(2,1)S(1)}, u32[]{:S(2)}, u32[]{:S(2)}) collective-permute-start(bf16[64,512]{1,0:T(8,128)(2,1)S(1)} %get-tuple-element.98.refs_0_), channel_id=1, source_target_pairs={{0,4},{2,6},{4,0},{6,2},{1,5},{3,7},{5,1},{7,3},{8,12},{10,14},{12... | collective-permute-start | bytes 196616 | tf_op jit(solution)/shard_map/ppermute | solution.py:20
  51.1 1.0 collective-permute-done.21.refs_3_
  52.1 1.9 %collective-permute-done.20.refs_2_ = bf16[64,512]{1,0:T(8,128)(2,1)S(1)} collective-permute-done((bf16[64,512]{1,0:T(8,128)(2,1)S(1)}, bf16[64,512]{1,0:T(8,128)(2,1)S(1)}, u32[]{:S(2)}, u32[]{:S(2)}) %collective-permute-start.20) | collective-permute-done | bytes 65568 | tf_op jit(solution)/shard_map/ppermute | solution.py:20
  53.9 1.3 %collective-permute-done.19.refs_1_ = bf16[64,512]{1,0:T(8,128)(2,1)S(1)} collective-permute-done((bf16[64,512]{1,0:T(8,128)(2,1)S(1)}, bf16[64,512]{1,0:T(8,128)(2,1)S(1)}, u32[]{:S(2)}, u32[]{:S(2)}) %collective-permute-start.19) | collective-permute-done | bytes 65568 | tf_op jit(solution)/shard_map/ppermute | solution.py:20
  55.3 1.9 %collective-permute-start.26 = (bf16[256,512]{1,0:T(8,128)(2,1)S(1)}, bf16[256,512]{1,0:T(8,128)(2,1)S(1)}, u32[]{:S(2)}, u32[]{:S(2)}) collective-permute-start(bf16[256,512]{1,0:T(8,128)(2,1)S(1)} %get-tuple-element.104.refs_3_), channel_id=1, source_target_pairs={{0,24},{8,16},{16,8},{24,0},{1,25},{9,17},{17,9},{25,1},{2,26},{10... | collective-permute-start | bytes 786440 | tf_op jit(solution)/shard_map/ppermute | solution.py:20
  57.3 2.0 %collective-permute-start.18 = (bf16[64,512]{1,0:T(8,128)(2,1)S(1)}, bf16[64,512]{1,0:T(8,128)(2,1)S(1)}, u32[]{:S(2)}, u32[]{:S(2)}) collective-permute-start(bf16[64,512]{1,0:T(8,128)(2,1)S(1)} %get-tuple-element.97.refs_0_), channel_id=1, source_target_pairs={{0,6},{2,4},{4,2},{6,0},{1,7},{3,5},{5,3},{7,1},{8,14},{10,12},{12... | collective-permute-start | bytes 196616 | tf_op jit(solution)/shard_map/ppermute | solution.py:20
  59.3 1.8 %collective-permute-start.17 = (bf16[64,512]{1,0:T(8,128)(2,1)S(1)}, bf16[64,512]{1,0:T(8,128)(2,1)S(1)}, u32[]{:S(2)}, u32[]{:S(2)}) collective-permute-start(bf16[64,512]{1,0:T(8,128)(2,1)S(1)} %get-tuple-element.97.refs_0_), channel_id=1, source_target_pairs={{0,4},{2,6},{4,0},{6,2},{1,5},{3,7},{5,1},{7,3},{8,12},{10,14},{12... | collective-permute-start | bytes 196616 | tf_op jit(solution)/shard_map/ppermute | solution.py:20
  61.1 1.2 %collective-permute-done.18.refs_3_ = bf16[64,512]{1,0:T(8,128)(2,1)S(1)} collective-permute-done((bf16[64,512]{1,0:T(8,128)(2,1)S(1)}, bf16[64,512]{1,0:T(8,128)(2,1)S(1)}, u32[]{:S(2)}, u32[]{:S(2)}) %collective-permute-start.18) | collective-permute-done | bytes 65568 | tf_op jit(solution)/shard_map/ppermute | solution.py:20
  62.3 2.3 %collective-permute-done.17.refs_2_ = bf16[64,512]{1,0:T(8,128)(2,1)S(1)} collective-permute-done((bf16[64,512]{1,0:T(8,128)(2,1)S(1)}, bf16[64,512]{1,0:T(8,128)(2,1)S(1)}, u32[]{:S(2)}, u32[]{:S(2)}) %collective-permute-start.17) | collective-permute-done | bytes 65568 | tf_op jit(solution)/shard_map/ppermute | solution.py:20
  64.5 0.8 collective-permute-done.16.refs_1_
  65.9 1.2 %collective-permute-start.23 = (bf16[256,512]{1,0:T(8,128)(2,1)S(1)}, bf16[256,512]{1,0:T(8,128)(2,1)S(1)}, u32[]{:S(2)}, u32[]{:S(2)}) collective-permute-start(bf16[256,512]{1,0:T(8,128)(2,1)S(1)} %get-tuple-element.101.refs_4_), channel_id=1, source_target_pairs={{0,24},{8,16},{16,8},{24,0},{1,25},{9,17},{17,9},{25,1},{2,26},{10... | collective-permute-start | bytes 786440 | tf_op jit(solution)/shard_map/ppermute | solution.py:20
  67.2 0.8 collective-permute-start.22
  68.0 1.2 %collective-permute-start.27 = (bf16[256,512]{1,0:T(8,128)(2,1)S(1)}, bf16[256,512]{1,0:T(8,128)(2,1)S(1)}, u32[]{:S(2)}, u32[]{:S(2)}) collective-permute-start(bf16[256,512]{1,0:T(8,128)(2,1)S(1)} %collective-permute-done.26.refs_4_), channel_id=1, source_target_pairs={{0,8},{8,0},{16,24},{24,16},{1,9},{9,1},{17,25},{25,17},{2,10},{10... | collective-permute-start | bytes 786440 | tf_op jit(solution)/shard_map/ppermute | solution.py:20
  69.2 5.2 %collective-permute-done.23.refs_4_ = bf16[256,512]{1,0:T(8,128)(2,1)S(1)} collective-permute-done((bf16[256,512]{1,0:T(8,128)(2,1)S(1)}, bf16[256,512]{1,0:T(8,128)(2,1)S(1)}, u32[]{:S(2)}, u32[]{:S(2)}) %collective-permute-start.23) | collective-permute-done | bytes 262176 | tf_op jit(solution)/shard_map/ppermute | solution.py:20
  74.4 2.0 %collective-permute-start.24 = (bf16[256,512]{1,0:T(8,128)(2,1)S(1)}, bf16[256,512]{1,0:T(8,128)(2,1)S(1)}, u32[]{:S(2)}, u32[]{:S(2)}) collective-permute-start(bf16[256,512]{1,0:T(8,128)(2,1)S(1)} %collective-permute-done.22.refs_3_), channel_id=1, source_target_pairs={{0,24},{8,16},{16,8},{24,0},{1,25},{9,17},{17,9},{25,1},{2,26},{10... | collective-permute-start | bytes 786440 | tf_op jit(solution)/shard_map/ppermute | solution.py:20
  76.3 1.3 %shard_map.87 = (f32[512,512]{1,0:T(8,128)S(1)}, f32[512,512]{1,0:T(8,128)S(1)}) custom-call(s32[4]{0:T(128)S(1)} %pad_add_fusion.refs_0_, f32[32,128]{1,0:T(8,128)S(1)} %get-tuple-element.86.refs_4_.refs_1_, f32[32,128]{1,0:T(8,128)S(1)} %get-tuple-element.87.refs_2_, bf16[256,512]{1,0:T(8,128)(2,1)S(1)} %get-tuple-element.104.refs_3_, ...), custom_call_target="tpu_custom_call" | custom-call | flops 536870912 | bytes 557072 | tf_op jit(solution)/shard_map/pallas_call | solution.py:35
  77.7 1.3 %shard_map.88 = (f32[512,512]{1,0:T(8,128)S(1)}, f32[512,512]{1,0:T(8,128)S(1)}) custom-call(s32[4]{0:T(128)S(1)} %pad_add_fusion.refs_0_, f32[32,128]{1,0:T(8,128)S(1)} %get-tuple-element.86.refs_4_.refs_1_, f32[32,128]{1,0:T(8,128)S(1)} %get-tuple-element.87.refs_2_, bf16[256,512]{1,0:T(8,128)(2,1)S(1)} %collective-permute-done.25.refs_3_, ...), custom_call_target="tpu_custom_call" | custom-call | flops 536870912 | bytes 2654224 | tf_op jit(solution)/shard_map/pallas_call | solution.py:35
  79.0 1.6 %shard_map.89 = (f32[512,512]{1,0:T(8,128)S(1)}, f32[512,512]{1,0:T(8,128)S(1)}) custom-call(s32[4]{0:T(128)S(1)} %pad_add_fusion.refs_0_, f32[32,128]{1,0:T(8,128)S(1)} %get-tuple-element.86.refs_4_.refs_1_, f32[32,128]{1,0:T(8,128)S(1)} %get-tuple-element.87.refs_2_, bf16[256,512]{1,0:T(8,128)(2,1)S(1)} %collective-permute-done.22.refs_3_, ...), custom_call_target="tpu_custom_call" | custom-call | flops 805306368 | bytes 2916368 | tf_op jit(solution)/shard_map/pallas_call | solution.py:35
  80.6 1.4 %collective-permute-done.24.refs_3_ = bf16[256,512]{1,0:T(8,128)(2,1)S(1)} collective-permute-done((bf16[256,512]{1,0:T(8,128)(2,1)S(1)}, bf16[256,512]{1,0:T(8,128)(2,1)S(1)}, u32[]{:S(2)}, u32[]{:S(2)}) %collective-permute-start.24) | collective-permute-done | bytes 262176 | tf_op jit(solution)/shard_map/ppermute | solution.py:20
  82.0 1.0 shard_map.90
  83.1 2.6 %collective-permute-done.28.refs_2_ = f32[512,512]{1,0:T(8,128)S(1)} collective-permute-done((f32[512,512]{1,0:T(8,128)S(1)}, f32[512,512]{1,0:T(8,128)S(1)}, u32[]{:S(2)}, u32[]{:S(2)}) %collective-permute-start.28) | collective-permute-done | bytes 1048608 | tf_op jit(solution)/shard_map/ppermute | solution.py:20
  85.8 0.8 shard_map.91
  86.5 3.3 %collective-permute-start.29 = (s16[144,512]{1,0:T(8,128)(2,1)S(1)}, s16[144,512]{1,0:T(8,128)(2,1)S(1)}, u32[]{:S(2)}, u32[]{:S(2)}) collective-permute-start(s16[144,512]{1,0:T(8,128)(2,1)S(1)} %get-tuple-element.116), channel_id=1, source_target_pairs={{0,128},{32,160},{64,192},{96,224},{128,0},{160,32},{192,64},{224,... | collective-permute-start | bytes 442376 | tf_op jit(solution)/shard_map/ppermute | solution.py:20
  89.8 1.1 collective-permute-start.30
  90.9 3.2 %collective-permute-done.29.refs_2_ = s16[144,512]{1,0:T(8,128)(2,1)S(1)} collective-permute-done((s16[144,512]{1,0:T(8,128)(2,1)S(1)}, s16[144,512]{1,0:T(8,128)(2,1)S(1)}, u32[]{:S(2)}, u32[]{:S(2)}) %collective-permute-start.29) | collective-permute-done | bytes 147488 | tf_op jit(solution)/shard_map/ppermute | solution.py:20
  94.1 3.1 %collective-permute-done.30.refs_3_ = s16[144,512]{1,0:T(8,128)(2,1)S(1)} collective-permute-done((s16[144,512]{1,0:T(8,128)(2,1)S(1)}, s16[144,512]{1,0:T(8,128)(2,1)S(1)}, u32[]{:S(2)}, u32[]{:S(2)}) %collective-permute-start.30) | collective-permute-done | bytes 147488 | tf_op jit(solution)/shard_map/ppermute | solution.py:20
  97.6 0.8 shard_map.92
  98.3 8.0 %collective-permute-start.32 = (s16[80,512]{1,0:T(8,128)(2,1)S(1)}, s16[80,512]{1,0:T(8,128)(2,1)S(1)}, u32[]{:S(2)}, u32[]{:S(2)}) collective-permute-start(s16[80,512]{1,0:T(8,128)(2,1)S(1)} %get-tuple-element.120), channel_id=1, source_target_pairs={{0,32},{32,0},{64,96},{96,64},{128,160},{160,128},{192,224},{224,1... | collective-permute-start | bytes 245768 | tf_op jit(solution)/shard_map/ppermute | solution.py:20
  106.3 3.7 %collective-permute-done.32.refs_1_ = s16[80,512]{1,0:T(8,128)(2,1)S(1)} collective-permute-done((s16[80,512]{1,0:T(8,128)(2,1)S(1)}, s16[80,512]{1,0:T(8,128)(2,1)S(1)}, u32[]{:S(2)}, u32[]{:S(2)}) %collective-permute-start.32) | collective-permute-done | bytes 81952 | tf_op jit(solution)/shard_map/ppermute | solution.py:20
  (51 shorter events, 7.0 us)
Async XLA Ops:
  0.7 1.2 %copy-start = (bf16[1024,512]{1,0:T(8,128)(2,1)S(1)}, bf16[1024,512]{1,0:T(8,128)(2,1)}, u32[]{:S(2)}) copy-start(bf16[1024,512]{1,0:T(8,128)(2,1)} %refs_2_.6) | copy-start | bytes 3145732
  5.3 4.8 %collective-permute-start = (f32[1032,512]{1,0:T(8,128)S(1)}, f32[1032,512]{1,0:T(8,128)S(1)}, u32[]{:S(2)}, u32[]{:S(2)}) collective-permute-start(f32[1032,512]{1,0:T(8,128)S(1)} %get-tuple-element.65), channel_id=1, source_target_pairs={{0,1},{1,0},{2,3},{3,2},{4,5},{5,4},{6,7},{7,6},{8,9},{9,8},{10,11... | collective-permute-start | bytes 6340616 | tf_op jit(solution)/shard_map/ppermute | solution.py:20
  10.2 8.0 %collective-permute-start.1 = (f32[1024,512]{1,0:T(8,128)S(1)}, f32[1024,512]{1,0:T(8,128)S(1)}, u32[]{:S(2)}, u32[]{:S(2)}) collective-permute-start(f32[1024,512]{1,0:T(8,128)S(1)} %get-tuple-element.69), channel_id=1, source_target_pairs={{0,1},{1,0},{2,3},{3,2},{4,5},{5,4},{6,7},{7,6},{8,9},{9,8},{10,11... | collective-permute-start | bytes 6291464 | tf_op jit(solution)/shard_map/ppermute | solution.py:20
  11.1 8.7 %collective-permute-start.4 = (s16[272,512]{1,0:T(8,128)(2,1)S(1)}, s16[272,512]{1,0:T(8,128)(2,1)S(1)}, u32[]{:S(2)}, u32[]{:S(2)}) collective-permute-start(s16[272,512]{1,0:T(8,128)(2,1)S(1)} %get-tuple-element.74), channel_id=1, source_target_pairs={{0,8},{8,0},{16,24},{24,16},{1,9},{9,1},{17,25},{25,17},{2,10},{10... | collective-permute-start | bytes 835592 | tf_op jit(solution)/shard_map/ppermute | solution.py:20
  12.7 9.5 %collective-permute-start.5 = (s16[272,512]{1,0:T(8,128)(2,1)S(1)}, s16[272,512]{1,0:T(8,128)(2,1)S(1)}, u32[]{:S(2)}, u32[]{:S(2)}) collective-permute-start(s16[272,512]{1,0:T(8,128)(2,1)S(1)} %get-tuple-element.75), channel_id=1, source_target_pairs={{0,24},{8,16},{16,8},{24,0},{1,25},{9,17},{17,9},{25,1},{2,26},{10... | collective-permute-start | bytes 835592 | tf_op jit(solution)/shard_map/ppermute | solution.py:20
  18.5 8.8 %collective-permute-start.2 = (s16[272,512]{1,0:T(8,128)(2,1)S(1)}, s16[272,512]{1,0:T(8,128)(2,1)S(1)}, u32[]{:S(2)}, u32[]{:S(2)}) collective-permute-start(s16[272,512]{1,0:T(8,128)(2,1)S(1)} %get-tuple-element.71), channel_id=1, source_target_pairs={{0,8},{8,0},{16,24},{24,16},{1,9},{9,1},{17,25},{25,17},{2,10},{10... | collective-permute-start | bytes 835592 | tf_op jit(solution)/shard_map/ppermute | solution.py:20
  19.2 10.6 %collective-permute-start.3 = (s16[272,512]{1,0:T(8,128)(2,1)S(1)}, s16[272,512]{1,0:T(8,128)(2,1)S(1)}, u32[]{:S(2)}, u32[]{:S(2)}) collective-permute-start(s16[272,512]{1,0:T(8,128)(2,1)S(1)} %get-tuple-element.72), channel_id=1, source_target_pairs={{0,24},{8,16},{16,8},{24,0},{1,25},{9,17},{17,9},{25,1},{2,26},{10... | collective-permute-start | bytes 835592 | tf_op jit(solution)/shard_map/ppermute | solution.py:20
  22.2 20.8 %copy-start.1 = (s32[4096]{0:T(1024)S(1)}, s32[4096]{0:T(1024)}, u32[]{:S(2)}) copy-start(s32[4096]{0:T(1024)} %param.12) | copy-start | bytes 49156
  22.2 20.8 %copy-start.2 = (s32[4096]{0:T(1024)S(1)}, s32[4096]{0:T(1024)}, u32[]{:S(2)}) copy-start(s32[4096]{0:T(1024)} %param.11) | copy-start | bytes 49156
  22.2 20.8 %copy-start.3 = (f32[2048]{0:T(1024)S(1)}, f32[2048]{0:T(1024)}, u32[]{:S(2)}) copy-start(f32[2048]{0:T(1024)} %param.10) | copy-start | bytes 24580
  22.2 20.8 %copy-start.4 = (f32[16]{0:T(128)S(1)}, f32[16]{0:T(128)}, u32[]{:S(2)}) copy-start(f32[16]{0:T(128)} %refs_1_.6) | copy-start | bytes 196
  22.4 9.5 %collective-permute-start.8 = (s16[144,512]{1,0:T(8,128)(2,1)S(1)}, s16[144,512]{1,0:T(8,128)(2,1)S(1)}, u32[]{:S(2)}, u32[]{:S(2)}) collective-permute-start(s16[144,512]{1,0:T(8,128)(2,1)S(1)} %get-tuple-element.81), channel_id=1, source_target_pairs={{0,24},{8,16},{16,8},{24,0},{1,25},{9,17},{17,9},{25,1},{2,26},{10... | collective-permute-start | bytes 442376 | tf_op jit(solution)/shard_map/ppermute | solution.py:20
  25.7 6.2 %collective-permute-start.9 = (s16[144,512]{1,0:T(8,128)(2,1)S(1)}, s16[144,512]{1,0:T(8,128)(2,1)S(1)}, u32[]{:S(2)}, u32[]{:S(2)}) collective-permute-start(s16[144,512]{1,0:T(8,128)(2,1)S(1)} %get-tuple-element.82), channel_id=1, source_target_pairs={{0,8},{8,0},{16,24},{24,16},{1,9},{9,1},{17,25},{25,17},{2,10},{10... | collective-permute-start | bytes 442376 | tf_op jit(solution)/shard_map/ppermute | solution.py:20
  30.0 7.5 %collective-permute-start.6 = (s16[144,512]{1,0:T(8,128)(2,1)S(1)}, s16[144,512]{1,0:T(8,128)(2,1)S(1)}, u32[]{:S(2)}, u32[]{:S(2)}) collective-permute-start(s16[144,512]{1,0:T(8,128)(2,1)S(1)} %get-tuple-element.78), channel_id=1, source_target_pairs={{0,24},{8,16},{16,8},{24,0},{1,25},{9,17},{17,9},{25,1},{2,26},{10... | collective-permute-start | bytes 442376 | tf_op jit(solution)/shard_map/ppermute | solution.py:20
  31.7 5.8 %collective-permute-start.7 = (s16[144,512]{1,0:T(8,128)(2,1)S(1)}, s16[144,512]{1,0:T(8,128)(2,1)S(1)}, u32[]{:S(2)}, u32[]{:S(2)}) collective-permute-start(s16[144,512]{1,0:T(8,128)(2,1)S(1)} %get-tuple-element.79), channel_id=1, source_target_pairs={{0,8},{8,0},{16,24},{24,16},{1,9},{9,1},{17,25},{25,17},{2,10},{10... | collective-permute-start | bytes 442376 | tf_op jit(solution)/shard_map/ppermute | solution.py:20
  32.7 8.9 %collective-permute-start.13 = (s16[80,512]{1,0:T(8,128)(2,1)S(1)}, s16[80,512]{1,0:T(8,128)(2,1)S(1)}, u32[]{:S(2)}, u32[]{:S(2)}) collective-permute-start(s16[80,512]{1,0:T(8,128)(2,1)S(1)} %get-tuple-element.93), channel_id=1, source_target_pairs={{0,6},{2,4},{4,2},{6,0},{1,7},{3,5},{5,3},{7,1},{8,14},{10,12},{12... | collective-permute-start | bytes 245768 | tf_op jit(solution)/shard_map/ppermute | solution.py:20
  34.7 9.1 %collective-permute-start.14 = (s16[80,512]{1,0:T(8,128)(2,1)S(1)}, s16[80,512]{1,0:T(8,128)(2,1)S(1)}, u32[]{:S(2)}, u32[]{:S(2)}) collective-permute-start(s16[80,512]{1,0:T(8,128)(2,1)S(1)} %get-tuple-element.94), channel_id=1, source_target_pairs={{0,4},{2,6},{4,0},{6,2},{1,5},{3,7},{5,1},{7,3},{8,12},{10,14},{12... | collective-permute-start | bytes 245768 | tf_op jit(solution)/shard_map/ppermute | solution.py:20
  36.2 7.7 %collective-permute-start.15 = (s16[80,512]{1,0:T(8,128)(2,1)S(1)}, s16[80,512]{1,0:T(8,128)(2,1)S(1)}, u32[]{:S(2)}, u32[]{:S(2)}) collective-permute-start(s16[80,512]{1,0:T(8,128)(2,1)S(1)} %get-tuple-element.95), channel_id=1, source_target_pairs={{0,2},{2,0},{4,6},{6,4},{1,3},{3,1},{5,7},{7,5},{8,10},{10,8},{12,... | collective-permute-start | bytes 245768 | tf_op jit(solution)/shard_map/ppermute | solution.py:20
  38.3 12.7 %collective-permute-start.10 = (s16[80,512]{1,0:T(8,128)(2,1)S(1)}, s16[80,512]{1,0:T(8,128)(2,1)S(1)}, u32[]{:S(2)}, u32[]{:S(2)}) collective-permute-start(s16[80,512]{1,0:T(8,128)(2,1)S(1)} %get-tuple-element.89), channel_id=1, source_target_pairs={{0,6},{2,4},{4,2},{6,0},{1,7},{3,5},{5,3},{7,1},{8,14},{10,12},{12... | collective-permute-start | bytes 245768 | tf_op jit(solution)/shard_map/ppermute | solution.py:20
  40.0 11.0 %collective-permute-start.11 = (s16[80,512]{1,0:T(8,128)(2,1)S(1)}, s16[80,512]{1,0:T(8,128)(2,1)S(1)}, u32[]{:S(2)}, u32[]{:S(2)}) collective-permute-start(s16[80,512]{1,0:T(8,128)(2,1)S(1)} %get-tuple-element.90), channel_id=1, source_target_pairs={{0,4},{2,6},{4,0},{6,2},{1,5},{3,7},{5,1},{7,3},{8,12},{10,14},{12... | collective-permute-start | bytes 245768 | tf_op jit(solution)/shard_map/ppermute | solution.py:20
  41.6 9.4 %collective-permute-start.12 = (s16[80,512]{1,0:T(8,128)(2,1)S(1)}, s16[80,512]{1,0:T(8,128)(2,1)S(1)}, u32[]{:S(2)}, u32[]{:S(2)}) collective-permute-start(s16[80,512]{1,0:T(8,128)(2,1)S(1)} %get-tuple-element.91), channel_id=1, source_target_pairs={{0,2},{2,0},{4,6},{6,4},{1,3},{3,1},{5,7},{7,5},{8,10},{10,8},{12,... | collective-permute-start | bytes 245768 | tf_op jit(solution)/shard_map/ppermute | solution.py:20
  43.9 8.1 %collective-permute-start.21 = (bf16[64,512]{1,0:T(8,128)(2,1)S(1)}, bf16[64,512]{1,0:T(8,128)(2,1)S(1)}, u32[]{:S(2)}, u32[]{:S(2)}) collective-permute-start(bf16[64,512]{1,0:T(8,128)(2,1)S(1)} %get-tuple-element.98.refs_0_), channel_id=1, source_target_pairs={{0,6},{2,4},{4,2},{6,0},{1,7},{3,5},{5,3},{7,1},{8,14},{10,12},{12... | collective-permute-start | bytes 196616 | tf_op jit(solution)/shard_map/ppermute | solution.py:20
  45.5 8.4 %collective-permute-start.20 = (bf16[64,512]{1,0:T(8,128)(2,1)S(1)}, bf16[64,512]{1,0:T(8,128)(2,1)S(1)}, u32[]{:S(2)}, u32[]{:S(2)}) collective-permute-start(bf16[64,512]{1,0:T(8,128)(2,1)S(1)} %get-tuple-element.98.refs_0_), channel_id=1, source_target_pairs={{0,4},{2,6},{4,0},{6,2},{1,5},{3,7},{5,1},{7,3},{8,12},{10,14},{12... | collective-permute-start | bytes 196616 | tf_op jit(solution)/shard_map/ppermute | solution.py:20
  51.0 4.3 %collective-permute-start.19 = (bf16[64,512]{1,0:T(8,128)(2,1)S(1)}, bf16[64,512]{1,0:T(8,128)(2,1)S(1)}, u32[]{:S(2)}, u32[]{:S(2)}) collective-permute-start(bf16[64,512]{1,0:T(8,128)(2,1)S(1)} %get-tuple-element.98.refs_0_), channel_id=1, source_target_pairs={{0,2},{2,0},{4,6},{6,4},{1,3},{3,1},{5,7},{7,5},{8,10},{10,8},{12,... | collective-permute-start | bytes 196616 | tf_op jit(solution)/shard_map/ppermute | solution.py:20
  55.3 12.7 %collective-permute-start.26 = (bf16[256,512]{1,0:T(8,128)(2,1)S(1)}, bf16[256,512]{1,0:T(8,128)(2,1)S(1)}, u32[]{:S(2)}, u32[]{:S(2)}) collective-permute-start(bf16[256,512]{1,0:T(8,128)(2,1)S(1)} %get-tuple-element.104.refs_3_), channel_id=1, source_target_pairs={{0,24},{8,16},{16,8},{24,0},{1,25},{9,17},{17,9},{25,1},{2,26},{10... | collective-permute-start | bytes 786440 | tf_op jit(solution)/shard_map/ppermute | solution.py:20
  57.2 10.8 %collective-permute-start.25 = (bf16[256,512]{1,0:T(8,128)(2,1)S(1)}, bf16[256,512]{1,0:T(8,128)(2,1)S(1)}, u32[]{:S(2)}, u32[]{:S(2)}) collective-permute-start(bf16[256,512]{1,0:T(8,128)(2,1)S(1)} %get-tuple-element.104.refs_3_), channel_id=1, source_target_pairs={{0,8},{8,0},{16,24},{24,16},{1,9},{9,1},{17,25},{25,17},{2,10},{10... | collective-permute-start | bytes 786440 | tf_op jit(solution)/shard_map/ppermute | solution.py:20
  57.3 5.0 %collective-permute-start.18 = (bf16[64,512]{1,0:T(8,128)(2,1)S(1)}, bf16[64,512]{1,0:T(8,128)(2,1)S(1)}, u32[]{:S(2)}, u32[]{:S(2)}) collective-permute-start(bf16[64,512]{1,0:T(8,128)(2,1)S(1)} %get-tuple-element.97.refs_0_), channel_id=1, source_target_pairs={{0,6},{2,4},{4,2},{6,0},{1,7},{3,5},{5,3},{7,1},{8,14},{10,12},{12... | collective-permute-start | bytes 196616 | tf_op jit(solution)/shard_map/ppermute | solution.py:20
  59.3 5.3 %collective-permute-start.17 = (bf16[64,512]{1,0:T(8,128)(2,1)S(1)}, bf16[64,512]{1,0:T(8,128)(2,1)S(1)}, u32[]{:S(2)}, u32[]{:S(2)}) collective-permute-start(bf16[64,512]{1,0:T(8,128)(2,1)S(1)} %get-tuple-element.97.refs_0_), channel_id=1, source_target_pairs={{0,4},{2,6},{4,0},{6,2},{1,5},{3,7},{5,1},{7,3},{8,12},{10,14},{12... | collective-permute-start | bytes 196616 | tf_op jit(solution)/shard_map/ppermute | solution.py:20
  61.1 4.3 %collective-permute-start.16 = (bf16[64,512]{1,0:T(8,128)(2,1)S(1)}, bf16[64,512]{1,0:T(8,128)(2,1)S(1)}, u32[]{:S(2)}, u32[]{:S(2)}) collective-permute-start(bf16[64,512]{1,0:T(8,128)(2,1)S(1)} %get-tuple-element.97.refs_0_), channel_id=1, source_target_pairs={{0,2},{2,0},{4,6},{6,4},{1,3},{3,1},{5,7},{7,5},{8,10},{10,8},{12,... | collective-permute-start | bytes 196616 | tf_op jit(solution)/shard_map/ppermute | solution.py:20
  65.9 8.4 %collective-permute-start.23 = (bf16[256,512]{1,0:T(8,128)(2,1)S(1)}, bf16[256,512]{1,0:T(8,128)(2,1)S(1)}, u32[]{:S(2)}, u32[]{:S(2)}) collective-permute-start(bf16[256,512]{1,0:T(8,128)(2,1)S(1)} %get-tuple-element.101.refs_4_), channel_id=1, source_target_pairs={{0,24},{8,16},{16,8},{24,0},{1,25},{9,17},{17,9},{25,1},{2,26},{10... | collective-permute-start | bytes 786440 | tf_op jit(solution)/shard_map/ppermute | solution.py:20
  67.2 7.2 %collective-permute-start.22 = (bf16[256,512]{1,0:T(8,128)(2,1)S(1)}, bf16[256,512]{1,0:T(8,128)(2,1)S(1)}, u32[]{:S(2)}, u32[]{:S(2)}) collective-permute-start(bf16[256,512]{1,0:T(8,128)(2,1)S(1)} %get-tuple-element.101.refs_4_), channel_id=1, source_target_pairs={{0,8},{8,0},{16,24},{24,16},{1,9},{9,1},{17,25},{25,17},{2,10},{10... | collective-permute-start | bytes 786440 | tf_op jit(solution)/shard_map/ppermute | solution.py:20
  68.0 11.0 %collective-permute-start.27 = (bf16[256,512]{1,0:T(8,128)(2,1)S(1)}, bf16[256,512]{1,0:T(8,128)(2,1)S(1)}, u32[]{:S(2)}, u32[]{:S(2)}) collective-permute-start(bf16[256,512]{1,0:T(8,128)(2,1)S(1)} %collective-permute-done.26.refs_4_), channel_id=1, source_target_pairs={{0,8},{8,0},{16,24},{24,16},{1,9},{9,1},{17,25},{25,17},{2,10},{10... | collective-permute-start | bytes 786440 | tf_op jit(solution)/shard_map/ppermute | solution.py:20
  74.4 7.6 %collective-permute-start.24 = (bf16[256,512]{1,0:T(8,128)(2,1)S(1)}, bf16[256,512]{1,0:T(8,128)(2,1)S(1)}, u32[]{:S(2)}, u32[]{:S(2)}) collective-permute-start(bf16[256,512]{1,0:T(8,128)(2,1)S(1)} %collective-permute-done.22.refs_3_), channel_id=1, source_target_pairs={{0,24},{8,16},{16,8},{24,0},{1,25},{9,17},{17,9},{25,1},{2,26},{10... | collective-permute-start | bytes 786440 | tf_op jit(solution)/shard_map/ppermute | solution.py:20
  83.0 2.7 %collective-permute-start.28 = (f32[512,512]{1,0:T(8,128)S(1)}, f32[512,512]{1,0:T(8,128)S(1)}, u32[]{:S(2)}, u32[]{:S(2)}) collective-permute-start(f32[512,512]{1,0:T(8,128)S(1)} %get-tuple-element.114), channel_id=1, source_target_pairs={{0,1},{1,0},{2,3},{3,2},{4,5},{5,4},{6,7},{7,6},{8,9},{9,8},{10,11... | collective-permute-start | bytes 3145736 | tf_op jit(solution)/shard_map/ppermute | solution.py:20
  86.5 7.5 %collective-permute-start.29 = (s16[144,512]{1,0:T(8,128)(2,1)S(1)}, s16[144,512]{1,0:T(8,128)(2,1)S(1)}, u32[]{:S(2)}, u32[]{:S(2)}) collective-permute-start(s16[144,512]{1,0:T(8,128)(2,1)S(1)} %get-tuple-element.116), channel_id=1, source_target_pairs={{0,128},{32,160},{64,192},{96,224},{128,0},{160,32},{192,64},{224,... | collective-permute-start | bytes 442376 | tf_op jit(solution)/shard_map/ppermute | solution.py:20
  89.8 7.4 %collective-permute-start.30 = (s16[144,512]{1,0:T(8,128)(2,1)S(1)}, s16[144,512]{1,0:T(8,128)(2,1)S(1)}, u32[]{:S(2)}, u32[]{:S(2)}) collective-permute-start(s16[144,512]{1,0:T(8,128)(2,1)S(1)} %get-tuple-element.117), channel_id=1, source_target_pairs={{0,192},{32,224},{64,128},{96,160},{128,64},{160,96},{192,0},{224,... | collective-permute-start | bytes 442376 | tf_op jit(solution)/shard_map/ppermute | solution.py:20
  90.9 6.7 %collective-permute-start.31 = (s16[144,512]{1,0:T(8,128)(2,1)S(1)}, s16[144,512]{1,0:T(8,128)(2,1)S(1)}, u32[]{:S(2)}, u32[]{:S(2)}) collective-permute-start(s16[144,512]{1,0:T(8,128)(2,1)S(1)} %get-tuple-element.118), channel_id=1, source_target_pairs={{0,64},{32,96},{64,0},{96,32},{128,192},{160,224},{192,128},{224,1... | collective-permute-start | bytes 442376 | tf_op jit(solution)/shard_map/ppermute | solution.py:20
  98.3 11.8 %collective-permute-start.32 = (s16[80,512]{1,0:T(8,128)(2,1)S(1)}, s16[80,512]{1,0:T(8,128)(2,1)S(1)}, u32[]{:S(2)}, u32[]{:S(2)}) collective-permute-start(s16[80,512]{1,0:T(8,128)(2,1)S(1)} %get-tuple-element.120), channel_id=1, source_target_pairs={{0,32},{32,0},{64,96},{96,64},{128,160},{160,128},{192,224},{224,1... | collective-permute-start | bytes 245768 | tf_op jit(solution)/shard_map/ppermute | solution.py:20

commit v7 on v6

--- a/solution.py
+++ b/solution.py
@@ -10,7 +10,7 @@
 F32, BF16, I16 = jnp.float32, jnp.bfloat16, jnp.int16
 TAIL = 16
 Z_ORDER, Y_ORDER = (3, 2, 1), (2, 3, 1)
-VMEM_LIMIT, VMEM_LARGE = 24 * 1024 * 1024, 46 * 1024 * 1024
+VMEM_LIMIT, VMEM_LARGE = 24 * 1024 * 1024, 40 * 1024 * 1024
 SMEM, VMEM = pl.BlockSpec(memory_space=pltpu.SMEM), pl.BlockSpec(memory_space=pltpu.VMEM)
 ANY = pl.BlockSpec(memory_space=pl.ANY)
 
@@ -47,31 +47,25 @@
 KEPT = ((0, 0), (3, 0), (0, 1), (1, 1))
 
 
-def products(here_ref, a_ref, b_ref, out_refs, held, sems, parts):
+def fetch(here_ref, a_ref, held, sems, first, parts):
     order = SENT + KEPT
-    per = len(order)
-    rows = held.shape[0] // (len(parts) * per)
+    rows = held.shape[0] // (len(parts) * len(order))
     copies = []
     for own, stream in parts:
         base = (here_ref[2] if own else 1 - here_ref[2]) * 16 + stream * 2
         for owner, part in order:
             start = (base + lax.bitwise_xor(here_ref[0], owner) * 4 + part) * rows
             to = held.at[pl.ds(rows * len(copies), rows), :]
-            copies.append(
-                pltpu.make_async_copy(a_ref.at[pl.ds(pl.multiple_of(start, rows), rows), :], to, sems.at[len(copies)])
-            )
+            block = a_ref.at[pl.ds(pl.multiple_of(start, rows), rows), :]
+            copies.append(pltpu.make_async_copy(block, to, sems.at[first + len(copies)]))
     for copy in copies:
         copy.start()
-    for o, out_ref in enumerate(out_refs):
-        for copy in copies[o * per : (o + 1) * per]:
-            copy.wait()
-        here = held[o * per * rows : (o + 1) * per * rows, :]
-        out_ref[: per * rows, :] = jnp.dot(here, b_ref[...], preferred_element_type=F32)
-
-
-def product_scratch(pair_elements, parts):
-    rows, depth = pair_elements.shape
-    return [pltpu.VMEM((rows // 4 * parts, depth), BF16), pltpu.SemaphoreType.DMA((8 * parts,))]
+    return copies
+
+
+def multiply(a_ref, b_ref, out_ref, at):
+    rows = a_ref.shape[0] // 3
+    out_ref[...] = jnp.dot(a_ref[at * rows : (at + 1) * rows, :], b_ref[...], preferred_element_type=F32)
 
 
 def pack(ref, value):
@@ -166,7 +160,7 @@
         out_ref[...] = 2.0 * spacing / (spacing * spacing + freq * freq)
 
 
-def gram_step(here, weights, pieces, places, grams, after=()):
+def gram_step(here, weights, pieces, places, grams, extra=0):
     width = pieces[0].shape[1]
     count, kinds = len(pieces), len(weights)
 
@@ -194,9 +188,8 @@
         *weights,
         *pieces,
         *grams,
-        cost=2 * kinds * width * width * sum(p.shape[0] for p in pieces),
+        cost=2 * kinds * width * width * sum(p.shape[0] for p in pieces) + extra,
         specs=[SMEM] + [VMEM] * (kinds + count + len(grams)),
-        after=after,
     )
 
 
@@ -208,30 +201,45 @@
     sums = lambda count: ((count, width), F32)
     both = range(2)
 
-    def product_call(body, outs, *args, after=(), flag=False, parts=1):
-        specs = [SMEM] * (len(args) + 1) + [ANY, VMEM]
-        scratch, cost = product_scratch(pair_elements, parts), 2 * parts * 16 * unit * pair_elements.shape[1] * width
-        arrays = (here, *args, pair_elements, subspace)
-        return call(body, outs, *arrays, specs=specs, after=after, flag=flag, cost=cost, scratch=scratch, limit=VMEM_LARGE)
-
-    def first_other(here_ref, freq_ref, a_ref, b_ref, out_ref, held, sems):
+    def first_other(here_ref, freq_ref, a_ref, b_ref, out_ref, held_ref, work_ref, sems):
+        now = fetch(here_ref, a_ref, work_ref, sems, 0, [(False, 0)])
+        later = fetch(here_ref, a_ref, held_ref, sems, 8, [(True, 0), (False, 1), (True, 1)])
         out_ref[16 * unit :, :] = jnp.full((8, width), freq_ref[0], F32)
-        products(here_ref, a_ref, b_ref, (out_ref,), held, sems, [(False, 0)])
-
-    def first_own(here_ref, a_ref, b_ref, own_ref, other_ref, held, sems):
-        products(here_ref, a_ref, b_ref, (own_ref, other_ref), held, sems, [(True, 0), (False, 1)])
-
-    def second_own(here_ref, a_ref, b_ref, own_ref, held, sems):
-        products(here_ref, a_ref, b_ref, (own_ref,), held, sems, [(True, 1)])
+        for copy in now:
+            copy.wait()
+        out_ref[: 16 * unit, :] = jnp.dot(work_ref[...], b_ref[...], preferred_element_type=F32)
+        for copy in later:
+            copy.wait()
+
+    def first_own(a_ref, b_ref, own_ref, other_ref):
+        multiply(a_ref, b_ref, own_ref, 0)
+        multiply(a_ref, b_ref, other_ref, 1)
+
+    def second_own(a_ref, b_ref, own_ref):
+        multiply(a_ref, b_ref, own_ref, 2)
 
     kept, a, b = [None] * 2, [None] * 2, [None] * 2
     first = [sums(8 * unit)] + [message(4 * unit)] * 2
-    other, done = product_call(first_other, [sums(16 * unit + 8)], frequencies, flag=True)
+    depth = pair_elements.shape[1]
+    cost = 2 * 16 * unit * depth * width
+    other, held, done = call(
+        first_other,
+        [sums(16 * unit + 8), ((48 * unit, depth), BF16)],
+        here,
+        frequencies,
+        pair_elements,
+        subspace,
+        specs=[SMEM, SMEM, ANY, VMEM],
+        flag=True,
+        cost=cost,
+        scratch=[pltpu.VMEM((16 * unit, depth), BF16), pltpu.SemaphoreType.DMA((32,))],
+        limit=VMEM_LARGE,
+    )
     other_in = xor_permute(other, "pw_c", 1)
-    own, other = product_call(first_own, [sums(16 * unit)] * 2, after=[done], parts=2)
+    own, other = call(first_own, [sums(16 * unit)] * 2, held, subspace, after=[done], cost=2 * cost)
     other, other_in = lax.optimization_barrier((other, other_in))
     kept[0], a[0], b[0], done = call(first_messages, first, own, other_in, flag=True)
-    own = product_call(second_own, [sums(16 * unit)], after=[done])[0]
+    own = call(second_own, [sums(16 * unit)], held, subspace, after=[done], cost=cost)[0]
     kept[1], a[1], b[1] = call(first_messages, first, own, xor_permute(other, "pw_c", 1))
 
     last = None
@@ -282,8 +290,9 @@
         quarters[s], last = call(join, [((4 * unit, width), BF16)], *pieces[s], after=[last], flag=True)
         near[s], far[s] = xor_permute(quarters[s], "pw_x", 1), xor_permute(quarters[s], "pw_x", 3)
         near[s], far[s] = lax.optimization_barrier((near[s], far[s]))
+    grams = gram_step(here, weights, quarters, [(0, 0), (1, 0)], [], 3_000_000_000)
+    near[0], far[0], grams = lax.optimization_barrier((near[0], far[0], grams))
     across = [xor_permute(far[0], "pw_x", 1), xor_permute(near[1], "pw_x", 3)]
-    grams = gram_step(here, weights, quarters, [(0, 0), (1, 0)], [])
     grams = gram_step(here, weights, [near[0], far[0]], [(0, 1), (0, 3)], grams)
     grams = gram_step(here, weights, [near[1], far[1], across[0]], [(1, 1), (1, 3), (0, 2)], grams)
     mine, theirs = gram_step(here, weights, [across[1]], [(1, 2)], grams)

time: 111 us -> 108 us (0.973)
  waiting for transfers between devices: 34.6 us -> 43 us
  starting transfers between devices: 50.7 us -> 43 us
  Pallas kernels: 23.2 us -> 19.5 us
    ppermute x33, waiting for transfers between devices: 34.6 us -> 43 us  [xor_permute(): return lax.ppermute(value, axis, [(i, i ^ mask) for i in range(count)])]
    ppermute x33, starting transfers between devices: 50.7 us -> 43 us  [xor_permute(): return lax.ppermute(value, axis, [(i, i ^ mask) for i in range(count)])]
    pallas_call x21, Pallas kernels: 23.2 us -> 19.5 us  [call(): pl.pallas_call(kernel, out_shape=[jax.ShapeDtypeStruct(shape, dtype) for...]
  transfers between devices with their start and end apart: 33 -> 33, of which waited for: 17 -> 22; matrix products, arithmetic and copies ran while one was open for 0% -> 0% of each run, Pallas kernels for 15% -> 11%
where the time goes in v7:
time: 108 us
  starting transfers between devices  43 us (40%)
  waiting for transfers between devices  43 us (40%)
  Pallas kernels  19.5 us (18%)
  local copies, waits for them, and re-layouts  1.24 us (1%)
    ppermute x33, waiting for transfers between devices, xor_permute(): return lax.ppermute(value, axis, [(i, i ^ mask) for i in range(count)])  43 us
    ppermute x33, starting transfers between devices, xor_permute(): return lax.ppermute(value, axis, [(i, i ^ mask) for i in range(count)])  43 us
    pallas_call x21, Pallas kernels, call(): pl.pallas_call(kernel, out_shape=[jax.ShapeDtypeStruct(shape, dtype) for...  19.5 us
  transfers between devices with their start and end apart: 33, of which 22 were waited for; matrix products, arithmetic and copies ran while one was open for 0% of the time, Pallas kernels for 11%

profile of v7, /device:TPU:32, one launch (start us, length us, event | category | flops | bytes accessed | tf_op | source)
XLA Modules:
  0.0 107.6 jit_solution(4573530898739121705)
XLA Ops:
  0.7 1.2 %copy-done = bf16[1024,512]{1,0:T(8,128)(2,1)S(1)} copy-done((bf16[1024,512]{1,0:T(8,128)(2,1)S(1)}, bf16[1024,512]{1,0:T(8,128)(2,1)}, u32[]{:S(2)}) %copy-start) | copy-done | bytes 1048600
  2.0 4.2 %shard_map.73 = (f32[1032,512]{1,0:T(8,128)S(1)}, bf16[3072,1024]{1,0:T(8,128)(2,1)S(1)}, f32[8,128]{1,0:T(8,128)S(1)}) custom-call(s32[4]{0:T(128)S(1)} %pad_add_fusion.refs_0_, f32[1]{0:T(128)S(6)} %copy.8.refs_1_.refs_2_, bf16[4096,1024]{1,0:T(8,128)(2,1)} %refs_2_.2, bf16[1024,512]{1,0:T(8,128)(2,1)S(1)} %copy-done), custom_call_target="tpu_custom_call" | custom-call | flops 1073741824 | bytes 9437204 | tf_op jit(solution)/shard_map/pallas_call | solution.py:35
  6.3 2.3 %shard_map.74 = (f32[1024,512]{1,0:T(8,128)S(1)}, f32[1024,512]{1,0:T(8,128)S(1)}) custom-call(bf16[3072,1024]{1,0:T(8,128)(2,1)S(1)} %get-tuple-element.68.refs_0_, bf16[1024,512]{1,0:T(8,128)(2,1)S(1)} %copy-done, f32[8,128]{1,0:T(8,128)S(1)} %get-tuple-element.69.refs_2_), custom_call_target="tpu_custom_call" | custom-call | flops 2147483648 | bytes 7340032 | tf_op jit(solution)/shard_map/pallas_call | solution.py:35
  8.6 1.8 %collective-permute-done.refs_1_ = f32[1032,512]{1,0:T(8,128)S(1)} collective-permute-done((f32[1032,512]{1,0:T(8,128)S(1)}, f32[1032,512]{1,0:T(8,128)S(1)}, u32[]{:S(2)}, u32[]{:S(2)}) %collective-permute-start) | collective-permute-done | bytes 2113568 | tf_op jit(solution)/shard_map/ppermute | solution.py:20
  10.9 1.6 %collective-permute-start.4 = (s16[272,512]{1,0:T(8,128)(2,1)S(1)}, s16[272,512]{1,0:T(8,128)(2,1)S(1)}, u32[]{:S(2)}, u32[]{:S(2)}) collective-permute-start(s16[272,512]{1,0:T(8,128)(2,1)S(1)} %get-tuple-element.80), channel_id=1, source_target_pairs={{0,8},{8,0},{16,24},{24,16},{1,9},{9,1},{17,25},{25,17},{2,10},{10... | collective-permute-start | bytes 835592 | tf_op jit(solution)/shard_map/ppermute | solution.py:20
  12.5 2.1 %collective-permute-start.5 = (s16[272,512]{1,0:T(8,128)(2,1)S(1)}, s16[272,512]{1,0:T(8,128)(2,1)S(1)}, u32[]{:S(2)}, u32[]{:S(2)}) collective-permute-start(s16[272,512]{1,0:T(8,128)(2,1)S(1)} %get-tuple-element.81), channel_id=1, source_target_pairs={{0,24},{8,16},{16,8},{24,0},{1,25},{9,17},{17,9},{25,1},{2,26},{10... | collective-permute-start | bytes 835592 | tf_op jit(solution)/shard_map/ppermute | solution.py:20
  14.6 1.2 %shard_map.76.refs_0_ = f32[1024,512]{1,0:T(8,128)S(1)} custom-call(bf16[3072,1024]{1,0:T(8,128)(2,1)S(1)} %get-tuple-element.68.refs_0_, bf16[1024,512]{1,0:T(8,128)(2,1)S(1)} %copy-done, f32[8,128]{1,0:T(8,128)S(1)} %get-tuple-element.74.refs_2_), custom_call_target="tpu_custom_call" | custom-call | flops 1073741824 | bytes 7340032 | tf_op jit(solution)/shard_map/pallas_call | solution.py:35
  16.9 1.7 %collective-permute-start.3 = (s16[272,512]{1,0:T(8,128)(2,1)S(1)}, s16[272,512]{1,0:T(8,128)(2,1)S(1)}, u32[]{:S(2)}, u32[]{:S(2)}) collective-permute-start(s16[272,512]{1,0:T(8,128)(2,1)S(1)} %get-tuple-element.78), channel_id=1, source_target_pairs={{0,24},{8,16},{16,8},{24,0},{1,25},{9,17},{17,9},{25,1},{2,26},{10... | collective-permute-start | bytes 835592 | tf_op jit(solution)/shard_map/ppermute | solution.py:20
  18.6 1.9 %collective-permute-done.4.refs_1_ = s16[272,512]{1,0:T(8,128)(2,1)S(1)} collective-permute-done((s16[272,512]{1,0:T(8,128)(2,1)S(1)}, s16[272,512]{1,0:T(8,128)(2,1)S(1)}, u32[]{:S(2)}, u32[]{:S(2)}) %collective-permute-start.4) | collective-permute-done | bytes 278560 | tf_op jit(solution)/shard_map/ppermute | solution.py:20
  20.5 2.7 %collective-permute-done.5.refs_2_ = s16[272,512]{1,0:T(8,128)(2,1)S(1)} collective-permute-done((s16[272,512]{1,0:T(8,128)(2,1)S(1)}, s16[272,512]{1,0:T(8,128)(2,1)S(1)}, u32[]{:S(2)}, u32[]{:S(2)}) %collective-permute-start.5) | collective-permute-done | bytes 278560 | tf_op jit(solution)/shard_map/ppermute | solution.py:20
  23.5 2.2 %collective-permute-start.8 = (s16[144,512]{1,0:T(8,128)(2,1)S(1)}, s16[144,512]{1,0:T(8,128)(2,1)S(1)}, u32[]{:S(2)}, u32[]{:S(2)}) collective-permute-start(s16[144,512]{1,0:T(8,128)(2,1)S(1)} %get-tuple-element.87), channel_id=1, source_target_pairs={{0,24},{8,16},{16,8},{24,0},{1,25},{9,17},{17,9},{25,1},{2,26},{10... | collective-permute-start | bytes 442376 | tf_op jit(solution)/shard_map/ppermute | solution.py:20
  25.9 3.3 %collective-permute-done.3.refs_2_ = s16[272,512]{1,0:T(8,128)(2,1)S(1)} collective-permute-done((s16[272,512]{1,0:T(8,128)(2,1)S(1)}, s16[272,512]{1,0:T(8,128)(2,1)S(1)}, u32[]{:S(2)}, u32[]{:S(2)}) %collective-permute-start.3) | collective-permute-done | bytes 278560 | tf_op jit(solution)/shard_map/ppermute | solution.py:20
  29.5 2.2 %collective-permute-start.6 = (s16[144,512]{1,0:T(8,128)(2,1)S(1)}, s16[144,512]{1,0:T(8,128)(2,1)S(1)}, u32[]{:S(2)}, u32[]{:S(2)}) collective-permute-start(s16[144,512]{1,0:T(8,128)(2,1)S(1)} %get-tuple-element.84), channel_id=1, source_target_pairs={{0,24},{8,16},{16,8},{24,0},{1,25},{9,17},{17,9},{25,1},{2,26},{10... | collective-permute-start | bytes 442376 | tf_op jit(solution)/shard_map/ppermute | solution.py:20
  31.6 0.7 shard_map.80
  32.4 2.0 %collective-permute-start.13 = (s16[80,512]{1,0:T(8,128)(2,1)S(1)}, s16[80,512]{1,0:T(8,128)(2,1)S(1)}, u32[]{:S(2)}, u32[]{:S(2)}) collective-permute-start(s16[80,512]{1,0:T(8,128)(2,1)S(1)} %get-tuple-element.99), channel_id=1, source_target_pairs={{0,6},{2,4},{4,2},{6,0},{1,7},{3,5},{5,3},{7,1},{8,14},{10,12},{12... | collective-permute-start | bytes 245768 | tf_op jit(solution)/shard_map/ppermute | solution.py:20
  34.4 1.5 %collective-permute-start.14 = (s16[80,512]{1,0:T(8,128)(2,1)S(1)}, s16[80,512]{1,0:T(8,128)(2,1)S(1)}, u32[]{:S(2)}, u32[]{:S(2)}) collective-permute-start(s16[80,512]{1,0:T(8,128)(2,1)S(1)} %get-tuple-element.100), channel_id=1, source_target_pairs={{0,4},{2,6},{4,0},{6,2},{1,5},{3,7},{5,1},{7,3},{8,12},{10,14},{12... | collective-permute-start | bytes 245768 | tf_op jit(solution)/shard_map/ppermute | solution.py:20
  35.9 1.4 %collective-permute-start.15 = (s16[80,512]{1,0:T(8,128)(2,1)S(1)}, s16[80,512]{1,0:T(8,128)(2,1)S(1)}, u32[]{:S(2)}, u32[]{:S(2)}) collective-permute-start(s16[80,512]{1,0:T(8,128)(2,1)S(1)} %get-tuple-element.101), channel_id=1, source_target_pairs={{0,2},{2,0},{4,6},{6,4},{1,3},{3,1},{5,7},{7,5},{8,10},{10,8},{12,... | collective-permute-start | bytes 245768 | tf_op jit(solution)/shard_map/ppermute | solution.py:20
  37.2 0.7 shard_map.81
  38.0 1.7 %collective-permute-start.10 = (s16[80,512]{1,0:T(8,128)(2,1)S(1)}, s16[80,512]{1,0:T(8,128)(2,1)S(1)}, u32[]{:S(2)}, u32[]{:S(2)}) collective-permute-start(s16[80,512]{1,0:T(8,128)(2,1)S(1)} %get-tuple-element.95), channel_id=1, source_target_pairs={{0,6},{2,4},{4,2},{6,0},{1,7},{3,5},{5,3},{7,1},{8,14},{10,12},{12... | collective-permute-start | bytes 245768 | tf_op jit(solution)/shard_map/ppermute | solution.py:20
  39.7 1.6 %collective-permute-start.11 = (s16[80,512]{1,0:T(8,128)(2,1)S(1)}, s16[80,512]{1,0:T(8,128)(2,1)S(1)}, u32[]{:S(2)}, u32[]{:S(2)}) collective-permute-start(s16[80,512]{1,0:T(8,128)(2,1)S(1)} %get-tuple-element.96), channel_id=1, source_target_pairs={{0,4},{2,6},{4,0},{6,2},{1,5},{3,7},{5,1},{7,3},{8,12},{10,14},{12... | collective-permute-start | bytes 245768 | tf_op jit(solution)/shard_map/ppermute | solution.py:20
  42.7 0.9 shard_map.82
  43.5 2.7 %collective-permute-done.14.refs_2_ = s16[80,512]{1,0:T(8,128)(2,1)S(1)} collective-permute-done((s16[80,512]{1,0:T(8,128)(2,1)S(1)}, s16[80,512]{1,0:T(8,128)(2,1)S(1)}, u32[]{:S(2)}, u32[]{:S(2)}) %collective-permute-start.14) | collective-permute-done | bytes 81952 | tf_op jit(solution)/shard_map/ppermute | solution.py:20
  46.4 4.0 %collective-permute-start.20 = (bf16[64,512]{1,0:T(8,128)(2,1)S(1)}, bf16[64,512]{1,0:T(8,128)(2,1)S(1)}, u32[]{:S(2)}, u32[]{:S(2)}) collective-permute-start(bf16[64,512]{1,0:T(8,128)(2,1)S(1)} %get-tuple-element.104.refs_0_), channel_id=1, source_target_pairs={{0,4},{2,6},{4,0},{6,2},{1,5},{3,7},{5,1},{7,3},{8,12},{10,14},{12... | collective-permute-start | bytes 196616 | tf_op jit(solution)/shard_map/ppermute | solution.py:20
  50.4 1.4 %collective-permute-start.19 = (bf16[64,512]{1,0:T(8,128)(2,1)S(1)}, bf16[64,512]{1,0:T(8,128)(2,1)S(1)}, u32[]{:S(2)}, u32[]{:S(2)}) collective-permute-start(bf16[64,512]{1,0:T(8,128)(2,1)S(1)} %get-tuple-element.104.refs_0_), channel_id=1, source_target_pairs={{0,2},{2,0},{4,6},{6,4},{1,3},{3,1},{5,7},{7,5},{8,10},{10,8},{12,... | collective-permute-start | bytes 196616 | tf_op jit(solution)/shard_map/ppermute | solution.py:20
  51.9 1.6 %collective-permute-start.18 = (bf16[64,512]{1,0:T(8,128)(2,1)S(1)}, bf16[64,512]{1,0:T(8,128)(2,1)S(1)}, u32[]{:S(2)}, u32[]{:S(2)}) collective-permute-start(bf16[64,512]{1,0:T(8,128)(2,1)S(1)} %get-tuple-element.103.refs_0_), channel_id=1, source_target_pairs={{0,6},{2,4},{4,2},{6,0},{1,7},{3,5},{5,3},{7,1},{8,14},{10,12},{12... | collective-permute-start | bytes 196616 | tf_op jit(solution)/shard_map/ppermute | solution.py:20
  53.4 1.5 %collective-permute-start.17 = (bf16[64,512]{1,0:T(8,128)(2,1)S(1)}, bf16[64,512]{1,0:T(8,128)(2,1)S(1)}, u32[]{:S(2)}, u32[]{:S(2)}) collective-permute-start(bf16[64,512]{1,0:T(8,128)(2,1)S(1)} %get-tuple-element.103.refs_0_), channel_id=1, source_target_pairs={{0,4},{2,6},{4,0},{6,2},{1,5},{3,7},{5,1},{7,3},{8,12},{10,14},{12... | collective-permute-start | bytes 196616 | tf_op jit(solution)/shard_map/ppermute | solution.py:20
  55.0 1.4 %collective-permute-start.16 = (bf16[64,512]{1,0:T(8,128)(2,1)S(1)}, bf16[64,512]{1,0:T(8,128)(2,1)S(1)}, u32[]{:S(2)}, u32[]{:S(2)}) collective-permute-start(bf16[64,512]{1,0:T(8,128)(2,1)S(1)} %get-tuple-element.103.refs_0_), channel_id=1, source_target_pairs={{0,2},{2,0},{4,6},{6,4},{1,3},{3,1},{5,7},{7,5},{8,10},{10,8},{12,... | collective-permute-start | bytes 196616 | tf_op jit(solution)/shard_map/ppermute | solution.py:20
  56.5 0.7 collective-permute-done.19.refs_1_
  57.2 1.7 %collective-permute-start.26 = (bf16[256,512]{1,0:T(8,128)(2,1)S(1)}, bf16[256,512]{1,0:T(8,128)(2,1)S(1)}, u32[]{:S(2)}, u32[]{:S(2)}) collective-permute-start(bf16[256,512]{1,0:T(8,128)(2,1)S(1)} %get-tuple-element.110.refs_3_), channel_id=1, source_target_pairs={{0,24},{8,16},{16,8},{24,0},{1,25},{9,17},{17,9},{25,1},{2,26},{10... | collective-permute-start | bytes 786440 | tf_op jit(solution)/shard_map/ppermute | solution.py:20
  60.6 1.9 %collective-permute-start.23 = (bf16[256,512]{1,0:T(8,128)(2,1)S(1)}, bf16[256,512]{1,0:T(8,128)(2,1)S(1)}, u32[]{:S(2)}, u32[]{:S(2)}) collective-permute-start(bf16[256,512]{1,0:T(8,128)(2,1)S(1)} %get-tuple-element.107.refs_4_), channel_id=1, source_target_pairs={{0,24},{8,16},{16,8},{24,0},{1,25},{9,17},{17,9},{25,1},{2,26},{10... | collective-permute-start | bytes 786440 | tf_op jit(solution)/shard_map/ppermute | solution.py:20
  63.0 1.3 %shard_map.87 = (f32[512,512]{1,0:T(8,128)S(1)}, f32[512,512]{1,0:T(8,128)S(1)}) custom-call(s32[4]{0:T(128)S(1)} %pad_add_fusion.refs_0_, f32[32,128]{1,0:T(8,128)S(1)} %get-tuple-element.92.refs_4_.refs_1_, f32[32,128]{1,0:T(8,128)S(1)} %get-tuple-element.93.refs_2_, bf16[256,512]{1,0:T(8,128)(2,1)S(1)} %get-tuple-element.110.refs_3_, ...), custom_call_target="tpu_custom_call" | custom-call | flops 3536870912 | bytes 557072 | tf_op jit(solution)/shard_map/pallas_call | solution.py:35
  64.3 3.4 %collective-permute-done.26.refs_4_ = bf16[256,512]{1,0:T(8,128)(2,1)S(1)} collective-permute-done((bf16[256,512]{1,0:T(8,128)(2,1)S(1)}, bf16[256,512]{1,0:T(8,128)(2,1)S(1)}, u32[]{:S(2)}, u32[]{:S(2)}) %collective-permute-start.26) | collective-permute-done | bytes 262176 | tf_op jit(solution)/shard_map/ppermute | solution.py:20
  68.1 2.4 %collective-permute-done.23.refs_4_ = bf16[256,512]{1,0:T(8,128)(2,1)S(1)} collective-permute-done((bf16[256,512]{1,0:T(8,128)(2,1)S(1)}, bf16[256,512]{1,0:T(8,128)(2,1)S(1)}, u32[]{:S(2)}, u32[]{:S(2)}) %collective-permute-start.23) | collective-permute-done | bytes 262176 | tf_op jit(solution)/shard_map/ppermute | solution.py:20
  70.5 3.2 %collective-permute-done.22.refs_3_ = bf16[256,512]{1,0:T(8,128)(2,1)S(1)} collective-permute-done((bf16[256,512]{1,0:T(8,128)(2,1)S(1)}, bf16[256,512]{1,0:T(8,128)(2,1)S(1)}, u32[]{:S(2)}, u32[]{:S(2)}) %collective-permute-start.22) | collective-permute-done | bytes 262176 | tf_op jit(solution)/shard_map/ppermute | solution.py:20
  73.8 1.3 %collective-permute-start.24 = (bf16[256,512]{1,0:T(8,128)(2,1)S(1)}, bf16[256,512]{1,0:T(8,128)(2,1)S(1)}, u32[]{:S(2)}, u32[]{:S(2)}) collective-permute-start(bf16[256,512]{1,0:T(8,128)(2,1)S(1)} %collective-permute-done.22.refs_3_), channel_id=1, source_target_pairs={{0,24},{8,16},{16,8},{24,0},{1,25},{9,17},{17,9},{25,1},{2,26},{10... | collective-permute-start | bytes 786440 | tf_op jit(solution)/shard_map/ppermute | solution.py:20
  75.1 1.3 %shard_map.88 = (f32[512,512]{1,0:T(8,128)S(1)}, f32[512,512]{1,0:T(8,128)S(1)}) custom-call(s32[4]{0:T(128)S(1)} %pad_add_fusion.refs_0_, f32[32,128]{1,0:T(8,128)S(1)} %get-tuple-element.92.refs_4_.refs_1_, f32[32,128]{1,0:T(8,128)S(1)} %get-tuple-element.93.refs_2_, bf16[256,512]{1,0:T(8,128)(2,1)S(1)} %collective-permute-done.25.refs_3_, ...), custom_call_target="tpu_custom_call" | custom-call | flops 536870912 | bytes 2654224 | tf_op jit(solution)/shard_map/pallas_call | solution.py:35
  76.6 1.6 %shard_map.89 = (f32[512,512]{1,0:T(8,128)S(1)}, f32[512,512]{1,0:T(8,128)S(1)}) custom-call(s32[4]{0:T(128)S(1)} %pad_add_fusion.refs_0_, f32[32,128]{1,0:T(8,128)S(1)} %get-tuple-element.92.refs_4_.refs_1_, f32[32,128]{1,0:T(8,128)S(1)} %get-tuple-element.93.refs_2_, bf16[256,512]{1,0:T(8,128)(2,1)S(1)} %collective-permute-done.22.refs_3_, ...), custom_call_target="tpu_custom_call" | custom-call | flops 805306368 | bytes 2916368 | tf_op jit(solution)/shard_map/pallas_call | solution.py:35
  78.2 3.2 %collective-permute-done.24.refs_3_ = bf16[256,512]{1,0:T(8,128)(2,1)S(1)} collective-permute-done((bf16[256,512]{1,0:T(8,128)(2,1)S(1)}, bf16[256,512]{1,0:T(8,128)(2,1)S(1)}, u32[]{:S(2)}, u32[]{:S(2)}) %collective-permute-start.24) | collective-permute-done | bytes 262176 | tf_op jit(solution)/shard_map/ppermute | solution.py:20
  81.3 1.0 shard_map.90
  82.5 2.6 %collective-permute-done.28.refs_2_ = f32[512,512]{1,0:T(8,128)S(1)} collective-permute-done((f32[512,512]{1,0:T(8,128)S(1)}, f32[512,512]{1,0:T(8,128)S(1)}, u32[]{:S(2)}, u32[]{:S(2)}) %collective-permute-start.28) | collective-permute-done | bytes 1048608 | tf_op jit(solution)/shard_map/ppermute | solution.py:20
  85.1 0.8 shard_map.91
  85.9 3.3 %collective-permute-start.29 = (s16[144,512]{1,0:T(8,128)(2,1)S(1)}, s16[144,512]{1,0:T(8,128)(2,1)S(1)}, u32[]{:S(2)}, u32[]{:S(2)}) collective-permute-start(s16[144,512]{1,0:T(8,128)(2,1)S(1)} %get-tuple-element.126), channel_id=1, source_target_pairs={{0,128},{32,160},{64,192},{96,224},{128,0},{160,32},{192,64},{224,... | collective-permute-start | bytes 442376 | tf_op jit(solution)/shard_map/ppermute | solution.py:20
  89.2 1.1 collective-permute-start.30
  90.3 3.2 %collective-permute-done.29.refs_2_ = s16[144,512]{1,0:T(8,128)(2,1)S(1)} collective-permute-done((s16[144,512]{1,0:T(8,128)(2,1)S(1)}, s16[144,512]{1,0:T(8,128)(2,1)S(1)}, u32[]{:S(2)}, u32[]{:S(2)}) %collective-permute-start.29) | collective-permute-done | bytes 147488 | tf_op jit(solution)/shard_map/ppermute | solution.py:20
  93.5 3.1 %collective-permute-done.30.refs_3_ = s16[144,512]{1,0:T(8,128)(2,1)S(1)} collective-permute-done((s16[144,512]{1,0:T(8,128)(2,1)S(1)}, s16[144,512]{1,0:T(8,128)(2,1)S(1)}, u32[]{:S(2)}, u32[]{:S(2)}) %collective-permute-start.30) | collective-permute-done | bytes 147488 | tf_op jit(solution)/shard_map/ppermute | solution.py:20
  96.9 0.8 shard_map.92
  97.7 3.8 %collective-permute-start.32 = (s16[80,512]{1,0:T(8,128)(2,1)S(1)}, s16[80,512]{1,0:T(8,128)(2,1)S(1)}, u32[]{:S(2)}, u32[]{:S(2)}) collective-permute-start(s16[80,512]{1,0:T(8,128)(2,1)S(1)} %get-tuple-element.130), channel_id=1, source_target_pairs={{0,32},{32,0},{64,96},{96,64},{128,160},{160,128},{192,224},{224,1... | collective-permute-start | bytes 245768 | tf_op jit(solution)/shard_map/ppermute | solution.py:20
  101.5 5.5 %collective-permute-done.32.refs_1_ = s16[80,512]{1,0:T(8,128)(2,1)S(1)} collective-permute-done((s16[80,512]{1,0:T(8,128)(2,1)S(1)}, s16[80,512]{1,0:T(8,128)(2,1)S(1)}, u32[]{:S(2)}, u32[]{:S(2)}) %collective-permute-start.32) | collective-permute-done | bytes 81952 | tf_op jit(solution)/shard_map/ppermute | solution.py:20
  (51 shorter events, 8.0 us)
Async XLA Ops:
  0.7 1.2 %copy-start = (bf16[1024,512]{1,0:T(8,128)(2,1)S(1)}, bf16[1024,512]{1,0:T(8,128)(2,1)}, u32[]{:S(2)}) copy-start(bf16[1024,512]{1,0:T(8,128)(2,1)} %refs_1_.5) | copy-start | bytes 3145732
  6.2 4.3 %collective-permute-start = (f32[1032,512]{1,0:T(8,128)S(1)}, f32[1032,512]{1,0:T(8,128)S(1)}, u32[]{:S(2)}, u32[]{:S(2)}) collective-permute-start(f32[1032,512]{1,0:T(8,128)S(1)} %get-tuple-element.71), channel_id=1, source_target_pairs={{0,1},{1,0},{2,3},{3,2},{4,5},{5,4},{6,7},{7,6},{8,9},{9,8},{10,11... | collective-permute-start | bytes 6340616 | tf_op jit(solution)/shard_map/ppermute | solution.py:20
  10.4 5.4 %collective-permute-start.1 = (f32[1024,512]{1,0:T(8,128)S(1)}, f32[1024,512]{1,0:T(8,128)S(1)}, u32[]{:S(2)}, u32[]{:S(2)}) collective-permute-start(f32[1024,512]{1,0:T(8,128)S(1)} %get-tuple-element.75), channel_id=1, source_target_pairs={{0,1},{1,0},{2,3},{3,2},{4,5},{5,4},{6,7},{7,6},{8,9},{9,8},{10,11... | collective-permute-start | bytes 6291464 | tf_op jit(solution)/shard_map/ppermute | solution.py:20
  10.9 9.6 %collective-permute-start.4 = (s16[272,512]{1,0:T(8,128)(2,1)S(1)}, s16[272,512]{1,0:T(8,128)(2,1)S(1)}, u32[]{:S(2)}, u32[]{:S(2)}) collective-permute-start(s16[272,512]{1,0:T(8,128)(2,1)S(1)} %get-tuple-element.80), channel_id=1, source_target_pairs={{0,8},{8,0},{16,24},{24,16},{1,9},{9,1},{17,25},{25,17},{2,10},{10... | collective-permute-start | bytes 835592 | tf_op jit(solution)/shard_map/ppermute | solution.py:20
  12.5 10.7 %collective-permute-start.5 = (s16[272,512]{1,0:T(8,128)(2,1)S(1)}, s16[272,512]{1,0:T(8,128)(2,1)S(1)}, u32[]{:S(2)}, u32[]{:S(2)}) collective-permute-start(s16[272,512]{1,0:T(8,128)(2,1)S(1)} %get-tuple-element.81), channel_id=1, source_target_pairs={{0,24},{8,16},{16,8},{24,0},{1,25},{9,17},{17,9},{25,1},{2,26},{10... | collective-permute-start | bytes 835592 | tf_op jit(solution)/shard_map/ppermute | solution.py:20
  16.2 9.7 %collective-permute-start.2 = (s16[272,512]{1,0:T(8,128)(2,1)S(1)}, s16[272,512]{1,0:T(8,128)(2,1)S(1)}, u32[]{:S(2)}, u32[]{:S(2)}) collective-permute-start(s16[272,512]{1,0:T(8,128)(2,1)S(1)} %get-tuple-element.77), channel_id=1, source_target_pairs={{0,8},{8,0},{16,24},{24,16},{1,9},{9,1},{17,25},{25,17},{2,10},{10... | collective-permute-start | bytes 835592 | tf_op jit(solution)/shard_map/ppermute | solution.py:20
  16.9 12.3 %collective-permute-start.3 = (s16[272,512]{1,0:T(8,128)(2,1)S(1)}, s16[272,512]{1,0:T(8,128)(2,1)S(1)}, u32[]{:S(2)}, u32[]{:S(2)}) collective-permute-start(s16[272,512]{1,0:T(8,128)(2,1)S(1)} %get-tuple-element.78), channel_id=1, source_target_pairs={{0,24},{8,16},{16,8},{24,0},{1,25},{9,17},{17,9},{25,1},{2,26},{10... | collective-permute-start | bytes 835592 | tf_op jit(solution)/shard_map/ppermute | solution.py:20
  23.2 19.4 %copy-start.1 = (s32[4096]{0:T(1024)S(1)}, s32[4096]{0:T(1024)}, u32[]{:S(2)}) copy-start(s32[4096]{0:T(1024)} %param.12) | copy-start | bytes 49156
  23.2 19.4 %copy-start.2 = (s32[4096]{0:T(1024)S(1)}, s32[4096]{0:T(1024)}, u32[]{:S(2)}) copy-start(s32[4096]{0:T(1024)} %param.11) | copy-start | bytes 49156
  23.2 19.4 %copy-start.3 = (f32[2048]{0:T(1024)S(1)}, f32[2048]{0:T(1024)}, u32[]{:S(2)}) copy-start(f32[2048]{0:T(1024)} %param.10) | copy-start | bytes 24580
  23.2 19.4 %copy-start.4 = (f32[16]{0:T(128)S(1)}, f32[16]{0:T(128)}, u32[]{:S(2)}) copy-start(f32[16]{0:T(128)} %refs_1_.6) | copy-start | bytes 196
  23.5 8.2 %collective-permute-start.8 = (s16[144,512]{1,0:T(8,128)(2,1)S(1)}, s16[144,512]{1,0:T(8,128)(2,1)S(1)}, u32[]{:S(2)}, u32[]{:S(2)}) collective-permute-start(s16[144,512]{1,0:T(8,128)(2,1)S(1)} %get-tuple-element.87), channel_id=1, source_target_pairs={{0,24},{8,16},{16,8},{24,0},{1,25},{9,17},{17,9},{25,1},{2,26},{10... | collective-permute-start | bytes 442376 | tf_op jit(solution)/shard_map/ppermute | solution.py:20
  25.7 6.0 %collective-permute-start.9 = (s16[144,512]{1,0:T(8,128)(2,1)S(1)}, s16[144,512]{1,0:T(8,128)(2,1)S(1)}, u32[]{:S(2)}, u32[]{:S(2)}) collective-permute-start(s16[144,512]{1,0:T(8,128)(2,1)S(1)} %get-tuple-element.88), channel_id=1, source_target_pairs={{0,8},{8,0},{16,24},{24,16},{1,9},{9,1},{17,25},{25,17},{2,10},{10... | collective-permute-start | bytes 442376 | tf_op jit(solution)/shard_map/ppermute | solution.py:20
  29.5 7.8 %collective-permute-start.6 = (s16[144,512]{1,0:T(8,128)(2,1)S(1)}, s16[144,512]{1,0:T(8,128)(2,1)S(1)}, u32[]{:S(2)}, u32[]{:S(2)}) collective-permute-start(s16[144,512]{1,0:T(8,128)(2,1)S(1)} %get-tuple-element.84), channel_id=1, source_target_pairs={{0,24},{8,16},{16,8},{24,0},{1,25},{9,17},{17,9},{25,1},{2,26},{10... | collective-permute-start | bytes 442376 | tf_op jit(solution)/shard_map/ppermute | solution.py:20
  31.6 5.6 %collective-permute-start.7 = (s16[144,512]{1,0:T(8,128)(2,1)S(1)}, s16[144,512]{1,0:T(8,128)(2,1)S(1)}, u32[]{:S(2)}, u32[]{:S(2)}) collective-permute-start(s16[144,512]{1,0:T(8,128)(2,1)S(1)} %get-tuple-element.85), channel_id=1, source_target_pairs={{0,8},{8,0},{16,24},{24,16},{1,9},{9,1},{17,25},{25,17},{2,10},{10... | collective-permute-start | bytes 442376 | tf_op jit(solution)/shard_map/ppermute | solution.py:20
  32.4 9.6 %collective-permute-start.13 = (s16[80,512]{1,0:T(8,128)(2,1)S(1)}, s16[80,512]{1,0:T(8,128)(2,1)S(1)}, u32[]{:S(2)}, u32[]{:S(2)}) collective-permute-start(s16[80,512]{1,0:T(8,128)(2,1)S(1)} %get-tuple-element.99), channel_id=1, source_target_pairs={{0,6},{2,4},{4,2},{6,0},{1,7},{3,5},{5,3},{7,1},{8,14},{10,12},{12... | collective-permute-start | bytes 245768 | tf_op jit(solution)/shard_map/ppermute | solution.py:20
  34.4 11.9 %collective-permute-start.14 = (s16[80,512]{1,0:T(8,128)(2,1)S(1)}, s16[80,512]{1,0:T(8,128)(2,1)S(1)}, u32[]{:S(2)}, u32[]{:S(2)}) collective-permute-start(s16[80,512]{1,0:T(8,128)(2,1)S(1)} %get-tuple-element.100), channel_id=1, source_target_pairs={{0,4},{2,6},{4,0},{6,2},{1,5},{3,7},{5,1},{7,3},{8,12},{10,14},{12... | collective-permute-start | bytes 245768 | tf_op jit(solution)/shard_map/ppermute | solution.py:20
  35.9 10.4 %collective-permute-start.15 = (s16[80,512]{1,0:T(8,128)(2,1)S(1)}, s16[80,512]{1,0:T(8,128)(2,1)S(1)}, u32[]{:S(2)}, u32[]{:S(2)}) collective-permute-start(s16[80,512]{1,0:T(8,128)(2,1)S(1)} %get-tuple-element.101), channel_id=1, source_target_pairs={{0,2},{2,0},{4,6},{6,4},{1,3},{3,1},{5,7},{7,5},{8,10},{10,8},{12,... | collective-permute-start | bytes 245768 | tf_op jit(solution)/shard_map/ppermute | solution.py:20
  38.0 12.4 %collective-permute-start.10 = (s16[80,512]{1,0:T(8,128)(2,1)S(1)}, s16[80,512]{1,0:T(8,128)(2,1)S(1)}, u32[]{:S(2)}, u32[]{:S(2)}) collective-permute-start(s16[80,512]{1,0:T(8,128)(2,1)S(1)} %get-tuple-element.95), channel_id=1, source_target_pairs={{0,6},{2,4},{4,2},{6,0},{1,7},{3,5},{5,3},{7,1},{8,14},{10,12},{12... | collective-permute-start | bytes 245768 | tf_op jit(solution)/shard_map/ppermute | solution.py:20
  39.7 12.1 %collective-permute-start.11 = (s16[80,512]{1,0:T(8,128)(2,1)S(1)}, s16[80,512]{1,0:T(8,128)(2,1)S(1)}, u32[]{:S(2)}, u32[]{:S(2)}) collective-permute-start(s16[80,512]{1,0:T(8,128)(2,1)S(1)} %get-tuple-element.96), channel_id=1, source_target_pairs={{0,4},{2,6},{4,0},{6,2},{1,5},{3,7},{5,1},{7,3},{8,12},{10,14},{12... | collective-permute-start | bytes 245768 | tf_op jit(solution)/shard_map/ppermute | solution.py:20
  42.0 9.8 %collective-permute-start.12 = (s16[80,512]{1,0:T(8,128)(2,1)S(1)}, s16[80,512]{1,0:T(8,128)(2,1)S(1)}, u32[]{:S(2)}, u32[]{:S(2)}) collective-permute-start(s16[80,512]{1,0:T(8,128)(2,1)S(1)} %get-tuple-element.97), channel_id=1, source_target_pairs={{0,2},{2,0},{4,6},{6,4},{1,3},{3,1},{5,7},{7,5},{8,10},{10,8},{12,... | collective-permute-start | bytes 245768 | tf_op jit(solution)/shard_map/ppermute | solution.py:20
  46.3 8.6 %collective-permute-start.21 = (bf16[64,512]{1,0:T(8,128)(2,1)S(1)}, bf16[64,512]{1,0:T(8,128)(2,1)S(1)}, u32[]{:S(2)}, u32[]{:S(2)}) collective-permute-start(bf16[64,512]{1,0:T(8,128)(2,1)S(1)} %get-tuple-element.104.refs_0_), channel_id=1, source_target_pairs={{0,6},{2,4},{4,2},{6,0},{1,7},{3,5},{5,3},{7,1},{8,14},{10,12},{12... | collective-permute-start | bytes 196616 | tf_op jit(solution)/shard_map/ppermute | solution.py:20
  46.4 10.0 %collective-permute-start.20 = (bf16[64,512]{1,0:T(8,128)(2,1)S(1)}, bf16[64,512]{1,0:T(8,128)(2,1)S(1)}, u32[]{:S(2)}, u32[]{:S(2)}) collective-permute-start(bf16[64,512]{1,0:T(8,128)(2,1)S(1)} %get-tuple-element.104.refs_0_), channel_id=1, source_target_pairs={{0,4},{2,6},{4,0},{6,2},{1,5},{3,7},{5,1},{7,3},{8,12},{10,14},{12... | collective-permute-start | bytes 196616 | tf_op jit(solution)/shard_map/ppermute | solution.py:20
  50.4 6.8 %collective-permute-start.19 = (bf16[64,512]{1,0:T(8,128)(2,1)S(1)}, bf16[64,512]{1,0:T(8,128)(2,1)S(1)}, u32[]{:S(2)}, u32[]{:S(2)}) collective-permute-start(bf16[64,512]{1,0:T(8,128)(2,1)S(1)} %get-tuple-element.104.refs_0_), channel_id=1, source_target_pairs={{0,2},{2,0},{4,6},{6,4},{1,3},{3,1},{5,7},{7,5},{8,10},{10,8},{12,... | collective-permute-start | bytes 196616 | tf_op jit(solution)/shard_map/ppermute | solution.py:20
  51.9 7.6 %collective-permute-start.18 = (bf16[64,512]{1,0:T(8,128)(2,1)S(1)}, bf16[64,512]{1,0:T(8,128)(2,1)S(1)}, u32[]{:S(2)}, u32[]{:S(2)}) collective-permute-start(bf16[64,512]{1,0:T(8,128)(2,1)S(1)} %get-tuple-element.103.refs_0_), channel_id=1, source_target_pairs={{0,6},{2,4},{4,2},{6,0},{1,7},{3,5},{5,3},{7,1},{8,14},{10,12},{12... | collective-permute-start | bytes 196616 | tf_op jit(solution)/shard_map/ppermute | solution.py:20
  53.4 6.0 %collective-permute-start.17 = (bf16[64,512]{1,0:T(8,128)(2,1)S(1)}, bf16[64,512]{1,0:T(8,128)(2,1)S(1)}, u32[]{:S(2)}, u32[]{:S(2)}) collective-permute-start(bf16[64,512]{1,0:T(8,128)(2,1)S(1)} %get-tuple-element.103.refs_0_), channel_id=1, source_target_pairs={{0,4},{2,6},{4,0},{6,2},{1,5},{3,7},{5,1},{7,3},{8,12},{10,14},{12... | collective-permute-start | bytes 196616 | tf_op jit(solution)/shard_map/ppermute | solution.py:20
  55.0 5.0 %collective-permute-start.16 = (bf16[64,512]{1,0:T(8,128)(2,1)S(1)}, bf16[64,512]{1,0:T(8,128)(2,1)S(1)}, u32[]{:S(2)}, u32[]{:S(2)}) collective-permute-start(bf16[64,512]{1,0:T(8,128)(2,1)S(1)} %get-tuple-element.103.refs_0_), channel_id=1, source_target_pairs={{0,2},{2,0},{4,6},{6,4},{1,3},{3,1},{5,7},{7,5},{8,10},{10,8},{12,... | collective-permute-start | bytes 196616 | tf_op jit(solution)/shard_map/ppermute | solution.py:20
  57.2 10.5 %collective-permute-start.26 = (bf16[256,512]{1,0:T(8,128)(2,1)S(1)}, bf16[256,512]{1,0:T(8,128)(2,1)S(1)}, u32[]{:S(2)}, u32[]{:S(2)}) collective-permute-start(bf16[256,512]{1,0:T(8,128)(2,1)S(1)} %get-tuple-element.110.refs_3_), channel_id=1, source_target_pairs={{0,24},{8,16},{16,8},{24,0},{1,25},{9,17},{17,9},{25,1},{2,26},{10... | collective-permute-start | bytes 786440 | tf_op jit(solution)/shard_map/ppermute | solution.py:20
  59.0 9.2 %collective-permute-start.25 = (bf16[256,512]{1,0:T(8,128)(2,1)S(1)}, bf16[256,512]{1,0:T(8,128)(2,1)S(1)}, u32[]{:S(2)}, u32[]{:S(2)}) collective-permute-start(bf16[256,512]{1,0:T(8,128)(2,1)S(1)} %get-tuple-element.110.refs_3_), channel_id=1, source_target_pairs={{0,8},{8,0},{16,24},{24,16},{1,9},{9,1},{17,25},{25,17},{2,10},{10... | collective-permute-start | bytes 786440 | tf_op jit(solution)/shard_map/ppermute | solution.py:20
  60.6 9.9 %collective-permute-start.23 = (bf16[256,512]{1,0:T(8,128)(2,1)S(1)}, bf16[256,512]{1,0:T(8,128)(2,1)S(1)}, u32[]{:S(2)}, u32[]{:S(2)}) collective-permute-start(bf16[256,512]{1,0:T(8,128)(2,1)S(1)} %get-tuple-element.107.refs_4_), channel_id=1, source_target_pairs={{0,24},{8,16},{16,8},{24,0},{1,25},{9,17},{17,9},{25,1},{2,26},{10... | collective-permute-start | bytes 786440 | tf_op jit(solution)/shard_map/ppermute | solution.py:20
  62.6 11.2 %collective-permute-start.22 = (bf16[256,512]{1,0:T(8,128)(2,1)S(1)}, bf16[256,512]{1,0:T(8,128)(2,1)S(1)}, u32[]{:S(2)}, u32[]{:S(2)}) collective-permute-start(bf16[256,512]{1,0:T(8,128)(2,1)S(1)} %get-tuple-element.107.refs_4_), channel_id=1, source_target_pairs={{0,8},{8,0},{16,24},{24,16},{1,9},{9,1},{17,25},{25,17},{2,10},{10... | collective-permute-start | bytes 786440 | tf_op jit(solution)/shard_map/ppermute | solution.py:20
  68.1 8.4 %collective-permute-start.27 = (bf16[256,512]{1,0:T(8,128)(2,1)S(1)}, bf16[256,512]{1,0:T(8,128)(2,1)S(1)}, u32[]{:S(2)}, u32[]{:S(2)}) collective-permute-start(bf16[256,512]{1,0:T(8,128)(2,1)S(1)} %collective-permute-done.26.refs_4_), channel_id=1, source_target_pairs={{0,8},{8,0},{16,24},{24,16},{1,9},{9,1},{17,25},{25,17},{2,10},{10... | collective-permute-start | bytes 786440 | tf_op jit(solution)/shard_map/ppermute | solution.py:20
  73.8 7.6 %collective-permute-start.24 = (bf16[256,512]{1,0:T(8,128)(2,1)S(1)}, bf16[256,512]{1,0:T(8,128)(2,1)S(1)}, u32[]{:S(2)}, u32[]{:S(2)}) collective-permute-start(bf16[256,512]{1,0:T(8,128)(2,1)S(1)} %collective-permute-done.22.refs_3_), channel_id=1, source_target_pairs={{0,24},{8,16},{16,8},{24,0},{1,25},{9,17},{17,9},{25,1},{2,26},{10... | collective-permute-start | bytes 786440 | tf_op jit(solution)/shard_map/ppermute | solution.py:20
  82.4 2.7 %collective-permute-start.28 = (f32[512,512]{1,0:T(8,128)S(1)}, f32[512,512]{1,0:T(8,128)S(1)}, u32[]{:S(2)}, u32[]{:S(2)}) collective-permute-start(f32[512,512]{1,0:T(8,128)S(1)} %get-tuple-element.124), channel_id=1, source_target_pairs={{0,1},{1,0},{2,3},{3,2},{4,5},{5,4},{6,7},{7,6},{8,9},{9,8},{10,11... | collective-permute-start | bytes 3145736 | tf_op jit(solution)/shard_map/ppermute | solution.py:20
  85.9 7.5 %collective-permute-start.29 = (s16[144,512]{1,0:T(8,128)(2,1)S(1)}, s16[144,512]{1,0:T(8,128)(2,1)S(1)}, u32[]{:S(2)}, u32[]{:S(2)}) collective-permute-start(s16[144,512]{1,0:T(8,128)(2,1)S(1)} %get-tuple-element.126), channel_id=1, source_target_pairs={{0,128},{32,160},{64,192},{96,224},{128,0},{160,32},{192,64},{224,... | collective-permute-start | bytes 442376 | tf_op jit(solution)/shard_map/ppermute | solution.py:20
  89.2 7.4 %collective-permute-start.30 = (s16[144,512]{1,0:T(8,128)(2,1)S(1)}, s16[144,512]{1,0:T(8,128)(2,1)S(1)}, u32[]{:S(2)}, u32[]{:S(2)}) collective-permute-start(s16[144,512]{1,0:T(8,128)(2,1)S(1)} %get-tuple-element.127), channel_id=1, source_target_pairs={{0,192},{32,224},{64,128},{96,160},{128,64},{160,96},{192,0},{224,... | collective-permute-start | bytes 442376 | tf_op jit(solution)/shard_map/ppermute | solution.py:20
  90.3 6.7 %collective-permute-start.31 = (s16[144,512]{1,0:T(8,128)(2,1)S(1)}, s16[144,512]{1,0:T(8,128)(2,1)S(1)}, u32[]{:S(2)}, u32[]{:S(2)}) collective-permute-start(s16[144,512]{1,0:T(8,128)(2,1)S(1)} %get-tuple-element.128), channel_id=1, source_target_pairs={{0,64},{32,96},{64,0},{96,32},{128,192},{160,224},{192,128},{224,1... | collective-permute-start | bytes 442376 | tf_op jit(solution)/shard_map/ppermute | solution.py:20
  97.7 9.2 %collective-permute-start.32 = (s16[80,512]{1,0:T(8,128)(2,1)S(1)}, s16[80,512]{1,0:T(8,128)(2,1)S(1)}, u32[]{:S(2)}, u32[]{:S(2)}) collective-permute-start(s16[80,512]{1,0:T(8,128)(2,1)S(1)} %get-tuple-element.130), channel_id=1, source_target_pairs={{0,32},{32,0},{64,96},{96,64},{128,160},{160,128},{192,224},{224,1... | collective-permute-start | bytes 245768 | tf_op jit(solution)/shard_map/ppermute | solution.py:20

commit v8 on v7

--- a/solution.py
+++ b/solution.py
@@ -121,10 +121,10 @@
     out_ref[...] = (own_ref[...] + unpack(m1_in) + unpack(m2_in) + unpack(m3_in)).astype(BF16)
 
 
-def join(p0_ref, p1_ref, p2_ref, p3_ref, out_ref):
-    rows = p0_ref.shape[0]
-    for i, ref in enumerate((p0_ref, p1_ref, p2_ref, p3_ref)):
-        out_ref[rows * i : rows * (i + 1), :] = ref[...]
+def join(first_ref, second_ref, out_ref):
+    rows = first_ref.shape[0]
+    out_ref[:rows, :] = first_ref[...]
+    out_ref[rows:, :] = second_ref[...]
 
 
 def gram_messages(here_ref, mine_ref, came_ref, own_ref, m1_ref, m2_ref, m3_ref, work_ref):
@@ -167,8 +167,8 @@
     def body(here_ref, *refs):
         w_refs, came, before, out_refs = refs[:kinds], refs[kinds : kinds + count], refs[kinds + count : -kinds], refs[-kinds:]
         totals = [ref[...] for ref in before] or [None] * kinds
-        for ref, (stream, owner) in zip(came, places):
-            first = (here_ref[2] * 4 + lax.bitwise_xor(here_ref[0], owner)) * 4 + stream * 2
+        for ref, (stream, owner, core) in zip(came, places):
+            first = (lax.bitwise_xor(here_ref[2], core) * 4 + lax.bitwise_xor(here_ref[0], owner)) * 4 + stream * 2
             parts = [[] for _ in range(kinds)]
             for j in range(2):
                 rows = ref[128 * j : 128 * (j + 1), :].astype(F32).T
@@ -281,21 +281,27 @@
     )
 
     last = weights[0]
-    pieces = [None] * 2
+    pieces, near, far, quarters = [None] * 2, [None] * 2, [None] * 2, [None] * 2
     for s in both:
         own, last = call(last_sum, [((unit, width), BF16)], *came[s], after=[last], flag=True)
-        pieces[s] = [own] + [xor_permute(own, "pw_z", mask) for mask in (1, 2, 3)]
-    quarters, near, far = [None] * 2, [None] * 2, [None] * 2
+        pieces[s] = own, xor_permute(own, "pw_z", 1)
+    for s in both:
+        own, last = call(join, [((2 * unit, width), BF16)], *pieces[s], after=[last], flag=True)
+        pieces[s] = own, xor_permute(own, "pw_z", 2)
     for s in both:
         quarters[s], last = call(join, [((4 * unit, width), BF16)], *pieces[s], after=[last], flag=True)
         near[s], far[s] = xor_permute(quarters[s], "pw_x", 1), xor_permute(quarters[s], "pw_x", 3)
         near[s], far[s] = lax.optimization_barrier((near[s], far[s]))
-    grams = gram_step(here, weights, quarters, [(0, 0), (1, 0)], [], 3_000_000_000)
+    grams = gram_step(here, weights, quarters, [(0, 0, 0), (1, 0, 0)], [], 3_000_000_000)
     near[0], far[0], grams = lax.optimization_barrier((near[0], far[0], grams))
     across = [xor_permute(far[0], "pw_x", 1), xor_permute(near[1], "pw_x", 3)]
-    grams = gram_step(here, weights, [near[0], far[0]], [(0, 1), (0, 3)], grams)
-    grams = gram_step(here, weights, [near[1], far[1], across[0]], [(1, 1), (1, 3), (0, 2)], grams)
-    mine, theirs = gram_step(here, weights, [across[1]], [(1, 2)], grams)
+    grams = gram_step(here, weights, [near[0], far[0]], [(0, 1, 0), (0, 3, 0)], grams)
+    grams = gram_step(here, weights, [near[1], far[1], across[0]], [(1, 1, 0), (1, 3, 0), (0, 2, 0)], grams)
+    mine, theirs = grams
+    theirs = xor_permute(theirs, "pw_c", 1)
+    other = xor_permute(across[1], "pw_c", 1)
+    mine = gram_step(here, weights[:1], [across[1]], [(1, 2, 0)], [mine], 4_000_000_000)
+    mine = gram_step(here, weights[:1], [other], [(1, 2, 1)], mine, 5_000_000_000)[0]
 
     part = width // 4
     own, *out = call(
@@ -303,7 +309,7 @@
         [sums(part)] + [message(part)] * 3,
         here,
         mine,
-        xor_permute(theirs, "pw_c", 1),
+        theirs,
         specs=[SMEM] + [VMEM] * 2,
         scratch=[pltpu.VMEM((width, width), F32)],
     )

time: 108 us -> 112 us (1.037)
  the two profiles are of different devices: /device:TPU:32 before, /device:TPU:8 now
where the time goes in v8:
time: 112 us
  waiting for transfers between devices  47.8 us (43%)
  starting transfers between devices  41.3 us (37%)
  Pallas kernels  20.3 us (18%)
  local copies, waits for them, and re-layouts  1.24 us (1%)
    ppermute x32, waiting for transfers between devices, xor_permute(): return lax.ppermute(value, axis, [(i, i ^ mask) for i in range(count)])  47.8 us
    ppermute x32, starting transfers between devices, xor_permute(): return lax.ppermute(value, axis, [(i, i ^ mask) for i in range(count)])  41.3 us
    pallas_call x24, Pallas kernels, call(): pl.pallas_call(kernel, out_shape=[jax.ShapeDtypeStruct(shape, dtype) for...  20.3 us
  transfers between devices with their start and end apart: 32, of which 21 were waited for; matrix products, arithmetic and copies ran while one was open for 0% of the time, Pallas kernels for 12%

profile of v8, /device:TPU:8, one launch (start us, length us, event | category | flops | bytes accessed | tf_op | source)
XLA Modules:
  0.0 111.5 jit_solution(13769566843933885759)
XLA Ops:
  0.7 1.2 %copy-done = bf16[1024,512]{1,0:T(8,128)(2,1)S(1)} copy-done((bf16[1024,512]{1,0:T(8,128)(2,1)S(1)}, bf16[1024,512]{1,0:T(8,128)(2,1)}, u32[]{:S(2)}) %copy-start) | copy-done | bytes 1048600
  2.0 4.2 %shard_map.73 = (f32[1032,512]{1,0:T(8,128)S(1)}, bf16[3072,1024]{1,0:T(8,128)(2,1)S(1)}, f32[8,128]{1,0:T(8,128)S(1)}) custom-call(s32[4]{0:T(128)S(1)} %pad_add_fusion.refs_0_, f32[1]{0:T(128)S(6)} %copy.8.refs_1_.refs_2_, bf16[4096,1024]{1,0:T(8,128)(2,1)} %refs_2_.2, bf16[1024,512]{1,0:T(8,128)(2,1)S(1)} %copy-done), custom_call_target="tpu_custom_call" | custom-call | flops 1073741824 | bytes 9437204 | tf_op jit(solution)/shard_map/pallas_call | solution.py:35
  6.3 2.3 %shard_map.74 = (f32[1024,512]{1,0:T(8,128)S(1)}, f32[1024,512]{1,0:T(8,128)S(1)}) custom-call(bf16[3072,1024]{1,0:T(8,128)(2,1)S(1)} %get-tuple-element.70.refs_0_, bf16[1024,512]{1,0:T(8,128)(2,1)S(1)} %copy-done, f32[8,128]{1,0:T(8,128)S(1)} %get-tuple-element.71.refs_2_), custom_call_target="tpu_custom_call" | custom-call | flops 2147483648 | bytes 7340032 | tf_op jit(solution)/shard_map/pallas_call | solution.py:35
  8.6 1.8 %collective-permute-done.refs_1_ = f32[1032,512]{1,0:T(8,128)S(1)} collective-permute-done((f32[1032,512]{1,0:T(8,128)S(1)}, f32[1032,512]{1,0:T(8,128)S(1)}, u32[]{:S(2)}, u32[]{:S(2)}) %collective-permute-start) | collective-permute-done | bytes 2113568 | tf_op jit(solution)/shard_map/ppermute | solution.py:20
  10.9 1.6 %collective-permute-start.4 = (s16[272,512]{1,0:T(8,128)(2,1)S(1)}, s16[272,512]{1,0:T(8,128)(2,1)S(1)}, u32[]{:S(2)}, u32[]{:S(2)}) collective-permute-start(s16[272,512]{1,0:T(8,128)(2,1)S(1)} %get-tuple-element.82), channel_id=1, source_target_pairs={{0,8},{8,0},{16,24},{24,16},{1,9},{9,1},{17,25},{25,17},{2,10},{10... | collective-permute-start | bytes 835592 | tf_op jit(solution)/shard_map/ppermute | solution.py:20
  12.5 2.1 %collective-permute-start.5 = (s16[272,512]{1,0:T(8,128)(2,1)S(1)}, s16[272,512]{1,0:T(8,128)(2,1)S(1)}, u32[]{:S(2)}, u32[]{:S(2)}) collective-permute-start(s16[272,512]{1,0:T(8,128)(2,1)S(1)} %get-tuple-element.83), channel_id=1, source_target_pairs={{0,24},{8,16},{16,8},{24,0},{1,25},{9,17},{17,9},{25,1},{2,26},{10... | collective-permute-start | bytes 835592 | tf_op jit(solution)/shard_map/ppermute | solution.py:20
  14.6 1.2 %shard_map.76.refs_0_ = f32[1024,512]{1,0:T(8,128)S(1)} custom-call(bf16[3072,1024]{1,0:T(8,128)(2,1)S(1)} %get-tuple-element.70.refs_0_, bf16[1024,512]{1,0:T(8,128)(2,1)S(1)} %copy-done, f32[8,128]{1,0:T(8,128)S(1)} %get-tuple-element.76.refs_2_), custom_call_target="tpu_custom_call" | custom-call | flops 1073741824 | bytes 7340032 | tf_op jit(solution)/shard_map/pallas_call | solution.py:35
  16.9 1.7 %collective-permute-start.3 = (s16[272,512]{1,0:T(8,128)(2,1)S(1)}, s16[272,512]{1,0:T(8,128)(2,1)S(1)}, u32[]{:S(2)}, u32[]{:S(2)}) collective-permute-start(s16[272,512]{1,0:T(8,128)(2,1)S(1)} %get-tuple-element.80), channel_id=1, source_target_pairs={{0,24},{8,16},{16,8},{24,0},{1,25},{9,17},{17,9},{25,1},{2,26},{10... | collective-permute-start | bytes 835592 | tf_op jit(solution)/shard_map/ppermute | solution.py:20
  18.6 1.9 %collective-permute-done.4.refs_1_ = s16[272,512]{1,0:T(8,128)(2,1)S(1)} collective-permute-done((s16[272,512]{1,0:T(8,128)(2,1)S(1)}, s16[272,512]{1,0:T(8,128)(2,1)S(1)}, u32[]{:S(2)}, u32[]{:S(2)}) %collective-permute-start.4) | collective-permute-done | bytes 278560 | tf_op jit(solution)/shard_map/ppermute | solution.py:20
  20.5 2.7 %collective-permute-done.5.refs_2_ = s16[272,512]{1,0:T(8,128)(2,1)S(1)} collective-permute-done((s16[272,512]{1,0:T(8,128)(2,1)S(1)}, s16[272,512]{1,0:T(8,128)(2,1)S(1)}, u32[]{:S(2)}, u32[]{:S(2)}) %collective-permute-start.5) | collective-permute-done | bytes 278560 | tf_op jit(solution)/shard_map/ppermute | solution.py:20
  23.5 2.2 %collective-permute-start.8 = (s16[144,512]{1,0:T(8,128)(2,1)S(1)}, s16[144,512]{1,0:T(8,128)(2,1)S(1)}, u32[]{:S(2)}, u32[]{:S(2)}) collective-permute-start(s16[144,512]{1,0:T(8,128)(2,1)S(1)} %get-tuple-element.89), channel_id=1, source_target_pairs={{0,24},{8,16},{16,8},{24,0},{1,25},{9,17},{17,9},{25,1},{2,26},{10... | collective-permute-start | bytes 442376 | tf_op jit(solution)/shard_map/ppermute | solution.py:20
  25.9 3.3 %collective-permute-done.3.refs_2_ = s16[272,512]{1,0:T(8,128)(2,1)S(1)} collective-permute-done((s16[272,512]{1,0:T(8,128)(2,1)S(1)}, s16[272,512]{1,0:T(8,128)(2,1)S(1)}, u32[]{:S(2)}, u32[]{:S(2)}) %collective-permute-start.3) | collective-permute-done | bytes 278560 | tf_op jit(solution)/shard_map/ppermute | solution.py:20
  29.5 2.2 %collective-permute-start.6 = (s16[144,512]{1,0:T(8,128)(2,1)S(1)}, s16[144,512]{1,0:T(8,128)(2,1)S(1)}, u32[]{:S(2)}, u32[]{:S(2)}) collective-permute-start(s16[144,512]{1,0:T(8,128)(2,1)S(1)} %get-tuple-element.86), channel_id=1, source_target_pairs={{0,24},{8,16},{16,8},{24,0},{1,25},{9,17},{17,9},{25,1},{2,26},{10... | collective-permute-start | bytes 442376 | tf_op jit(solution)/shard_map/ppermute | solution.py:20
  31.6 0.7 shard_map.80
  32.4 4.7 %collective-permute-start.13 = (s16[80,512]{1,0:T(8,128)(2,1)S(1)}, s16[80,512]{1,0:T(8,128)(2,1)S(1)}, u32[]{:S(2)}, u32[]{:S(2)}) collective-permute-start(s16[80,512]{1,0:T(8,128)(2,1)S(1)} %get-tuple-element.100), channel_id=1, source_target_pairs={{0,6},{2,4},{4,2},{6,0},{1,7},{3,5},{5,3},{7,1},{8,14},{10,12},{12... | collective-permute-start | bytes 245768 | tf_op jit(solution)/shard_map/ppermute | solution.py:20
  37.8 0.7 shard_map.81
  38.5 4.0 %collective-permute-start.10 = (s16[80,512]{1,0:T(8,128)(2,1)S(1)}, s16[80,512]{1,0:T(8,128)(2,1)S(1)}, u32[]{:S(2)}, u32[]{:S(2)}) collective-permute-start(s16[80,512]{1,0:T(8,128)(2,1)S(1)} %get-tuple-element.96), channel_id=1, source_target_pairs={{0,6},{2,4},{4,2},{6,0},{1,7},{3,5},{5,3},{7,1},{8,14},{10,12},{12... | collective-permute-start | bytes 245768 | tf_op jit(solution)/shard_map/ppermute | solution.py:20
  42.5 1.4 %collective-permute-start.12 = (s16[80,512]{1,0:T(8,128)(2,1)S(1)}, s16[80,512]{1,0:T(8,128)(2,1)S(1)}, u32[]{:S(2)}, u32[]{:S(2)}) collective-permute-start(s16[80,512]{1,0:T(8,128)(2,1)S(1)} %get-tuple-element.98), channel_id=1, source_target_pairs={{0,2},{2,0},{4,6},{6,4},{1,3},{3,1},{5,7},{7,5},{8,10},{10,8},{12,... | collective-permute-start | bytes 245768 | tf_op jit(solution)/shard_map/ppermute | solution.py:20
  43.9 0.9 shard_map.82
  44.8 2.4 %collective-permute-done.14.refs_2_ = s16[80,512]{1,0:T(8,128)(2,1)S(1)} collective-permute-done((s16[80,512]{1,0:T(8,128)(2,1)S(1)}, s16[80,512]{1,0:T(8,128)(2,1)S(1)}, u32[]{:S(2)}, u32[]{:S(2)}) %collective-permute-start.14) | collective-permute-done | bytes 81952 | tf_op jit(solution)/shard_map/ppermute | solution.py:20
  47.4 2.8 %collective-permute-done.11.refs_2_ = s16[80,512]{1,0:T(8,128)(2,1)S(1)} collective-permute-done((s16[80,512]{1,0:T(8,128)(2,1)S(1)}, s16[80,512]{1,0:T(8,128)(2,1)S(1)}, u32[]{:S(2)}, u32[]{:S(2)}) %collective-permute-start.11) | collective-permute-done | bytes 81952 | tf_op jit(solution)/shard_map/ppermute | solution.py:20
  50.4 1.3 %collective-permute-done.17.refs_1_ = bf16[64,512]{1,0:T(8,128)(2,1)S(1)} collective-permute-done((bf16[64,512]{1,0:T(8,128)(2,1)S(1)}, bf16[64,512]{1,0:T(8,128)(2,1)S(1)}, u32[]{:S(2)}, u32[]{:S(2)}) %collective-permute-start.17) | collective-permute-done | bytes 65568 | tf_op jit(solution)/shard_map/ppermute | solution.py:20
  51.7 2.1 %collective-permute-start.19 = (bf16[128,512]{1,0:T(8,128)(2,1)S(1)}, bf16[128,512]{1,0:T(8,128)(2,1)S(1)}, u32[]{:S(2)}, u32[]{:S(2)}) collective-permute-start(bf16[128,512]{1,0:T(8,128)(2,1)S(1)} %get-tuple-element.109.refs_0_), channel_id=1, source_target_pairs={{0,4},{2,6},{4,0},{6,2},{1,5},{3,7},{5,1},{7,3},{8,12},{10,14},{12... | collective-permute-start | bytes 393224 | tf_op jit(solution)/shard_map/ppermute | solution.py:20
  53.8 1.7 %collective-permute-done.16.refs_1_ = bf16[64,512]{1,0:T(8,128)(2,1)S(1)} collective-permute-done((bf16[64,512]{1,0:T(8,128)(2,1)S(1)}, bf16[64,512]{1,0:T(8,128)(2,1)S(1)}, u32[]{:S(2)}, u32[]{:S(2)}) %collective-permute-start.16) | collective-permute-done | bytes 65568 | tf_op jit(solution)/shard_map/ppermute | solution.py:20
  55.5 1.2 %collective-permute-start.18 = (bf16[128,512]{1,0:T(8,128)(2,1)S(1)}, bf16[128,512]{1,0:T(8,128)(2,1)S(1)}, u32[]{:S(2)}, u32[]{:S(2)}) collective-permute-start(bf16[128,512]{1,0:T(8,128)(2,1)S(1)} %get-tuple-element.108.refs_0_), channel_id=1, source_target_pairs={{0,4},{2,6},{4,0},{6,2},{1,5},{3,7},{5,1},{7,3},{8,12},{10,14},{12... | collective-permute-start | bytes 393224 | tf_op jit(solution)/shard_map/ppermute | solution.py:20
  56.7 7.0 %collective-permute-done.19.refs_1_ = bf16[128,512]{1,0:T(8,128)(2,1)S(1)} collective-permute-done((bf16[128,512]{1,0:T(8,128)(2,1)S(1)}, bf16[128,512]{1,0:T(8,128)(2,1)S(1)}, u32[]{:S(2)}, u32[]{:S(2)}) %collective-permute-start.19) | collective-permute-done | bytes 131104 | tf_op jit(solution)/shard_map/ppermute | solution.py:20
  63.7 2.2 %collective-permute-start.25 = (bf16[256,512]{1,0:T(8,128)(2,1)S(1)}, bf16[256,512]{1,0:T(8,128)(2,1)S(1)}, u32[]{:S(2)}, u32[]{:S(2)}) collective-permute-start(bf16[256,512]{1,0:T(8,128)(2,1)S(1)} %get-tuple-element.116.refs_3_), channel_id=1, source_target_pairs={{0,24},{8,16},{16,8},{24,0},{1,25},{9,17},{17,9},{25,1},{2,26},{10... | collective-permute-start | bytes 786440 | tf_op jit(solution)/shard_map/ppermute | solution.py:20
  66.5 1.3 %collective-permute-start.21 = (bf16[256,512]{1,0:T(8,128)(2,1)S(1)}, bf16[256,512]{1,0:T(8,128)(2,1)S(1)}, u32[]{:S(2)}, u32[]{:S(2)}) collective-permute-start(bf16[256,512]{1,0:T(8,128)(2,1)S(1)} %get-tuple-element.112.refs_4_), channel_id=1, source_target_pairs={{0,24},{8,16},{16,8},{24,0},{1,25},{9,17},{17,9},{25,1},{2,26},{10... | collective-permute-start | bytes 786440 | tf_op jit(solution)/shard_map/ppermute | solution.py:20
  67.8 1.3 %collective-permute-start.20 = (bf16[256,512]{1,0:T(8,128)(2,1)S(1)}, bf16[256,512]{1,0:T(8,128)(2,1)S(1)}, u32[]{:S(2)}, u32[]{:S(2)}) collective-permute-start(bf16[256,512]{1,0:T(8,128)(2,1)S(1)} %get-tuple-element.112.refs_4_), channel_id=1, source_target_pairs={{0,8},{8,0},{16,24},{24,16},{1,9},{9,1},{17,25},{25,17},{2,10},{10... | collective-permute-start | bytes 786440 | tf_op jit(solution)/shard_map/ppermute | solution.py:20
  69.1 1.3 %shard_map.89 = (f32[512,512]{1,0:T(8,128)S(1)}, f32[512,512]{1,0:T(8,128)S(1)}) custom-call(s32[4]{0:T(128)S(1)} %pad_add_fusion.refs_0_, f32[32,128]{1,0:T(8,128)S(1)} %get-tuple-element.94.refs_4_.refs_1_, f32[32,128]{1,0:T(8,128)S(1)} %get-tuple-element.114.refs_2_, bf16[256,512]{1,0:T(8,128)(2,1)S(1)} %get-tuple-element.116.refs_3_, ...), custom_call_target="tpu_custom_call" | custom-call | flops 3536870912 | bytes 557072 | tf_op jit(solution)/shard_map/pallas_call | solution.py:35
  70.4 3.5 %collective-permute-done.25.refs_4_ = bf16[256,512]{1,0:T(8,128)(2,1)S(1)} collective-permute-done((bf16[256,512]{1,0:T(8,128)(2,1)S(1)}, bf16[256,512]{1,0:T(8,128)(2,1)S(1)}, u32[]{:S(2)}, u32[]{:S(2)}) %collective-permute-start.25) | collective-permute-done | bytes 262176 | tf_op jit(solution)/shard_map/ppermute | solution.py:20
  73.8 1.2 %collective-permute-done.24.refs_3_ = bf16[256,512]{1,0:T(8,128)(2,1)S(1)} collective-permute-done((bf16[256,512]{1,0:T(8,128)(2,1)S(1)}, bf16[256,512]{1,0:T(8,128)(2,1)S(1)}, u32[]{:S(2)}, u32[]{:S(2)}) %collective-permute-start.24) | collective-permute-done | bytes 262176 | tf_op jit(solution)/shard_map/ppermute | solution.py:20
  75.0 1.6 %collective-permute-done.21.refs_4_ = bf16[256,512]{1,0:T(8,128)(2,1)S(1)} collective-permute-done((bf16[256,512]{1,0:T(8,128)(2,1)S(1)}, bf16[256,512]{1,0:T(8,128)(2,1)S(1)}, u32[]{:S(2)}, u32[]{:S(2)}) %collective-permute-start.21) | collective-permute-done | bytes 262176 | tf_op jit(solution)/shard_map/ppermute | solution.py:20
  76.6 3.4 %collective-permute-done.20.refs_3_ = bf16[256,512]{1,0:T(8,128)(2,1)S(1)} collective-permute-done((bf16[256,512]{1,0:T(8,128)(2,1)S(1)}, bf16[256,512]{1,0:T(8,128)(2,1)S(1)}, u32[]{:S(2)}, u32[]{:S(2)}) %collective-permute-start.20) | collective-permute-done | bytes 262176 | tf_op jit(solution)/shard_map/ppermute | solution.py:20
  80.0 1.1 %collective-permute-start.22 = (bf16[256,512]{1,0:T(8,128)(2,1)S(1)}, bf16[256,512]{1,0:T(8,128)(2,1)S(1)}, u32[]{:S(2)}, u32[]{:S(2)}) collective-permute-start(bf16[256,512]{1,0:T(8,128)(2,1)S(1)} %collective-permute-done.20.refs_3_), channel_id=1, source_target_pairs={{0,24},{8,16},{16,8},{24,0},{1,25},{9,17},{17,9},{25,1},{2,26},{10... | collective-permute-start | bytes 786440 | tf_op jit(solution)/shard_map/ppermute | solution.py:20
  81.2 1.3 %shard_map.90 = (f32[512,512]{1,0:T(8,128)S(1)}, f32[512,512]{1,0:T(8,128)S(1)}) custom-call(s32[4]{0:T(128)S(1)} %pad_add_fusion.refs_0_, f32[32,128]{1,0:T(8,128)S(1)} %get-tuple-element.94.refs_4_.refs_1_, f32[32,128]{1,0:T(8,128)S(1)} %get-tuple-element.114.refs_2_, bf16[256,512]{1,0:T(8,128)(2,1)S(1)} %collective-permute-done.24.refs_3_, ...), custom_call_target="tpu_custom_call" | custom-call | flops 536870912 | bytes 2654224 | tf_op jit(solution)/shard_map/pallas_call | solution.py:35
  82.8 1.6 %shard_map.91 = (f32[512,512]{1,0:T(8,128)S(1)}, f32[512,512]{1,0:T(8,128)S(1)}) custom-call(s32[4]{0:T(128)S(1)} %pad_add_fusion.refs_0_, f32[32,128]{1,0:T(8,128)S(1)} %get-tuple-element.94.refs_4_.refs_1_, f32[32,128]{1,0:T(8,128)S(1)} %get-tuple-element.114.refs_2_, bf16[256,512]{1,0:T(8,128)(2,1)S(1)} %collective-permute-done.20.refs_3_, ...), custom_call_target="tpu_custom_call" | custom-call | flops 805306368 | bytes 2916368 | tf_op jit(solution)/shard_map/pallas_call | solution.py:35
  84.5 3.1 %collective-permute-done.22.refs_2_ = bf16[256,512]{1,0:T(8,128)(2,1)S(1)} collective-permute-done((bf16[256,512]{1,0:T(8,128)(2,1)S(1)}, bf16[256,512]{1,0:T(8,128)(2,1)S(1)}, u32[]{:S(2)}, u32[]{:S(2)}) %collective-permute-start.22) | collective-permute-done | bytes 262176 | tf_op jit(solution)/shard_map/ppermute | solution.py:20
  87.6 0.9 shard_map.92.refs_3_
  89.2 0.9 shard_map.93.refs_1_
  90.1 0.8 shard_map.94
  90.9 2.4 %collective-permute-start.28 = (s16[144,512]{1,0:T(8,128)(2,1)S(1)}, s16[144,512]{1,0:T(8,128)(2,1)S(1)}, u32[]{:S(2)}, u32[]{:S(2)}) collective-permute-start(s16[144,512]{1,0:T(8,128)(2,1)S(1)} %get-tuple-element.130), channel_id=1, source_target_pairs={{0,128},{32,160},{64,192},{96,224},{128,0},{160,32},{192,64},{224,... | collective-permute-start | bytes 442376 | tf_op jit(solution)/shard_map/ppermute | solution.py:20
  93.2 2.4 %collective-permute-start.30 = (s16[144,512]{1,0:T(8,128)(2,1)S(1)}, s16[144,512]{1,0:T(8,128)(2,1)S(1)}, u32[]{:S(2)}, u32[]{:S(2)}) collective-permute-start(s16[144,512]{1,0:T(8,128)(2,1)S(1)} %get-tuple-element.132), channel_id=1, source_target_pairs={{0,64},{32,96},{64,0},{96,32},{128,192},{160,224},{192,128},{224,1... | collective-permute-start | bytes 442376 | tf_op jit(solution)/shard_map/ppermute | solution.py:20
  95.6 3.5 %collective-permute-done.28.refs_2_ = s16[144,512]{1,0:T(8,128)(2,1)S(1)} collective-permute-done((s16[144,512]{1,0:T(8,128)(2,1)S(1)}, s16[144,512]{1,0:T(8,128)(2,1)S(1)}, u32[]{:S(2)}, u32[]{:S(2)}) %collective-permute-start.28) | collective-permute-done | bytes 147488 | tf_op jit(solution)/shard_map/ppermute | solution.py:20
  99.2 2.3 %collective-permute-done.29.refs_3_ = s16[144,512]{1,0:T(8,128)(2,1)S(1)} collective-permute-done((s16[144,512]{1,0:T(8,128)(2,1)S(1)}, s16[144,512]{1,0:T(8,128)(2,1)S(1)}, u32[]{:S(2)}, u32[]{:S(2)}) %collective-permute-start.29) | collective-permute-done | bytes 147488 | tf_op jit(solution)/shard_map/ppermute | solution.py:20
  101.7 0.8 shard_map.95
  102.4 5.6 %collective-permute-start.31 = (s16[80,512]{1,0:T(8,128)(2,1)S(1)}, s16[80,512]{1,0:T(8,128)(2,1)S(1)}, u32[]{:S(2)}, u32[]{:S(2)}) collective-permute-start(s16[80,512]{1,0:T(8,128)(2,1)S(1)} %get-tuple-element.134), channel_id=1, source_target_pairs={{0,32},{32,0},{64,96},{96,64},{128,160},{160,128},{192,224},{224,1... | collective-permute-start | bytes 245768 | tf_op jit(solution)/shard_map/ppermute | solution.py:20
  108.0 2.8 %collective-permute-done.31.refs_1_ = s16[80,512]{1,0:T(8,128)(2,1)S(1)} collective-permute-done((s16[80,512]{1,0:T(8,128)(2,1)S(1)}, s16[80,512]{1,0:T(8,128)(2,1)S(1)}, u32[]{:S(2)}, u32[]{:S(2)}) %collective-permute-start.31) | collective-permute-done | bytes 81952 | tf_op jit(solution)/shard_map/ppermute | solution.py:20
  (52 shorter events, 6.0 us)
Async XLA Ops:
  0.7 1.2 %copy-start = (bf16[1024,512]{1,0:T(8,128)(2,1)S(1)}, bf16[1024,512]{1,0:T(8,128)(2,1)}, u32[]{:S(2)}) copy-start(bf16[1024,512]{1,0:T(8,128)(2,1)} %refs_1_.5) | copy-start | bytes 3145732
  6.2 4.3 %collective-permute-start = (f32[1032,512]{1,0:T(8,128)S(1)}, f32[1032,512]{1,0:T(8,128)S(1)}, u32[]{:S(2)}, u32[]{:S(2)}) collective-permute-start(f32[1032,512]{1,0:T(8,128)S(1)} %get-tuple-element.73), channel_id=1, source_target_pairs={{0,1},{1,0},{2,3},{3,2},{4,5},{5,4},{6,7},{7,6},{8,9},{9,8},{10,11... | collective-permute-start | bytes 6340616 | tf_op jit(solution)/shard_map/ppermute | solution.py:20
  10.4 5.4 %collective-permute-start.1 = (f32[1024,512]{1,0:T(8,128)S(1)}, f32[1024,512]{1,0:T(8,128)S(1)}, u32[]{:S(2)}, u32[]{:S(2)}) collective-permute-start(f32[1024,512]{1,0:T(8,128)S(1)} %get-tuple-element.77), channel_id=1, source_target_pairs={{0,1},{1,0},{2,3},{3,2},{4,5},{5,4},{6,7},{7,6},{8,9},{9,8},{10,11... | collective-permute-start | bytes 6291464 | tf_op jit(solution)/shard_map/ppermute | solution.py:20
  10.9 9.6 %collective-permute-start.4 = (s16[272,512]{1,0:T(8,128)(2,1)S(1)}, s16[272,512]{1,0:T(8,128)(2,1)S(1)}, u32[]{:S(2)}, u32[]{:S(2)}) collective-permute-start(s16[272,512]{1,0:T(8,128)(2,1)S(1)} %get-tuple-element.82), channel_id=1, source_target_pairs={{0,8},{8,0},{16,24},{24,16},{1,9},{9,1},{17,25},{25,17},{2,10},{10... | collective-permute-start | bytes 835592 | tf_op jit(solution)/shard_map/ppermute | solution.py:20
  12.5 10.7 %collective-permute-start.5 = (s16[272,512]{1,0:T(8,128)(2,1)S(1)}, s16[272,512]{1,0:T(8,128)(2,1)S(1)}, u32[]{:S(2)}, u32[]{:S(2)}) collective-permute-start(s16[272,512]{1,0:T(8,128)(2,1)S(1)} %get-tuple-element.83), channel_id=1, source_target_pairs={{0,24},{8,16},{16,8},{24,0},{1,25},{9,17},{17,9},{25,1},{2,26},{10... | collective-permute-start | bytes 835592 | tf_op jit(solution)/shard_map/ppermute | solution.py:20
  16.2 9.7 %collective-permute-start.2 = (s16[272,512]{1,0:T(8,128)(2,1)S(1)}, s16[272,512]{1,0:T(8,128)(2,1)S(1)}, u32[]{:S(2)}, u32[]{:S(2)}) collective-permute-start(s16[272,512]{1,0:T(8,128)(2,1)S(1)} %get-tuple-element.79), channel_id=1, source_target_pairs={{0,8},{8,0},{16,24},{24,16},{1,9},{9,1},{17,25},{25,17},{2,10},{10... | collective-permute-start | bytes 835592 | tf_op jit(solution)/shard_map/ppermute | solution.py:20
  16.9 12.3 %collective-permute-start.3 = (s16[272,512]{1,0:T(8,128)(2,1)S(1)}, s16[272,512]{1,0:T(8,128)(2,1)S(1)}, u32[]{:S(2)}, u32[]{:S(2)}) collective-permute-start(s16[272,512]{1,0:T(8,128)(2,1)S(1)} %get-tuple-element.80), channel_id=1, source_target_pairs={{0,24},{8,16},{16,8},{24,0},{1,25},{9,17},{17,9},{25,1},{2,26},{10... | collective-permute-start | bytes 835592 | tf_op jit(solution)/shard_map/ppermute | solution.py:20
  23.2 20.7 %copy-start.1 = (s32[4096]{0:T(1024)S(1)}, s32[4096]{0:T(1024)}, u32[]{:S(2)}) copy-start(s32[4096]{0:T(1024)} %param.12) | copy-start | bytes 49156
  23.2 20.7 %copy-start.2 = (s32[4096]{0:T(1024)S(1)}, s32[4096]{0:T(1024)}, u32[]{:S(2)}) copy-start(s32[4096]{0:T(1024)} %param.11) | copy-start | bytes 49156
  23.2 20.7 %copy-start.3 = (f32[2048]{0:T(1024)S(1)}, f32[2048]{0:T(1024)}, u32[]{:S(2)}) copy-start(f32[2048]{0:T(1024)} %param.10) | copy-start | bytes 24580
  23.2 20.7 %copy-start.4 = (f32[16]{0:T(128)S(1)}, f32[16]{0:T(128)}, u32[]{:S(2)}) copy-start(f32[16]{0:T(128)} %refs_1_.6) | copy-start | bytes 196
  23.5 8.2 %collective-permute-start.8 = (s16[144,512]{1,0:T(8,128)(2,1)S(1)}, s16[144,512]{1,0:T(8,128)(2,1)S(1)}, u32[]{:S(2)}, u32[]{:S(2)}) collective-permute-start(s16[144,512]{1,0:T(8,128)(2,1)S(1)} %get-tuple-element.89), channel_id=1, source_target_pairs={{0,24},{8,16},{16,8},{24,0},{1,25},{9,17},{17,9},{25,1},{2,26},{10... | collective-permute-start | bytes 442376 | tf_op jit(solution)/shard_map/ppermute | solution.py:20
  25.7 6.0 %collective-permute-start.9 = (s16[144,512]{1,0:T(8,128)(2,1)S(1)}, s16[144,512]{1,0:T(8,128)(2,1)S(1)}, u32[]{:S(2)}, u32[]{:S(2)}) collective-permute-start(s16[144,512]{1,0:T(8,128)(2,1)S(1)} %get-tuple-element.90), channel_id=1, source_target_pairs={{0,8},{8,0},{16,24},{24,16},{1,9},{9,1},{17,25},{25,17},{2,10},{10... | collective-permute-start | bytes 442376 | tf_op jit(solution)/shard_map/ppermute | solution.py:20
  29.5 8.3 %collective-permute-start.6 = (s16[144,512]{1,0:T(8,128)(2,1)S(1)}, s16[144,512]{1,0:T(8,128)(2,1)S(1)}, u32[]{:S(2)}, u32[]{:S(2)}) collective-permute-start(s16[144,512]{1,0:T(8,128)(2,1)S(1)} %get-tuple-element.86), channel_id=1, source_target_pairs={{0,24},{8,16},{16,8},{24,0},{1,25},{9,17},{17,9},{25,1},{2,26},{10... | collective-permute-start | bytes 442376 | tf_op jit(solution)/shard_map/ppermute | solution.py:20
  31.6 6.1 %collective-permute-start.7 = (s16[144,512]{1,0:T(8,128)(2,1)S(1)}, s16[144,512]{1,0:T(8,128)(2,1)S(1)}, u32[]{:S(2)}, u32[]{:S(2)}) collective-permute-start(s16[144,512]{1,0:T(8,128)(2,1)S(1)} %get-tuple-element.87), channel_id=1, source_target_pairs={{0,8},{8,0},{16,24},{24,16},{1,9},{9,1},{17,25},{25,17},{2,10},{10... | collective-permute-start | bytes 442376 | tf_op jit(solution)/shard_map/ppermute | solution.py:20
  32.4 10.1 %collective-permute-start.13 = (s16[80,512]{1,0:T(8,128)(2,1)S(1)}, s16[80,512]{1,0:T(8,128)(2,1)S(1)}, u32[]{:S(2)}, u32[]{:S(2)}) collective-permute-start(s16[80,512]{1,0:T(8,128)(2,1)S(1)} %get-tuple-element.100), channel_id=1, source_target_pairs={{0,6},{2,4},{4,2},{6,0},{1,7},{3,5},{5,3},{7,1},{8,14},{10,12},{12... | collective-permute-start | bytes 245768 | tf_op jit(solution)/shard_map/ppermute | solution.py:20
  37.1 10.1 %collective-permute-start.14 = (s16[80,512]{1,0:T(8,128)(2,1)S(1)}, s16[80,512]{1,0:T(8,128)(2,1)S(1)}, u32[]{:S(2)}, u32[]{:S(2)}) collective-permute-start(s16[80,512]{1,0:T(8,128)(2,1)S(1)} %get-tuple-element.101), channel_id=1, source_target_pairs={{0,4},{2,6},{4,0},{6,2},{1,5},{3,7},{5,1},{7,3},{8,12},{10,14},{12... | collective-permute-start | bytes 245768 | tf_op jit(solution)/shard_map/ppermute | solution.py:20
  37.1 10.1 %collective-permute-start.15 = (s16[80,512]{1,0:T(8,128)(2,1)S(1)}, s16[80,512]{1,0:T(8,128)(2,1)S(1)}, u32[]{:S(2)}, u32[]{:S(2)}) collective-permute-start(s16[80,512]{1,0:T(8,128)(2,1)S(1)} %get-tuple-element.102), channel_id=1, source_target_pairs={{0,2},{2,0},{4,6},{6,4},{1,3},{3,1},{5,7},{7,5},{8,10},{10,8},{12,... | collective-permute-start | bytes 245768 | tf_op jit(solution)/shard_map/ppermute | solution.py:20
  38.5 8.9 %collective-permute-start.10 = (s16[80,512]{1,0:T(8,128)(2,1)S(1)}, s16[80,512]{1,0:T(8,128)(2,1)S(1)}, u32[]{:S(2)}, u32[]{:S(2)}) collective-permute-start(s16[80,512]{1,0:T(8,128)(2,1)S(1)} %get-tuple-element.96), channel_id=1, source_target_pairs={{0,6},{2,4},{4,2},{6,0},{1,7},{3,5},{5,3},{7,1},{8,14},{10,12},{12... | collective-permute-start | bytes 245768 | tf_op jit(solution)/shard_map/ppermute | solution.py:20
  42.5 7.7 %collective-permute-start.11 = (s16[80,512]{1,0:T(8,128)(2,1)S(1)}, s16[80,512]{1,0:T(8,128)(2,1)S(1)}, u32[]{:S(2)}, u32[]{:S(2)}) collective-permute-start(s16[80,512]{1,0:T(8,128)(2,1)S(1)} %get-tuple-element.97), channel_id=1, source_target_pairs={{0,4},{2,6},{4,0},{6,2},{1,5},{3,7},{5,1},{7,3},{8,12},{10,14},{12... | collective-permute-start | bytes 245768 | tf_op jit(solution)/shard_map/ppermute | solution.py:20
  42.5 7.7 %collective-permute-start.12 = (s16[80,512]{1,0:T(8,128)(2,1)S(1)}, s16[80,512]{1,0:T(8,128)(2,1)S(1)}, u32[]{:S(2)}, u32[]{:S(2)}) collective-permute-start(s16[80,512]{1,0:T(8,128)(2,1)S(1)} %get-tuple-element.98), channel_id=1, source_target_pairs={{0,2},{2,0},{4,6},{6,4},{1,3},{3,1},{5,7},{7,5},{8,10},{10,8},{12,... | collective-permute-start | bytes 245768 | tf_op jit(solution)/shard_map/ppermute | solution.py:20
  47.3 4.4 %collective-permute-start.17 = (bf16[64,512]{1,0:T(8,128)(2,1)S(1)}, bf16[64,512]{1,0:T(8,128)(2,1)S(1)}, u32[]{:S(2)}, u32[]{:S(2)}) collective-permute-start(bf16[64,512]{1,0:T(8,128)(2,1)S(1)} %get-tuple-element.105.refs_0_), channel_id=1, source_target_pairs={{0,2},{2,0},{4,6},{6,4},{1,3},{3,1},{5,7},{7,5},{8,10},{10,8},{12,... | collective-permute-start | bytes 196616 | tf_op jit(solution)/shard_map/ppermute | solution.py:20
  50.3 5.2 %collective-permute-start.16 = (bf16[64,512]{1,0:T(8,128)(2,1)S(1)}, bf16[64,512]{1,0:T(8,128)(2,1)S(1)}, u32[]{:S(2)}, u32[]{:S(2)}) collective-permute-start(bf16[64,512]{1,0:T(8,128)(2,1)S(1)} %get-tuple-element.104.refs_0_), channel_id=1, source_target_pairs={{0,2},{2,0},{4,6},{6,4},{1,3},{3,1},{5,7},{7,5},{8,10},{10,8},{12,... | collective-permute-start | bytes 196616 | tf_op jit(solution)/shard_map/ppermute | solution.py:20
  51.7 12.0 %collective-permute-start.19 = (bf16[128,512]{1,0:T(8,128)(2,1)S(1)}, bf16[128,512]{1,0:T(8,128)(2,1)S(1)}, u32[]{:S(2)}, u32[]{:S(2)}) collective-permute-start(bf16[128,512]{1,0:T(8,128)(2,1)S(1)} %get-tuple-element.109.refs_0_), channel_id=1, source_target_pairs={{0,4},{2,6},{4,0},{6,2},{1,5},{3,7},{5,1},{7,3},{8,12},{10,14},{12... | collective-permute-start | bytes 393224 | tf_op jit(solution)/shard_map/ppermute | solution.py:20
  55.5 10.4 %collective-permute-start.18 = (bf16[128,512]{1,0:T(8,128)(2,1)S(1)}, bf16[128,512]{1,0:T(8,128)(2,1)S(1)}, u32[]{:S(2)}, u32[]{:S(2)}) collective-permute-start(bf16[128,512]{1,0:T(8,128)(2,1)S(1)} %get-tuple-element.108.refs_0_), channel_id=1, source_target_pairs={{0,4},{2,6},{4,0},{6,2},{1,5},{3,7},{5,1},{7,3},{8,12},{10,14},{12... | collective-permute-start | bytes 393224 | tf_op jit(solution)/shard_map/ppermute | solution.py:20
  63.7 10.1 %collective-permute-start.25 = (bf16[256,512]{1,0:T(8,128)(2,1)S(1)}, bf16[256,512]{1,0:T(8,128)(2,1)S(1)}, u32[]{:S(2)}, u32[]{:S(2)}) collective-permute-start(bf16[256,512]{1,0:T(8,128)(2,1)S(1)} %get-tuple-element.116.refs_3_), channel_id=1, source_target_pairs={{0,24},{8,16},{16,8},{24,0},{1,25},{9,17},{17,9},{25,1},{2,26},{10... | collective-permute-start | bytes 786440 | tf_op jit(solution)/shard_map/ppermute | solution.py:20
  65.9 9.1 %collective-permute-start.24 = (bf16[256,512]{1,0:T(8,128)(2,1)S(1)}, bf16[256,512]{1,0:T(8,128)(2,1)S(1)}, u32[]{:S(2)}, u32[]{:S(2)}) collective-permute-start(bf16[256,512]{1,0:T(8,128)(2,1)S(1)} %get-tuple-element.116.refs_3_), channel_id=1, source_target_pairs={{0,8},{8,0},{16,24},{24,16},{1,9},{9,1},{17,25},{25,17},{2,10},{10... | collective-permute-start | bytes 786440 | tf_op jit(solution)/shard_map/ppermute | solution.py:20
  66.5 10.1 %collective-permute-start.21 = (bf16[256,512]{1,0:T(8,128)(2,1)S(1)}, bf16[256,512]{1,0:T(8,128)(2,1)S(1)}, u32[]{:S(2)}, u32[]{:S(2)}) collective-permute-start(bf16[256,512]{1,0:T(8,128)(2,1)S(1)} %get-tuple-element.112.refs_4_), channel_id=1, source_target_pairs={{0,24},{8,16},{16,8},{24,0},{1,25},{9,17},{17,9},{25,1},{2,26},{10... | collective-permute-start | bytes 786440 | tf_op jit(solution)/shard_map/ppermute | solution.py:20
  67.8 12.3 %collective-permute-start.20 = (bf16[256,512]{1,0:T(8,128)(2,1)S(1)}, bf16[256,512]{1,0:T(8,128)(2,1)S(1)}, u32[]{:S(2)}, u32[]{:S(2)}) collective-permute-start(bf16[256,512]{1,0:T(8,128)(2,1)S(1)} %get-tuple-element.112.refs_4_), channel_id=1, source_target_pairs={{0,8},{8,0},{16,24},{24,16},{1,9},{9,1},{17,25},{25,17},{2,10},{10... | collective-permute-start | bytes 786440 | tf_op jit(solution)/shard_map/ppermute | solution.py:20
  75.0 7.8 %collective-permute-start.26 = (bf16[256,512]{1,0:T(8,128)(2,1)S(1)}, bf16[256,512]{1,0:T(8,128)(2,1)S(1)}, u32[]{:S(2)}, u32[]{:S(2)}) collective-permute-start(bf16[256,512]{1,0:T(8,128)(2,1)S(1)} %collective-permute-done.25.refs_4_), channel_id=1, source_target_pairs={{0,8},{8,0},{16,24},{24,16},{1,9},{9,1},{17,25},{25,17},{2,10},{10... | collective-permute-start | bytes 786440 | tf_op jit(solution)/shard_map/ppermute | solution.py:20
  80.0 7.6 %collective-permute-start.22 = (bf16[256,512]{1,0:T(8,128)(2,1)S(1)}, bf16[256,512]{1,0:T(8,128)(2,1)S(1)}, u32[]{:S(2)}, u32[]{:S(2)}) collective-permute-start(bf16[256,512]{1,0:T(8,128)(2,1)S(1)} %collective-permute-done.20.refs_3_), channel_id=1, source_target_pairs={{0,24},{8,16},{16,8},{24,0},{1,25},{9,17},{17,9},{25,1},{2,26},{10... | collective-permute-start | bytes 786440 | tf_op jit(solution)/shard_map/ppermute | solution.py:20
  84.4 5.6 %collective-permute-start.27 = (f32[512,512]{1,0:T(8,128)S(1)}, f32[512,512]{1,0:T(8,128)S(1)}, u32[]{:S(2)}, u32[]{:S(2)}) collective-permute-start(f32[512,512]{1,0:T(8,128)S(1)} %get-tuple-element.128), channel_id=1, source_target_pairs={{0,1},{1,0},{2,3},{3,2},{4,5},{5,4},{6,7},{7,6},{8,9},{9,8},{10,11... | collective-permute-start | bytes 3145736 | tf_op jit(solution)/shard_map/ppermute | solution.py:20
  87.6 1.5 %collective-permute-start.23 = (bf16[256,512]{1,0:T(8,128)(2,1)S(1)}, bf16[256,512]{1,0:T(8,128)(2,1)S(1)}, u32[]{:S(2)}, u32[]{:S(2)}) collective-permute-start(bf16[256,512]{1,0:T(8,128)(2,1)S(1)} %collective-permute-done.22.refs_2_), channel_id=1, source_target_pairs={{0,1},{1,0},{2,3},{3,2},{4,5},{5,4},{6,7},{7,6},{8,9},{9,8},{10,11... | collective-permute-start | bytes 786440 | tf_op jit(solution)/shard_map/ppermute | solution.py:20
  90.9 8.3 %collective-permute-start.28 = (s16[144,512]{1,0:T(8,128)(2,1)S(1)}, s16[144,512]{1,0:T(8,128)(2,1)S(1)}, u32[]{:S(2)}, u32[]{:S(2)}) collective-permute-start(s16[144,512]{1,0:T(8,128)(2,1)S(1)} %get-tuple-element.130), channel_id=1, source_target_pairs={{0,128},{32,160},{64,192},{96,224},{128,0},{160,32},{192,64},{224,... | collective-permute-start | bytes 442376 | tf_op jit(solution)/shard_map/ppermute | solution.py:20
  93.2 8.3 %collective-permute-start.29 = (s16[144,512]{1,0:T(8,128)(2,1)S(1)}, s16[144,512]{1,0:T(8,128)(2,1)S(1)}, u32[]{:S(2)}, u32[]{:S(2)}) collective-permute-start(s16[144,512]{1,0:T(8,128)(2,1)S(1)} %get-tuple-element.131), channel_id=1, source_target_pairs={{0,192},{32,224},{64,128},{96,160},{128,64},{160,96},{192,0},{224,... | collective-permute-start | bytes 442376 | tf_op jit(solution)/shard_map/ppermute | solution.py:20
  93.2 8.4 %collective-permute-start.30 = (s16[144,512]{1,0:T(8,128)(2,1)S(1)}, s16[144,512]{1,0:T(8,128)(2,1)S(1)}, u32[]{:S(2)}, u32[]{:S(2)}) collective-permute-start(s16[144,512]{1,0:T(8,128)(2,1)S(1)} %get-tuple-element.132), channel_id=1, source_target_pairs={{0,64},{32,96},{64,0},{96,32},{128,192},{160,224},{192,128},{224,1... | collective-permute-start | bytes 442376 | tf_op jit(solution)/shard_map/ppermute | solution.py:20
  102.4 8.4 %collective-permute-start.31 = (s16[80,512]{1,0:T(8,128)(2,1)S(1)}, s16[80,512]{1,0:T(8,128)(2,1)S(1)}, u32[]{:S(2)}, u32[]{:S(2)}) collective-permute-start(s16[80,512]{1,0:T(8,128)(2,1)S(1)} %get-tuple-element.134), channel_id=1, source_target_pairs={{0,32},{32,0},{64,96},{96,64},{128,160},{160,128},{192,224},{224,1... | collective-permute-start | bytes 245768 | tf_op jit(solution)/shard_map/ppermute | solution.py:20

commit v9 on v8

--- a/solution.py
+++ b/solution.py
@@ -121,10 +121,10 @@
     out_ref[...] = (own_ref[...] + unpack(m1_in) + unpack(m2_in) + unpack(m3_in)).astype(BF16)
 
 
-def join(first_ref, second_ref, out_ref):
-    rows = first_ref.shape[0]
-    out_ref[:rows, :] = first_ref[...]
-    out_ref[rows:, :] = second_ref[...]
+def join(p0_ref, p1_ref, p2_ref, p3_ref, out_ref):
+    rows = p0_ref.shape[0]
+    for i, ref in enumerate((p0_ref, p1_ref, p2_ref, p3_ref)):
+        out_ref[rows * i : rows * (i + 1), :] = ref[...]
 
 
 def gram_messages(here_ref, mine_ref, came_ref, own_ref, m1_ref, m2_ref, m3_ref, work_ref):
@@ -281,15 +281,14 @@
     )
 
     last = weights[0]
-    pieces, near, far, quarters = [None] * 2, [None] * 2, [None] * 2, [None] * 2
+    pieces = [None] * 2
     for s in both:
         own, last = call(last_sum, [((unit, width), BF16)], *came[s], after=[last], flag=True)
-        pieces[s] = own, xor_permute(own, "pw_z", 1)
-    for s in both:
-        own, last = call(join, [((2 * unit, width), BF16)], *pieces[s], after=[last], flag=True)
-        pieces[s] = own, xor_permute(own, "pw_z", 2)
-    for s in both:
-        quarters[s], last = call(join, [((4 * unit, width), BF16)], *pieces[s], after=[last], flag=True)
+        pieces[s] = [own] + [xor_permute(own, "pw_z", mask) for mask in (1, 2, 3)]
+    quarters, near, far = [None] * 2, [None] * 2, [None] * 2
+    last = [last]
+    for s in both:
+        quarters[s], *last = call(join, [((4 * unit, width), BF16)], *pieces[s], after=last, flag=s == 0)
         near[s], far[s] = xor_permute(quarters[s], "pw_x", 1), xor_permute(quarters[s], "pw_x", 3)
         near[s], far[s] = lax.optimization_barrier((near[s], far[s]))
     grams = gram_step(here, weights, quarters, [(0, 0, 0), (1, 0, 0)], [], 3_000_000_000)

time: 112 us -> 106 us (0.946)
  the two profiles are of different devices: /device:TPU:8 before, /device:TPU:32 now
where the time goes in v9:
time: 106 us; the launch traced here: 105 us
  starting transfers between devices  43.1 us (41%)
  waiting for transfers between devices  40.2 us (38%)
  Pallas kernels  19.7 us (19%)
  local copies, waits for them, and re-layouts  1.24 us (1%)
    ppermute x34, starting transfers between devices, xor_permute(): return lax.ppermute(value, axis, [(i, i ^ mask) for i in range(count)])  43.1 us
    ppermute x34, waiting for transfers between devices, xor_permute(): return lax.ppermute(value, axis, [(i, i ^ mask) for i in range(count)])  40.2 us
    pallas_call x22, Pallas kernels, call(): pl.pallas_call(kernel, out_shape=[jax.ShapeDtypeStruct(shape, dtype) for...  19.7 us
  transfers between devices with their start and end apart: 34, of which 22 were waited for; matrix products, arithmetic and copies ran while one was open for 0% of the time, Pallas kernels for 13%

profile of v9, /device:TPU:32, one launch (start us, length us, event | category | flops | bytes accessed | tf_op | source)
XLA Modules:
  0.0 105.1 jit_solution(14212500160805030082)
XLA Ops:
  0.7 1.2 %copy-done = bf16[1024,512]{1,0:T(8,128)(2,1)S(1)} copy-done((bf16[1024,512]{1,0:T(8,128)(2,1)S(1)}, bf16[1024,512]{1,0:T(8,128)(2,1)}, u32[]{:S(2)}) %copy-start) | copy-done | bytes 1048600
  2.0 4.2 %shard_map.73 = (f32[1032,512]{1,0:T(8,128)S(1)}, bf16[3072,1024]{1,0:T(8,128)(2,1)S(1)}, f32[8,128]{1,0:T(8,128)S(1)}) custom-call(s32[4]{0:T(128)S(1)} %pad_add_fusion.refs_0_, f32[1]{0:T(128)S(6)} %copy.8.refs_1_.refs_2_, bf16[4096,1024]{1,0:T(8,128)(2,1)} %refs_2_.2, bf16[1024,512]{1,0:T(8,128)(2,1)S(1)} %copy-done), custom_call_target="tpu_custom_call" | custom-call | flops 1073741824 | bytes 9437204 | tf_op jit(solution)/shard_map/pallas_call | solution.py:35
  6.3 2.3 %shard_map.74 = (f32[1024,512]{1,0:T(8,128)S(1)}, f32[1024,512]{1,0:T(8,128)S(1)}) custom-call(bf16[3072,1024]{1,0:T(8,128)(2,1)S(1)} %get-tuple-element.65.refs_0_, bf16[1024,512]{1,0:T(8,128)(2,1)S(1)} %copy-done, f32[8,128]{1,0:T(8,128)S(1)} %get-tuple-element.66.refs_2_), custom_call_target="tpu_custom_call" | custom-call | flops 2147483648 | bytes 7340032 | tf_op jit(solution)/shard_map/pallas_call | solution.py:35
  8.6 1.8 %collective-permute-done.refs_1_ = f32[1032,512]{1,0:T(8,128)S(1)} collective-permute-done((f32[1032,512]{1,0:T(8,128)S(1)}, f32[1032,512]{1,0:T(8,128)S(1)}, u32[]{:S(2)}, u32[]{:S(2)}) %collective-permute-start) | collective-permute-done | bytes 2113568 | tf_op jit(solution)/shard_map/ppermute | solution.py:20
  10.9 1.6 %collective-permute-start.4 = (s16[272,512]{1,0:T(8,128)(2,1)S(1)}, s16[272,512]{1,0:T(8,128)(2,1)S(1)}, u32[]{:S(2)}, u32[]{:S(2)}) collective-permute-start(s16[272,512]{1,0:T(8,128)(2,1)S(1)} %get-tuple-element.77), channel_id=1, source_target_pairs={{0,8},{8,0},{16,24},{24,16},{1,9},{9,1},{17,25},{25,17},{2,10},{10... | collective-permute-start | bytes 835592 | tf_op jit(solution)/shard_map/ppermute | solution.py:20
  12.5 2.1 %collective-permute-start.5 = (s16[272,512]{1,0:T(8,128)(2,1)S(1)}, s16[272,512]{1,0:T(8,128)(2,1)S(1)}, u32[]{:S(2)}, u32[]{:S(2)}) collective-permute-start(s16[272,512]{1,0:T(8,128)(2,1)S(1)} %get-tuple-element.78), channel_id=1, source_target_pairs={{0,24},{8,16},{16,8},{24,0},{1,25},{9,17},{17,9},{25,1},{2,26},{10... | collective-permute-start | bytes 835592 | tf_op jit(solution)/shard_map/ppermute | solution.py:20
  14.6 1.2 %shard_map.76.refs_0_ = f32[1024,512]{1,0:T(8,128)S(1)} custom-call(bf16[3072,1024]{1,0:T(8,128)(2,1)S(1)} %get-tuple-element.65.refs_0_, bf16[1024,512]{1,0:T(8,128)(2,1)S(1)} %copy-done, f32[8,128]{1,0:T(8,128)S(1)} %get-tuple-element.71.refs_2_), custom_call_target="tpu_custom_call" | custom-call | flops 1073741824 | bytes 7340032 | tf_op jit(solution)/shard_map/pallas_call | solution.py:35
  16.9 1.7 %collective-permute-start.3 = (s16[272,512]{1,0:T(8,128)(2,1)S(1)}, s16[272,512]{1,0:T(8,128)(2,1)S(1)}, u32[]{:S(2)}, u32[]{:S(2)}) collective-permute-start(s16[272,512]{1,0:T(8,128)(2,1)S(1)} %get-tuple-element.75), channel_id=1, source_target_pairs={{0,24},{8,16},{16,8},{24,0},{1,25},{9,17},{17,9},{25,1},{2,26},{10... | collective-permute-start | bytes 835592 | tf_op jit(solution)/shard_map/ppermute | solution.py:20
  18.6 1.9 %collective-permute-done.4.refs_1_ = s16[272,512]{1,0:T(8,128)(2,1)S(1)} collective-permute-done((s16[272,512]{1,0:T(8,128)(2,1)S(1)}, s16[272,512]{1,0:T(8,128)(2,1)S(1)}, u32[]{:S(2)}, u32[]{:S(2)}) %collective-permute-start.4) | collective-permute-done | bytes 278560 | tf_op jit(solution)/shard_map/ppermute | solution.py:20
  20.5 2.7 %collective-permute-done.5.refs_2_ = s16[272,512]{1,0:T(8,128)(2,1)S(1)} collective-permute-done((s16[272,512]{1,0:T(8,128)(2,1)S(1)}, s16[272,512]{1,0:T(8,128)(2,1)S(1)}, u32[]{:S(2)}, u32[]{:S(2)}) %collective-permute-start.5) | collective-permute-done | bytes 278560 | tf_op jit(solution)/shard_map/ppermute | solution.py:20
  23.5 2.2 %collective-permute-start.8 = (s16[144,512]{1,0:T(8,128)(2,1)S(1)}, s16[144,512]{1,0:T(8,128)(2,1)S(1)}, u32[]{:S(2)}, u32[]{:S(2)}) collective-permute-start(s16[144,512]{1,0:T(8,128)(2,1)S(1)} %get-tuple-element.84), channel_id=1, source_target_pairs={{0,24},{8,16},{16,8},{24,0},{1,25},{9,17},{17,9},{25,1},{2,26},{10... | collective-permute-start | bytes 442376 | tf_op jit(solution)/shard_map/ppermute | solution.py:20
  25.9 3.3 %collective-permute-done.3.refs_2_ = s16[272,512]{1,0:T(8,128)(2,1)S(1)} collective-permute-done((s16[272,512]{1,0:T(8,128)(2,1)S(1)}, s16[272,512]{1,0:T(8,128)(2,1)S(1)}, u32[]{:S(2)}, u32[]{:S(2)}) %collective-permute-start.3) | collective-permute-done | bytes 278560 | tf_op jit(solution)/shard_map/ppermute | solution.py:20
  29.5 2.2 %collective-permute-start.6 = (s16[144,512]{1,0:T(8,128)(2,1)S(1)}, s16[144,512]{1,0:T(8,128)(2,1)S(1)}, u32[]{:S(2)}, u32[]{:S(2)}) collective-permute-start(s16[144,512]{1,0:T(8,128)(2,1)S(1)} %get-tuple-element.81), channel_id=1, source_target_pairs={{0,24},{8,16},{16,8},{24,0},{1,25},{9,17},{17,9},{25,1},{2,26},{10... | collective-permute-start | bytes 442376 | tf_op jit(solution)/shard_map/ppermute | solution.py:20
  32.4 2.0 %collective-permute-start.13 = (s16[80,512]{1,0:T(8,128)(2,1)S(1)}, s16[80,512]{1,0:T(8,128)(2,1)S(1)}, u32[]{:S(2)}, u32[]{:S(2)}) collective-permute-start(s16[80,512]{1,0:T(8,128)(2,1)S(1)} %get-tuple-element.95), channel_id=1, source_target_pairs={{0,6},{2,4},{4,2},{6,0},{1,7},{3,5},{5,3},{7,1},{8,14},{10,12},{12... | collective-permute-start | bytes 245768 | tf_op jit(solution)/shard_map/ppermute | solution.py:20
  34.4 1.5 %collective-permute-start.14 = (s16[80,512]{1,0:T(8,128)(2,1)S(1)}, s16[80,512]{1,0:T(8,128)(2,1)S(1)}, u32[]{:S(2)}, u32[]{:S(2)}) collective-permute-start(s16[80,512]{1,0:T(8,128)(2,1)S(1)} %get-tuple-element.96), channel_id=1, source_target_pairs={{0,4},{2,6},{4,0},{6,2},{1,5},{3,7},{5,1},{7,3},{8,12},{10,14},{12... | collective-permute-start | bytes 245768 | tf_op jit(solution)/shard_map/ppermute | solution.py:20
  35.9 1.4 %collective-permute-start.15 = (s16[80,512]{1,0:T(8,128)(2,1)S(1)}, s16[80,512]{1,0:T(8,128)(2,1)S(1)}, u32[]{:S(2)}, u32[]{:S(2)}) collective-permute-start(s16[80,512]{1,0:T(8,128)(2,1)S(1)} %get-tuple-element.97), channel_id=1, source_target_pairs={{0,2},{2,0},{4,6},{6,4},{1,3},{3,1},{5,7},{7,5},{8,10},{10,8},{12,... | collective-permute-start | bytes 245768 | tf_op jit(solution)/shard_map/ppermute | solution.py:20
  37.2 0.7 shard_map.81
  38.0 1.7 %collective-permute-start.10 = (s16[80,512]{1,0:T(8,128)(2,1)S(1)}, s16[80,512]{1,0:T(8,128)(2,1)S(1)}, u32[]{:S(2)}, u32[]{:S(2)}) collective-permute-start(s16[80,512]{1,0:T(8,128)(2,1)S(1)} %get-tuple-element.91), channel_id=1, source_target_pairs={{0,6},{2,4},{4,2},{6,0},{1,7},{3,5},{5,3},{7,1},{8,14},{10,12},{12... | collective-permute-start | bytes 245768 | tf_op jit(solution)/shard_map/ppermute | solution.py:20
  39.7 1.6 %collective-permute-start.11 = (s16[80,512]{1,0:T(8,128)(2,1)S(1)}, s16[80,512]{1,0:T(8,128)(2,1)S(1)}, u32[]{:S(2)}, u32[]{:S(2)}) collective-permute-start(s16[80,512]{1,0:T(8,128)(2,1)S(1)} %get-tuple-element.92), channel_id=1, source_target_pairs={{0,4},{2,6},{4,0},{6,2},{1,5},{3,7},{5,1},{7,3},{8,12},{10,14},{12... | collective-permute-start | bytes 245768 | tf_op jit(solution)/shard_map/ppermute | solution.py:20
  42.7 0.9 shard_map.82
  43.5 2.7 %collective-permute-done.14.refs_2_ = s16[80,512]{1,0:T(8,128)(2,1)S(1)} collective-permute-done((s16[80,512]{1,0:T(8,128)(2,1)S(1)}, s16[80,512]{1,0:T(8,128)(2,1)S(1)}, u32[]{:S(2)}, u32[]{:S(2)}) %collective-permute-start.14) | collective-permute-done | bytes 81952 | tf_op jit(solution)/shard_map/ppermute | solution.py:20
  46.5 4.0 %collective-permute-start.20 = (bf16[64,512]{1,0:T(8,128)(2,1)S(1)}, bf16[64,512]{1,0:T(8,128)(2,1)S(1)}, u32[]{:S(2)}, u32[]{:S(2)}) collective-permute-start(bf16[64,512]{1,0:T(8,128)(2,1)S(1)} %get-tuple-element.100.refs_0_), channel_id=1, source_target_pairs={{0,4},{2,6},{4,0},{6,2},{1,5},{3,7},{5,1},{7,3},{8,12},{10,14},{12... | collective-permute-start | bytes 196616 | tf_op jit(solution)/shard_map/ppermute | solution.py:20
  50.4 1.4 %collective-permute-start.19 = (bf16[64,512]{1,0:T(8,128)(2,1)S(1)}, bf16[64,512]{1,0:T(8,128)(2,1)S(1)}, u32[]{:S(2)}, u32[]{:S(2)}) collective-permute-start(bf16[64,512]{1,0:T(8,128)(2,1)S(1)} %get-tuple-element.100.refs_0_), channel_id=1, source_target_pairs={{0,2},{2,0},{4,6},{6,4},{1,3},{3,1},{5,7},{7,5},{8,10},{10,8},{12,... | collective-permute-start | bytes 196616 | tf_op jit(solution)/shard_map/ppermute | solution.py:20
  51.9 1.6 %collective-permute-start.18 = (bf16[64,512]{1,0:T(8,128)(2,1)S(1)}, bf16[64,512]{1,0:T(8,128)(2,1)S(1)}, u32[]{:S(2)}, u32[]{:S(2)}) collective-permute-start(bf16[64,512]{1,0:T(8,128)(2,1)S(1)} %get-tuple-element.99.refs_0_), channel_id=1, source_target_pairs={{0,6},{2,4},{4,2},{6,0},{1,7},{3,5},{5,3},{7,1},{8,14},{10,12},{12... | collective-permute-start | bytes 196616 | tf_op jit(solution)/shard_map/ppermute | solution.py:20
  53.4 1.5 %collective-permute-start.17 = (bf16[64,512]{1,0:T(8,128)(2,1)S(1)}, bf16[64,512]{1,0:T(8,128)(2,1)S(1)}, u32[]{:S(2)}, u32[]{:S(2)}) collective-permute-start(bf16[64,512]{1,0:T(8,128)(2,1)S(1)} %get-tuple-element.99.refs_0_), channel_id=1, source_target_pairs={{0,4},{2,6},{4,0},{6,2},{1,5},{3,7},{5,1},{7,3},{8,12},{10,14},{12... | collective-permute-start | bytes 196616 | tf_op jit(solution)/shard_map/ppermute | solution.py:20
  55.0 1.4 %collective-permute-start.16 = (bf16[64,512]{1,0:T(8,128)(2,1)S(1)}, bf16[64,512]{1,0:T(8,128)(2,1)S(1)}, u32[]{:S(2)}, u32[]{:S(2)}) collective-permute-start(bf16[64,512]{1,0:T(8,128)(2,1)S(1)} %get-tuple-element.99.refs_0_), channel_id=1, source_target_pairs={{0,2},{2,0},{4,6},{6,4},{1,3},{3,1},{5,7},{7,5},{8,10},{10,8},{12,... | collective-permute-start | bytes 196616 | tf_op jit(solution)/shard_map/ppermute | solution.py:20
  56.5 0.8 collective-permute-done.19.refs_1_
  57.3 1.7 %collective-permute-start.27 = (bf16[256,512]{1,0:T(8,128)(2,1)S(1)}, bf16[256,512]{1,0:T(8,128)(2,1)S(1)}, u32[]{:S(2)}, u32[]{:S(2)}) collective-permute-start(bf16[256,512]{1,0:T(8,128)(2,1)S(1)} %get-tuple-element.106.refs_3_), channel_id=1, source_target_pairs={{0,24},{8,16},{16,8},{24,0},{1,25},{9,17},{17,9},{25,1},{2,26},{10... | collective-permute-start | bytes 786440 | tf_op jit(solution)/shard_map/ppermute | solution.py:20
  60.0 2.0 %collective-permute-start.23 = (bf16[256,512]{1,0:T(8,128)(2,1)S(1)}, bf16[256,512]{1,0:T(8,128)(2,1)S(1)}, u32[]{:S(2)}, u32[]{:S(2)}) collective-permute-start(bf16[256,512]{1,0:T(8,128)(2,1)S(1)} %shard_map.86.refs_4_), channel_id=1, source_target_pairs={{0,24},{8,16},{16,8},{24,0},{1,25},{9,17},{17,9},{25,1},{2,26},{10... | collective-permute-start | bytes 786440 | tf_op jit(solution)/shard_map/ppermute | solution.py:20
  62.5 1.3 %shard_map.87 = (f32[512,512]{1,0:T(8,128)S(1)}, f32[512,512]{1,0:T(8,128)S(1)}) custom-call(s32[4]{0:T(128)S(1)} %pad_add_fusion.refs_0_, f32[32,128]{1,0:T(8,128)S(1)} %get-tuple-element.89.refs_4_.refs_1_, f32[32,128]{1,0:T(8,128)S(1)} %get-tuple-element.104.refs_2_, bf16[256,512]{1,0:T(8,128)(2,1)S(1)} %get-tuple-element.106.refs_3_, ...), custom_call_target="tpu_custom_call" | custom-call | flops 3536870912 | bytes 557072 | tf_op jit(solution)/shard_map/pallas_call | solution.py:35
  63.8 3.4 %collective-permute-done.27.refs_4_ = bf16[256,512]{1,0:T(8,128)(2,1)S(1)} collective-permute-done((bf16[256,512]{1,0:T(8,128)(2,1)S(1)}, bf16[256,512]{1,0:T(8,128)(2,1)S(1)}, u32[]{:S(2)}, u32[]{:S(2)}) %collective-permute-start.27) | collective-permute-done | bytes 262176 | tf_op jit(solution)/shard_map/ppermute | solution.py:20
  67.2 0.9 collective-permute-done.26.refs_3_
  68.1 1.9 %collective-permute-done.23.refs_4_ = bf16[256,512]{1,0:T(8,128)(2,1)S(1)} collective-permute-done((bf16[256,512]{1,0:T(8,128)(2,1)S(1)}, bf16[256,512]{1,0:T(8,128)(2,1)S(1)}, u32[]{:S(2)}, u32[]{:S(2)}) %collective-permute-start.23) | collective-permute-done | bytes 262176 | tf_op jit(solution)/shard_map/ppermute | solution.py:20
  70.0 3.2 %collective-permute-done.22.refs_3_ = bf16[256,512]{1,0:T(8,128)(2,1)S(1)} collective-permute-done((bf16[256,512]{1,0:T(8,128)(2,1)S(1)}, bf16[256,512]{1,0:T(8,128)(2,1)S(1)}, u32[]{:S(2)}, u32[]{:S(2)}) %collective-permute-start.22) | collective-permute-done | bytes 262176 | tf_op jit(solution)/shard_map/ppermute | solution.py:20
  73.3 1.3 %collective-permute-start.24 = (bf16[256,512]{1,0:T(8,128)(2,1)S(1)}, bf16[256,512]{1,0:T(8,128)(2,1)S(1)}, u32[]{:S(2)}, u32[]{:S(2)}) collective-permute-start(bf16[256,512]{1,0:T(8,128)(2,1)S(1)} %collective-permute-done.22.refs_3_), channel_id=1, source_target_pairs={{0,24},{8,16},{16,8},{24,0},{1,25},{9,17},{17,9},{25,1},{2,26},{10... | collective-permute-start | bytes 786440 | tf_op jit(solution)/shard_map/ppermute | solution.py:20
  74.6 1.3 %shard_map.88 = (f32[512,512]{1,0:T(8,128)S(1)}, f32[512,512]{1,0:T(8,128)S(1)}) custom-call(s32[4]{0:T(128)S(1)} %pad_add_fusion.refs_0_, f32[32,128]{1,0:T(8,128)S(1)} %get-tuple-element.89.refs_4_.refs_1_, f32[32,128]{1,0:T(8,128)S(1)} %get-tuple-element.104.refs_2_, bf16[256,512]{1,0:T(8,128)(2,1)S(1)} %collective-permute-done.26.refs_3_, ...), custom_call_target="tpu_custom_call" | custom-call | flops 536870912 | bytes 2654224 | tf_op jit(solution)/shard_map/pallas_call | solution.py:35
  76.1 1.6 %shard_map.89 = (f32[512,512]{1,0:T(8,128)S(1)}, f32[512,512]{1,0:T(8,128)S(1)}) custom-call(s32[4]{0:T(128)S(1)} %pad_add_fusion.refs_0_, f32[32,128]{1,0:T(8,128)S(1)} %get-tuple-element.89.refs_4_.refs_1_, f32[32,128]{1,0:T(8,128)S(1)} %get-tuple-element.104.refs_2_, bf16[256,512]{1,0:T(8,128)(2,1)S(1)} %collective-permute-done.22.refs_3_, ...), custom_call_target="tpu_custom_call" | custom-call | flops 805306368 | bytes 2916368 | tf_op jit(solution)/shard_map/pallas_call | solution.py:35
  77.8 3.1 %collective-permute-done.24.refs_2_ = bf16[256,512]{1,0:T(8,128)(2,1)S(1)} collective-permute-done((bf16[256,512]{1,0:T(8,128)(2,1)S(1)}, bf16[256,512]{1,0:T(8,128)(2,1)S(1)}, u32[]{:S(2)}, u32[]{:S(2)}) %collective-permute-start.24) | collective-permute-done | bytes 262176 | tf_op jit(solution)/shard_map/ppermute | solution.py:20
  80.9 0.9 shard_map.90.refs_3_
  82.4 0.9 shard_map.91.refs_1_
  83.3 0.8 shard_map.92
  84.1 3.3 %collective-permute-start.30 = (s16[144,512]{1,0:T(8,128)(2,1)S(1)}, s16[144,512]{1,0:T(8,128)(2,1)S(1)}, u32[]{:S(2)}, u32[]{:S(2)}) collective-permute-start(s16[144,512]{1,0:T(8,128)(2,1)S(1)} %get-tuple-element.120), channel_id=1, source_target_pairs={{0,128},{32,160},{64,192},{96,224},{128,0},{160,32},{192,64},{224,... | collective-permute-start | bytes 442376 | tf_op jit(solution)/shard_map/ppermute | solution.py:20
  87.4 1.1 %collective-permute-start.31 = (s16[144,512]{1,0:T(8,128)(2,1)S(1)}, s16[144,512]{1,0:T(8,128)(2,1)S(1)}, u32[]{:S(2)}, u32[]{:S(2)}) collective-permute-start(s16[144,512]{1,0:T(8,128)(2,1)S(1)} %get-tuple-element.121), channel_id=1, source_target_pairs={{0,192},{32,224},{64,128},{96,160},{128,64},{160,96},{192,0},{224,... | collective-permute-start | bytes 442376 | tf_op jit(solution)/shard_map/ppermute | solution.py:20
  88.4 3.2 %collective-permute-done.30.refs_2_ = s16[144,512]{1,0:T(8,128)(2,1)S(1)} collective-permute-done((s16[144,512]{1,0:T(8,128)(2,1)S(1)}, s16[144,512]{1,0:T(8,128)(2,1)S(1)}, u32[]{:S(2)}, u32[]{:S(2)}) %collective-permute-start.30) | collective-permute-done | bytes 147488 | tf_op jit(solution)/shard_map/ppermute | solution.py:20
  91.6 3.1 %collective-permute-done.31.refs_3_ = s16[144,512]{1,0:T(8,128)(2,1)S(1)} collective-permute-done((s16[144,512]{1,0:T(8,128)(2,1)S(1)}, s16[144,512]{1,0:T(8,128)(2,1)S(1)}, u32[]{:S(2)}, u32[]{:S(2)}) %collective-permute-start.31) | collective-permute-done | bytes 147488 | tf_op jit(solution)/shard_map/ppermute | solution.py:20
  95.1 0.8 shard_map.93
  95.9 3.8 %collective-permute-start.33 = (s16[80,512]{1,0:T(8,128)(2,1)S(1)}, s16[80,512]{1,0:T(8,128)(2,1)S(1)}, u32[]{:S(2)}, u32[]{:S(2)}) collective-permute-start(s16[80,512]{1,0:T(8,128)(2,1)S(1)} %get-tuple-element.124), channel_id=1, source_target_pairs={{0,32},{32,0},{64,96},{96,64},{128,160},{160,128},{192,224},{224,1... | collective-permute-start | bytes 245768 | tf_op jit(solution)/shard_map/ppermute | solution.py:20
  99.6 4.8 %collective-permute-done.33.refs_1_ = s16[80,512]{1,0:T(8,128)(2,1)S(1)} collective-permute-done((s16[80,512]{1,0:T(8,128)(2,1)S(1)}, s16[80,512]{1,0:T(8,128)(2,1)S(1)}, u32[]{:S(2)}, u32[]{:S(2)}) %collective-permute-start.33) | collective-permute-done | bytes 81952 | tf_op jit(solution)/shard_map/ppermute | solution.py:20
  (54 shorter events, 8.5 us)
Async XLA Ops:
  0.7 1.2 %copy-start = (bf16[1024,512]{1,0:T(8,128)(2,1)S(1)}, bf16[1024,512]{1,0:T(8,128)(2,1)}, u32[]{:S(2)}) copy-start(bf16[1024,512]{1,0:T(8,128)(2,1)} %refs_1_.5) | copy-start | bytes 3145732
  6.2 4.3 %collective-permute-start = (f32[1032,512]{1,0:T(8,128)S(1)}, f32[1032,512]{1,0:T(8,128)S(1)}, u32[]{:S(2)}, u32[]{:S(2)}) collective-permute-start(f32[1032,512]{1,0:T(8,128)S(1)} %get-tuple-element.68), channel_id=1, source_target_pairs={{0,1},{1,0},{2,3},{3,2},{4,5},{5,4},{6,7},{7,6},{8,9},{9,8},{10,11... | collective-permute-start | bytes 6340616 | tf_op jit(solution)/shard_map/ppermute | solution.py:20
  10.4 5.4 %collective-permute-start.1 = (f32[1024,512]{1,0:T(8,128)S(1)}, f32[1024,512]{1,0:T(8,128)S(1)}, u32[]{:S(2)}, u32[]{:S(2)}) collective-permute-start(f32[1024,512]{1,0:T(8,128)S(1)} %get-tuple-element.72), channel_id=1, source_target_pairs={{0,1},{1,0},{2,3},{3,2},{4,5},{5,4},{6,7},{7,6},{8,9},{9,8},{10,11... | collective-permute-start | bytes 6291464 | tf_op jit(solution)/shard_map/ppermute | solution.py:20
  10.9 9.6 %collective-permute-start.4 = (s16[272,512]{1,0:T(8,128)(2,1)S(1)}, s16[272,512]{1,0:T(8,128)(2,1)S(1)}, u32[]{:S(2)}, u32[]{:S(2)}) collective-permute-start(s16[272,512]{1,0:T(8,128)(2,1)S(1)} %get-tuple-element.77), channel_id=1, source_target_pairs={{0,8},{8,0},{16,24},{24,16},{1,9},{9,1},{17,25},{25,17},{2,10},{10... | collective-permute-start | bytes 835592 | tf_op jit(solution)/shard_map/ppermute | solution.py:20
  12.5 10.7 %collective-permute-start.5 = (s16[272,512]{1,0:T(8,128)(2,1)S(1)}, s16[272,512]{1,0:T(8,128)(2,1)S(1)}, u32[]{:S(2)}, u32[]{:S(2)}) collective-permute-start(s16[272,512]{1,0:T(8,128)(2,1)S(1)} %get-tuple-element.78), channel_id=1, source_target_pairs={{0,24},{8,16},{16,8},{24,0},{1,25},{9,17},{17,9},{25,1},{2,26},{10... | collective-permute-start | bytes 835592 | tf_op jit(solution)/shard_map/ppermute | solution.py:20
  16.2 9.7 %collective-permute-start.2 = (s16[272,512]{1,0:T(8,128)(2,1)S(1)}, s16[272,512]{1,0:T(8,128)(2,1)S(1)}, u32[]{:S(2)}, u32[]{:S(2)}) collective-permute-start(s16[272,512]{1,0:T(8,128)(2,1)S(1)} %get-tuple-element.74), channel_id=1, source_target_pairs={{0,8},{8,0},{16,24},{24,16},{1,9},{9,1},{17,25},{25,17},{2,10},{10... | collective-permute-start | bytes 835592 | tf_op jit(solution)/shard_map/ppermute | solution.py:20
  16.9 12.3 %collective-permute-start.3 = (s16[272,512]{1,0:T(8,128)(2,1)S(1)}, s16[272,512]{1,0:T(8,128)(2,1)S(1)}, u32[]{:S(2)}, u32[]{:S(2)}) collective-permute-start(s16[272,512]{1,0:T(8,128)(2,1)S(1)} %get-tuple-element.75), channel_id=1, source_target_pairs={{0,24},{8,16},{16,8},{24,0},{1,25},{9,17},{17,9},{25,1},{2,26},{10... | collective-permute-start | bytes 835592 | tf_op jit(solution)/shard_map/ppermute | solution.py:20
  23.2 19.4 %copy-start.1 = (s32[4096]{0:T(1024)S(1)}, s32[4096]{0:T(1024)}, u32[]{:S(2)}) copy-start(s32[4096]{0:T(1024)} %param.12) | copy-start | bytes 49156
  23.2 19.4 %copy-start.2 = (s32[4096]{0:T(1024)S(1)}, s32[4096]{0:T(1024)}, u32[]{:S(2)}) copy-start(s32[4096]{0:T(1024)} %param.11) | copy-start | bytes 49156
  23.2 19.4 %copy-start.3 = (f32[2048]{0:T(1024)S(1)}, f32[2048]{0:T(1024)}, u32[]{:S(2)}) copy-start(f32[2048]{0:T(1024)} %param.10) | copy-start | bytes 24580
  23.2 19.4 %copy-start.4 = (f32[16]{0:T(128)S(1)}, f32[16]{0:T(128)}, u32[]{:S(2)}) copy-start(f32[16]{0:T(128)} %refs_1_.6) | copy-start | bytes 196
  23.5 8.2 %collective-permute-start.8 = (s16[144,512]{1,0:T(8,128)(2,1)S(1)}, s16[144,512]{1,0:T(8,128)(2,1)S(1)}, u32[]{:S(2)}, u32[]{:S(2)}) collective-permute-start(s16[144,512]{1,0:T(8,128)(2,1)S(1)} %get-tuple-element.84), channel_id=1, source_target_pairs={{0,24},{8,16},{16,8},{24,0},{1,25},{9,17},{17,9},{25,1},{2,26},{10... | collective-permute-start | bytes 442376 | tf_op jit(solution)/shard_map/ppermute | solution.py:20
  25.7 6.0 %collective-permute-start.9 = (s16[144,512]{1,0:T(8,128)(2,1)S(1)}, s16[144,512]{1,0:T(8,128)(2,1)S(1)}, u32[]{:S(2)}, u32[]{:S(2)}) collective-permute-start(s16[144,512]{1,0:T(8,128)(2,1)S(1)} %get-tuple-element.85), channel_id=1, source_target_pairs={{0,8},{8,0},{16,24},{24,16},{1,9},{9,1},{17,25},{25,17},{2,10},{10... | collective-permute-start | bytes 442376 | tf_op jit(solution)/shard_map/ppermute | solution.py:20
  29.5 7.8 %collective-permute-start.6 = (s16[144,512]{1,0:T(8,128)(2,1)S(1)}, s16[144,512]{1,0:T(8,128)(2,1)S(1)}, u32[]{:S(2)}, u32[]{:S(2)}) collective-permute-start(s16[144,512]{1,0:T(8,128)(2,1)S(1)} %get-tuple-element.81), channel_id=1, source_target_pairs={{0,24},{8,16},{16,8},{24,0},{1,25},{9,17},{17,9},{25,1},{2,26},{10... | collective-permute-start | bytes 442376 | tf_op jit(solution)/shard_map/ppermute | solution.py:20
  31.6 5.6 %collective-permute-start.7 = (s16[144,512]{1,0:T(8,128)(2,1)S(1)}, s16[144,512]{1,0:T(8,128)(2,1)S(1)}, u32[]{:S(2)}, u32[]{:S(2)}) collective-permute-start(s16[144,512]{1,0:T(8,128)(2,1)S(1)} %get-tuple-element.82), channel_id=1, source_target_pairs={{0,8},{8,0},{16,24},{24,16},{1,9},{9,1},{17,25},{25,17},{2,10},{10... | collective-permute-start | bytes 442376 | tf_op jit(solution)/shard_map/ppermute | solution.py:20
  32.4 9.6 %collective-permute-start.13 = (s16[80,512]{1,0:T(8,128)(2,1)S(1)}, s16[80,512]{1,0:T(8,128)(2,1)S(1)}, u32[]{:S(2)}, u32[]{:S(2)}) collective-permute-start(s16[80,512]{1,0:T(8,128)(2,1)S(1)} %get-tuple-element.95), channel_id=1, source_target_pairs={{0,6},{2,4},{4,2},{6,0},{1,7},{3,5},{5,3},{7,1},{8,14},{10,12},{12... | collective-permute-start | bytes 245768 | tf_op jit(solution)/shard_map/ppermute | solution.py:20
  34.4 11.9 %collective-permute-start.14 = (s16[80,512]{1,0:T(8,128)(2,1)S(1)}, s16[80,512]{1,0:T(8,128)(2,1)S(1)}, u32[]{:S(2)}, u32[]{:S(2)}) collective-permute-start(s16[80,512]{1,0:T(8,128)(2,1)S(1)} %get-tuple-element.96), channel_id=1, source_target_pairs={{0,4},{2,6},{4,0},{6,2},{1,5},{3,7},{5,1},{7,3},{8,12},{10,14},{12... | collective-permute-start | bytes 245768 | tf_op jit(solution)/shard_map/ppermute | solution.py:20
  35.9 10.4 %collective-permute-start.15 = (s16[80,512]{1,0:T(8,128)(2,1)S(1)}, s16[80,512]{1,0:T(8,128)(2,1)S(1)}, u32[]{:S(2)}, u32[]{:S(2)}) collective-permute-start(s16[80,512]{1,0:T(8,128)(2,1)S(1)} %get-tuple-element.97), channel_id=1, source_target_pairs={{0,2},{2,0},{4,6},{6,4},{1,3},{3,1},{5,7},{7,5},{8,10},{10,8},{12,... | collective-permute-start | bytes 245768 | tf_op jit(solution)/shard_map/ppermute | solution.py:20
  38.0 12.4 %collective-permute-start.10 = (s16[80,512]{1,0:T(8,128)(2,1)S(1)}, s16[80,512]{1,0:T(8,128)(2,1)S(1)}, u32[]{:S(2)}, u32[]{:S(2)}) collective-permute-start(s16[80,512]{1,0:T(8,128)(2,1)S(1)} %get-tuple-element.91), channel_id=1, source_target_pairs={{0,6},{2,4},{4,2},{6,0},{1,7},{3,5},{5,3},{7,1},{8,14},{10,12},{12... | collective-permute-start | bytes 245768 | tf_op jit(solution)/shard_map/ppermute | solution.py:20
  39.7 12.1 %collective-permute-start.11 = (s16[80,512]{1,0:T(8,128)(2,1)S(1)}, s16[80,512]{1,0:T(8,128)(2,1)S(1)}, u32[]{:S(2)}, u32[]{:S(2)}) collective-permute-start(s16[80,512]{1,0:T(8,128)(2,1)S(1)} %get-tuple-element.92), channel_id=1, source_target_pairs={{0,4},{2,6},{4,0},{6,2},{1,5},{3,7},{5,1},{7,3},{8,12},{10,14},{12... | collective-permute-start | bytes 245768 | tf_op jit(solution)/shard_map/ppermute | solution.py:20
  42.0 9.8 %collective-permute-start.12 = (s16[80,512]{1,0:T(8,128)(2,1)S(1)}, s16[80,512]{1,0:T(8,128)(2,1)S(1)}, u32[]{:S(2)}, u32[]{:S(2)}) collective-permute-start(s16[80,512]{1,0:T(8,128)(2,1)S(1)} %get-tuple-element.93), channel_id=1, source_target_pairs={{0,2},{2,0},{4,6},{6,4},{1,3},{3,1},{5,7},{7,5},{8,10},{10,8},{12,... | collective-permute-start | bytes 245768 | tf_op jit(solution)/shard_map/ppermute | solution.py:20
  46.4 8.6 %collective-permute-start.21 = (bf16[64,512]{1,0:T(8,128)(2,1)S(1)}, bf16[64,512]{1,0:T(8,128)(2,1)S(1)}, u32[]{:S(2)}, u32[]{:S(2)}) collective-permute-start(bf16[64,512]{1,0:T(8,128)(2,1)S(1)} %get-tuple-element.100.refs_0_), channel_id=1, source_target_pairs={{0,6},{2,4},{4,2},{6,0},{1,7},{3,5},{5,3},{7,1},{8,14},{10,12},{12... | collective-permute-start | bytes 196616 | tf_op jit(solution)/shard_map/ppermute | solution.py:20
  46.5 10.0 %collective-permute-start.20 = (bf16[64,512]{1,0:T(8,128)(2,1)S(1)}, bf16[64,512]{1,0:T(8,128)(2,1)S(1)}, u32[]{:S(2)}, u32[]{:S(2)}) collective-permute-start(bf16[64,512]{1,0:T(8,128)(2,1)S(1)} %get-tuple-element.100.refs_0_), channel_id=1, source_target_pairs={{0,4},{2,6},{4,0},{6,2},{1,5},{3,7},{5,1},{7,3},{8,12},{10,14},{12... | collective-permute-start | bytes 196616 | tf_op jit(solution)/shard_map/ppermute | solution.py:20
  50.4 6.8 %collective-permute-start.19 = (bf16[64,512]{1,0:T(8,128)(2,1)S(1)}, bf16[64,512]{1,0:T(8,128)(2,1)S(1)}, u32[]{:S(2)}, u32[]{:S(2)}) collective-permute-start(bf16[64,512]{1,0:T(8,128)(2,1)S(1)} %get-tuple-element.100.refs_0_), channel_id=1, source_target_pairs={{0,2},{2,0},{4,6},{6,4},{1,3},{3,1},{5,7},{7,5},{8,10},{10,8},{12,... | collective-permute-start | bytes 196616 | tf_op jit(solution)/shard_map/ppermute | solution.py:20
  51.9 7.6 %collective-permute-start.18 = (bf16[64,512]{1,0:T(8,128)(2,1)S(1)}, bf16[64,512]{1,0:T(8,128)(2,1)S(1)}, u32[]{:S(2)}, u32[]{:S(2)}) collective-permute-start(bf16[64,512]{1,0:T(8,128)(2,1)S(1)} %get-tuple-element.99.refs_0_), channel_id=1, source_target_pairs={{0,6},{2,4},{4,2},{6,0},{1,7},{3,5},{5,3},{7,1},{8,14},{10,12},{12... | collective-permute-start | bytes 196616 | tf_op jit(solution)/shard_map/ppermute | solution.py:20
  53.4 6.0 %collective-permute-start.17 = (bf16[64,512]{1,0:T(8,128)(2,1)S(1)}, bf16[64,512]{1,0:T(8,128)(2,1)S(1)}, u32[]{:S(2)}, u32[]{:S(2)}) collective-permute-start(bf16[64,512]{1,0:T(8,128)(2,1)S(1)} %get-tuple-element.99.refs_0_), channel_id=1, source_target_pairs={{0,4},{2,6},{4,0},{6,2},{1,5},{3,7},{5,1},{7,3},{8,12},{10,14},{12... | collective-permute-start | bytes 196616 | tf_op jit(solution)/shard_map/ppermute | solution.py:20
  55.0 5.0 %collective-permute-start.16 = (bf16[64,512]{1,0:T(8,128)(2,1)S(1)}, bf16[64,512]{1,0:T(8,128)(2,1)S(1)}, u32[]{:S(2)}, u32[]{:S(2)}) collective-permute-start(bf16[64,512]{1,0:T(8,128)(2,1)S(1)} %get-tuple-element.99.refs_0_), channel_id=1, source_target_pairs={{0,2},{2,0},{4,6},{6,4},{1,3},{3,1},{5,7},{7,5},{8,10},{10,8},{12,... | collective-permute-start | bytes 196616 | tf_op jit(solution)/shard_map/ppermute | solution.py:20
  57.3 10.0 %collective-permute-start.27 = (bf16[256,512]{1,0:T(8,128)(2,1)S(1)}, bf16[256,512]{1,0:T(8,128)(2,1)S(1)}, u32[]{:S(2)}, u32[]{:S(2)}) collective-permute-start(bf16[256,512]{1,0:T(8,128)(2,1)S(1)} %get-tuple-element.106.refs_3_), channel_id=1, source_target_pairs={{0,24},{8,16},{16,8},{24,0},{1,25},{9,17},{17,9},{25,1},{2,26},{10... | collective-permute-start | bytes 786440 | tf_op jit(solution)/shard_map/ppermute | solution.py:20
  59.0 9.1 %collective-permute-start.26 = (bf16[256,512]{1,0:T(8,128)(2,1)S(1)}, bf16[256,512]{1,0:T(8,128)(2,1)S(1)}, u32[]{:S(2)}, u32[]{:S(2)}) collective-permute-start(bf16[256,512]{1,0:T(8,128)(2,1)S(1)} %get-tuple-element.106.refs_3_), channel_id=1, source_target_pairs={{0,8},{8,0},{16,24},{24,16},{1,9},{9,1},{17,25},{25,17},{2,10},{10... | collective-permute-start | bytes 786440 | tf_op jit(solution)/shard_map/ppermute | solution.py:20
  60.0 10.0 %collective-permute-start.23 = (bf16[256,512]{1,0:T(8,128)(2,1)S(1)}, bf16[256,512]{1,0:T(8,128)(2,1)S(1)}, u32[]{:S(2)}, u32[]{:S(2)}) collective-permute-start(bf16[256,512]{1,0:T(8,128)(2,1)S(1)} %shard_map.86.refs_4_), channel_id=1, source_target_pairs={{0,24},{8,16},{16,8},{24,0},{1,25},{9,17},{17,9},{25,1},{2,26},{10... | collective-permute-start | bytes 786440 | tf_op jit(solution)/shard_map/ppermute | solution.py:20
  62.1 11.2 %collective-permute-start.22 = (bf16[256,512]{1,0:T(8,128)(2,1)S(1)}, bf16[256,512]{1,0:T(8,128)(2,1)S(1)}, u32[]{:S(2)}, u32[]{:S(2)}) collective-permute-start(bf16[256,512]{1,0:T(8,128)(2,1)S(1)} %shard_map.86.refs_4_), channel_id=1, source_target_pairs={{0,8},{8,0},{16,24},{24,16},{1,9},{9,1},{17,25},{25,17},{2,10},{10... | collective-permute-start | bytes 786440 | tf_op jit(solution)/shard_map/ppermute | solution.py:20
  68.1 8.0 %collective-permute-start.28 = (bf16[256,512]{1,0:T(8,128)(2,1)S(1)}, bf16[256,512]{1,0:T(8,128)(2,1)S(1)}, u32[]{:S(2)}, u32[]{:S(2)}) collective-permute-start(bf16[256,512]{1,0:T(8,128)(2,1)S(1)} %collective-permute-done.27.refs_4_), channel_id=1, source_target_pairs={{0,8},{8,0},{16,24},{24,16},{1,9},{9,1},{17,25},{25,17},{2,10},{10... | collective-permute-start | bytes 786440 | tf_op jit(solution)/shard_map/ppermute | solution.py:20
  73.3 7.6 %collective-permute-start.24 = (bf16[256,512]{1,0:T(8,128)(2,1)S(1)}, bf16[256,512]{1,0:T(8,128)(2,1)S(1)}, u32[]{:S(2)}, u32[]{:S(2)}) collective-permute-start(bf16[256,512]{1,0:T(8,128)(2,1)S(1)} %collective-permute-done.22.refs_3_), channel_id=1, source_target_pairs={{0,24},{8,16},{16,8},{24,0},{1,25},{9,17},{17,9},{25,1},{2,26},{10... | collective-permute-start | bytes 786440 | tf_op jit(solution)/shard_map/ppermute | solution.py:20
  77.7 5.6 %collective-permute-start.29 = (f32[512,512]{1,0:T(8,128)S(1)}, f32[512,512]{1,0:T(8,128)S(1)}, u32[]{:S(2)}, u32[]{:S(2)}) collective-permute-start(f32[512,512]{1,0:T(8,128)S(1)} %get-tuple-element.118), channel_id=1, source_target_pairs={{0,1},{1,0},{2,3},{3,2},{4,5},{5,4},{6,7},{7,6},{8,9},{9,8},{10,11... | collective-permute-start | bytes 3145736 | tf_op jit(solution)/shard_map/ppermute | solution.py:20
  80.9 1.5 %collective-permute-start.25 = (bf16[256,512]{1,0:T(8,128)(2,1)S(1)}, bf16[256,512]{1,0:T(8,128)(2,1)S(1)}, u32[]{:S(2)}, u32[]{:S(2)}) collective-permute-start(bf16[256,512]{1,0:T(8,128)(2,1)S(1)} %collective-permute-done.24.refs_2_), channel_id=1, source_target_pairs={{0,1},{1,0},{2,3},{3,2},{4,5},{5,4},{6,7},{7,6},{8,9},{9,8},{10,11... | collective-permute-start | bytes 786440 | tf_op jit(solution)/shard_map/ppermute | solution.py:20
  84.1 7.5 %collective-permute-start.30 = (s16[144,512]{1,0:T(8,128)(2,1)S(1)}, s16[144,512]{1,0:T(8,128)(2,1)S(1)}, u32[]{:S(2)}, u32[]{:S(2)}) collective-permute-start(s16[144,512]{1,0:T(8,128)(2,1)S(1)} %get-tuple-element.120), channel_id=1, source_target_pairs={{0,128},{32,160},{64,192},{96,224},{128,0},{160,32},{192,64},{224,... | collective-permute-start | bytes 442376 | tf_op jit(solution)/shard_map/ppermute | solution.py:20
  87.4 7.4 %collective-permute-start.31 = (s16[144,512]{1,0:T(8,128)(2,1)S(1)}, s16[144,512]{1,0:T(8,128)(2,1)S(1)}, u32[]{:S(2)}, u32[]{:S(2)}) collective-permute-start(s16[144,512]{1,0:T(8,128)(2,1)S(1)} %get-tuple-element.121), channel_id=1, source_target_pairs={{0,192},{32,224},{64,128},{96,160},{128,64},{160,96},{192,0},{224,... | collective-permute-start | bytes 442376 | tf_op jit(solution)/shard_map/ppermute | solution.py:20
  88.4 6.7 %collective-permute-start.32 = (s16[144,512]{1,0:T(8,128)(2,1)S(1)}, s16[144,512]{1,0:T(8,128)(2,1)S(1)}, u32[]{:S(2)}, u32[]{:S(2)}) collective-permute-start(s16[144,512]{1,0:T(8,128)(2,1)S(1)} %get-tuple-element.122), channel_id=1, source_target_pairs={{0,64},{32,96},{64,0},{96,32},{128,192},{160,224},{192,128},{224,1... | collective-permute-start | bytes 442376 | tf_op jit(solution)/shard_map/ppermute | solution.py:20
  95.9 8.5 %collective-permute-start.33 = (s16[80,512]{1,0:T(8,128)(2,1)S(1)}, s16[80,512]{1,0:T(8,128)(2,1)S(1)}, u32[]{:S(2)}, u32[]{:S(2)}) collective-permute-start(s16[80,512]{1,0:T(8,128)(2,1)S(1)} %get-tuple-element.124), channel_id=1, source_target_pairs={{0,32},{32,0},{64,96},{96,64},{128,160},{160,128},{192,224},{224,1... | collective-permute-start | bytes 245768 | tf_op jit(solution)/shard_map/ppermute | solution.py:20

commit v10 on v9

--- a/solution.py
+++ b/solution.py
@@ -127,8 +127,8 @@
         out_ref[rows * i : rows * (i + 1), :] = ref[...]
 
 
-def gram_messages(here_ref, mine_ref, came_ref, own_ref, m1_ref, m2_ref, m3_ref, work_ref):
-    work_ref[...] = mine_ref[...] + came_ref[...]
+def gram_messages(here_ref, mine_ref, came_ref, w_ref, other_ref, own_ref, m1_ref, m2_ref, m3_ref, work_ref):
+    work_ref[...] = mine_ref[...] + came_ref[...] + gram_terms(here_ref, other_ref, (1, 2, 1), [w_ref])[0]
     split_four(here_ref[3] // 2, work_ref, own_ref, (m1_ref, m2_ref, m3_ref), Y_ORDER)
 
 
@@ -160,6 +160,18 @@
         out_ref[...] = 2.0 * spacing / (spacing * spacing + freq * freq)
 
 
+def gram_terms(here_ref, ref, place, w_refs):
+    stream, owner, core = place
+    first = (lax.bitwise_xor(here_ref[2], core) * 4 + lax.bitwise_xor(here_ref[0], owner)) * 4 + stream * 2
+    parts = [[] for _ in w_refs]
+    for j in range(2):
+        rows = ref[128 * j : 128 * (j + 1), :].astype(F32).T
+        for part, w_ref in zip(parts, w_refs):
+            w = w_ref[pl.ds(first + lax.bitwise_xor(here_ref[1] // 2, j), 1), :]
+            part.append((rows * w).astype(BF16))
+    return [jnp.dot(jnp.concatenate(part, axis=1), ref[...], preferred_element_type=F32) for part in parts]
+
+
 def gram_step(here, weights, pieces, places, grams, extra=0):
     width = pieces[0].shape[1]
     count, kinds = len(pieces), len(weights)
@@ -167,16 +179,8 @@
     def body(here_ref, *refs):
         w_refs, came, before, out_refs = refs[:kinds], refs[kinds : kinds + count], refs[kinds + count : -kinds], refs[-kinds:]
         totals = [ref[...] for ref in before] or [None] * kinds
-        for ref, (stream, owner, core) in zip(came, places):
-            first = (lax.bitwise_xor(here_ref[2], core) * 4 + lax.bitwise_xor(here_ref[0], owner)) * 4 + stream * 2
-            parts = [[] for _ in range(kinds)]
-            for j in range(2):
-                rows = ref[128 * j : 128 * (j + 1), :].astype(F32).T
-                for part, w_ref in zip(parts, w_refs):
-                    w = w_ref[pl.ds(first + lax.bitwise_xor(here_ref[1] // 2, j), 1), :]
-                    part.append((rows * w).astype(BF16))
-            for kind, part in enumerate(parts):
-                term = jnp.dot(jnp.concatenate(part, axis=1), ref[...], preferred_element_type=F32)
+        for ref, place in zip(came, places):
+            for kind, term in enumerate(gram_terms(here_ref, ref, place, w_refs)):
                 totals[kind] = term if totals[kind] is None else totals[kind] + term
         for out_ref, total in zip(out_refs, totals):
             out_ref[...] = total
@@ -297,10 +301,10 @@
     grams = gram_step(here, weights, [near[0], far[0]], [(0, 1, 0), (0, 3, 0)], grams)
     grams = gram_step(here, weights, [near[1], far[1], across[0]], [(1, 1, 0), (1, 3, 0), (0, 2, 0)], grams)
     mine, theirs = grams
+    theirs, last = lax.optimization_barrier((theirs, across[1]))
+    other = xor_permute(last, "pw_c", 1)
     theirs = xor_permute(theirs, "pw_c", 1)
-    other = xor_permute(across[1], "pw_c", 1)
-    mine = gram_step(here, weights[:1], [across[1]], [(1, 2, 0)], [mine], 4_000_000_000)
-    mine = gram_step(here, weights[:1], [other], [(1, 2, 1)], mine, 5_000_000_000)[0]
+    mine = gram_step(here, weights[:1], [last], [(1, 2, 0)], [mine])[0]
 
     part = width // 4
     own, *out = call(
@@ -309,7 +313,9 @@
         here,
         mine,
         theirs,
-        specs=[SMEM] + [VMEM] * 2,
+        weights[0],
+        other,
+        specs=[SMEM] + [VMEM] * 4,
         scratch=[pltpu.VMEM((width, width), F32)],
     )
     came = [xor_permute(value, "pair", 2 * mask) for mask, value in zip(Y_ORDER, out)]

time: 106 us -> 107 us (level)
  waiting for transfers between devices: 40.2 us -> 41.3 us
    ppermute x34, waiting for transfers between devices: 40.2 us -> 41.3 us  [xor_permute(): return lax.ppermute(value, axis, [(i, i ^ mask) for i in range(count)])]
    pallas_call x22 -> x21, Pallas kernels: 19.7 us -> 19 us  [call(): pl.pallas_call(kernel, out_shape=[jax.ShapeDtypeStruct(shape, dtype) for...]
  transfers between devices with their start and end apart: 34 -> 34, of which waited for: 22 -> 22; matrix products, arithmetic and copies ran while one was open for 0% -> 0% of each run, Pallas kernels for 13% -> 12%
where the time goes in v10:
time: 107 us; the launch traced here: 106 us
  starting transfers between devices  43.5 us (41%)
  waiting for transfers between devices  41.3 us (39%)
  Pallas kernels  19 us (18%)
  local copies, waits for them, and re-layouts  1.24 us (1%)
    ppermute x34, starting transfers between devices, xor_permute(): return lax.ppermute(value, axis, [(i, i ^ mask) for i in range(count)])  43.5 us
    ppermute x34, waiting for transfers between devices, xor_permute(): return lax.ppermute(value, axis, [(i, i ^ mask) for i in range(count)])  41.3 us
    pallas_call x21, Pallas kernels, call(): pl.pallas_call(kernel, out_shape=[jax.ShapeDtypeStruct(shape, dtype) for...  19 us
  transfers between devices with their start and end apart: 34, of which 22 were waited for; matrix products, arithmetic and copies ran while one was open for 0% of the time, Pallas kernels for 12%

profile of v10, /device:TPU:32, one launch (start us, length us, event | category | flops | bytes accessed | tf_op | source)
XLA Modules:
  0.0 105.9 jit_solution(12535329964990633901)
XLA Ops:
  0.7 1.2 %copy-done = bf16[1024,512]{1,0:T(8,128)(2,1)S(1)} copy-done((bf16[1024,512]{1,0:T(8,128)(2,1)S(1)}, bf16[1024,512]{1,0:T(8,128)(2,1)}, u32[]{:S(2)}) %copy-start) | copy-done | bytes 1048600
  2.0 4.2 %shard_map.73 = (f32[1032,512]{1,0:T(8,128)S(1)}, bf16[3072,1024]{1,0:T(8,128)(2,1)S(1)}, f32[8,128]{1,0:T(8,128)S(1)}) custom-call(s32[4]{0:T(128)S(1)} %pad_add_fusion.refs_0_, f32[1]{0:T(128)S(6)} %copy.8.refs_1_.refs_2_, bf16[4096,1024]{1,0:T(8,128)(2,1)} %refs_2_.2, bf16[1024,512]{1,0:T(8,128)(2,1)S(1)} %copy-done), custom_call_target="tpu_custom_call" | custom-call | flops 1073741824 | bytes 9437204 | tf_op jit(solution)/shard_map/pallas_call | solution.py:35
  6.3 2.3 %shard_map.74 = (f32[1024,512]{1,0:T(8,128)S(1)}, f32[1024,512]{1,0:T(8,128)S(1)}) custom-call(bf16[3072,1024]{1,0:T(8,128)(2,1)S(1)} %get-tuple-element.67.refs_0_, bf16[1024,512]{1,0:T(8,128)(2,1)S(1)} %copy-done, f32[8,128]{1,0:T(8,128)S(1)} %get-tuple-element.68.refs_2_), custom_call_target="tpu_custom_call" | custom-call | flops 2147483648 | bytes 7340032 | tf_op jit(solution)/shard_map/pallas_call | solution.py:35
  8.6 1.8 %collective-permute-done.refs_1_ = f32[1032,512]{1,0:T(8,128)S(1)} collective-permute-done((f32[1032,512]{1,0:T(8,128)S(1)}, f32[1032,512]{1,0:T(8,128)S(1)}, u32[]{:S(2)}, u32[]{:S(2)}) %collective-permute-start) | collective-permute-done | bytes 2113568 | tf_op jit(solution)/shard_map/ppermute | solution.py:20
  10.9 1.6 %collective-permute-start.4 = (s16[272,512]{1,0:T(8,128)(2,1)S(1)}, s16[272,512]{1,0:T(8,128)(2,1)S(1)}, u32[]{:S(2)}, u32[]{:S(2)}) collective-permute-start(s16[272,512]{1,0:T(8,128)(2,1)S(1)} %get-tuple-element.79), channel_id=1, source_target_pairs={{0,8},{8,0},{16,24},{24,16},{1,9},{9,1},{17,25},{25,17},{2,10},{10... | collective-permute-start | bytes 835592 | tf_op jit(solution)/shard_map/ppermute | solution.py:20
  12.5 2.1 %collective-permute-start.5 = (s16[272,512]{1,0:T(8,128)(2,1)S(1)}, s16[272,512]{1,0:T(8,128)(2,1)S(1)}, u32[]{:S(2)}, u32[]{:S(2)}) collective-permute-start(s16[272,512]{1,0:T(8,128)(2,1)S(1)} %get-tuple-element.80), channel_id=1, source_target_pairs={{0,24},{8,16},{16,8},{24,0},{1,25},{9,17},{17,9},{25,1},{2,26},{10... | collective-permute-start | bytes 835592 | tf_op jit(solution)/shard_map/ppermute | solution.py:20
  14.6 1.2 %shard_map.76.refs_0_ = f32[1024,512]{1,0:T(8,128)S(1)} custom-call(bf16[3072,1024]{1,0:T(8,128)(2,1)S(1)} %get-tuple-element.67.refs_0_, bf16[1024,512]{1,0:T(8,128)(2,1)S(1)} %copy-done, f32[8,128]{1,0:T(8,128)S(1)} %get-tuple-element.73.refs_2_), custom_call_target="tpu_custom_call" | custom-call | flops 1073741824 | bytes 7340032 | tf_op jit(solution)/shard_map/pallas_call | solution.py:35
  16.9 1.7 %collective-permute-start.3 = (s16[272,512]{1,0:T(8,128)(2,1)S(1)}, s16[272,512]{1,0:T(8,128)(2,1)S(1)}, u32[]{:S(2)}, u32[]{:S(2)}) collective-permute-start(s16[272,512]{1,0:T(8,128)(2,1)S(1)} %get-tuple-element.77), channel_id=1, source_target_pairs={{0,24},{8,16},{16,8},{24,0},{1,25},{9,17},{17,9},{25,1},{2,26},{10... | collective-permute-start | bytes 835592 | tf_op jit(solution)/shard_map/ppermute | solution.py:20
  18.6 1.9 %collective-permute-done.4.refs_1_ = s16[272,512]{1,0:T(8,128)(2,1)S(1)} collective-permute-done((s16[272,512]{1,0:T(8,128)(2,1)S(1)}, s16[272,512]{1,0:T(8,128)(2,1)S(1)}, u32[]{:S(2)}, u32[]{:S(2)}) %collective-permute-start.4) | collective-permute-done | bytes 278560 | tf_op jit(solution)/shard_map/ppermute | solution.py:20
  20.5 2.7 %collective-permute-done.5.refs_2_ = s16[272,512]{1,0:T(8,128)(2,1)S(1)} collective-permute-done((s16[272,512]{1,0:T(8,128)(2,1)S(1)}, s16[272,512]{1,0:T(8,128)(2,1)S(1)}, u32[]{:S(2)}, u32[]{:S(2)}) %collective-permute-start.5) | collective-permute-done | bytes 278560 | tf_op jit(solution)/shard_map/ppermute | solution.py:20
  23.5 2.2 %collective-permute-start.8 = (s16[144,512]{1,0:T(8,128)(2,1)S(1)}, s16[144,512]{1,0:T(8,128)(2,1)S(1)}, u32[]{:S(2)}, u32[]{:S(2)}) collective-permute-start(s16[144,512]{1,0:T(8,128)(2,1)S(1)} %get-tuple-element.86), channel_id=1, source_target_pairs={{0,24},{8,16},{16,8},{24,0},{1,25},{9,17},{17,9},{25,1},{2,26},{10... | collective-permute-start | bytes 442376 | tf_op jit(solution)/shard_map/ppermute | solution.py:20
  25.9 3.3 %collective-permute-done.3.refs_2_ = s16[272,512]{1,0:T(8,128)(2,1)S(1)} collective-permute-done((s16[272,512]{1,0:T(8,128)(2,1)S(1)}, s16[272,512]{1,0:T(8,128)(2,1)S(1)}, u32[]{:S(2)}, u32[]{:S(2)}) %collective-permute-start.3) | collective-permute-done | bytes 278560 | tf_op jit(solution)/shard_map/ppermute | solution.py:20
  29.5 2.2 %collective-permute-start.6 = (s16[144,512]{1,0:T(8,128)(2,1)S(1)}, s16[144,512]{1,0:T(8,128)(2,1)S(1)}, u32[]{:S(2)}, u32[]{:S(2)}) collective-permute-start(s16[144,512]{1,0:T(8,128)(2,1)S(1)} %get-tuple-element.83), channel_id=1, source_target_pairs={{0,24},{8,16},{16,8},{24,0},{1,25},{9,17},{17,9},{25,1},{2,26},{10... | collective-permute-start | bytes 442376 | tf_op jit(solution)/shard_map/ppermute | solution.py:20
  31.6 0.7 shard_map.80
  32.4 2.0 %collective-permute-start.13 = (s16[80,512]{1,0:T(8,128)(2,1)S(1)}, s16[80,512]{1,0:T(8,128)(2,1)S(1)}, u32[]{:S(2)}, u32[]{:S(2)}) collective-permute-start(s16[80,512]{1,0:T(8,128)(2,1)S(1)} %get-tuple-element.98), channel_id=1, source_target_pairs={{0,6},{2,4},{4,2},{6,0},{1,7},{3,5},{5,3},{7,1},{8,14},{10,12},{12... | collective-permute-start | bytes 245768 | tf_op jit(solution)/shard_map/ppermute | solution.py:20
  34.4 1.5 %collective-permute-start.14 = (s16[80,512]{1,0:T(8,128)(2,1)S(1)}, s16[80,512]{1,0:T(8,128)(2,1)S(1)}, u32[]{:S(2)}, u32[]{:S(2)}) collective-permute-start(s16[80,512]{1,0:T(8,128)(2,1)S(1)} %get-tuple-element.99), channel_id=1, source_target_pairs={{0,4},{2,6},{4,0},{6,2},{1,5},{3,7},{5,1},{7,3},{8,12},{10,14},{12... | collective-permute-start | bytes 245768 | tf_op jit(solution)/shard_map/ppermute | solution.py:20
  35.9 1.4 %collective-permute-start.15 = (s16[80,512]{1,0:T(8,128)(2,1)S(1)}, s16[80,512]{1,0:T(8,128)(2,1)S(1)}, u32[]{:S(2)}, u32[]{:S(2)}) collective-permute-start(s16[80,512]{1,0:T(8,128)(2,1)S(1)} %get-tuple-element.100), channel_id=1, source_target_pairs={{0,2},{2,0},{4,6},{6,4},{1,3},{3,1},{5,7},{7,5},{8,10},{10,8},{12,... | collective-permute-start | bytes 245768 | tf_op jit(solution)/shard_map/ppermute | solution.py:20
  37.2 0.7 shard_map.81
  38.0 1.7 %collective-permute-start.10 = (s16[80,512]{1,0:T(8,128)(2,1)S(1)}, s16[80,512]{1,0:T(8,128)(2,1)S(1)}, u32[]{:S(2)}, u32[]{:S(2)}) collective-permute-start(s16[80,512]{1,0:T(8,128)(2,1)S(1)} %get-tuple-element.94), channel_id=1, source_target_pairs={{0,6},{2,4},{4,2},{6,0},{1,7},{3,5},{5,3},{7,1},{8,14},{10,12},{12... | collective-permute-start | bytes 245768 | tf_op jit(solution)/shard_map/ppermute | solution.py:20
  39.7 1.6 %collective-permute-start.11 = (s16[80,512]{1,0:T(8,128)(2,1)S(1)}, s16[80,512]{1,0:T(8,128)(2,1)S(1)}, u32[]{:S(2)}, u32[]{:S(2)}) collective-permute-start(s16[80,512]{1,0:T(8,128)(2,1)S(1)} %get-tuple-element.95), channel_id=1, source_target_pairs={{0,4},{2,6},{4,0},{6,2},{1,5},{3,7},{5,1},{7,3},{8,12},{10,14},{12... | collective-permute-start | bytes 245768 | tf_op jit(solution)/shard_map/ppermute | solution.py:20
  42.7 0.9 shard_map.82
  43.5 2.7 %collective-permute-done.14.refs_2_ = s16[80,512]{1,0:T(8,128)(2,1)S(1)} collective-permute-done((s16[80,512]{1,0:T(8,128)(2,1)S(1)}, s16[80,512]{1,0:T(8,128)(2,1)S(1)}, u32[]{:S(2)}, u32[]{:S(2)}) %collective-permute-start.14) | collective-permute-done | bytes 81952 | tf_op jit(solution)/shard_map/ppermute | solution.py:20
  46.4 4.0 %collective-permute-start.20 = (bf16[64,512]{1,0:T(8,128)(2,1)S(1)}, bf16[64,512]{1,0:T(8,128)(2,1)S(1)}, u32[]{:S(2)}, u32[]{:S(2)}) collective-permute-start(bf16[64,512]{1,0:T(8,128)(2,1)S(1)} %get-tuple-element.103.refs_0_), channel_id=1, source_target_pairs={{0,4},{2,6},{4,0},{6,2},{1,5},{3,7},{5,1},{7,3},{8,12},{10,14},{12... | collective-permute-start | bytes 196616 | tf_op jit(solution)/shard_map/ppermute | solution.py:20
  50.4 1.4 %collective-permute-start.19 = (bf16[64,512]{1,0:T(8,128)(2,1)S(1)}, bf16[64,512]{1,0:T(8,128)(2,1)S(1)}, u32[]{:S(2)}, u32[]{:S(2)}) collective-permute-start(bf16[64,512]{1,0:T(8,128)(2,1)S(1)} %get-tuple-element.103.refs_0_), channel_id=1, source_target_pairs={{0,2},{2,0},{4,6},{6,4},{1,3},{3,1},{5,7},{7,5},{8,10},{10,8},{12,... | collective-permute-start | bytes 196616 | tf_op jit(solution)/shard_map/ppermute | solution.py:20
  51.9 1.6 %collective-permute-start.18 = (bf16[64,512]{1,0:T(8,128)(2,1)S(1)}, bf16[64,512]{1,0:T(8,128)(2,1)S(1)}, u32[]{:S(2)}, u32[]{:S(2)}) collective-permute-start(bf16[64,512]{1,0:T(8,128)(2,1)S(1)} %get-tuple-element.102.refs_0_), channel_id=1, source_target_pairs={{0,6},{2,4},{4,2},{6,0},{1,7},{3,5},{5,3},{7,1},{8,14},{10,12},{12... | collective-permute-start | bytes 196616 | tf_op jit(solution)/shard_map/ppermute | solution.py:20
  53.4 1.5 %collective-permute-start.17 = (bf16[64,512]{1,0:T(8,128)(2,1)S(1)}, bf16[64,512]{1,0:T(8,128)(2,1)S(1)}, u32[]{:S(2)}, u32[]{:S(2)}) collective-permute-start(bf16[64,512]{1,0:T(8,128)(2,1)S(1)} %get-tuple-element.102.refs_0_), channel_id=1, source_target_pairs={{0,4},{2,6},{4,0},{6,2},{1,5},{3,7},{5,1},{7,3},{8,12},{10,14},{12... | collective-permute-start | bytes 196616 | tf_op jit(solution)/shard_map/ppermute | solution.py:20
  55.0 1.4 %collective-permute-start.16 = (bf16[64,512]{1,0:T(8,128)(2,1)S(1)}, bf16[64,512]{1,0:T(8,128)(2,1)S(1)}, u32[]{:S(2)}, u32[]{:S(2)}) collective-permute-start(bf16[64,512]{1,0:T(8,128)(2,1)S(1)} %get-tuple-element.102.refs_0_), channel_id=1, source_target_pairs={{0,2},{2,0},{4,6},{6,4},{1,3},{3,1},{5,7},{7,5},{8,10},{10,8},{12,... | collective-permute-start | bytes 196616 | tf_op jit(solution)/shard_map/ppermute | solution.py:20
  57.2 1.7 %collective-permute-start.25 = (bf16[256,512]{1,0:T(8,128)(2,1)S(1)}, bf16[256,512]{1,0:T(8,128)(2,1)S(1)}, u32[]{:S(2)}, u32[]{:S(2)}) collective-permute-start(bf16[256,512]{1,0:T(8,128)(2,1)S(1)} %get-tuple-element.108.refs_3_), channel_id=1, source_target_pairs={{0,24},{8,16},{16,8},{24,0},{1,25},{9,17},{17,9},{25,1},{2,26},{10... | collective-permute-start | bytes 786440 | tf_op jit(solution)/shard_map/ppermute | solution.py:20
  60.0 2.0 %collective-permute-start.23 = (bf16[256,512]{1,0:T(8,128)(2,1)S(1)}, bf16[256,512]{1,0:T(8,128)(2,1)S(1)}, u32[]{:S(2)}, u32[]{:S(2)}) collective-permute-start(bf16[256,512]{1,0:T(8,128)(2,1)S(1)} %shard_map.86.refs_4_), channel_id=1, source_target_pairs={{0,24},{8,16},{16,8},{24,0},{1,25},{9,17},{17,9},{25,1},{2,26},{10... | collective-permute-start | bytes 786440 | tf_op jit(solution)/shard_map/ppermute | solution.py:20
  62.5 1.3 %shard_map.87 = (f32[512,512]{1,0:T(8,128)S(1)}, f32[512,512]{1,0:T(8,128)S(1)}) custom-call(s32[4]{0:T(128)S(1)} %pad_add_fusion.refs_0_, f32[32,128]{1,0:T(8,128)S(1)} %get-tuple-element.91.refs_4_.refs_1_.refs_3_, f32[32,128]{1,0:T(8,128)S(1)} %get-tuple-element.92.refs_2_, bf16[256,512]{1,0:T(8,128)(2,1)S(1)} %get-tuple-element.108.refs_3_, ...), custom_call_target="tpu_custom_call" | custom-call | flops 3536870912 | bytes 557072 | tf_op jit(solution)/shard_map/pallas_call | solution.py:35
  63.8 3.4 %collective-permute-done.25.refs_4_ = bf16[256,512]{1,0:T(8,128)(2,1)S(1)} collective-permute-done((bf16[256,512]{1,0:T(8,128)(2,1)S(1)}, bf16[256,512]{1,0:T(8,128)(2,1)S(1)}, u32[]{:S(2)}, u32[]{:S(2)}) %collective-permute-start.25) | collective-permute-done | bytes 262176 | tf_op jit(solution)/shard_map/ppermute | solution.py:20
  67.2 0.9 collective-permute-done.24.refs_3_
  68.1 1.9 %collective-permute-done.23.refs_4_ = bf16[256,512]{1,0:T(8,128)(2,1)S(1)} collective-permute-done((bf16[256,512]{1,0:T(8,128)(2,1)S(1)}, bf16[256,512]{1,0:T(8,128)(2,1)S(1)}, u32[]{:S(2)}, u32[]{:S(2)}) %collective-permute-start.23) | collective-permute-done | bytes 262176 | tf_op jit(solution)/shard_map/ppermute | solution.py:20
  70.0 3.3 %collective-permute-done.22.refs_3_ = bf16[256,512]{1,0:T(8,128)(2,1)S(1)} collective-permute-done((bf16[256,512]{1,0:T(8,128)(2,1)S(1)}, bf16[256,512]{1,0:T(8,128)(2,1)S(1)}, u32[]{:S(2)}, u32[]{:S(2)}) %collective-permute-start.22) | collective-permute-done | bytes 262176 | tf_op jit(solution)/shard_map/ppermute | solution.py:20
  73.3 1.3 %collective-permute-start.27 = (bf16[256,512]{1,0:T(8,128)(2,1)S(1)}, bf16[256,512]{1,0:T(8,128)(2,1)S(1)}, u32[]{:S(2)}, u32[]{:S(2)}) collective-permute-start(bf16[256,512]{1,0:T(8,128)(2,1)S(1)} %collective-permute-done.22.refs_3_), channel_id=1, source_target_pairs={{0,24},{8,16},{16,8},{24,0},{1,25},{9,17},{17,9},{25,1},{2,26},{10... | collective-permute-start | bytes 786440 | tf_op jit(solution)/shard_map/ppermute | solution.py:20
  74.6 1.3 %shard_map.88 = (f32[512,512]{1,0:T(8,128)S(1)}, f32[512,512]{1,0:T(8,128)S(1)}) custom-call(s32[4]{0:T(128)S(1)} %pad_add_fusion.refs_0_, f32[32,128]{1,0:T(8,128)S(1)} %get-tuple-element.91.refs_4_.refs_1_.refs_3_, f32[32,128]{1,0:T(8,128)S(1)} %get-tuple-element.92.refs_2_, bf16[256,512]{1,0:T(8,128)(2,1)S(1)} %collective-permute-done.24.refs_3_, ...), custom_call_target="tpu_custom_call" | custom-call | flops 536870912 | bytes 2654224 | tf_op jit(solution)/shard_map/pallas_call | solution.py:35
  76.1 1.6 %shard_map.89 = (f32[512,512]{1,0:T(8,128)S(1)}, f32[512,512]{1,0:T(8,128)S(1)}) custom-call(s32[4]{0:T(128)S(1)} %pad_add_fusion.refs_0_, f32[32,128]{1,0:T(8,128)S(1)} %get-tuple-element.91.refs_4_.refs_1_.refs_3_, f32[32,128]{1,0:T(8,128)S(1)} %get-tuple-element.92.refs_2_, bf16[256,512]{1,0:T(8,128)(2,1)S(1)} %collective-permute-done.22.refs_3_, ...), custom_call_target="tpu_custom_call" | custom-call | flops 805306368 | bytes 2916368 | tf_op jit(solution)/shard_map/pallas_call | solution.py:35
  77.7 3.2 %collective-permute-done.27.refs_2_ = bf16[256,512]{1,0:T(8,128)(2,1)S(1)} collective-permute-done((bf16[256,512]{1,0:T(8,128)(2,1)S(1)}, bf16[256,512]{1,0:T(8,128)(2,1)S(1)}, u32[]{:S(2)}, u32[]{:S(2)}) %collective-permute-start.27) | collective-permute-done | bytes 262176 | tf_op jit(solution)/shard_map/ppermute | solution.py:20
  81.4 0.9 shard_map.90.refs_1_
  82.3 1.6 %collective-permute-done.29.refs_4_ = bf16[256,512]{1,0:T(8,128)(2,1)S(1)} collective-permute-done((bf16[256,512]{1,0:T(8,128)(2,1)S(1)}, bf16[256,512]{1,0:T(8,128)(2,1)S(1)}, u32[]{:S(2)}, u32[]{:S(2)}) %collective-permute-start.29) | collective-permute-done | bytes 262176 | tf_op jit(solution)/shard_map/ppermute | solution.py:20
  83.9 1.0 shard_map.91
  84.9 3.3 %collective-permute-start.30 = (s16[144,512]{1,0:T(8,128)(2,1)S(1)}, s16[144,512]{1,0:T(8,128)(2,1)S(1)}, u32[]{:S(2)}, u32[]{:S(2)}) collective-permute-start(s16[144,512]{1,0:T(8,128)(2,1)S(1)} %get-tuple-element.124), channel_id=1, source_target_pairs={{0,128},{32,160},{64,192},{96,224},{128,0},{160,32},{192,64},{224,... | collective-permute-start | bytes 442376 | tf_op jit(solution)/shard_map/ppermute | solution.py:20
  88.2 1.1 collective-permute-start.31
  89.3 3.2 %collective-permute-done.30.refs_2_ = s16[144,512]{1,0:T(8,128)(2,1)S(1)} collective-permute-done((s16[144,512]{1,0:T(8,128)(2,1)S(1)}, s16[144,512]{1,0:T(8,128)(2,1)S(1)}, u32[]{:S(2)}, u32[]{:S(2)}) %collective-permute-start.30) | collective-permute-done | bytes 147488 | tf_op jit(solution)/shard_map/ppermute | solution.py:20
  92.5 3.1 %collective-permute-done.31.refs_3_ = s16[144,512]{1,0:T(8,128)(2,1)S(1)} collective-permute-done((s16[144,512]{1,0:T(8,128)(2,1)S(1)}, s16[144,512]{1,0:T(8,128)(2,1)S(1)}, u32[]{:S(2)}, u32[]{:S(2)}) %collective-permute-start.31) | collective-permute-done | bytes 147488 | tf_op jit(solution)/shard_map/ppermute | solution.py:20
  95.9 0.8 shard_map.92
  96.7 3.7 %collective-permute-start.33 = (s16[80,512]{1,0:T(8,128)(2,1)S(1)}, s16[80,512]{1,0:T(8,128)(2,1)S(1)}, u32[]{:S(2)}, u32[]{:S(2)}) collective-permute-start(s16[80,512]{1,0:T(8,128)(2,1)S(1)} %get-tuple-element.128), channel_id=1, source_target_pairs={{0,32},{32,0},{64,96},{96,64},{128,160},{160,128},{192,224},{224,1... | collective-permute-start | bytes 245768 | tf_op jit(solution)/shard_map/ppermute | solution.py:20
  100.5 4.8 %collective-permute-done.33.refs_1_ = s16[80,512]{1,0:T(8,128)(2,1)S(1)} collective-permute-done((s16[80,512]{1,0:T(8,128)(2,1)S(1)}, s16[80,512]{1,0:T(8,128)(2,1)S(1)}, u32[]{:S(2)}, u32[]{:S(2)}) %collective-permute-start.33) | collective-permute-done | bytes 81952 | tf_op jit(solution)/shard_map/ppermute | solution.py:20
  (53 shorter events, 8.3 us)
Async XLA Ops:
  0.7 1.2 %copy-start = (bf16[1024,512]{1,0:T(8,128)(2,1)S(1)}, bf16[1024,512]{1,0:T(8,128)(2,1)}, u32[]{:S(2)}) copy-start(bf16[1024,512]{1,0:T(8,128)(2,1)} %refs_1_.5) | copy-start | bytes 3145732
  6.2 4.3 %collective-permute-start = (f32[1032,512]{1,0:T(8,128)S(1)}, f32[1032,512]{1,0:T(8,128)S(1)}, u32[]{:S(2)}, u32[]{:S(2)}) collective-permute-start(f32[1032,512]{1,0:T(8,128)S(1)} %get-tuple-element.70), channel_id=1, source_target_pairs={{0,1},{1,0},{2,3},{3,2},{4,5},{5,4},{6,7},{7,6},{8,9},{9,8},{10,11... | collective-permute-start | bytes 6340616 | tf_op jit(solution)/shard_map/ppermute | solution.py:20
  10.4 5.4 %collective-permute-start.1 = (f32[1024,512]{1,0:T(8,128)S(1)}, f32[1024,512]{1,0:T(8,128)S(1)}, u32[]{:S(2)}, u32[]{:S(2)}) collective-permute-start(f32[1024,512]{1,0:T(8,128)S(1)} %get-tuple-element.74), channel_id=1, source_target_pairs={{0,1},{1,0},{2,3},{3,2},{4,5},{5,4},{6,7},{7,6},{8,9},{9,8},{10,11... | collective-permute-start | bytes 6291464 | tf_op jit(solution)/shard_map/ppermute | solution.py:20
  10.9 9.6 %collective-permute-start.4 = (s16[272,512]{1,0:T(8,128)(2,1)S(1)}, s16[272,512]{1,0:T(8,128)(2,1)S(1)}, u32[]{:S(2)}, u32[]{:S(2)}) collective-permute-start(s16[272,512]{1,0:T(8,128)(2,1)S(1)} %get-tuple-element.79), channel_id=1, source_target_pairs={{0,8},{8,0},{16,24},{24,16},{1,9},{9,1},{17,25},{25,17},{2,10},{10... | collective-permute-start | bytes 835592 | tf_op jit(solution)/shard_map/ppermute | solution.py:20
  12.5 10.7 %collective-permute-start.5 = (s16[272,512]{1,0:T(8,128)(2,1)S(1)}, s16[272,512]{1,0:T(8,128)(2,1)S(1)}, u32[]{:S(2)}, u32[]{:S(2)}) collective-permute-start(s16[272,512]{1,0:T(8,128)(2,1)S(1)} %get-tuple-element.80), channel_id=1, source_target_pairs={{0,24},{8,16},{16,8},{24,0},{1,25},{9,17},{17,9},{25,1},{2,26},{10... | collective-permute-start | bytes 835592 | tf_op jit(solution)/shard_map/ppermute | solution.py:20
  16.2 9.7 %collective-permute-start.2 = (s16[272,512]{1,0:T(8,128)(2,1)S(1)}, s16[272,512]{1,0:T(8,128)(2,1)S(1)}, u32[]{:S(2)}, u32[]{:S(2)}) collective-permute-start(s16[272,512]{1,0:T(8,128)(2,1)S(1)} %get-tuple-element.76), channel_id=1, source_target_pairs={{0,8},{8,0},{16,24},{24,16},{1,9},{9,1},{17,25},{25,17},{2,10},{10... | collective-permute-start | bytes 835592 | tf_op jit(solution)/shard_map/ppermute | solution.py:20
  16.9 12.3 %collective-permute-start.3 = (s16[272,512]{1,0:T(8,128)(2,1)S(1)}, s16[272,512]{1,0:T(8,128)(2,1)S(1)}, u32[]{:S(2)}, u32[]{:S(2)}) collective-permute-start(s16[272,512]{1,0:T(8,128)(2,1)S(1)} %get-tuple-element.77), channel_id=1, source_target_pairs={{0,24},{8,16},{16,8},{24,0},{1,25},{9,17},{17,9},{25,1},{2,26},{10... | collective-permute-start | bytes 835592 | tf_op jit(solution)/shard_map/ppermute | solution.py:20
  23.2 19.4 %copy-start.1 = (s32[4096]{0:T(1024)S(1)}, s32[4096]{0:T(1024)}, u32[]{:S(2)}) copy-start(s32[4096]{0:T(1024)} %param.12) | copy-start | bytes 49156
  23.2 19.4 %copy-start.2 = (s32[4096]{0:T(1024)S(1)}, s32[4096]{0:T(1024)}, u32[]{:S(2)}) copy-start(s32[4096]{0:T(1024)} %param.11) | copy-start | bytes 49156
  23.2 19.4 %copy-start.3 = (f32[2048]{0:T(1024)S(1)}, f32[2048]{0:T(1024)}, u32[]{:S(2)}) copy-start(f32[2048]{0:T(1024)} %param.10) | copy-start | bytes 24580
  23.2 19.4 %copy-start.4 = (f32[16]{0:T(128)S(1)}, f32[16]{0:T(128)}, u32[]{:S(2)}) copy-start(f32[16]{0:T(128)} %refs_1_.6) | copy-start | bytes 196
  23.5 8.2 %collective-permute-start.8 = (s16[144,512]{1,0:T(8,128)(2,1)S(1)}, s16[144,512]{1,0:T(8,128)(2,1)S(1)}, u32[]{:S(2)}, u32[]{:S(2)}) collective-permute-start(s16[144,512]{1,0:T(8,128)(2,1)S(1)} %get-tuple-element.86), channel_id=1, source_target_pairs={{0,24},{8,16},{16,8},{24,0},{1,25},{9,17},{17,9},{25,1},{2,26},{10... | collective-permute-start | bytes 442376 | tf_op jit(solution)/shard_map/ppermute | solution.py:20
  25.7 6.0 %collective-permute-start.9 = (s16[144,512]{1,0:T(8,128)(2,1)S(1)}, s16[144,512]{1,0:T(8,128)(2,1)S(1)}, u32[]{:S(2)}, u32[]{:S(2)}) collective-permute-start(s16[144,512]{1,0:T(8,128)(2,1)S(1)} %get-tuple-element.87), channel_id=1, source_target_pairs={{0,8},{8,0},{16,24},{24,16},{1,9},{9,1},{17,25},{25,17},{2,10},{10... | collective-permute-start | bytes 442376 | tf_op jit(solution)/shard_map/ppermute | solution.py:20
  29.5 7.8 %collective-permute-start.6 = (s16[144,512]{1,0:T(8,128)(2,1)S(1)}, s16[144,512]{1,0:T(8,128)(2,1)S(1)}, u32[]{:S(2)}, u32[]{:S(2)}) collective-permute-start(s16[144,512]{1,0:T(8,128)(2,1)S(1)} %get-tuple-element.83), channel_id=1, source_target_pairs={{0,24},{8,16},{16,8},{24,0},{1,25},{9,17},{17,9},{25,1},{2,26},{10... | collective-permute-start | bytes 442376 | tf_op jit(solution)/shard_map/ppermute | solution.py:20
  31.6 5.6 %collective-permute-start.7 = (s16[144,512]{1,0:T(8,128)(2,1)S(1)}, s16[144,512]{1,0:T(8,128)(2,1)S(1)}, u32[]{:S(2)}, u32[]{:S(2)}) collective-permute-start(s16[144,512]{1,0:T(8,128)(2,1)S(1)} %get-tuple-element.84), channel_id=1, source_target_pairs={{0,8},{8,0},{16,24},{24,16},{1,9},{9,1},{17,25},{25,17},{2,10},{10... | collective-permute-start | bytes 442376 | tf_op jit(solution)/shard_map/ppermute | solution.py:20
  32.4 9.6 %collective-permute-start.13 = (s16[80,512]{1,0:T(8,128)(2,1)S(1)}, s16[80,512]{1,0:T(8,128)(2,1)S(1)}, u32[]{:S(2)}, u32[]{:S(2)}) collective-permute-start(s16[80,512]{1,0:T(8,128)(2,1)S(1)} %get-tuple-element.98), channel_id=1, source_target_pairs={{0,6},{2,4},{4,2},{6,0},{1,7},{3,5},{5,3},{7,1},{8,14},{10,12},{12... | collective-permute-start | bytes 245768 | tf_op jit(solution)/shard_map/ppermute | solution.py:20
  34.4 11.9 %collective-permute-start.14 = (s16[80,512]{1,0:T(8,128)(2,1)S(1)}, s16[80,512]{1,0:T(8,128)(2,1)S(1)}, u32[]{:S(2)}, u32[]{:S(2)}) collective-permute-start(s16[80,512]{1,0:T(8,128)(2,1)S(1)} %get-tuple-element.99), channel_id=1, source_target_pairs={{0,4},{2,6},{4,0},{6,2},{1,5},{3,7},{5,1},{7,3},{8,12},{10,14},{12... | collective-permute-start | bytes 245768 | tf_op jit(solution)/shard_map/ppermute | solution.py:20
  35.9 10.4 %collective-permute-start.15 = (s16[80,512]{1,0:T(8,128)(2,1)S(1)}, s16[80,512]{1,0:T(8,128)(2,1)S(1)}, u32[]{:S(2)}, u32[]{:S(2)}) collective-permute-start(s16[80,512]{1,0:T(8,128)(2,1)S(1)} %get-tuple-element.100), channel_id=1, source_target_pairs={{0,2},{2,0},{4,6},{6,4},{1,3},{3,1},{5,7},{7,5},{8,10},{10,8},{12,... | collective-permute-start | bytes 245768 | tf_op jit(solution)/shard_map/ppermute | solution.py:20
  38.0 12.4 %collective-permute-start.10 = (s16[80,512]{1,0:T(8,128)(2,1)S(1)}, s16[80,512]{1,0:T(8,128)(2,1)S(1)}, u32[]{:S(2)}, u32[]{:S(2)}) collective-permute-start(s16[80,512]{1,0:T(8,128)(2,1)S(1)} %get-tuple-element.94), channel_id=1, source_target_pairs={{0,6},{2,4},{4,2},{6,0},{1,7},{3,5},{5,3},{7,1},{8,14},{10,12},{12... | collective-permute-start | bytes 245768 | tf_op jit(solution)/shard_map/ppermute | solution.py:20
  39.7 12.1 %collective-permute-start.11 = (s16[80,512]{1,0:T(8,128)(2,1)S(1)}, s16[80,512]{1,0:T(8,128)(2,1)S(1)}, u32[]{:S(2)}, u32[]{:S(2)}) collective-permute-start(s16[80,512]{1,0:T(8,128)(2,1)S(1)} %get-tuple-element.95), channel_id=1, source_target_pairs={{0,4},{2,6},{4,0},{6,2},{1,5},{3,7},{5,1},{7,3},{8,12},{10,14},{12... | collective-permute-start | bytes 245768 | tf_op jit(solution)/shard_map/ppermute | solution.py:20
  42.0 9.8 %collective-permute-start.12 = (s16[80,512]{1,0:T(8,128)(2,1)S(1)}, s16[80,512]{1,0:T(8,128)(2,1)S(1)}, u32[]{:S(2)}, u32[]{:S(2)}) collective-permute-start(s16[80,512]{1,0:T(8,128)(2,1)S(1)} %get-tuple-element.96), channel_id=1, source_target_pairs={{0,2},{2,0},{4,6},{6,4},{1,3},{3,1},{5,7},{7,5},{8,10},{10,8},{12,... | collective-permute-start | bytes 245768 | tf_op jit(solution)/shard_map/ppermute | solution.py:20
  46.3 8.6 %collective-permute-start.21 = (bf16[64,512]{1,0:T(8,128)(2,1)S(1)}, bf16[64,512]{1,0:T(8,128)(2,1)S(1)}, u32[]{:S(2)}, u32[]{:S(2)}) collective-permute-start(bf16[64,512]{1,0:T(8,128)(2,1)S(1)} %get-tuple-element.103.refs_0_), channel_id=1, source_target_pairs={{0,6},{2,4},{4,2},{6,0},{1,7},{3,5},{5,3},{7,1},{8,14},{10,12},{12... | collective-permute-start | bytes 196616 | tf_op jit(solution)/shard_map/ppermute | solution.py:20
  46.4 10.0 %collective-permute-start.20 = (bf16[64,512]{1,0:T(8,128)(2,1)S(1)}, bf16[64,512]{1,0:T(8,128)(2,1)S(1)}, u32[]{:S(2)}, u32[]{:S(2)}) collective-permute-start(bf16[64,512]{1,0:T(8,128)(2,1)S(1)} %get-tuple-element.103.refs_0_), channel_id=1, source_target_pairs={{0,4},{2,6},{4,0},{6,2},{1,5},{3,7},{5,1},{7,3},{8,12},{10,14},{12... | collective-permute-start | bytes 196616 | tf_op jit(solution)/shard_map/ppermute | solution.py:20
  50.4 6.8 %collective-permute-start.19 = (bf16[64,512]{1,0:T(8,128)(2,1)S(1)}, bf16[64,512]{1,0:T(8,128)(2,1)S(1)}, u32[]{:S(2)}, u32[]{:S(2)}) collective-permute-start(bf16[64,512]{1,0:T(8,128)(2,1)S(1)} %get-tuple-element.103.refs_0_), channel_id=1, source_target_pairs={{0,2},{2,0},{4,6},{6,4},{1,3},{3,1},{5,7},{7,5},{8,10},{10,8},{12,... | collective-permute-start | bytes 196616 | tf_op jit(solution)/shard_map/ppermute | solution.py:20
  51.9 7.6 %collective-permute-start.18 = (bf16[64,512]{1,0:T(8,128)(2,1)S(1)}, bf16[64,512]{1,0:T(8,128)(2,1)S(1)}, u32[]{:S(2)}, u32[]{:S(2)}) collective-permute-start(bf16[64,512]{1,0:T(8,128)(2,1)S(1)} %get-tuple-element.102.refs_0_), channel_id=1, source_target_pairs={{0,6},{2,4},{4,2},{6,0},{1,7},{3,5},{5,3},{7,1},{8,14},{10,12},{12... | collective-permute-start | bytes 196616 | tf_op jit(solution)/shard_map/ppermute | solution.py:20
  53.4 6.0 %collective-permute-start.17 = (bf16[64,512]{1,0:T(8,128)(2,1)S(1)}, bf16[64,512]{1,0:T(8,128)(2,1)S(1)}, u32[]{:S(2)}, u32[]{:S(2)}) collective-permute-start(bf16[64,512]{1,0:T(8,128)(2,1)S(1)} %get-tuple-element.102.refs_0_), channel_id=1, source_target_pairs={{0,4},{2,6},{4,0},{6,2},{1,5},{3,7},{5,1},{7,3},{8,12},{10,14},{12... | collective-permute-start | bytes 196616 | tf_op jit(solution)/shard_map/ppermute | solution.py:20
  55.0 5.0 %collective-permute-start.16 = (bf16[64,512]{1,0:T(8,128)(2,1)S(1)}, bf16[64,512]{1,0:T(8,128)(2,1)S(1)}, u32[]{:S(2)}, u32[]{:S(2)}) collective-permute-start(bf16[64,512]{1,0:T(8,128)(2,1)S(1)} %get-tuple-element.102.refs_0_), channel_id=1, source_target_pairs={{0,2},{2,0},{4,6},{6,4},{1,3},{3,1},{5,7},{7,5},{8,10},{10,8},{12,... | collective-permute-start | bytes 196616 | tf_op jit(solution)/shard_map/ppermute | solution.py:20
  57.2 10.0 %collective-permute-start.25 = (bf16[256,512]{1,0:T(8,128)(2,1)S(1)}, bf16[256,512]{1,0:T(8,128)(2,1)S(1)}, u32[]{:S(2)}, u32[]{:S(2)}) collective-permute-start(bf16[256,512]{1,0:T(8,128)(2,1)S(1)} %get-tuple-element.108.refs_3_), channel_id=1, source_target_pairs={{0,24},{8,16},{16,8},{24,0},{1,25},{9,17},{17,9},{25,1},{2,26},{10... | collective-permute-start | bytes 786440 | tf_op jit(solution)/shard_map/ppermute | solution.py:20
  59.0 9.1 %collective-permute-start.24 = (bf16[256,512]{1,0:T(8,128)(2,1)S(1)}, bf16[256,512]{1,0:T(8,128)(2,1)S(1)}, u32[]{:S(2)}, u32[]{:S(2)}) collective-permute-start(bf16[256,512]{1,0:T(8,128)(2,1)S(1)} %get-tuple-element.108.refs_3_), channel_id=1, source_target_pairs={{0,8},{8,0},{16,24},{24,16},{1,9},{9,1},{17,25},{25,17},{2,10},{10... | collective-permute-start | bytes 786440 | tf_op jit(solution)/shard_map/ppermute | solution.py:20
  60.0 10.0 %collective-permute-start.23 = (bf16[256,512]{1,0:T(8,128)(2,1)S(1)}, bf16[256,512]{1,0:T(8,128)(2,1)S(1)}, u32[]{:S(2)}, u32[]{:S(2)}) collective-permute-start(bf16[256,512]{1,0:T(8,128)(2,1)S(1)} %shard_map.86.refs_4_), channel_id=1, source_target_pairs={{0,24},{8,16},{16,8},{24,0},{1,25},{9,17},{17,9},{25,1},{2,26},{10... | collective-permute-start | bytes 786440 | tf_op jit(solution)/shard_map/ppermute | solution.py:20
  62.1 11.2 %collective-permute-start.22 = (bf16[256,512]{1,0:T(8,128)(2,1)S(1)}, bf16[256,512]{1,0:T(8,128)(2,1)S(1)}, u32[]{:S(2)}, u32[]{:S(2)}) collective-permute-start(bf16[256,512]{1,0:T(8,128)(2,1)S(1)} %shard_map.86.refs_4_), channel_id=1, source_target_pairs={{0,8},{8,0},{16,24},{24,16},{1,9},{9,1},{17,25},{25,17},{2,10},{10... | collective-permute-start | bytes 786440 | tf_op jit(solution)/shard_map/ppermute | solution.py:20
  68.1 8.0 %collective-permute-start.26 = (bf16[256,512]{1,0:T(8,128)(2,1)S(1)}, bf16[256,512]{1,0:T(8,128)(2,1)S(1)}, u32[]{:S(2)}, u32[]{:S(2)}) collective-permute-start(bf16[256,512]{1,0:T(8,128)(2,1)S(1)} %collective-permute-done.25.refs_4_), channel_id=1, source_target_pairs={{0,8},{8,0},{16,24},{24,16},{1,9},{9,1},{17,25},{25,17},{2,10},{10... | collective-permute-start | bytes 786440 | tf_op jit(solution)/shard_map/ppermute | solution.py:20
  73.3 7.6 %collective-permute-start.27 = (bf16[256,512]{1,0:T(8,128)(2,1)S(1)}, bf16[256,512]{1,0:T(8,128)(2,1)S(1)}, u32[]{:S(2)}, u32[]{:S(2)}) collective-permute-start(bf16[256,512]{1,0:T(8,128)(2,1)S(1)} %collective-permute-done.22.refs_3_), channel_id=1, source_target_pairs={{0,24},{8,16},{16,8},{24,0},{1,25},{9,17},{17,9},{25,1},{2,26},{10... | collective-permute-start | bytes 786440 | tf_op jit(solution)/shard_map/ppermute | solution.py:20
  80.9 3.0 %collective-permute-start.28 = (f32[512,512]{1,0:T(8,128)S(1)}, f32[512,512]{1,0:T(8,128)S(1)}, u32[]{:S(2)}, u32[]{:S(2)}) collective-permute-start(f32[512,512]{1,0:T(8,128)S(1)} %get-tuple-element.122), channel_id=1, source_target_pairs={{0,1},{1,0},{2,3},{3,2},{4,5},{5,4},{6,7},{7,6},{8,9},{9,8},{10,11... | collective-permute-start | bytes 3145736 | tf_op jit(solution)/shard_map/ppermute | solution.py:20
  80.9 3.0 %collective-permute-start.29 = (bf16[256,512]{1,0:T(8,128)(2,1)S(1)}, bf16[256,512]{1,0:T(8,128)(2,1)S(1)}, u32[]{:S(2)}, u32[]{:S(2)}) collective-permute-start(bf16[256,512]{1,0:T(8,128)(2,1)S(1)} %collective-permute-done.27.refs_2_), channel_id=1, source_target_pairs={{0,1},{1,0},{2,3},{3,2},{4,5},{5,4},{6,7},{7,6},{8,9},{9,8},{10,11... | collective-permute-start | bytes 786440 | tf_op jit(solution)/shard_map/ppermute | solution.py:20
  84.9 7.5 %collective-permute-start.30 = (s16[144,512]{1,0:T(8,128)(2,1)S(1)}, s16[144,512]{1,0:T(8,128)(2,1)S(1)}, u32[]{:S(2)}, u32[]{:S(2)}) collective-permute-start(s16[144,512]{1,0:T(8,128)(2,1)S(1)} %get-tuple-element.124), channel_id=1, source_target_pairs={{0,128},{32,160},{64,192},{96,224},{128,0},{160,32},{192,64},{224,... | collective-permute-start | bytes 442376 | tf_op jit(solution)/shard_map/ppermute | solution.py:20
  88.2 7.4 %collective-permute-start.31 = (s16[144,512]{1,0:T(8,128)(2,1)S(1)}, s16[144,512]{1,0:T(8,128)(2,1)S(1)}, u32[]{:S(2)}, u32[]{:S(2)}) collective-permute-start(s16[144,512]{1,0:T(8,128)(2,1)S(1)} %get-tuple-element.125), channel_id=1, source_target_pairs={{0,192},{32,224},{64,128},{96,160},{128,64},{160,96},{192,0},{224,... | collective-permute-start | bytes 442376 | tf_op jit(solution)/shard_map/ppermute | solution.py:20
  89.3 6.7 %collective-permute-start.32 = (s16[144,512]{1,0:T(8,128)(2,1)S(1)}, s16[144,512]{1,0:T(8,128)(2,1)S(1)}, u32[]{:S(2)}, u32[]{:S(2)}) collective-permute-start(s16[144,512]{1,0:T(8,128)(2,1)S(1)} %get-tuple-element.126), channel_id=1, source_target_pairs={{0,64},{32,96},{64,0},{96,32},{128,192},{160,224},{192,128},{224,1... | collective-permute-start | bytes 442376 | tf_op jit(solution)/shard_map/ppermute | solution.py:20
  96.7 8.5 %collective-permute-start.33 = (s16[80,512]{1,0:T(8,128)(2,1)S(1)}, s16[80,512]{1,0:T(8,128)(2,1)S(1)}, u32[]{:S(2)}, u32[]{:S(2)}) collective-permute-start(s16[80,512]{1,0:T(8,128)(2,1)S(1)} %get-tuple-element.128), channel_id=1, source_target_pairs={{0,32},{32,0},{64,96},{96,64},{128,160},{160,128},{192,224},{224,1... | collective-permute-start | bytes 245768 | tf_op jit(solution)/shard_map/ppermute | solution.py:20

commit v11 on v10

--- a/solution.py
+++ b/solution.py
@@ -301,10 +301,9 @@
     grams = gram_step(here, weights, [near[0], far[0]], [(0, 1, 0), (0, 3, 0)], grams)
     grams = gram_step(here, weights, [near[1], far[1], across[0]], [(1, 1, 0), (1, 3, 0), (0, 2, 0)], grams)
     mine, theirs = grams
-    theirs, last = lax.optimization_barrier((theirs, across[1]))
-    other = xor_permute(last, "pw_c", 1)
+    other = xor_permute(across[1], "pw_c", 1)
     theirs = xor_permute(theirs, "pw_c", 1)
-    mine = gram_step(here, weights[:1], [last], [(1, 2, 0)], [mine])[0]
+    mine = gram_step(here, weights[:1], [across[1]], [(1, 2, 0)], [mine], 9_000_000_000)[0]
 
     part = width // 4
     own, *out = call(
@@ -316,6 +315,7 @@
         weights[0],
         other,
         specs=[SMEM] + [VMEM] * 4,
+        cost=0,
         scratch=[pltpu.VMEM((width, width), F32)],
     )
     came = [xor_permute(value, "pair", 2 * mask) for mask, value in zip(Y_ORDER, out)]

time: 107 us -> 106 us (level)
  waiting for transfers between devices: 41.3 us -> 40.2 us
    ppermute x34, waiting for transfers between devices: 41.3 us -> 40.2 us  [xor_permute(): return lax.ppermute(value, axis, [(i, i ^ mask) for i in range(count)])]
where the time goes in v11:
time: 106 us; the launch traced here: 104 us
  starting transfers between devices  43.1 us (41%)
  waiting for transfers between devices  40.2 us (38%)
  Pallas kernels  19 us (18%)
  local copies, waits for them, and re-layouts  1.24 us (1%)
    ppermute x34, starting transfers between devices, xor_permute(): return lax.ppermute(value, axis, [(i, i ^ mask) for i in range(count)])  43.1 us
    ppermute x34, waiting for transfers between devices, xor_permute(): return lax.ppermute(value, axis, [(i, i ^ mask) for i in range(count)])  40.2 us
    pallas_call x21, Pallas kernels, call(): pl.pallas_call(kernel, out_shape=[jax.ShapeDtypeStruct(shape, dtype) for...  19 us
  transfers between devices with their start and end apart: 34, of which 22 were waited for; matrix products, arithmetic and copies ran while one was open for 0% of the time, Pallas kernels for 12%

profile of v11, /device:TPU:32, one launch (start us, length us, event | category | flops | bytes accessed | tf_op | source)
XLA Modules:
  0.0 104.4 jit_solution(2129820336909547487)
XLA Ops:
  0.7 1.2 %copy-done = bf16[1024,512]{1,0:T(8,128)(2,1)S(1)} copy-done((bf16[1024,512]{1,0:T(8,128)(2,1)S(1)}, bf16[1024,512]{1,0:T(8,128)(2,1)}, u32[]{:S(2)}) %copy-start) | copy-done | bytes 1048600
  2.0 4.2 %shard_map.73 = (f32[1032,512]{1,0:T(8,128)S(1)}, bf16[3072,1024]{1,0:T(8,128)(2,1)S(1)}, f32[8,128]{1,0:T(8,128)S(1)}) custom-call(s32[4]{0:T(128)S(1)} %pad_add_fusion.refs_0_, f32[1]{0:T(128)S(6)} %copy.8.refs_1_.refs_2_, bf16[4096,1024]{1,0:T(8,128)(2,1)} %refs_2_.2, bf16[1024,512]{1,0:T(8,128)(2,1)S(1)} %copy-done), custom_call_target="tpu_custom_call" | custom-call | flops 1073741824 | bytes 9437204 | tf_op jit(solution)/shard_map/pallas_call | solution.py:35
  6.3 2.3 %shard_map.74 = (f32[1024,512]{1,0:T(8,128)S(1)}, f32[1024,512]{1,0:T(8,128)S(1)}) custom-call(bf16[3072,1024]{1,0:T(8,128)(2,1)S(1)} %get-tuple-element.65.refs_0_, bf16[1024,512]{1,0:T(8,128)(2,1)S(1)} %copy-done, f32[8,128]{1,0:T(8,128)S(1)} %get-tuple-element.66.refs_2_), custom_call_target="tpu_custom_call" | custom-call | flops 2147483648 | bytes 7340032 | tf_op jit(solution)/shard_map/pallas_call | solution.py:35
  8.6 1.8 %collective-permute-done.refs_1_ = f32[1032,512]{1,0:T(8,128)S(1)} collective-permute-done((f32[1032,512]{1,0:T(8,128)S(1)}, f32[1032,512]{1,0:T(8,128)S(1)}, u32[]{:S(2)}, u32[]{:S(2)}) %collective-permute-start) | collective-permute-done | bytes 2113568 | tf_op jit(solution)/shard_map/ppermute | solution.py:20
  10.9 1.6 %collective-permute-start.4 = (s16[272,512]{1,0:T(8,128)(2,1)S(1)}, s16[272,512]{1,0:T(8,128)(2,1)S(1)}, u32[]{:S(2)}, u32[]{:S(2)}) collective-permute-start(s16[272,512]{1,0:T(8,128)(2,1)S(1)} %get-tuple-element.77), channel_id=1, source_target_pairs={{0,8},{8,0},{16,24},{24,16},{1,9},{9,1},{17,25},{25,17},{2,10},{10... | collective-permute-start | bytes 835592 | tf_op jit(solution)/shard_map/ppermute | solution.py:20
  12.5 2.1 %collective-permute-start.5 = (s16[272,512]{1,0:T(8,128)(2,1)S(1)}, s16[272,512]{1,0:T(8,128)(2,1)S(1)}, u32[]{:S(2)}, u32[]{:S(2)}) collective-permute-start(s16[272,512]{1,0:T(8,128)(2,1)S(1)} %get-tuple-element.78), channel_id=1, source_target_pairs={{0,24},{8,16},{16,8},{24,0},{1,25},{9,17},{17,9},{25,1},{2,26},{10... | collective-permute-start | bytes 835592 | tf_op jit(solution)/shard_map/ppermute | solution.py:20
  14.6 1.2 %shard_map.76.refs_0_ = f32[1024,512]{1,0:T(8,128)S(1)} custom-call(bf16[3072,1024]{1,0:T(8,128)(2,1)S(1)} %get-tuple-element.65.refs_0_, bf16[1024,512]{1,0:T(8,128)(2,1)S(1)} %copy-done, f32[8,128]{1,0:T(8,128)S(1)} %get-tuple-element.71.refs_2_), custom_call_target="tpu_custom_call" | custom-call | flops 1073741824 | bytes 7340032 | tf_op jit(solution)/shard_map/pallas_call | solution.py:35
  16.9 1.7 %collective-permute-start.3 = (s16[272,512]{1,0:T(8,128)(2,1)S(1)}, s16[272,512]{1,0:T(8,128)(2,1)S(1)}, u32[]{:S(2)}, u32[]{:S(2)}) collective-permute-start(s16[272,512]{1,0:T(8,128)(2,1)S(1)} %get-tuple-element.75), channel_id=1, source_target_pairs={{0,24},{8,16},{16,8},{24,0},{1,25},{9,17},{17,9},{25,1},{2,26},{10... | collective-permute-start | bytes 835592 | tf_op jit(solution)/shard_map/ppermute | solution.py:20
  18.6 1.9 %collective-permute-done.4.refs_1_ = s16[272,512]{1,0:T(8,128)(2,1)S(1)} collective-permute-done((s16[272,512]{1,0:T(8,128)(2,1)S(1)}, s16[272,512]{1,0:T(8,128)(2,1)S(1)}, u32[]{:S(2)}, u32[]{:S(2)}) %collective-permute-start.4) | collective-permute-done | bytes 278560 | tf_op jit(solution)/shard_map/ppermute | solution.py:20
  20.5 2.7 %collective-permute-done.5.refs_2_ = s16[272,512]{1,0:T(8,128)(2,1)S(1)} collective-permute-done((s16[272,512]{1,0:T(8,128)(2,1)S(1)}, s16[272,512]{1,0:T(8,128)(2,1)S(1)}, u32[]{:S(2)}, u32[]{:S(2)}) %collective-permute-start.5) | collective-permute-done | bytes 278560 | tf_op jit(solution)/shard_map/ppermute | solution.py:20
  23.5 2.2 %collective-permute-start.8 = (s16[144,512]{1,0:T(8,128)(2,1)S(1)}, s16[144,512]{1,0:T(8,128)(2,1)S(1)}, u32[]{:S(2)}, u32[]{:S(2)}) collective-permute-start(s16[144,512]{1,0:T(8,128)(2,1)S(1)} %get-tuple-element.84), channel_id=1, source_target_pairs={{0,24},{8,16},{16,8},{24,0},{1,25},{9,17},{17,9},{25,1},{2,26},{10... | collective-permute-start | bytes 442376 | tf_op jit(solution)/shard_map/ppermute | solution.py:20
  25.9 3.3 %collective-permute-done.3.refs_2_ = s16[272,512]{1,0:T(8,128)(2,1)S(1)} collective-permute-done((s16[272,512]{1,0:T(8,128)(2,1)S(1)}, s16[272,512]{1,0:T(8,128)(2,1)S(1)}, u32[]{:S(2)}, u32[]{:S(2)}) %collective-permute-start.3) | collective-permute-done | bytes 278560 | tf_op jit(solution)/shard_map/ppermute | solution.py:20
  29.5 2.2 %collective-permute-start.6 = (s16[144,512]{1,0:T(8,128)(2,1)S(1)}, s16[144,512]{1,0:T(8,128)(2,1)S(1)}, u32[]{:S(2)}, u32[]{:S(2)}) collective-permute-start(s16[144,512]{1,0:T(8,128)(2,1)S(1)} %get-tuple-element.81), channel_id=1, source_target_pairs={{0,24},{8,16},{16,8},{24,0},{1,25},{9,17},{17,9},{25,1},{2,26},{10... | collective-permute-start | bytes 442376 | tf_op jit(solution)/shard_map/ppermute | solution.py:20
  31.6 0.7 shard_map.80
  32.4 2.0 %collective-permute-start.13 = (s16[80,512]{1,0:T(8,128)(2,1)S(1)}, s16[80,512]{1,0:T(8,128)(2,1)S(1)}, u32[]{:S(2)}, u32[]{:S(2)}) collective-permute-start(s16[80,512]{1,0:T(8,128)(2,1)S(1)} %get-tuple-element.95), channel_id=1, source_target_pairs={{0,6},{2,4},{4,2},{6,0},{1,7},{3,5},{5,3},{7,1},{8,14},{10,12},{12... | collective-permute-start | bytes 245768 | tf_op jit(solution)/shard_map/ppermute | solution.py:20
  34.4 1.5 %collective-permute-start.14 = (s16[80,512]{1,0:T(8,128)(2,1)S(1)}, s16[80,512]{1,0:T(8,128)(2,1)S(1)}, u32[]{:S(2)}, u32[]{:S(2)}) collective-permute-start(s16[80,512]{1,0:T(8,128)(2,1)S(1)} %get-tuple-element.96), channel_id=1, source_target_pairs={{0,4},{2,6},{4,0},{6,2},{1,5},{3,7},{5,1},{7,3},{8,12},{10,14},{12... | collective-permute-start | bytes 245768 | tf_op jit(solution)/shard_map/ppermute | solution.py:20
  35.9 1.4 %collective-permute-start.15 = (s16[80,512]{1,0:T(8,128)(2,1)S(1)}, s16[80,512]{1,0:T(8,128)(2,1)S(1)}, u32[]{:S(2)}, u32[]{:S(2)}) collective-permute-start(s16[80,512]{1,0:T(8,128)(2,1)S(1)} %get-tuple-element.97), channel_id=1, source_target_pairs={{0,2},{2,0},{4,6},{6,4},{1,3},{3,1},{5,7},{7,5},{8,10},{10,8},{12,... | collective-permute-start | bytes 245768 | tf_op jit(solution)/shard_map/ppermute | solution.py:20
  37.2 0.7 shard_map.81
  38.0 1.7 %collective-permute-start.10 = (s16[80,512]{1,0:T(8,128)(2,1)S(1)}, s16[80,512]{1,0:T(8,128)(2,1)S(1)}, u32[]{:S(2)}, u32[]{:S(2)}) collective-permute-start(s16[80,512]{1,0:T(8,128)(2,1)S(1)} %get-tuple-element.91), channel_id=1, source_target_pairs={{0,6},{2,4},{4,2},{6,0},{1,7},{3,5},{5,3},{7,1},{8,14},{10,12},{12... | collective-permute-start | bytes 245768 | tf_op jit(solution)/shard_map/ppermute | solution.py:20
  39.7 1.6 %collective-permute-start.11 = (s16[80,512]{1,0:T(8,128)(2,1)S(1)}, s16[80,512]{1,0:T(8,128)(2,1)S(1)}, u32[]{:S(2)}, u32[]{:S(2)}) collective-permute-start(s16[80,512]{1,0:T(8,128)(2,1)S(1)} %get-tuple-element.92), channel_id=1, source_target_pairs={{0,4},{2,6},{4,0},{6,2},{1,5},{3,7},{5,1},{7,3},{8,12},{10,14},{12... | collective-permute-start | bytes 245768 | tf_op jit(solution)/shard_map/ppermute | solution.py:20
  42.7 0.9 shard_map.82
  43.5 2.7 %collective-permute-done.14.refs_2_ = s16[80,512]{1,0:T(8,128)(2,1)S(1)} collective-permute-done((s16[80,512]{1,0:T(8,128)(2,1)S(1)}, s16[80,512]{1,0:T(8,128)(2,1)S(1)}, u32[]{:S(2)}, u32[]{:S(2)}) %collective-permute-start.14) | collective-permute-done | bytes 81952 | tf_op jit(solution)/shard_map/ppermute | solution.py:20
  46.4 4.0 %collective-permute-start.20 = (bf16[64,512]{1,0:T(8,128)(2,1)S(1)}, bf16[64,512]{1,0:T(8,128)(2,1)S(1)}, u32[]{:S(2)}, u32[]{:S(2)}) collective-permute-start(bf16[64,512]{1,0:T(8,128)(2,1)S(1)} %get-tuple-element.100.refs_0_), channel_id=1, source_target_pairs={{0,4},{2,6},{4,0},{6,2},{1,5},{3,7},{5,1},{7,3},{8,12},{10,14},{12... | collective-permute-start | bytes 196616 | tf_op jit(solution)/shard_map/ppermute | solution.py:20
  50.4 1.4 %collective-permute-start.19 = (bf16[64,512]{1,0:T(8,128)(2,1)S(1)}, bf16[64,512]{1,0:T(8,128)(2,1)S(1)}, u32[]{:S(2)}, u32[]{:S(2)}) collective-permute-start(bf16[64,512]{1,0:T(8,128)(2,1)S(1)} %get-tuple-element.100.refs_0_), channel_id=1, source_target_pairs={{0,2},{2,0},{4,6},{6,4},{1,3},{3,1},{5,7},{7,5},{8,10},{10,8},{12,... | collective-permute-start | bytes 196616 | tf_op jit(solution)/shard_map/ppermute | solution.py:20
  51.9 1.6 %collective-permute-start.18 = (bf16[64,512]{1,0:T(8,128)(2,1)S(1)}, bf16[64,512]{1,0:T(8,128)(2,1)S(1)}, u32[]{:S(2)}, u32[]{:S(2)}) collective-permute-start(bf16[64,512]{1,0:T(8,128)(2,1)S(1)} %get-tuple-element.99.refs_0_), channel_id=1, source_target_pairs={{0,6},{2,4},{4,2},{6,0},{1,7},{3,5},{5,3},{7,1},{8,14},{10,12},{12... | collective-permute-start | bytes 196616 | tf_op jit(solution)/shard_map/ppermute | solution.py:20
  53.4 1.5 %collective-permute-start.17 = (bf16[64,512]{1,0:T(8,128)(2,1)S(1)}, bf16[64,512]{1,0:T(8,128)(2,1)S(1)}, u32[]{:S(2)}, u32[]{:S(2)}) collective-permute-start(bf16[64,512]{1,0:T(8,128)(2,1)S(1)} %get-tuple-element.99.refs_0_), channel_id=1, source_target_pairs={{0,4},{2,6},{4,0},{6,2},{1,5},{3,7},{5,1},{7,3},{8,12},{10,14},{12... | collective-permute-start | bytes 196616 | tf_op jit(solution)/shard_map/ppermute | solution.py:20
  55.0 1.4 %collective-permute-start.16 = (bf16[64,512]{1,0:T(8,128)(2,1)S(1)}, bf16[64,512]{1,0:T(8,128)(2,1)S(1)}, u32[]{:S(2)}, u32[]{:S(2)}) collective-permute-start(bf16[64,512]{1,0:T(8,128)(2,1)S(1)} %get-tuple-element.99.refs_0_), channel_id=1, source_target_pairs={{0,2},{2,0},{4,6},{6,4},{1,3},{3,1},{5,7},{7,5},{8,10},{10,8},{12,... | collective-permute-start | bytes 196616 | tf_op jit(solution)/shard_map/ppermute | solution.py:20
  56.5 0.7 collective-permute-done.19.refs_1_
  57.2 1.7 %collective-permute-start.26 = (bf16[256,512]{1,0:T(8,128)(2,1)S(1)}, bf16[256,512]{1,0:T(8,128)(2,1)S(1)}, u32[]{:S(2)}, u32[]{:S(2)}) collective-permute-start(bf16[256,512]{1,0:T(8,128)(2,1)S(1)} %get-tuple-element.106.refs_3_), channel_id=1, source_target_pairs={{0,24},{8,16},{16,8},{24,0},{1,25},{9,17},{17,9},{25,1},{2,26},{10... | collective-permute-start | bytes 786440 | tf_op jit(solution)/shard_map/ppermute | solution.py:20
  60.0 2.0 %collective-permute-start.23 = (bf16[256,512]{1,0:T(8,128)(2,1)S(1)}, bf16[256,512]{1,0:T(8,128)(2,1)S(1)}, u32[]{:S(2)}, u32[]{:S(2)}) collective-permute-start(bf16[256,512]{1,0:T(8,128)(2,1)S(1)} %shard_map.86.refs_4_), channel_id=1, source_target_pairs={{0,24},{8,16},{16,8},{24,0},{1,25},{9,17},{17,9},{25,1},{2,26},{10... | collective-permute-start | bytes 786440 | tf_op jit(solution)/shard_map/ppermute | solution.py:20
  62.5 1.3 %shard_map.87 = (f32[512,512]{1,0:T(8,128)S(1)}, f32[512,512]{1,0:T(8,128)S(1)}) custom-call(s32[4]{0:T(128)S(1)} %pad_add_fusion.refs_0_, f32[32,128]{1,0:T(8,128)S(1)} %get-tuple-element.89.refs_4_.refs_1_.refs_3_, f32[32,128]{1,0:T(8,128)S(1)} %get-tuple-element.104.refs_2_, bf16[256,512]{1,0:T(8,128)(2,1)S(1)} %get-tuple-element.106.refs_3_, ...), custom_call_target="tpu_custom_call" | custom-call | flops 3536870912 | bytes 557072 | tf_op jit(solution)/shard_map/pallas_call | solution.py:35
  63.8 3.4 %collective-permute-done.26.refs_4_ = bf16[256,512]{1,0:T(8,128)(2,1)S(1)} collective-permute-done((bf16[256,512]{1,0:T(8,128)(2,1)S(1)}, bf16[256,512]{1,0:T(8,128)(2,1)S(1)}, u32[]{:S(2)}, u32[]{:S(2)}) %collective-permute-start.26) | collective-permute-done | bytes 262176 | tf_op jit(solution)/shard_map/ppermute | solution.py:20
  67.2 0.9 collective-permute-done.25.refs_3_
  68.1 1.3 %shard_map.88 = (f32[512,512]{1,0:T(8,128)S(1)}, f32[512,512]{1,0:T(8,128)S(1)}) custom-call(s32[4]{0:T(128)S(1)} %pad_add_fusion.refs_0_, f32[32,128]{1,0:T(8,128)S(1)} %get-tuple-element.89.refs_4_.refs_1_.refs_3_, f32[32,128]{1,0:T(8,128)S(1)} %get-tuple-element.104.refs_2_, bf16[256,512]{1,0:T(8,128)(2,1)S(1)} %collective-permute-done.25.refs_3_, ...), custom_call_target="tpu_custom_call" | custom-call | flops 536870912 | bytes 2654224 | tf_op jit(solution)/shard_map/pallas_call | solution.py:35
  70.0 3.3 %collective-permute-done.22.refs_3_ = bf16[256,512]{1,0:T(8,128)(2,1)S(1)} collective-permute-done((bf16[256,512]{1,0:T(8,128)(2,1)S(1)}, bf16[256,512]{1,0:T(8,128)(2,1)S(1)}, u32[]{:S(2)}, u32[]{:S(2)}) %collective-permute-start.22) | collective-permute-done | bytes 262176 | tf_op jit(solution)/shard_map/ppermute | solution.py:20
  73.3 1.3 %collective-permute-start.24 = (bf16[256,512]{1,0:T(8,128)(2,1)S(1)}, bf16[256,512]{1,0:T(8,128)(2,1)S(1)}, u32[]{:S(2)}, u32[]{:S(2)}) collective-permute-start(bf16[256,512]{1,0:T(8,128)(2,1)S(1)} %collective-permute-done.22.refs_3_), channel_id=1, source_target_pairs={{0,24},{8,16},{16,8},{24,0},{1,25},{9,17},{17,9},{25,1},{2,26},{10... | collective-permute-start | bytes 786440 | tf_op jit(solution)/shard_map/ppermute | solution.py:20
  74.6 1.5 %collective-permute-done.27.refs_5_ = bf16[256,512]{1,0:T(8,128)(2,1)S(1)} collective-permute-done((bf16[256,512]{1,0:T(8,128)(2,1)S(1)}, bf16[256,512]{1,0:T(8,128)(2,1)S(1)}, u32[]{:S(2)}, u32[]{:S(2)}) %collective-permute-start.27) | collective-permute-done | bytes 262176 | tf_op jit(solution)/shard_map/ppermute | solution.py:20
  76.1 1.6 %shard_map.89 = (f32[512,512]{1,0:T(8,128)S(1)}, f32[512,512]{1,0:T(8,128)S(1)}) custom-call(s32[4]{0:T(128)S(1)} %pad_add_fusion.refs_0_, f32[32,128]{1,0:T(8,128)S(1)} %get-tuple-element.89.refs_4_.refs_1_.refs_3_, f32[32,128]{1,0:T(8,128)S(1)} %get-tuple-element.104.refs_2_, bf16[256,512]{1,0:T(8,128)(2,1)S(1)} %collective-permute-done.22.refs_3_, ...), custom_call_target="tpu_custom_call" | custom-call | flops 805306368 | bytes 2916368 | tf_op jit(solution)/shard_map/pallas_call | solution.py:35
  77.8 3.1 %collective-permute-done.24.refs_2_ = bf16[256,512]{1,0:T(8,128)(2,1)S(1)} collective-permute-done((bf16[256,512]{1,0:T(8,128)(2,1)S(1)}, bf16[256,512]{1,0:T(8,128)(2,1)S(1)}, u32[]{:S(2)}, u32[]{:S(2)}) %collective-permute-start.24) | collective-permute-done | bytes 262176 | tf_op jit(solution)/shard_map/ppermute | solution.py:20
  80.9 0.9 shard_map.90.refs_1_
  82.4 1.0 shard_map.91
  83.4 3.3 %collective-permute-start.30 = (s16[144,512]{1,0:T(8,128)(2,1)S(1)}, s16[144,512]{1,0:T(8,128)(2,1)S(1)}, u32[]{:S(2)}, u32[]{:S(2)}) collective-permute-start(s16[144,512]{1,0:T(8,128)(2,1)S(1)} %get-tuple-element.120), channel_id=1, source_target_pairs={{0,128},{32,160},{64,192},{96,224},{128,0},{160,32},{192,64},{224,... | collective-permute-start | bytes 442376 | tf_op jit(solution)/shard_map/ppermute | solution.py:20
  86.7 1.1 %collective-permute-start.31 = (s16[144,512]{1,0:T(8,128)(2,1)S(1)}, s16[144,512]{1,0:T(8,128)(2,1)S(1)}, u32[]{:S(2)}, u32[]{:S(2)}) collective-permute-start(s16[144,512]{1,0:T(8,128)(2,1)S(1)} %get-tuple-element.121), channel_id=1, source_target_pairs={{0,192},{32,224},{64,128},{96,160},{128,64},{160,96},{192,0},{224,... | collective-permute-start | bytes 442376 | tf_op jit(solution)/shard_map/ppermute | solution.py:20
  87.8 3.2 %collective-permute-done.30.refs_2_ = s16[144,512]{1,0:T(8,128)(2,1)S(1)} collective-permute-done((s16[144,512]{1,0:T(8,128)(2,1)S(1)}, s16[144,512]{1,0:T(8,128)(2,1)S(1)}, u32[]{:S(2)}, u32[]{:S(2)}) %collective-permute-start.30) | collective-permute-done | bytes 147488 | tf_op jit(solution)/shard_map/ppermute | solution.py:20
  91.0 3.1 %collective-permute-done.31.refs_3_ = s16[144,512]{1,0:T(8,128)(2,1)S(1)} collective-permute-done((s16[144,512]{1,0:T(8,128)(2,1)S(1)}, s16[144,512]{1,0:T(8,128)(2,1)S(1)}, u32[]{:S(2)}, u32[]{:S(2)}) %collective-permute-start.31) | collective-permute-done | bytes 147488 | tf_op jit(solution)/shard_map/ppermute | solution.py:20
  94.4 0.8 shard_map.92
  95.2 3.7 %collective-permute-start.33 = (s16[80,512]{1,0:T(8,128)(2,1)S(1)}, s16[80,512]{1,0:T(8,128)(2,1)S(1)}, u32[]{:S(2)}, u32[]{:S(2)}) collective-permute-start(s16[80,512]{1,0:T(8,128)(2,1)S(1)} %get-tuple-element.124), channel_id=1, source_target_pairs={{0,32},{32,0},{64,96},{96,64},{128,160},{160,128},{192,224},{224,1... | collective-permute-start | bytes 245768 | tf_op jit(solution)/shard_map/ppermute | solution.py:20
  99.0 4.8 %collective-permute-done.33.refs_1_ = s16[80,512]{1,0:T(8,128)(2,1)S(1)} collective-permute-done((s16[80,512]{1,0:T(8,128)(2,1)S(1)}, s16[80,512]{1,0:T(8,128)(2,1)S(1)}, u32[]{:S(2)}, u32[]{:S(2)}) %collective-permute-start.33) | collective-permute-done | bytes 81952 | tf_op jit(solution)/shard_map/ppermute | solution.py:20
  (53 shorter events, 8.1 us)
Async XLA Ops:
  0.7 1.2 %copy-start = (bf16[1024,512]{1,0:T(8,128)(2,1)S(1)}, bf16[1024,512]{1,0:T(8,128)(2,1)}, u32[]{:S(2)}) copy-start(bf16[1024,512]{1,0:T(8,128)(2,1)} %refs_1_.5) | copy-start | bytes 3145732
  6.2 4.3 %collective-permute-start = (f32[1032,512]{1,0:T(8,128)S(1)}, f32[1032,512]{1,0:T(8,128)S(1)}, u32[]{:S(2)}, u32[]{:S(2)}) collective-permute-start(f32[1032,512]{1,0:T(8,128)S(1)} %get-tuple-element.68), channel_id=1, source_target_pairs={{0,1},{1,0},{2,3},{3,2},{4,5},{5,4},{6,7},{7,6},{8,9},{9,8},{10,11... | collective-permute-start | bytes 6340616 | tf_op jit(solution)/shard_map/ppermute | solution.py:20
  10.4 5.4 %collective-permute-start.1 = (f32[1024,512]{1,0:T(8,128)S(1)}, f32[1024,512]{1,0:T(8,128)S(1)}, u32[]{:S(2)}, u32[]{:S(2)}) collective-permute-start(f32[1024,512]{1,0:T(8,128)S(1)} %get-tuple-element.72), channel_id=1, source_target_pairs={{0,1},{1,0},{2,3},{3,2},{4,5},{5,4},{6,7},{7,6},{8,9},{9,8},{10,11... | collective-permute-start | bytes 6291464 | tf_op jit(solution)/shard_map/ppermute | solution.py:20
  10.9 9.6 %collective-permute-start.4 = (s16[272,512]{1,0:T(8,128)(2,1)S(1)}, s16[272,512]{1,0:T(8,128)(2,1)S(1)}, u32[]{:S(2)}, u32[]{:S(2)}) collective-permute-start(s16[272,512]{1,0:T(8,128)(2,1)S(1)} %get-tuple-element.77), channel_id=1, source_target_pairs={{0,8},{8,0},{16,24},{24,16},{1,9},{9,1},{17,25},{25,17},{2,10},{10... | collective-permute-start | bytes 835592 | tf_op jit(solution)/shard_map/ppermute | solution.py:20
  12.5 10.7 %collective-permute-start.5 = (s16[272,512]{1,0:T(8,128)(2,1)S(1)}, s16[272,512]{1,0:T(8,128)(2,1)S(1)}, u32[]{:S(2)}, u32[]{:S(2)}) collective-permute-start(s16[272,512]{1,0:T(8,128)(2,1)S(1)} %get-tuple-element.78), channel_id=1, source_target_pairs={{0,24},{8,16},{16,8},{24,0},{1,25},{9,17},{17,9},{25,1},{2,26},{10... | collective-permute-start | bytes 835592 | tf_op jit(solution)/shard_map/ppermute | solution.py:20
  16.2 9.7 %collective-permute-start.2 = (s16[272,512]{1,0:T(8,128)(2,1)S(1)}, s16[272,512]{1,0:T(8,128)(2,1)S(1)}, u32[]{:S(2)}, u32[]{:S(2)}) collective-permute-start(s16[272,512]{1,0:T(8,128)(2,1)S(1)} %get-tuple-element.74), channel_id=1, source_target_pairs={{0,8},{8,0},{16,24},{24,16},{1,9},{9,1},{17,25},{25,17},{2,10},{10... | collective-permute-start | bytes 835592 | tf_op jit(solution)/shard_map/ppermute | solution.py:20
  16.9 12.3 %collective-permute-start.3 = (s16[272,512]{1,0:T(8,128)(2,1)S(1)}, s16[272,512]{1,0:T(8,128)(2,1)S(1)}, u32[]{:S(2)}, u32[]{:S(2)}) collective-permute-start(s16[272,512]{1,0:T(8,128)(2,1)S(1)} %get-tuple-element.75), channel_id=1, source_target_pairs={{0,24},{8,16},{16,8},{24,0},{1,25},{9,17},{17,9},{25,1},{2,26},{10... | collective-permute-start | bytes 835592 | tf_op jit(solution)/shard_map/ppermute | solution.py:20
  23.2 19.4 %copy-start.1 = (s32[4096]{0:T(1024)S(1)}, s32[4096]{0:T(1024)}, u32[]{:S(2)}) copy-start(s32[4096]{0:T(1024)} %param.12) | copy-start | bytes 49156
  23.2 19.4 %copy-start.2 = (s32[4096]{0:T(1024)S(1)}, s32[4096]{0:T(1024)}, u32[]{:S(2)}) copy-start(s32[4096]{0:T(1024)} %param.11) | copy-start | bytes 49156
  23.2 19.4 %copy-start.3 = (f32[2048]{0:T(1024)S(1)}, f32[2048]{0:T(1024)}, u32[]{:S(2)}) copy-start(f32[2048]{0:T(1024)} %param.10) | copy-start | bytes 24580
  23.2 19.4 %copy-start.4 = (f32[16]{0:T(128)S(1)}, f32[16]{0:T(128)}, u32[]{:S(2)}) copy-start(f32[16]{0:T(128)} %refs_1_.6) | copy-start | bytes 196
  23.5 8.2 %collective-permute-start.8 = (s16[144,512]{1,0:T(8,128)(2,1)S(1)}, s16[144,512]{1,0:T(8,128)(2,1)S(1)}, u32[]{:S(2)}, u32[]{:S(2)}) collective-permute-start(s16[144,512]{1,0:T(8,128)(2,1)S(1)} %get-tuple-element.84), channel_id=1, source_target_pairs={{0,24},{8,16},{16,8},{24,0},{1,25},{9,17},{17,9},{25,1},{2,26},{10... | collective-permute-start | bytes 442376 | tf_op jit(solution)/shard_map/ppermute | solution.py:20
  25.7 6.0 %collective-permute-start.9 = (s16[144,512]{1,0:T(8,128)(2,1)S(1)}, s16[144,512]{1,0:T(8,128)(2,1)S(1)}, u32[]{:S(2)}, u32[]{:S(2)}) collective-permute-start(s16[144,512]{1,0:T(8,128)(2,1)S(1)} %get-tuple-element.85), channel_id=1, source_target_pairs={{0,8},{8,0},{16,24},{24,16},{1,9},{9,1},{17,25},{25,17},{2,10},{10... | collective-permute-start | bytes 442376 | tf_op jit(solution)/shard_map/ppermute | solution.py:20
  29.5 7.8 %collective-permute-start.6 = (s16[144,512]{1,0:T(8,128)(2,1)S(1)}, s16[144,512]{1,0:T(8,128)(2,1)S(1)}, u32[]{:S(2)}, u32[]{:S(2)}) collective-permute-start(s16[144,512]{1,0:T(8,128)(2,1)S(1)} %get-tuple-element.81), channel_id=1, source_target_pairs={{0,24},{8,16},{16,8},{24,0},{1,25},{9,17},{17,9},{25,1},{2,26},{10... | collective-permute-start | bytes 442376 | tf_op jit(solution)/shard_map/ppermute | solution.py:20
  31.6 5.6 %collective-permute-start.7 = (s16[144,512]{1,0:T(8,128)(2,1)S(1)}, s16[144,512]{1,0:T(8,128)(2,1)S(1)}, u32[]{:S(2)}, u32[]{:S(2)}) collective-permute-start(s16[144,512]{1,0:T(8,128)(2,1)S(1)} %get-tuple-element.82), channel_id=1, source_target_pairs={{0,8},{8,0},{16,24},{24,16},{1,9},{9,1},{17,25},{25,17},{2,10},{10... | collective-permute-start | bytes 442376 | tf_op jit(solution)/shard_map/ppermute | solution.py:20
  32.4 9.6 %collective-permute-start.13 = (s16[80,512]{1,0:T(8,128)(2,1)S(1)}, s16[80,512]{1,0:T(8,128)(2,1)S(1)}, u32[]{:S(2)}, u32[]{:S(2)}) collective-permute-start(s16[80,512]{1,0:T(8,128)(2,1)S(1)} %get-tuple-element.95), channel_id=1, source_target_pairs={{0,6},{2,4},{4,2},{6,0},{1,7},{3,5},{5,3},{7,1},{8,14},{10,12},{12... | collective-permute-start | bytes 245768 | tf_op jit(solution)/shard_map/ppermute | solution.py:20
  34.4 11.9 %collective-permute-start.14 = (s16[80,512]{1,0:T(8,128)(2,1)S(1)}, s16[80,512]{1,0:T(8,128)(2,1)S(1)}, u32[]{:S(2)}, u32[]{:S(2)}) collective-permute-start(s16[80,512]{1,0:T(8,128)(2,1)S(1)} %get-tuple-element.96), channel_id=1, source_target_pairs={{0,4},{2,6},{4,0},{6,2},{1,5},{3,7},{5,1},{7,3},{8,12},{10,14},{12... | collective-permute-start | bytes 245768 | tf_op jit(solution)/shard_map/ppermute | solution.py:20
  35.9 10.4 %collective-permute-start.15 = (s16[80,512]{1,0:T(8,128)(2,1)S(1)}, s16[80,512]{1,0:T(8,128)(2,1)S(1)}, u32[]{:S(2)}, u32[]{:S(2)}) collective-permute-start(s16[80,512]{1,0:T(8,128)(2,1)S(1)} %get-tuple-element.97), channel_id=1, source_target_pairs={{0,2},{2,0},{4,6},{6,4},{1,3},{3,1},{5,7},{7,5},{8,10},{10,8},{12,... | collective-permute-start | bytes 245768 | tf_op jit(solution)/shard_map/ppermute | solution.py:20
  38.0 12.4 %collective-permute-start.10 = (s16[80,512]{1,0:T(8,128)(2,1)S(1)}, s16[80,512]{1,0:T(8,128)(2,1)S(1)}, u32[]{:S(2)}, u32[]{:S(2)}) collective-permute-start(s16[80,512]{1,0:T(8,128)(2,1)S(1)} %get-tuple-element.91), channel_id=1, source_target_pairs={{0,6},{2,4},{4,2},{6,0},{1,7},{3,5},{5,3},{7,1},{8,14},{10,12},{12... | collective-permute-start | bytes 245768 | tf_op jit(solution)/shard_map/ppermute | solution.py:20
  39.7 12.1 %collective-permute-start.11 = (s16[80,512]{1,0:T(8,128)(2,1)S(1)}, s16[80,512]{1,0:T(8,128)(2,1)S(1)}, u32[]{:S(2)}, u32[]{:S(2)}) collective-permute-start(s16[80,512]{1,0:T(8,128)(2,1)S(1)} %get-tuple-element.92), channel_id=1, source_target_pairs={{0,4},{2,6},{4,0},{6,2},{1,5},{3,7},{5,1},{7,3},{8,12},{10,14},{12... | collective-permute-start | bytes 245768 | tf_op jit(solution)/shard_map/ppermute | solution.py:20
  42.0 9.8 %collective-permute-start.12 = (s16[80,512]{1,0:T(8,128)(2,1)S(1)}, s16[80,512]{1,0:T(8,128)(2,1)S(1)}, u32[]{:S(2)}, u32[]{:S(2)}) collective-permute-start(s16[80,512]{1,0:T(8,128)(2,1)S(1)} %get-tuple-element.93), channel_id=1, source_target_pairs={{0,2},{2,0},{4,6},{6,4},{1,3},{3,1},{5,7},{7,5},{8,10},{10,8},{12,... | collective-permute-start | bytes 245768 | tf_op jit(solution)/shard_map/ppermute | solution.py:20
  46.3 8.6 %collective-permute-start.21 = (bf16[64,512]{1,0:T(8,128)(2,1)S(1)}, bf16[64,512]{1,0:T(8,128)(2,1)S(1)}, u32[]{:S(2)}, u32[]{:S(2)}) collective-permute-start(bf16[64,512]{1,0:T(8,128)(2,1)S(1)} %get-tuple-element.100.refs_0_), channel_id=1, source_target_pairs={{0,6},{2,4},{4,2},{6,0},{1,7},{3,5},{5,3},{7,1},{8,14},{10,12},{12... | collective-permute-start | bytes 196616 | tf_op jit(solution)/shard_map/ppermute | solution.py:20
  46.4 10.0 %collective-permute-start.20 = (bf16[64,512]{1,0:T(8,128)(2,1)S(1)}, bf16[64,512]{1,0:T(8,128)(2,1)S(1)}, u32[]{:S(2)}, u32[]{:S(2)}) collective-permute-start(bf16[64,512]{1,0:T(8,128)(2,1)S(1)} %get-tuple-element.100.refs_0_), channel_id=1, source_target_pairs={{0,4},{2,6},{4,0},{6,2},{1,5},{3,7},{5,1},{7,3},{8,12},{10,14},{12... | collective-permute-start | bytes 196616 | tf_op jit(solution)/shard_map/ppermute | solution.py:20
  50.4 6.8 %collective-permute-start.19 = (bf16[64,512]{1,0:T(8,128)(2,1)S(1)}, bf16[64,512]{1,0:T(8,128)(2,1)S(1)}, u32[]{:S(2)}, u32[]{:S(2)}) collective-permute-start(bf16[64,512]{1,0:T(8,128)(2,1)S(1)} %get-tuple-element.100.refs_0_), channel_id=1, source_target_pairs={{0,2},{2,0},{4,6},{6,4},{1,3},{3,1},{5,7},{7,5},{8,10},{10,8},{12,... | collective-permute-start | bytes 196616 | tf_op jit(solution)/shard_map/ppermute | solution.py:20
  51.9 7.6 %collective-permute-start.18 = (bf16[64,512]{1,0:T(8,128)(2,1)S(1)}, bf16[64,512]{1,0:T(8,128)(2,1)S(1)}, u32[]{:S(2)}, u32[]{:S(2)}) collective-permute-start(bf16[64,512]{1,0:T(8,128)(2,1)S(1)} %get-tuple-element.99.refs_0_), channel_id=1, source_target_pairs={{0,6},{2,4},{4,2},{6,0},{1,7},{3,5},{5,3},{7,1},{8,14},{10,12},{12... | collective-permute-start | bytes 196616 | tf_op jit(solution)/shard_map/ppermute | solution.py:20
  53.4 6.0 %collective-permute-start.17 = (bf16[64,512]{1,0:T(8,128)(2,1)S(1)}, bf16[64,512]{1,0:T(8,128)(2,1)S(1)}, u32[]{:S(2)}, u32[]{:S(2)}) collective-permute-start(bf16[64,512]{1,0:T(8,128)(2,1)S(1)} %get-tuple-element.99.refs_0_), channel_id=1, source_target_pairs={{0,4},{2,6},{4,0},{6,2},{1,5},{3,7},{5,1},{7,3},{8,12},{10,14},{12... | collective-permute-start | bytes 196616 | tf_op jit(solution)/shard_map/ppermute | solution.py:20
  55.0 5.0 %collective-permute-start.16 = (bf16[64,512]{1,0:T(8,128)(2,1)S(1)}, bf16[64,512]{1,0:T(8,128)(2,1)S(1)}, u32[]{:S(2)}, u32[]{:S(2)}) collective-permute-start(bf16[64,512]{1,0:T(8,128)(2,1)S(1)} %get-tuple-element.99.refs_0_), channel_id=1, source_target_pairs={{0,2},{2,0},{4,6},{6,4},{1,3},{3,1},{5,7},{7,5},{8,10},{10,8},{12,... | collective-permute-start | bytes 196616 | tf_op jit(solution)/shard_map/ppermute | solution.py:20
  57.2 10.0 %collective-permute-start.26 = (bf16[256,512]{1,0:T(8,128)(2,1)S(1)}, bf16[256,512]{1,0:T(8,128)(2,1)S(1)}, u32[]{:S(2)}, u32[]{:S(2)}) collective-permute-start(bf16[256,512]{1,0:T(8,128)(2,1)S(1)} %get-tuple-element.106.refs_3_), channel_id=1, source_target_pairs={{0,24},{8,16},{16,8},{24,0},{1,25},{9,17},{17,9},{25,1},{2,26},{10... | collective-permute-start | bytes 786440 | tf_op jit(solution)/shard_map/ppermute | solution.py:20
  59.0 9.1 %collective-permute-start.25 = (bf16[256,512]{1,0:T(8,128)(2,1)S(1)}, bf16[256,512]{1,0:T(8,128)(2,1)S(1)}, u32[]{:S(2)}, u32[]{:S(2)}) collective-permute-start(bf16[256,512]{1,0:T(8,128)(2,1)S(1)} %get-tuple-element.106.refs_3_), channel_id=1, source_target_pairs={{0,8},{8,0},{16,24},{24,16},{1,9},{9,1},{17,25},{25,17},{2,10},{10... | collective-permute-start | bytes 786440 | tf_op jit(solution)/shard_map/ppermute | solution.py:20
  60.0 10.0 %collective-permute-start.23 = (bf16[256,512]{1,0:T(8,128)(2,1)S(1)}, bf16[256,512]{1,0:T(8,128)(2,1)S(1)}, u32[]{:S(2)}, u32[]{:S(2)}) collective-permute-start(bf16[256,512]{1,0:T(8,128)(2,1)S(1)} %shard_map.86.refs_4_), channel_id=1, source_target_pairs={{0,24},{8,16},{16,8},{24,0},{1,25},{9,17},{17,9},{25,1},{2,26},{10... | collective-permute-start | bytes 786440 | tf_op jit(solution)/shard_map/ppermute | solution.py:20
  62.1 11.2 %collective-permute-start.22 = (bf16[256,512]{1,0:T(8,128)(2,1)S(1)}, bf16[256,512]{1,0:T(8,128)(2,1)S(1)}, u32[]{:S(2)}, u32[]{:S(2)}) collective-permute-start(bf16[256,512]{1,0:T(8,128)(2,1)S(1)} %shard_map.86.refs_4_), channel_id=1, source_target_pairs={{0,8},{8,0},{16,24},{24,16},{1,9},{9,1},{17,25},{25,17},{2,10},{10... | collective-permute-start | bytes 786440 | tf_op jit(solution)/shard_map/ppermute | solution.py:20
  68.1 8.0 %collective-permute-start.27 = (bf16[256,512]{1,0:T(8,128)(2,1)S(1)}, bf16[256,512]{1,0:T(8,128)(2,1)S(1)}, u32[]{:S(2)}, u32[]{:S(2)}) collective-permute-start(bf16[256,512]{1,0:T(8,128)(2,1)S(1)} %collective-permute-done.26.refs_4_), channel_id=1, source_target_pairs={{0,8},{8,0},{16,24},{24,16},{1,9},{9,1},{17,25},{25,17},{2,10},{10... | collective-permute-start | bytes 786440 | tf_op jit(solution)/shard_map/ppermute | solution.py:20
  73.3 7.6 %collective-permute-start.24 = (bf16[256,512]{1,0:T(8,128)(2,1)S(1)}, bf16[256,512]{1,0:T(8,128)(2,1)S(1)}, u32[]{:S(2)}, u32[]{:S(2)}) collective-permute-start(bf16[256,512]{1,0:T(8,128)(2,1)S(1)} %collective-permute-done.22.refs_3_), channel_id=1, source_target_pairs={{0,24},{8,16},{16,8},{24,0},{1,25},{9,17},{17,9},{25,1},{2,26},{10... | collective-permute-start | bytes 786440 | tf_op jit(solution)/shard_map/ppermute | solution.py:20
  77.7 4.7 %collective-permute-start.28 = (f32[512,512]{1,0:T(8,128)S(1)}, f32[512,512]{1,0:T(8,128)S(1)}, u32[]{:S(2)}, u32[]{:S(2)}) collective-permute-start(f32[512,512]{1,0:T(8,128)S(1)} %get-tuple-element.118), channel_id=1, source_target_pairs={{0,1},{1,0},{2,3},{3,2},{4,5},{5,4},{6,7},{7,6},{8,9},{9,8},{10,11... | collective-permute-start | bytes 3145736 | tf_op jit(solution)/shard_map/ppermute | solution.py:20
  80.9 1.5 %collective-permute-start.29 = (bf16[256,512]{1,0:T(8,128)(2,1)S(1)}, bf16[256,512]{1,0:T(8,128)(2,1)S(1)}, u32[]{:S(2)}, u32[]{:S(2)}) collective-permute-start(bf16[256,512]{1,0:T(8,128)(2,1)S(1)} %collective-permute-done.24.refs_2_), channel_id=1, source_target_pairs={{0,1},{1,0},{2,3},{3,2},{4,5},{5,4},{6,7},{7,6},{8,9},{9,8},{10,11... | collective-permute-start | bytes 786440 | tf_op jit(solution)/shard_map/ppermute | solution.py:20
  83.4 7.5 %collective-permute-start.30 = (s16[144,512]{1,0:T(8,128)(2,1)S(1)}, s16[144,512]{1,0:T(8,128)(2,1)S(1)}, u32[]{:S(2)}, u32[]{:S(2)}) collective-permute-start(s16[144,512]{1,0:T(8,128)(2,1)S(1)} %get-tuple-element.120), channel_id=1, source_target_pairs={{0,128},{32,160},{64,192},{96,224},{128,0},{160,32},{192,64},{224,... | collective-permute-start | bytes 442376 | tf_op jit(solution)/shard_map/ppermute | solution.py:20
  86.7 7.4 %collective-permute-start.31 = (s16[144,512]{1,0:T(8,128)(2,1)S(1)}, s16[144,512]{1,0:T(8,128)(2,1)S(1)}, u32[]{:S(2)}, u32[]{:S(2)}) collective-permute-start(s16[144,512]{1,0:T(8,128)(2,1)S(1)} %get-tuple-element.121), channel_id=1, source_target_pairs={{0,192},{32,224},{64,128},{96,160},{128,64},{160,96},{192,0},{224,... | collective-permute-start | bytes 442376 | tf_op jit(solution)/shard_map/ppermute | solution.py:20
  87.8 6.7 %collective-permute-start.32 = (s16[144,512]{1,0:T(8,128)(2,1)S(1)}, s16[144,512]{1,0:T(8,128)(2,1)S(1)}, u32[]{:S(2)}, u32[]{:S(2)}) collective-permute-start(s16[144,512]{1,0:T(8,128)(2,1)S(1)} %get-tuple-element.122), channel_id=1, source_target_pairs={{0,64},{32,96},{64,0},{96,32},{128,192},{160,224},{192,128},{224,1... | collective-permute-start | bytes 442376 | tf_op jit(solution)/shard_map/ppermute | solution.py:20
  95.2 8.5 %collective-permute-start.33 = (s16[80,512]{1,0:T(8,128)(2,1)S(1)}, s16[80,512]{1,0:T(8,128)(2,1)S(1)}, u32[]{:S(2)}, u32[]{:S(2)}) collective-permute-start(s16[80,512]{1,0:T(8,128)(2,1)S(1)} %get-tuple-element.124), channel_id=1, source_target_pairs={{0,32},{32,0},{64,96},{96,64},{128,160},{160,128},{192,224},{224,1... | collective-permute-start | bytes 245768 | tf_op jit(solution)/shard_map/ppermute | solution.py:20
